TPU v7x, 32 devices: a whole 2x2x4 slice. The times are simulated.
32 devices in a mesh: shard: 4 (over z), ctx: 4 (over y, core), tp: 2 (over x).
Axes of the slice: x: 2, y: 2, z: 4, core: 2. Of those that a mesh axis runs over, the one named last changes fastest.
Arguments:
- tokens: bfloat16 [12, 1280, 1024], P('shard', 'ctx'), may hold values from -6 to 6
- cotangent: bfloat16 [12, 1280, 1024], P('shard', 'ctx'), may hold values from -6 to 6
- lengths: int32 [12], P('shard'), may hold values from 257 to 1025, as said below
- ln1_gain: float32 [1024], replicated, may hold values from 0.1 to 1.9
- qkv_weight: bfloat16 [3, 1024, 1024], P(None, 'shard', 'tp'), may hold values from -0.1875 to 0.1875
- attn_gain: float32 [1024], P('tp'), may hold values from 0.1 to 1.9
- proj_weight: bfloat16 [1024, 1024], P('tp', 'shard'), may hold values from -0.1875 to 0.1875
- ln2_gain: float32 [1024], replicated, may hold values from 0.1 to 1.9
- gate_up: bfloat16 [2, 1024, 2730], P(None, 'shard', 'tp'), may hold values from -0.1875 to 0.1875
- ffn_gain: float32 [2730], P('tp'), may hold values from 0.1 to 1.9
- down_weight: bfloat16 [2730, 1024], P('tp', 'shard'), may hold values from -0.109375 to 0.109375
Outputs:
- mixed: bfloat16 [12, 1280, 1024], P('shard', 'ctx')
- grad_tokens: bfloat16 [12, 1280, 1024], P('shard', 'ctx')
- grad_ln1_gain: float32 [1024], replicated
- grad_qkv_weight: float32 [3, 1024, 1024], P(None, 'shard', 'tp')
- grad_attn_gain: float32 [1024], P('tp')
- grad_proj_weight: float32 [1024, 1024], P('tp', 'shard')
- grad_ln2_gain: float32 [1024], replicated
- grad_gate_up: float32 [2, 1024, 2730], P(None, 'shard', 'tp')
- grad_ffn_gain: float32 [2730], P('tp')
- grad_down_weight: float32 [2730, 1024], P('tp', 'shard')
Inputs may be any that keep to these rules, and one draw needn't show every extreme that they name: `lengths`: every image has 257 to 1025 valid tokens; in each aligned block of 3 images at least one has exactly 1025.
All inputs are finite; a program needn't handle non-finite values.
Results may differ from a plain program's by a relative error of at most 0.02.
Values may be sent and summed in bfloat16 or wider, within the bound.
No kernel may reach another device: no remote copies, remote signals or barrier semaphores. Data moves between devices by JAX's collectives and lax.ppermute only.
A program may use at most 320 MiB of HBM per device.

v0:
```python
import math

import jax
import jax.numpy as jnp
from jax import lax
from jax.sharding import PartitionSpec as P

HEAD = 64
GRID = 32
MICRO = 3


epsilon = 1e-06


def rotary_tables(positions, quarter):
    patch_place = jnp.maximum(positions - 1, 0)
    row_pos = (patch_place // GRID).astype(jnp.float32)
    col_pos = (patch_place % GRID).astype(jnp.float32)
    frequency = jnp.exp(jnp.arange(quarter).astype(jnp.float32) * (-math.log(10000.0) / quarter))
    row_angle = row_pos[:, None] * frequency[None, :]
    col_angle = col_pos[:, None] * frequency[None, :]
    return (jnp.cos(row_angle), jnp.sin(row_angle), jnp.cos(col_angle), jnp.sin(col_angle))


def rotate(values, tables, turn_sign):
    cos_row, sin_row, cos_col, sin_col = tables
    quarter = values.shape[-1] // 4
    row_first = values[..., :quarter]
    row_second = values[..., quarter : 2 * quarter]
    col_first = values[..., 2 * quarter : 3 * quarter]
    col_second = values[..., 3 * quarter :]
    return jnp.concatenate(
        [
            row_first * cos_row - turn_sign * row_second * sin_row,
            row_second * cos_row + turn_sign * row_first * sin_row,
            col_first * cos_col - turn_sign * col_second * sin_col,
            col_second * cos_col + turn_sign * col_first * sin_col,
        ],
        axis=-1,
    )


def gather_rows(qkv_weight, proj_weight, gate_up, down_weight):
    return (
        lax.all_gather(qkv_weight, "shard", axis=1, tiled=True),
        lax.all_gather(proj_weight, "shard", axis=1, tiled=True),
        lax.all_gather(gate_up, "shard", axis=1, tiled=True),
        lax.all_gather(down_weight, "shard", axis=1, tiled=True),
    )


def local_norm(values):
    row_mean = jnp.mean(values, axis=-1, keepdims=True)
    centred = values - row_mean
    inv_std = lax.rsqrt(jnp.mean(centred * centred, axis=-1, keepdims=True) + epsilon)
    return (centred * inv_std, inv_std)


def local_norm_back(grad_normed, normed, inv_std, gain_vec):
    scaled = grad_normed * gain_vec
    return inv_std * (
        scaled
        - jnp.mean(scaled, axis=-1, keepdims=True)
        - normed * jnp.mean(scaled * normed, axis=-1, keepdims=True)
    )


def split_norm(values, sums, feature_count):
    row_mean = sums[0][:, None] / feature_count
    variance = sums[1][:, None] / feature_count - row_mean * row_mean
    inv_std = lax.rsqrt(variance + epsilon)
    return ((values - row_mean) * inv_std, inv_std)


def split_norm_back(scaled, normed, inv_std, sums, feature_count):
    return inv_std * (
        scaled - sums[0][:, None] / feature_count - normed * (sums[1][:, None] / feature_count)
    )


def attend(operand):
    queries, key_rows, value_rows, key_valid = operand
    scores = jnp.einsum(
        "qhd,khd->hqk", queries, key_rows, preferred_element_type=jnp.float32
    ) * HEAD ** (-0.5)
    scores = jnp.where(key_valid[None, None, :], scores, -1e30)
    row_max = jnp.max(scores, axis=-1, keepdims=True)
    exponent = jnp.exp(scores - row_max)
    row_total = jnp.sum(exponent, axis=-1, keepdims=True)
    attn_probs = (exponent / row_total).astype(jnp.bfloat16)
    result = jnp.einsum("hqk,khd->qhd", attn_probs, value_rows, preferred_element_type=jnp.float32)
    return (result, row_max + jnp.log(row_total))


def attend_back(operand):
    queries, key_rows, value_rows, key_valid, log_total, grad_heads = operand
    scores = jnp.einsum(
        "qhd,khd->hqk", queries, key_rows, preferred_element_type=jnp.float32
    ) * HEAD ** (-0.5)
    scores = jnp.where(key_valid[None, None, :], scores, -1e30)
    attn_probs = jnp.exp(scores - log_total)
    grad_probs = jnp.einsum(
        "qhd,khd->hqk", grad_heads, value_rows, preferred_element_type=jnp.float32
    )
    row_delta = jnp.sum(attn_probs * grad_probs, axis=-1, keepdims=True)
    grad_scores = (attn_probs * (grad_probs - row_delta)).astype(jnp.bfloat16)
    grad_query = jnp.einsum(
        "hqk,khd->qhd", grad_scores, key_rows, preferred_element_type=jnp.float32
    ) * HEAD ** (-0.5)
    grad_key = jnp.einsum(
        "hqk,qhd->khd", grad_scores, queries, preferred_element_type=jnp.float32
    ) * HEAD ** (-0.5)
    grad_value = jnp.einsum(
        "hqk,qhd->khd",
        attn_probs.astype(jnp.bfloat16),
        grad_heads,
        preferred_element_type=jnp.float32,
    )
    return (grad_query, grad_key, grad_value)


def local(
    tokens,
    cotangent,
    lengths,
    ln1_gain,
    qkv_weight,
    attn_gain,
    proj_weight,
    ln2_gain,
    gate_up,
    ffn_gain,
    down_weight,
):
    image_count = tokens.shape[0]
    per_micro = image_count // MICRO
    local_len = tokens.shape[1]
    model_width = tokens.shape[2]
    attn_width = attn_gain.shape[0]
    ffn_width = ffn_gain.shape[0]
    head_count = attn_width // HEAD
    tp_count = lax.axis_size("tp")
    full_len = local_len * lax.axis_size("ctx")
    micro_tokens = per_micro * local_len
    query_pos = lax.axis_index("ctx") * local_len + jnp.arange(local_len, dtype=jnp.int32)
    key_pos = jnp.arange(full_len, dtype=jnp.int32)
    query_tables = tuple((table[None, :, None, :] for table in rotary_tables(query_pos, HEAD // 4)))
    grad_qkv = jnp.zeros((3, model_width, attn_width), jnp.float32)
    grad_proj = jnp.zeros((attn_width, model_width), jnp.float32)
    grad_pairs = jnp.zeros((2, model_width, ffn_width), jnp.float32)
    grad_down = jnp.zeros((ffn_width, model_width), jnp.float32)
    grad_ln1 = jnp.zeros((model_width,), jnp.float32)
    grad_attn_gain = jnp.zeros((attn_width,), jnp.float32)
    grad_ln2 = jnp.zeros((model_width,), jnp.float32)
    grad_ffn_gain = jnp.zeros((ffn_width,), jnp.float32)
    mixed_parts = []
    input_parts = []
    for micro_index in range(MICRO):
        gathered = gather_rows(qkv_weight, proj_weight, gate_up, down_weight)
        full_qkv, full_proj, full_gate_up, full_down = gathered
        first_image = micro_index * per_micro
        micro_lengths = lengths[first_image : first_image + per_micro]
        inputs = (
            tokens[first_image : first_image + per_micro]
            .astype(jnp.float32)
            .reshape(micro_tokens, model_width)
        )
        normed_one, inv_one = local_norm(inputs)
        entry_one = (normed_one * ln1_gain).astype(jnp.bfloat16)
        projected = jnp.einsum(
            "nd,cde->cne", entry_one, full_qkv, preferred_element_type=jnp.float32
        )
        shaped = projected.reshape(3, per_micro, local_len, head_count, HEAD)
        queries = rotate(shaped[0], query_tables, 1.0).astype(jnp.bfloat16)
        key_rows = rotate(shaped[1], query_tables, 1.0).astype(jnp.bfloat16)
        value_rows = shaped[2].astype(jnp.bfloat16)
        key_all, value_all = (
            lax.all_gather(
                key_rows.reshape(per_micro, local_len, attn_width), "ctx", axis=1, tiled=True
            ),
            lax.all_gather(
                value_rows.reshape(per_micro, local_len, attn_width), "ctx", axis=1, tiled=True
            ),
        )
        key_all = key_all.reshape(per_micro, full_len, head_count, HEAD)
        value_all = value_all.reshape(per_micro, full_len, head_count, HEAD)
        key_valid = key_pos[None, :] < micro_lengths[:, None]
        mixed_heads, log_total = lax.map(attend, (queries, key_all, value_all, key_valid))
        mixed_heads = mixed_heads.reshape(micro_tokens, attn_width)
        attn_sums = lax.psum(
            (jnp.sum(mixed_heads, axis=1), jnp.sum(mixed_heads * mixed_heads, axis=1)), "tp"
        )
        normed_attn, inv_attn = split_norm(mixed_heads, attn_sums, attn_width * tp_count)
        entry_attn = (normed_attn * attn_gain).astype(jnp.bfloat16)
        attn_out = lax.psum(
            jnp.dot(entry_attn, full_proj, preferred_element_type=jnp.float32), "tp"
        )
        residual_one = inputs + attn_out
        normed_two, inv_two = local_norm(residual_one)
        entry_two = (normed_two * ln2_gain).astype(jnp.bfloat16)
        gate_up_pre = jnp.einsum(
            "nd,cde->cne", entry_two, full_gate_up, preferred_element_type=jnp.float32
        )
        gate_pre = gate_up_pre[0]
        up_pre = gate_up_pre[1]
        sigmoid_gate = jax.nn.sigmoid(gate_pre)
        activated = gate_pre * sigmoid_gate
        hidden = activated * up_pre
        ffn_sums = lax.psum((jnp.sum(hidden, axis=1), jnp.sum(hidden * hidden, axis=1)), "tp")
        normed_ffn, inv_ffn = split_norm(hidden, ffn_sums, ffn_width * tp_count)
        entry_ffn = (normed_ffn * ffn_gain).astype(jnp.bfloat16)
        ffn_out = lax.psum(
            jnp.dot(entry_ffn, full_down, preferred_element_type=jnp.float32).astype(jnp.bfloat16),
            "tp",
        ).astype(jnp.float32)
        result = residual_one + ffn_out
        mixed_parts.append(result.astype(jnp.bfloat16).reshape(per_micro, local_len, model_width))
        query_valid = (query_pos[None, :] < micro_lengths[:, None]).astype(jnp.float32)
        grad_out = (
            cotangent[first_image : first_image + per_micro].astype(jnp.float32)
            * query_valid[:, :, None]
        ).reshape(micro_tokens, model_width)
        grad_branch = grad_out.astype(jnp.bfloat16)
        grad_down = grad_down + jnp.einsum(
            "nf,nd->fd", entry_ffn, grad_branch, preferred_element_type=jnp.float32
        )
        grad_entry_ffn = jnp.einsum(
            "nd,fd->nf", grad_branch, full_down, preferred_element_type=jnp.float32
        )
        scaled_ffn = grad_entry_ffn * ffn_gain
        grad_ffn_gain = grad_ffn_gain + jnp.sum(grad_entry_ffn * normed_ffn, axis=0)
        ffn_back = lax.psum(
            (jnp.sum(scaled_ffn, axis=1), jnp.sum(scaled_ffn * normed_ffn, axis=1)), "tp"
        )
        grad_hidden = split_norm_back(
            scaled_ffn, normed_ffn, inv_ffn, ffn_back, ffn_width * tp_count
        )
        grad_gate = grad_hidden * up_pre * sigmoid_gate * (1.0 + gate_pre * (1.0 - sigmoid_gate))
        grad_up = grad_hidden * activated
        grad_stacked = jnp.stack([grad_gate, grad_up]).astype(jnp.bfloat16)
        grad_pairs = grad_pairs + jnp.einsum(
            "nd,cne->cde", entry_two, grad_stacked, preferred_element_type=jnp.float32
        )
        grad_entry_two = lax.psum(
            jnp.einsum(
                "cne,cde->nd", grad_stacked, full_gate_up, preferred_element_type=jnp.float32
            ).astype(jnp.bfloat16),
            "tp",
        ).astype(jnp.float32)
        grad_ln2 = grad_ln2 + jnp.sum(grad_entry_two * normed_two, axis=0)
        grad_residual = grad_out + local_norm_back(grad_entry_two, normed_two, inv_two, ln2_gain)
        grad_attn_branch = grad_residual.astype(jnp.bfloat16)
        grad_proj = grad_proj + jnp.einsum(
            "na,nd->ad", entry_attn, grad_attn_branch, preferred_element_type=jnp.float32
        )
        grad_entry_attn = jnp.einsum(
            "nd,ad->na", grad_attn_branch, full_proj, preferred_element_type=jnp.float32
        )
        scaled_attn = grad_entry_attn * attn_gain
        grad_attn_gain = grad_attn_gain + jnp.sum(grad_entry_attn * normed_attn, axis=0)
        attn_back = lax.psum(
            (jnp.sum(scaled_attn, axis=1), jnp.sum(scaled_attn * normed_attn, axis=1)), "tp"
        )
        grad_heads = split_norm_back(
            scaled_attn, normed_attn, inv_attn, attn_back, attn_width * tp_count
        )
        grad_heads = grad_heads.astype(jnp.bfloat16).reshape(per_micro, local_len, head_count, HEAD)
        grad_query, grad_key_all, grad_value_all = lax.map(
            attend_back, (queries, key_all, value_all, key_valid, log_total, grad_heads)
        )
        grad_key_part, grad_value_part = (
            lax.psum_scatter(
                grad_key_all.reshape(per_micro, full_len, attn_width).astype(jnp.bfloat16),
                "ctx",
                scatter_dimension=1,
                tiled=True,
            ).astype(jnp.float32),
            lax.psum_scatter(
                grad_value_all.reshape(per_micro, full_len, attn_width).astype(jnp.bfloat16),
                "ctx",
                scatter_dimension=1,
                tiled=True,
            ).astype(jnp.float32),
        )
        grad_query_pre = rotate(grad_query, query_tables, -1.0).reshape(micro_tokens, attn_width)
        grad_key_pre = rotate(
            grad_key_part.reshape(per_micro, local_len, head_count, HEAD), query_tables, -1.0
        ).reshape(micro_tokens, attn_width)
        grad_triple = jnp.stack(
            [grad_query_pre, grad_key_pre, grad_value_part.reshape(micro_tokens, attn_width)]
        ).astype(jnp.bfloat16)
        grad_qkv = grad_qkv + jnp.einsum(
            "nd,cne->cde", entry_one, grad_triple, preferred_element_type=jnp.float32
        )
        grad_entry_one = lax.psum(
            jnp.einsum(
                "cne,cde->nd", grad_triple, full_qkv, preferred_element_type=jnp.float32
            ).astype(jnp.bfloat16),
            "tp",
        ).astype(jnp.float32)
        grad_ln1 = grad_ln1 + jnp.sum(grad_entry_one * normed_one, axis=0)
        grad_input = grad_residual + local_norm_back(grad_entry_one, normed_one, inv_one, ln1_gain)
        input_parts.append(
            grad_input.astype(jnp.bfloat16).reshape(per_micro, local_len, model_width)
        )
    shard_qkv, shard_proj, shard_pairs, shard_down = (
        lax.psum_scatter(
            grad_qkv.astype(jnp.bfloat16), "shard", scatter_dimension=1, tiled=True
        ).astype(jnp.float32),
        lax.psum_scatter(
            grad_proj.astype(jnp.bfloat16), "shard", scatter_dimension=1, tiled=True
        ).astype(jnp.float32),
        lax.psum_scatter(
            grad_pairs.astype(jnp.bfloat16), "shard", scatter_dimension=1, tiled=True
        ).astype(jnp.float32),
        lax.psum_scatter(
            grad_down.astype(jnp.bfloat16), "shard", scatter_dimension=1, tiled=True
        ).astype(jnp.float32),
    )
    shard_qkv, shard_proj, shard_pairs, shard_down = (
        lax.psum(shard_qkv.astype(jnp.bfloat16), "ctx").astype(jnp.float32),
        lax.psum(shard_proj.astype(jnp.bfloat16), "ctx").astype(jnp.float32),
        lax.psum(shard_pairs.astype(jnp.bfloat16), "ctx").astype(jnp.float32),
        lax.psum(shard_down.astype(jnp.bfloat16), "ctx").astype(jnp.float32),
    )
    gain_ln1, gain_attn, gain_ln2, gain_ffn = lax.psum(
        (grad_ln1, grad_attn_gain, grad_ln2, grad_ffn_gain), ("shard", "ctx")
    )
    return (
        jnp.concatenate(mixed_parts, axis=0),
        jnp.concatenate(input_parts, axis=0),
        gain_ln1,
        shard_qkv,
        gain_attn,
        shard_proj,
        gain_ln2,
        shard_pairs,
        gain_ffn,
        shard_down,
    )


def solution(mesh):
    placed = (
        P("shard", "ctx", None),
        P("shard", "ctx", None),
        P("shard"),
        P(),
        P(None, "shard", "tp"),
        P("tp"),
        P("tp", "shard"),
        P(),
        P(None, "shard", "tp"),
        P("tp"),
        P("tp", "shard"),
    )
    return jax.shard_map(
        local,
        mesh=mesh,
        in_specs=placed,
        out_specs=(
            P("shard", "ctx", None),
            P("shard", "ctx", None),
            P(),
            P(None, "shard", "tp"),
            P("tp"),
            P("tp", "shard"),
            P(),
            P(None, "shard", "tp"),
            P("tp"),
            P("tp", "shard"),
        ),
        check_vma=False,
    )
```

profile of v0, /device:TPU:0, one launch (start us, length us, event | category | flops | bytes accessed | tf_op | source)
XLA Modules:
  0.0 1307.3 jit_solution(11008836919981282463)
XLA Ops:
  11.5 64.3 %all-gather.11.cloned.1.call-done = bf16[3,1024,512]{2,1,0:T(8,128)(2,1)} async-done(((bf16[3,256,512]{2,1,0:T(8,128)(2,1)}), bf16[3,1024,512]{2,1,0:T(8,128)(2,1)}) %all-gather.11.cloned.1.call-update) | async-done | bytes 3145744 | tf_op jit(solution)/shard_map/all_gather | solution.py:46
  115.6 4.7 copy-done.1
  123.9 7.4 fusion.173
  131.4 8.6 all-gather.29.cloned.1.call-done
  145.0 4.8 copy-done
  151.8 8.4 all-gather.27.cloned.1.call-done
  161.8 7.4 fusion.171
  169.3 10.7 all-gather.25.cloned.1.call-done
  181.6 6.7 fusion.295
  189.8 10.5 all-gather.23.cloned.1.call-done
  202.7 6.9 fusion.1
  218.5 8.0 all-reduce.4
  226.5 5.6 all-gather.17.cloned.1.call-done
  243.3 46.5 %all-gather.21.cloned.1.call-done = bf16[1365,1024]{1,0:T(8,128)(2,1)} async-done(((bf16[1365,256]{1,0:T(8,128)(2,1)}), bf16[1365,1024]{1,0:T(8,128)(2,1)}) %all-gather.21.cloned.1.call-update) | async-done | bytes 2795536 | tf_op jit(solution)/shard_map/all_gather | solution.py:49
  296.7 97.5 %all-reduce.14.cloned.1.call-done = (f32[320,1024]{1,0:T(8,128)}, f32[320,1024]{1,0:T(8,128)}, f32[320,1024]{1,0:T(8,128)}) async-done(((f32[320,1024]{1,0:T(8,128)}, f32[320,1024]{1,0:T(8,128)}, f32[320,1024]{1,0:T(8,128)}), (f32[320,1024]{1,0:T(8,128)}, f32[320,1024]{1,0:T(8,128)}, f32[320,1024]{1,0:T(8,128)})) %all-reduce.14.cloned.1.call-update) | async-done | bytes 3932176 | tf_op jit(solution)/shard_map/psum | solution.py:196
  398.3 101.7 %all-gather.19.cloned.1.call-done = bf16[2,1024,1365]{1,2,0:T(8,128)(2,1)} async-done(((bf16[2,256,1365]{1,2,0:T(8,128)(2,1)}), bf16[2,1024,1365]{1,2,0:T(8,128)(2,1)}) %all-gather.19.cloned.1.call-update) | async-done | bytes 5591056 | tf_op jit(solution)/shard_map/all_gather | solution.py:48
  500.0 4.8 convolution_bitcast_fusion
  515.8 8.4 all-reduce.3
  524.4 8.6 multiply_reduce_fusion.3
  533.0 7.1 all-reduce.2
  546.6 5.2 fusion.170
  561.4 58.1 %all-reduce.20.cloned.1.call-done = (bf16[320,1024]{1,0:T(8,128)(2,1)}, bf16[320,1024]{1,0:T(8,128)(2,1)}, bf16[320,1024]{1,0:T(8,128)(2,1)}) async-done(((bf16[320,1024]{1,0:T(8,128)(2,1)}, bf16[320,1024]{1,0:T(8,128)(2,1)}, bf16[320,1024]{1,0:T(8,128)(2,1)}), (bf16[320,1024]{1,0:T(8,128)(2,1)}, bf16[320,1024]{1,0:T(8,128)(2,1)}, bf16[320,1024]{1,0:T(8,128)(2,1)})) %all-reduce.20.cloned.1.call-update) | async-done | bytes 1966096 | tf_op jit(solution)/shard_map/psum | solution.py:245
  631.6 6.9 all-reduce.1
  644.4 12.0 multiply_reduce_fusion.2
  656.8 6.6 multiply_convert_fusion.2
  666.6 5.7 copy.120
  675.2 10.1 multiply_reduce_fusion
  686.2 9.9 multiply_convert_fusion
  699.2 5.7 copy.124
  707.8 11.5 multiply_reduce_fusion.1
  719.8 6.8 multiply_convert_fusion.1
  729.8 5.7 copy.122
  737.0 8.2 fusion.23
  752.5 4.7 convolution_convert_fusion.1
  765.5 8.1 fusion.26
  776.2 5.3 fusion.137
  800.6 23.0 %reduce-scatter.21.cloned.1.call-done = bf16[1,320,512]{2,1,0:T(8,128)(2,1)} async-done(((bf16[1,1280,512]{2,1,0:T(8,128)(2,1)}), bf16[1,320,512]{2,1,0:T(8,128)(2,1)}) %reduce-scatter.21.cloned.1.call-update) | async-done | bytes 327696 | tf_op jit(solution)/shard_map/reduce_scatter | solution.py:279
  827.6 25.7 %reduce-scatter.19.cloned.1.call-done = bf16[1,320,512]{2,1,0:T(8,128)(2,1)} async-done(((bf16[1,1280,512]{2,1,0:T(8,128)(2,1)}), bf16[1,320,512]{2,1,0:T(8,128)(2,1)}) %reduce-scatter.19.cloned.1.call-update) | async-done | bytes 327696 | tf_op jit(solution)/shard_map/reduce_scatter | solution.py:279
  887.2 7.7 fusion.140
  894.9 6.2 fusion.141
  901.1 11.6 fusion.18
  913.6 47.7 %all-reduce.18.cloned.1.call-done = (bf16[320,1024]{1,0:T(8,128)(2,1)}, bf16[320,1024]{1,0:T(8,128)(2,1)}, bf16[320,1024]{1,0:T(8,128)(2,1)}, bf16[320,1024]{1,0...) async-done(((bf16[320,1024]{1,0:T(8,128)(2,1)}, bf16[320,1024]{1,0:T(8,128)(2,1)}, bf16[320,1024]{1,0:T(8,128)(2,1)}, bf16[320,1024]{1,0:T(8,128)(2,1)}, ...) | async-done | bytes 3932176 | tf_op jit(solution)/shard_map/psum | solution.py:213
  968.7 22.6 %reduce-scatter.25.cloned.1.call-done = bf16[512,256]{1,0:T(8,128)(2,1)} async-done(((bf16[512,1024]{1,0:T(8,128)(2,1)}), bf16[512,256]{1,0:T(8,128)(2,1)}) %reduce-scatter.25.cloned.1.call-update) | async-done | bytes 262160 | tf_op jit(solution)/shard_map/reduce_scatter | solution.py:311
  991.3 56.1 %reduce-scatter.29.cloned.1.call-done = bf16[1365,256]{1,0:T(8,128)(2,1)} async-done(((bf16[1365,1024]{1,0:T(8,128)(2,1)}), bf16[1365,256]{1,0:T(8,128)(2,1)}) %reduce-scatter.29.cloned.1.call-update) | async-done | bytes 698896 | tf_op jit(solution)/shard_map/reduce_scatter | solution.py:317
  1047.4 62.5 %reduce-scatter.23.cloned.1.call-done = bf16[3,256,512]{1,2,0:T(8,128)(2,1)} async-done(((bf16[3,1024,512]{1,2,0:T(8,128)(2,1)}), bf16[3,256,512]{1,2,0:T(8,128)(2,1)}) %reduce-scatter.23.cloned.1.call-update) | async-done | bytes 786448 | tf_op jit(solution)/shard_map/reduce_scatter | solution.py:308
  1109.9 102.1 %reduce-scatter.27.cloned.1.call-done = bf16[2,256,1365]{1,2,0:T(8,128)(2,1)} async-done(((bf16[2,1024,1365]{1,2,0:T(8,128)(2,1)}), bf16[2,256,1365]{1,2,0:T(8,128)(2,1)}) %reduce-scatter.27.cloned.1.call-update) | async-done | bytes 1397776 | tf_op jit(solution)/shard_map/reduce_scatter | solution.py:314
  1214.6 62.5 %all-reduce = (f32[1024]{0:T(1024)}, f32[512]{0:T(512)}, f32[1024]{0:T(1024)}, f32[1365]{0:T(1024)}) all-reduce(f32[1024]{0:T(1024)S(1)} %add_add_fusion.2, f32[512]{0:T(512)S(1)} %add_add_fusion.3, f32[1024]{0:T(1024)S(1)} %add_add_fusion.1, f32[1365]{0:T(1024)S(1)} %add_add_fusion), channel_id=1, replica_groups=mesh['shard'=4,'ctx'=4,'tp'=2] {'shard','ctx'}, use_global_device_ids=true, to_apply=%region_102.103 | all-reduce | flops 3925 | bytes 31400 | tf_op jit(solution)/shard_map/psum | solution.py:327
  1291.3 8.6 copy.119
  (683 shorter events, 254.2 us)
Async XLA Ops:
  7.2 68.6 %all-gather.11.cloned.1.call-start = ((), (), s32[]{:S(2)}) async-start(), calls=%async_computation.10 | async-start | bytes 3932160 | tf_op jit(solution)/shard_map/all_gather | solution.py:46
  7.9 102.1 %all-gather.15.cloned.1.call-start = ((), (), s32[]{:S(2)}) async-start(), calls=%async_computation.12 | async-start | bytes 1638400 | tf_op jit(solution)/shard_map/all_gather | solution.py:179
  9.9 69.1 %copy-start.145 = (f32[320]{0:T(512)}, f32[320]{0:T(512)S(1)}, u32[]{:S(2)}) copy-start(f32[320]{0:T(512)S(1)} %broadcast_multiply_fusion.37) | copy-start | bytes 3844
  9.9 84.4 %copy-start.147 = (f32[320]{0:T(512)}, f32[320]{0:T(512)S(1)}, u32[]{:S(2)}) copy-start(f32[320]{0:T(512)S(1)} %broadcast_multiply_fusion.34) | copy-start | bytes 3844
  9.9 75.0 %copy-start.149 = (f32[320]{0:T(512)}, f32[320]{0:T(512)S(1)}, u32[]{:S(2)}) copy-start(f32[320]{0:T(512)S(1)} %broadcast_multiply_fusion.31) | copy-start | bytes 3844
  11.5 97.7 %copy-start.57 = (f32[320,16]{0,1:T(8,128)}, f32[320,16]{0,1:T(8,128)S(1)}, u32[]{:S(2)}) copy-start(f32[320,16]{0,1:T(8,128)S(1)} %get-tuple-element.406) | copy-start | bytes 61444
  11.5 97.7 %copy-start.59 = (f32[320,16]{0,1:T(8,128)}, f32[320,16]{0,1:T(8,128)S(1)}, u32[]{:S(2)}) copy-start(f32[320,16]{0,1:T(8,128)S(1)} %get-tuple-element.432) | copy-start | bytes 61444
  82.9 39.4 %all-gather.13.cloned.1.call-start = ((), (), s32[]{:S(2)}) async-start(), calls=%async_computation.11 | async-start | bytes 1638400 | tf_op jit(solution)/shard_map/all_gather | solution.py:182
  84.9 55.2 %all-gather.29.cloned.1.call-start = ((), (), s32[]{:S(2)}) async-start(), calls=%async_computation.19 | async-start | bytes 1638400 | tf_op jit(solution)/shard_map/all_gather | solution.py:179
  92.3 67.9 %all-gather.27.cloned.1.call-start = ((), (), s32[]{:S(2)}) async-start(), calls=%async_computation.18 | async-start | bytes 1638400 | tf_op jit(solution)/shard_map/all_gather | solution.py:182
  94.2 85.7 %all-gather.25.cloned.1.call-start = ((), (), s32[]{:S(2)}) async-start(), calls=%async_computation.17 | async-start | bytes 1638400 | tf_op jit(solution)/shard_map/all_gather | solution.py:179
  100.7 99.6 %all-gather.23.cloned.1.call-start = ((), (), s32[]{:S(2)}) async-start(), calls=%async_computation.16 | async-start | bytes 1638400 | tf_op jit(solution)/shard_map/all_gather | solution.py:182
  102.7 129.4 %all-gather.17.cloned.1.call-start = ((), (), s32[]{:S(2)}) async-start(), calls=%async_computation.13 | async-start | bytes 1310720 | tf_op jit(solution)/shard_map/all_gather | solution.py:47
  103.4 186.4 %all-gather.21.cloned.1.call-start = ((), (), s32[]{:S(2)}) async-start(), calls=%async_computation.15 | async-start | bytes 3502080 | tf_op jit(solution)/shard_map/all_gather | solution.py:49
  104.1 290.0 %all-reduce.14.cloned.1.call-start = ((), (), s32[]{:S(2)}) async-start(), calls=%async_computation.30 | async-start | bytes 7864320 | tf_op jit(solution)/shard_map/psum | solution.py:196
  238.3 261.7 %all-gather.19.cloned.1.call-start = ((), (), s32[]{:S(2)}) async-start(), calls=%async_computation.14 | async-start | bytes 7004160 | tf_op jit(solution)/shard_map/all_gather | solution.py:48
  241.0 378.4 %all-reduce.20.cloned.1.call-start = ((), (), s32[]{:S(2)}) async-start(), calls=%async_computation.33 | async-start | bytes 3932160 | tf_op jit(solution)/shard_map/psum | solution.py:245
  242.6 381.2 %copy-start.170 = (f32[320]{0:T(512)}, f32[320]{0:T(512)S(1)}, u32[]{:S(2)}) copy-start(f32[320]{0:T(512)S(1)} %fusion.242) | copy-start | bytes 3844
  243.3 381.2 %copy-start.172 = (f32[320]{0:T(512)}, f32[320]{0:T(512)S(1)}, u32[]{:S(2)}) copy-start(f32[320]{0:T(512)S(1)} %fusion.243) | copy-start | bytes 3844
  294.2 99.9 %copy-start.7 = (bf16[3,320,1024]{2,1,0:T(8,128)(2,1)S(1)}, bf16[3,320,1024]{2,1,0:T(8,128)(2,1)}, u32[]{:S(2)}) copy-start(bf16[3,320,1024]{2,1,0:T(8,128)(2,1)} %param.11) | copy-start | bytes 5898244
  396.8 227.7 %copy-start.9 = (f32[320,1024]{1,0:T(8,128)}, f32[320,1024]{1,0:T(8,128)S(1)}, u32[]{:S(2)}) copy-start(f32[320,1024]{1,0:T(8,128)S(1)} %get-tuple-element.309) | copy-start | bytes 3932164
  396.8 227.0 %copy-start.141 = (f32[320]{0:T(512)}, f32[320]{0:T(512)S(1)}, u32[]{:S(2)}) copy-start(f32[320]{0:T(512)S(1)} %broadcast_multiply_fusion.35) | copy-start | bytes 3844
  396.8 103.2 %copy-start.134 = (f32[1024]{0:T(1024)S(1)}, f32[1024]{0:T(1024)}, u32[]{:S(2)}) copy-start(f32[1024]{0:T(1024)} %param.18) | copy-start | bytes 12292
  397.1 227.4 %copy-start.139 = (f32[320]{0:T(512)}, f32[320]{0:T(512)S(1)}, u32[]{:S(2)}) copy-start(f32[320]{0:T(512)S(1)} %broadcast_multiply_fusion.29) | copy-start | bytes 3844
  397.4 227.1 %copy-start.143 = (f32[320]{0:T(512)}, f32[320]{0:T(512)S(1)}, u32[]{:S(2)}) copy-start(f32[320]{0:T(512)S(1)} %broadcast_multiply_fusion.32) | copy-start | bytes 3844
  398.3 225.5 %copy-start.155 = (f32[320]{0:T(512)}, f32[320]{0:T(512)S(1)}, u32[]{:S(2)}) copy-start(f32[320]{0:T(512)S(1)} %add_rsqrt_fusion.9) | copy-start | bytes 3844
  398.3 226.2 %copy-start.153 = (f32[320]{0:T(512)}, f32[320]{0:T(512)S(1)}, u32[]{:S(2)}) copy-start(f32[320]{0:T(512)S(1)} %add_rsqrt_fusion.1) | copy-start | bytes 3844
  398.3 226.2 %copy-start.157 = (f32[320]{0:T(512)}, f32[320]{0:T(512)S(1)}, u32[]{:S(2)}) copy-start(f32[320]{0:T(512)S(1)} %add_rsqrt_fusion.5) | copy-start | bytes 3844
  524.3 232.9 %copy-start.174 = (f32[320]{0:T(512)}, f32[320]{0:T(512)S(1)}, u32[]{:S(2)}) copy-start(f32[320]{0:T(512)S(1)} %get-tuple-element.419) | copy-start | bytes 3844
  524.3 232.9 %copy-start.176 = (f32[320]{0:T(512)}, f32[320]{0:T(512)S(1)}, u32[]{:S(2)}) copy-start(f32[320]{0:T(512)S(1)} %get-tuple-element.420) | copy-start | bytes 3844
  524.3 228.2 %copy-start.182 = (f32[320]{0:T(512)}, f32[320]{0:T(512)S(1)}, u32[]{:S(2)}) copy-start(f32[320]{0:T(512)S(1)} %get-tuple-element.421) | copy-start | bytes 3844
  524.3 228.2 %copy-start.184 = (f32[320]{0:T(512)}, f32[320]{0:T(512)S(1)}, u32[]{:S(2)}) copy-start(f32[320]{0:T(512)S(1)} %get-tuple-element.422) | copy-start | bytes 3844
  524.3 224.1 %copy-start.178 = (f32[320]{0:T(512)}, f32[320]{0:T(512)S(1)}, u32[]{:S(2)}) copy-start(f32[320]{0:T(512)S(1)} %get-tuple-element.423) | copy-start | bytes 3844
  524.3 224.1 %copy-start.180 = (f32[320]{0:T(512)}, f32[320]{0:T(512)S(1)}, u32[]{:S(2)}) copy-start(f32[320]{0:T(512)S(1)} %get-tuple-element.424) | copy-start | bytes 3844
  560.7 227.4 %reduce-scatter.31.cloned.1.call-start = ((), (), s32[]{:S(2)}) async-start(), calls=%async_computation.27 | async-start | bytes 1638400
  673.9 116.8 %reduce-scatter.35.cloned.1.call-start = ((), (), s32[]{:S(2)}) async-start(), calls=%async_computation.29 | async-start | bytes 1638400
  706.5 87.4 %reduce-scatter.33.cloned.1.call-start = ((), (), s32[]{:S(2)}) async-start(), calls=%async_computation.28 | async-start | bytes 1638400
  737.0 59.3 %reduce-scatter.17.cloned.1.call-start = ((), (), s32[]{:S(2)}) async-start(), calls=%async_computation.20 | async-start | bytes 1638400 | tf_op jit(solution)/shard_map/reduce_scatter | solution.py:279
  748.0 75.6 %reduce-scatter.21.cloned.1.call-start = ((), (), s32[]{:S(2)}) async-start(), calls=%async_computation.22 | async-start | bytes 1638400 | tf_op jit(solution)/shard_map/reduce_scatter | solution.py:279
  765.4 87.9 %reduce-scatter.19.cloned.1.call-start = ((), (), s32[]{:S(2)}) async-start(), calls=%async_computation.21 | async-start | bytes 1638400 | tf_op jit(solution)/shard_map/reduce_scatter | solution.py:279
  786.3 175.0 %all-reduce.18.cloned.1.call-start = ((), (), s32[]{:S(2)}) async-start(), calls=%async_computation.32 | async-start | bytes 7864320 | tf_op jit(solution)/shard_map/psum | solution.py:213
  857.4 133.9 %reduce-scatter.25.cloned.1.call-start = ((), (), s32[]{:S(2)}) async-start(), calls=%async_computation.24 | async-start | bytes 1310720 | tf_op jit(solution)/shard_map/reduce_scatter | solution.py:311
  864.0 183.4 %reduce-scatter.29.cloned.1.call-start = ((), (), s32[]{:S(2)}) async-start(), calls=%async_computation.26 | async-start | bytes 3502080 | tf_op jit(solution)/shard_map/reduce_scatter | solution.py:317
  875.1 234.7 %reduce-scatter.23.cloned.1.call-start = ((), (), s32[]{:S(2)}) async-start(), calls=%async_computation.23 | async-start | bytes 3932160 | tf_op jit(solution)/shard_map/reduce_scatter | solution.py:308
  885.9 326.1 %reduce-scatter.27.cloned.1.call-start = ((), (), s32[]{:S(2)}) async-start(), calls=%async_computation.25 | async-start | bytes 7004160 | tf_op jit(solution)/shard_map/reduce_scatter | solution.py:314
  912.9 372.8 %all-reduce.16.cloned.1.call-start = ((), (), s32[]{:S(2)}) async-start(), calls=%async_computation.31 | async-start | bytes 6299648 | tf_op jit(solution)/shard_map/psum | solution.py:322
  968.7 243.3 %copy-start.79 = (bf16[1,320,1024]{2,1,0:T(8,128)(2,1)S(1)}, bf16[1,320,1024]{2,1,0:T(8,128)(2,1)}, u32[]{:S(2)}) copy-start(bf16[1,320,1024]{2,1,0:T(8,128)(2,1)} %fusion.175) | copy-start | bytes 1966084
  968.7 243.3 %copy-start.80 = (bf16[1,320,1024]{2,1,0:T(8,128)(2,1)S(1)}, bf16[1,320,1024]{2,1,0:T(8,128)(2,1)}, u32[]{:S(2)}) copy-start(bf16[1,320,1024]{2,1,0:T(8,128)(2,1)} %fusion.179) | copy-start | bytes 1966084
  (189 other events, 1458.3 us)
Sparse Core Ops, SparseCore 0:
  9.6 66.1 all-gather.10
  83.1 16.8 all-gather.14
  102.1 18.2 all-gather.12
  121.8 18.1 all-gather.28
  142.0 18.1 all-gather.26
  161.6 18.2 all-gather.24
  182.1 18.1 all-gather.22
  201.9 30.1 all-gather.16
  233.7 56.0 all-gather.20
  292.7 101.4 all-reduce.13
  396.4 103.5 all-gather.18
  560.8 58.6 all-reduce.19
  674.0 27.6 reduce-scatter.30
  706.6 27.6 reduce-scatter.34
  737.1 27.7 reduce-scatter.32
  767.4 26.5 reduce-scatter.16
  797.0 26.5 reduce-scatter.20
  826.6 26.5 reduce-scatter.18
  857.5 103.7 all-reduce.17
  964.1 27.1 reduce-scatter.24
  993.6 53.7 reduce-scatter.28
  1049.8 60.0 reduce-scatter.22
  1112.3 99.6 reduce-scatter.26
  1214.6 70.9 all-reduce.15
where the time goes:
time: 1320 us; the launch traced here: 1310 us
  waiting for transfers between devices  757 us (57%)
  matrix products  230 us (17%)
  local copies, waits for them, and re-layouts  115 us (9%)
  blocking collectives  93 us (7%)
  other arithmetic  91.7 us (7%)
  between operations  17.9 us (1%)
    reduce_scatter x1, waiting for transfers between devices, local(): lax.psum_scatter(grad_pairs.astype(jnp.bfloat16), 'shard', scatter_dimens...  102 us
    all_gather x1, waiting for transfers between devices, gather_rows(): lax.all_gather(gate_up, 'shard', axis=1, tiled=True)  102 us
    psum x1, waiting for transfers between devices, local(): lax.psum(jnp.dot(entry_attn, full_proj, preferred_element_type=jnp.float3...  97.5 us
    unnamed x441, local copies, waits for them, and re-layouts  74 us
    all_gather x1, waiting for transfers between devices, gather_rows(): lax.all_gather(qkv_weight, 'shard', axis=1, tiled=True)  64.3 us
    reduce_scatter x1, waiting for transfers between devices, local(): lax.psum_scatter(grad_qkv.astype(jnp.bfloat16), 'shard', scatter_dimensio...  62.5 us
    psum x1, blocking collectives, local(): lax.psum((grad_ln1, grad_attn_gain, grad_ln2, grad_ffn_gain), ('shard', '...  62.5 us
    psum x1, waiting for transfers between devices, local(): lax.psum(jnp.einsum('cne,cde->nd', grad_stacked, full_gate_up, preferred_...  58.1 us
  transfers between devices with their start and end apart: 24, of which 18 were waited for; matrix products, arithmetic and copies ran while one was open for 22% of the time, Pallas kernels for 0%

commit v1 on v0

v1 whole, which is shorter than its diff:
```python
import functools
import math

import jax
import jax.numpy as jnp
from jax import lax
from jax.experimental import pallas as pl
from jax.experimental.pallas import tpu as pltpu
from jax.sharding import PartitionSpec as P

HEAD = 64
GRID = 32
LANES = 128
EPS = 1e-06
BF = jnp.bfloat16
F32 = jnp.float32
TAIL = 80


def dot_nn(a, b):
    return lax.dot_general(a, b, (((1,), (0,)), ((), ())), preferred_element_type=F32)


def dot_nt(a, b):
    return lax.dot_general(a, b, (((1,), (1,)), ((), ())), preferred_element_type=F32)


def dot_tn(a, b):
    return lax.dot_general(a, b, (((0,), (0,)), ((), ())), preferred_element_type=F32)


def tiles(width, step=256):
    return [(at, min(step, width - at)) for at in range(0, width, step)]


def pair_perm(size, flip):
    return [(at, at ^ flip) for at in range(size)]


def rope_tables(positions):
    quarter = HEAD // 4
    place = jnp.maximum(positions - 1, 0)
    row_pos = (place // GRID).astype(F32)
    col_pos = (place % GRID).astype(F32)
    frequency = jnp.exp(jnp.arange(quarter).astype(F32) * (-math.log(10000.0) / quarter))
    row_angle = row_pos[:, None] * frequency[None, :]
    col_angle = col_pos[:, None] * frequency[None, :]
    cr, sr, cc, sc = jnp.cos(row_angle), jnp.sin(row_angle), jnp.cos(col_angle), jnp.sin(col_angle)
    zero = jnp.zeros_like(sr)
    cos = jnp.concatenate([cr, cr, cc, cc], axis=1)
    up = jnp.concatenate([-sr, zero, -sc, zero], axis=1)
    down = jnp.concatenate([zero, sr, zero, sc], axis=1)
    return jnp.stack([jnp.concatenate([t, t], axis=1) for t in (cos, up, down)])


def turn(values, tables_ref, sign):
    shift = HEAD // 4
    return values * tables_ref[0] + sign * (
        pltpu.roll(values, LANES - shift, 1) * tables_ref[1]
        + pltpu.roll(values, shift, 1) * tables_ref[2]
    )


def row_norm(values, width):
    mean = jnp.sum(values, axis=1, keepdims=True) * (1.0 / width)
    centred = values - mean
    inv = lax.rsqrt(jnp.sum(centred * centred, axis=1, keepdims=True) * (1.0 / width) + EPS)
    return centred * inv, inv


def row_norm_back(scaled, normed, inv, width):
    first = jnp.sum(scaled, axis=1, keepdims=True) * (1.0 / width)
    second = jnp.sum(scaled * normed, axis=1, keepdims=True) * (1.0 / width)
    return inv * (scaled - first - normed * second)


def valid_rows(values, count):
    rows = lax.broadcasted_iota(jnp.int32, values.shape, 0)
    return jnp.where(rows < count, values, jnp.zeros_like(values))


def qkv_kernel(x_ref, gain_ref, w_ref, rope_ref, h_ref, q_ref, kv_ref):
    x = x_ref[0].astype(F32)
    normed, _ = row_norm(x, x.shape[1])
    h_ref[...] = (normed * gain_ref[...]).astype(BF)
    width = w_ref.shape[2]
    h = h_ref[...]
    for at, size in tiles(width):
        q = dot_nn(h, w_ref[0, :, at : at + size])
        k = dot_nn(h, w_ref[1, :, at : at + size])
        v = dot_nn(h, w_ref[2, :, at : at + size])
        for off in range(0, size, LANES):
            cols = slice(off, off + LANES)
            q_ref[:, at + off : at + off + LANES] = (
                turn(q[:, cols], rope_ref, 1.0) * HEAD ** (-0.5)
            ).astype(BF)
            kv_ref[:, at + off : at + off + LANES] = turn(k[:, cols], rope_ref, 1.0).astype(BF)
        kv_ref[:, width + at : width + at + size] = v.astype(BF)


def split_pair(values):
    lane = lax.broadcasted_iota(jnp.int32, values.shape, 1)
    zero = jnp.zeros_like(values)
    return jnp.concatenate(
        [jnp.where(lane < HEAD, values, zero), jnp.where(lane >= HEAD, values, zero)], axis=0
    )


def join_pair(values):
    rows = values.shape[0] // 2
    lane = lax.broadcasted_iota(jnp.int32, (rows, values.shape[1]), 1)
    return jnp.where(lane < HEAD, values[:rows], values[rows:])


def attend_kernel(n_ref, q_ref, kv0, kv1, kv2, kv3, o_ref, lse_ref, m_s, l_s, acc_s):
    rows, width = q_ref.shape
    for pair in range(width // LANES):
        cols = slice(pair * LANES, (pair + 1) * LANES)
        vcols = slice(width + pair * LANES, width + (pair + 1) * LANES)
        qb = split_pair(q_ref[:, cols])
        m_s[...] = jnp.full(m_s.shape, -1e30, F32)
        l_s[...] = jnp.zeros(l_s.shape, F32)
        acc_s[...] = jnp.zeros(acc_s.shape, F32)

        def step(kv_ref, count, size):
            s = dot_nt(kv_ref[:size, cols], qb)
            key = lax.broadcasted_iota(jnp.int32, s.shape, 0)
            s = jnp.where(key < count, s, -1e30)
            m_old = m_s[...]
            m_new = jnp.maximum(m_old, jnp.max(s, axis=0, keepdims=True))
            scale = jnp.exp(m_old - m_new)
            e = jnp.exp(s - m_new)
            m_s[...] = m_new
            l_s[...] = l_s[...] * scale + jnp.sum(e, axis=0, keepdims=True)
            acc_s[...] = acc_s[...] * scale + dot_tn(kv_ref[:size, vcols], e.astype(BF))

        for at, kv_ref in enumerate((kv0, kv1, kv2, kv3)):
            count = n_ref[at]

            @pl.when(count > TAIL)
            def _():
                step(kv_ref, count, kv_ref.shape[0])

            @pl.when((count > 0) & (count <= TAIL))
            def _():
                step(kv_ref, count, TAIL)

        total = l_s[...]
        out = acc_s[...] * (1.0 / total)
        o_ref[:, cols] = join_pair(out.T).astype(BF)
        lse_ref[pair : pair + 1, :] = m_s[...] + jnp.log(total)


def attend_back_kernel(
    n_ref, q_ref, kv0, kv1, kv2, kv3, o_ref, do_ref, lse_ref, rope_ref, dq_ref, keep_ref, send_ref, dq_s
):
    rows, width = q_ref.shape
    for pair in range(width // LANES):
        cols = slice(pair * LANES, (pair + 1) * LANES)
        vcols = slice(width + pair * LANES, width + (pair + 1) * LANES)
        qb = split_pair(q_ref[:, cols])
        do = do_ref[:, cols]
        dob = split_pair(do)
        prod = split_pair(do.astype(F32) * o_ref[:, cols].astype(F32))
        delta = jnp.sum(prod.T, axis=0, keepdims=True)
        lse = lse_ref[pair : pair + 1, :]
        dq_s[...] = jnp.zeros(dq_s.shape, F32)

        def step(kv_ref, out_ref, slot, count, size):
            k = kv_ref[:size, cols]
            s = dot_nt(k, qb)
            key = lax.broadcasted_iota(jnp.int32, s.shape, 0)
            p = jnp.where(key < count, jnp.exp(s - lse), 0.0)
            dp = dot_nt(kv_ref[:size, vcols], dob)
            ds = (p * (dp - delta)).astype(BF)
            out_ref[slot, :size, vcols] = dot_nn(p.astype(BF), dob).astype(BF)
            out_ref[slot, :size, cols] = dot_nn(ds, qb).astype(BF)
            dq_s[...] += dot_tn(k, ds)
            if size < rows:
                out_ref[slot, size:, vcols] = jnp.zeros((rows - size, LANES), BF)
                out_ref[slot, size:, cols] = jnp.zeros((rows - size, LANES), BF)

        for at, kv_ref in enumerate((kv0, kv1, kv2, kv3)):
            count = n_ref[at]
            out_ref = (keep_ref, send_ref)[at % 2]
            slot = at // 2

            @pl.when(count > TAIL)
            def _():
                step(kv_ref, out_ref, slot, count, kv_ref.shape[0])

            @pl.when((count > 0) & (count <= TAIL))
            def _():
                step(kv_ref, out_ref, slot, count, TAIL)

            @pl.when(count <= 0)
            def _():
                out_ref[slot, :, vcols] = jnp.zeros((rows, LANES), BF)
                out_ref[slot, :, cols] = jnp.zeros((rows, LANES), BF)

        dq = join_pair(dq_s[...].T) * HEAD ** (-0.5)
        dq_ref[:, cols] = turn(dq, rope_ref, -1.0).astype(BF)


def merge_heads(dst, own_ref, other_ref, tp, half):
    dst[:, pl.ds(pl.multiple_of(tp * half, half), half)] = own_ref[...]
    dst[:, pl.ds(pl.multiple_of((1 - tp) * half, half), half)] = other_ref[...]


def middle_kernel(
    sc_ref, x_ref, cot_ref, own_ref, other_ref, again_ref, ln2_ref, fgain_ref, w_ref,
    x1_ref, h2_ref, g_ref, u_ref, dm_ref, a_ref, st_ref,
    pj_s, gw_s, uw_s, dw_s, o_s, a_s, st_s, sem,
):
    width = x_ref.shape[2]
    half = own_ref.shape[1]
    rows = own_ref.shape[0]
    ff = g_ref.shape[1]
    loads = []
    at = 0
    for slot, dst in enumerate((pj_s, gw_s, uw_s, dw_s)):
        loads.append(
            pltpu.make_async_copy(w_ref.at[:, pl.ds(at, dst.shape[1])], dst, sem.at[slot])
        )
        at += dst.shape[1]
    for load in loads:
        load.start()
    tp = sc_ref[1]
    merge_heads(o_s, own_ref, other_ref, tp, half)
    normed, _ = row_norm(o_s[...].astype(F32), width)
    a_s[...] = (normed * again_ref[...]).astype(BF)
    a_ref[...] = a_s[:, pl.ds(pl.multiple_of(tp * half, half), half)]
    loads[0].wait()
    a = a_s[...]
    for at, size in tiles(width):
        x1_ref[:, at : at + size] = x_ref[0, :, at : at + size].astype(F32) + dot_nt(
            a, pj_s[at : at + size, :]
        )
    normed, _ = row_norm(x1_ref[...], width)
    h2_ref[...] = (normed * ln2_ref[...]).astype(BF)
    h2 = h2_ref[...]
    dyb = valid_rows(cot_ref[0], sc_ref[0])
    for load in loads[1:]:
        load.wait()
    sums = [jnp.zeros((rows, LANES), F32) for _ in range(4)]
    for at, size in tiles(ff):
        span = slice(at, at + size)
        g = dot_nn(h2, gw_s[:, span]).astype(BF)
        u = dot_nn(h2, uw_s[:, span]).astype(BF)
        dm = dot_nn(dyb, dw_s[:, span]).astype(BF)
        g_ref[:, span] = g
        u_ref[:, span] = u
        dm_ref[:, span] = dm
        gf = g.astype(F32)
        z = gf * jax.nn.sigmoid(gf) * u.astype(F32)
        e = dm.astype(F32) * fgain_ref[:, span]
        for off in range(0, size, LANES):
            zo = z[:, off : off + LANES]
            eo = e[:, off : off + LANES]
            sums = [sums[0] + zo, sums[1] + zo * zo, sums[2] + eo, sums[3] + eo * zo]
    lane = lax.broadcasted_iota(jnp.int32, (rows, LANES), 1)
    packed = jnp.zeros((rows, LANES), F32)
    for slot, part in enumerate(sums):
        packed = jnp.where(lane == slot, jnp.sum(part, axis=1, keepdims=True), packed)
    st_s[...] = jnp.zeros(st_s.shape, F32)
    st_s[:rows, :] = packed
    st_ref[...] = st_s[...].T[:8, :]


def ffn_kernel(
    sa_ref, sb_ref, g_ref, u_ref, dm_ref, fgain_ref, w_ref,
    m_ref, dg_ref, du_ref, out_ref, dh_ref, dgain_ref,
    gw_s, uw_s, dw_s, st_s, sem, *, total,
):
    rows, ff = g_ref.shape
    width = w_ref.shape[0]
    loads = []
    at = width
    for slot, dst in enumerate((gw_s, uw_s, dw_s)):
        loads.append(
            pltpu.make_async_copy(w_ref.at[:, pl.ds(at, dst.shape[1])], dst, sem.at[slot])
        )
        at += dst.shape[1]
    for load in loads:
        load.start()
    st_s[...] = jnp.zeros(st_s.shape, F32)
    st_s[:8, :] = sa_ref[...] + sb_ref[...]
    st = st_s[...].T[:rows, :]
    lane = lax.broadcasted_iota(jnp.int32, st.shape, 1)

    def column(slot):
        return jnp.sum(jnp.where(lane == slot, st, 0.0), axis=1, keepdims=True) * (1.0 / total)

    mean = column(0)
    inv = lax.rsqrt(jnp.maximum(column(1) - mean * mean, 0.0) + EPS)
    first = column(2)
    second = inv * (column(3) - mean * first)
    for at, size in tiles(ff):
        span = slice(at, at + size)
        g = g_ref[:, span].astype(F32)
        u = u_ref[:, span].astype(F32)
        dm = dm_ref[:, span].astype(F32)
        gain = fgain_ref[:, span]
        sig = jax.nn.sigmoid(g)
        act = g * sig
        normed = (act * u - mean) * inv
        m_ref[:, span] = (normed * gain).astype(BF)
        dgain_ref[:, span] = jnp.sum(dm * normed, axis=0, keepdims=True)
        dz = inv * (dm * gain - first - normed * second)
        dg_ref[:, span] = (dz * u * sig * (1.0 + g * (1.0 - sig))).astype(BF)
        du_ref[:, span] = (dz * act).astype(BF)
    loads[0].wait()
    loads[1].wait()
    dg = dg_ref[...]
    du = du_ref[...]
    for at, size in tiles(width):
        dh_ref[:, at : at + size] = (
            dot_nt(dg, gw_s[at : at + size, :]) + dot_nt(du, uw_s[at : at + size, :])
        ).astype(BF)
    loads[2].wait()
    m = m_ref[...]
    for at, size in tiles(width):
        out_ref[:, at : at + size] = dot_nt(m, dw_s[at : at + size, :]).astype(BF)


def attn_norm_back_kernel(
    sc_ref, dha_ref, dhb_ref, x1_ref, cot_ref, ln2_ref, own_ref, other_ref, again_ref, w_ref,
    dx_ref, dab_ref, do_ref, dln2_ref, dgain_ref,
    pj_s, o_s, e_s, f_s, sem,
):
    width = x1_ref.shape[1]
    half = own_ref.shape[1]
    load = pltpu.make_async_copy(w_ref.at[:, pl.ds(0, width)], pj_s, sem.at[0])
    load.start()
    tp = sc_ref[1]
    dh = dha_ref[...].astype(F32) + dhb_ref[...].astype(F32)
    normed, inv = row_norm(x1_ref[...], width)
    dln2_ref[...] = jnp.sum(dh * normed, axis=0, keepdims=True)
    dy = valid_rows(cot_ref[0].astype(F32), sc_ref[0])
    dx = dy + row_norm_back(dh * ln2_ref[...], normed, inv, width)
    dx_ref[...] = dx
    dab_ref[...] = dx.astype(BF)
    merge_heads(o_s, own_ref, other_ref, tp, half)
    normed, inv = row_norm(o_s[...].astype(F32), width)
    load.wait()
    dab = dab_ref[...]
    for at, size in tiles(width):
        da = dot_nn(dab, pj_s[:, at : at + size])
        e_s[:, at : at + size] = da
    da = e_s[...]
    f_s[...] = jnp.broadcast_to(jnp.sum(da * normed, axis=0, keepdims=True), f_s.shape)
    dgain_ref[...] = f_s[0:1, pl.ds(pl.multiple_of(tp * half, half), half)]
    e_s[...] = row_norm_back(da * again_ref[...], normed, inv, width)
    do_ref[...] = e_s[:, pl.ds(pl.multiple_of(tp * half, half), half)].astype(BF)


def qkv_back_kernel(keep_ref, recv_ref, far_ref, dq_ref, rope_ref, w_ref, dkv_ref, dh_ref):
    rows, half = dq_ref.shape
    total = keep_ref[0].astype(F32) + recv_ref[0].astype(F32) + far_ref[...].astype(F32)
    for at in range(0, half, LANES):
        dkv_ref[:, at : at + LANES] = turn(total[:, at : at + LANES], rope_ref, -1.0).astype(BF)
    dkv_ref[:, half:] = total[:, half:].astype(BF)
    dq = dq_ref[...]
    dk = dkv_ref[:, :half]
    dv = dkv_ref[:, half:]
    for at, size in tiles(w_ref.shape[1]):
        span = slice(at, at + size)
        dh_ref[:, span] = (
            dot_nt(dq, w_ref[0, span, :]) + dot_nt(dk, w_ref[1, span, :]) + dot_nt(dv, w_ref[2, span, :])
        ).astype(BF)


def tokens_back_kernel(da_ref, db_ref, x_ref, gain_ref, dx_ref, *rest):
    out_ref, dgain_ref = rest[-2:]
    width = dx_ref.shape[1]
    dh = da_ref[...].astype(F32) + db_ref[...].astype(F32)
    normed, inv = row_norm(x_ref[0].astype(F32), width)
    dgain_ref[...] = jnp.sum(dh * normed, axis=0, keepdims=True)
    out_ref[0] = (dx_ref[...] + row_norm_back(dh * gain_ref[...], normed, inv, width)).astype(BF)


def mixed_kernel(x1_ref, pa_ref, pb_ref, *rest):
    out_ref = rest[-1]
    out_ref[0] = (x1_ref[...] + (pa_ref[...].astype(F32) + pb_ref[...].astype(F32))).astype(BF)


VMEM = pl.BlockSpec(memory_space=pltpu.VMEM)
SMEM = pl.BlockSpec(memory_space=pltpu.SMEM)
ANY = pl.BlockSpec(memory_space=pl.ANY)


def shape(*dims, dtype=BF):
    return jax.ShapeDtypeStruct(dims, dtype)


def call(kernel, out_shape, in_specs, out_specs, scratch=(), name=None, flops=0, moved=0, aliases=None, mib=48):
    return pl.pallas_call(
        kernel,
        out_shape=out_shape,
        in_specs=in_specs,
        out_specs=out_specs,
        grid=(1,),
        scratch_shapes=list(scratch),
        input_output_aliases=aliases or {},
        name=name,
        cost_estimate=pl.CostEstimate(flops=flops, bytes_accessed=moved, transcendentals=0),
        compiler_params=pltpu.CompilerParams(vmem_limit_bytes=mib << 20),
    )


def whole(*dims):
    return pl.BlockSpec(dims, lambda i: (0,) * len(dims))


def image_of(index, rows, width):
    return pl.BlockSpec((1, rows, width), lambda i: (index, 0, 0))


def local(
    tokens, cotangent, lengths, ln1_gain, qkv_weight, attn_gain, proj_weight, ln2_gain, gate_up, ffn_gain, down_weight
):
    images, rows, width = tokens.shape
    half = attn_gain.shape[0]
    ff = ffn_gain.shape[0]
    ffp = -(-ff // LANES) * LANES
    pad = ffp - ff
    ctx_size = lax.axis_size("ctx")
    tp_size = lax.axis_size("tp")
    ctx = lax.axis_index("ctx")
    tp = lax.axis_index("tp")
    ff_total = ff * tp_size
    both = ("shard", "ctx")
    swap_tp = pair_perm(tp_size, 1)
    swap_near = pair_perm(ctx_size, 1)
    swap_far = pair_perm(ctx_size, 2)

    def swap(value):
        return lax.ppermute(value, "tp", swap_tp)

    def near(value):
        return lax.ppermute(value, "ctx", swap_near)

    def far(value):
        return lax.ppermute(value, "ctx", swap_far)

    def ordered(own, axis):
        other = swap(own)
        low = jnp.where(tp == 0, own, other)
        high = jnp.where(tp == 0, other, own)
        return jnp.concatenate([low, high], axis=axis)

    depth = qkv_weight.shape[1]
    part = depth // ctx_size
    first = ctx * part
    qkv_part = lax.dynamic_slice_in_dim(qkv_weight, first, part, axis=1)
    full_qkv = lax.all_gather(qkv_part, both, axis=1, tiled=True)
    proj_part = lax.dynamic_slice_in_dim(proj_weight, first, part, axis=1).T
    pairs_part = lax.dynamic_slice_in_dim(gate_up, first, part, axis=1)
    down_part = lax.dynamic_slice_in_dim(down_weight, first, part, axis=1).T
    rest_part = jnp.concatenate(
        [
            ordered(proj_part, 1),
            jnp.pad(pairs_part[0], ((0, 0), (0, pad))),
            jnp.pad(pairs_part[1], ((0, 0), (0, pad))),
            jnp.pad(down_part, ((0, 0), (0, pad))),
        ],
        axis=1,
    )
    rest = lax.all_gather(rest_part, both, axis=0, tiled=True)
    rest_width = rest.shape[1]

    ln1 = ln1_gain[None, :]
    ln2 = ln2_gain[None, :]
    again = ordered(attn_gain[None, :], 1)
    fgain = jnp.pad(ffn_gain, (0, pad))[None, :]
    tables = rope_tables(ctx * rows + jnp.arange(rows, dtype=jnp.int32))
    order = ctx ^ jnp.arange(4, dtype=jnp.int32)
    counts = jnp.clip(lengths[:, None] - rows * order[None, :], 0, rows)

    act = whole(rows, width)
    act_half = whole(rows, half)
    act_ff = whole(rows, ffp)
    line = whole(1, width)
    line_ff = whole(1, ffp)
    rope_spec = whole(3, rows, LANES)
    qkv_spec = whole(3, width, half)
    block_mb = rows * width

    st = [dict() for _ in range(images)]
    for i in range(images):
        s = st[i]
        s["n"] = counts[i]
        s["sc"] = jnp.stack([counts[i, 0], tp.astype(jnp.int32)])
        s["h1"], s["q"], s["kv"] = call(
            qkv_kernel,
            (shape(rows, width), shape(rows, half), shape(rows, 2 * half)),
            [image_of(i, rows, width), line, qkv_spec, rope_spec],
            [act, act_half, whole(rows, 2 * half)],
            name="qkv",
            flops=2 * rows * width * 3 * half,
            moved=6 * width * half + 8 * block_mb,
        )(tokens, ln1, full_qkv, tables)
        s["kvc"] = near(s["kv"])
        s["kvf"] = far(s["kv"])
        s["kvx"] = near(s["kvf"])
    for i in range(images):
        s = st[i]
        s["o"], s["lse"] = call(
            attend_kernel,
            (shape(rows, half), shape(8, 2 * rows, dtype=F32)),
            [SMEM, act_half] + [whole(rows, 2 * half)] * 4,
            [act_half, whole(8, 2 * rows)],
            [
                pltpu.VMEM((1, 2 * rows), F32),
                pltpu.VMEM((1, 2 * rows), F32),
                pltpu.VMEM((LANES, 2 * rows), F32),
            ],
            name="attend",
            flops=16 * rows * 4 * rows * half,
            moved=12 * block_mb,
        )(s["n"], s["q"], s["kv"], s["kvc"], s["kvf"], s["kvx"])
        s["ox"] = swap(s["o"])
    for i in range(images):
        s = st[i]
        s["x1"], s["h2"], s["g"], s["u"], s["dm"], s["a"], s["st"] = call(
            middle_kernel,
            (
                shape(rows, width, dtype=F32),
                shape(rows, width),
                shape(rows, ffp),
                shape(rows, ffp),
                shape(rows, ffp),
                shape(rows, half),
                shape(8, 384, dtype=F32),
            ),
            [SMEM, image_of(i, rows, width), image_of(i, rows, width), act_half, act_half, line, line, line_ff, ANY],
            [act, act, act_ff, act_ff, act_ff, act_half, whole(8, 384)],
            [
                pltpu.VMEM((width, width), BF),
                pltpu.VMEM((width, ffp), BF),
                pltpu.VMEM((width, ffp), BF),
                pltpu.VMEM((width, ffp), BF),
                pltpu.VMEM((rows, width), BF),
                pltpu.VMEM((rows, width), BF),
                pltpu.VMEM((384, LANES), F32),
                pltpu.SemaphoreType.DMA((4,)),
            ],
            name="middle",
            flops=2 * rows * width * (width + 3 * ffp),
            moved=2 * width * rest_width + 12 * block_mb + 6 * rows * ffp,
        )(s["sc"], tokens, cotangent, s["o"], s["ox"], again, ln2, fgain, rest)
        s["stx"] = swap(s["st"])
    for i in range(images):
        s = st[i]
        s["m"], s["dg"], s["du"], s["out"], s["dh2"], s["dffn"] = call(
            functools.partial(ffn_kernel, total=ff_total),
            (
                shape(rows, ffp),
                shape(rows, ffp),
                shape(rows, ffp),
                shape(rows, width),
                shape(rows, width),
                shape(1, ffp, dtype=F32),
            ),
            [whole(8, 384), whole(8, 384), act_ff, act_ff, act_ff, line_ff, ANY],
            [act_ff, act_ff, act_ff, act, act, line_ff],
            [
                pltpu.VMEM((width, ffp), BF),
                pltpu.VMEM((width, ffp), BF),
                pltpu.VMEM((width, ffp), BF),
                pltpu.VMEM((LANES, 384), F32),
                pltpu.SemaphoreType.DMA((3,)),
            ],
            name="ffn",
            flops=2 * rows * width * 3 * ffp,
            moved=6 * width * ffp + 12 * rows * ffp + 4 * block_mb,
        )(s["st"], s["stx"], s["g"], s["u"], s["dm"], fgain, rest)
        s["dh2x"] = swap(s["dh2"])
        s["outx"] = swap(s["out"])
    for i in range(images):
        s = st[i]
        s["dx"], s["dab"], s["do"], s["dln2"], s["dattn"] = call(
            attn_norm_back_kernel,
            (
                shape(rows, width, dtype=F32),
                shape(rows, width),
                shape(rows, half),
                shape(1, width, dtype=F32),
                shape(1, half, dtype=F32),
            ),
            [SMEM, act, act, act, image_of(i, rows, width), line, act_half, act_half, line, ANY],
            [act, act, act_half, line, whole(1, half)],
            [
                pltpu.VMEM((width, width), BF),
                pltpu.VMEM((rows, width), BF),
                pltpu.VMEM((rows, width), F32),
                pltpu.VMEM((8, width), F32),
                pltpu.SemaphoreType.DMA((1,)),
            ],
            name="attn_norm_back",
            flops=2 * rows * width * width,
            moved=2 * width * width + 16 * block_mb,
        )(s["sc"], s["dh2"], s["dh2x"], s["x1"], cotangent, ln2, s["o"], s["ox"], again, rest)
        s["dq"], s["keep"], s["send"] = call(
            attend_back_kernel,
            (shape(rows, half), shape(2, rows, 2 * half), shape(2, rows, 2 * half)),
            [SMEM, act_half] + [whole(rows, 2 * half)] * 4 + [act_half, act_half, whole(8, 2 * rows), rope_spec],
            [act_half, whole(2, rows, 2 * half), whole(2, rows, 2 * half)],
            [pltpu.VMEM((LANES, 2 * rows), F32)],
            name="attend_back",
            flops=40 * rows * 4 * rows * half,
            moved=20 * block_mb,
        )(s["n"], s["q"], s["kv"], s["kvc"], s["kvf"], s["kvx"], s["o"], s["do"], s["lse"], tables)
        s["recv"] = near(s["send"])
        s["far"] = far((s["keep"][1].astype(F32) + s["recv"][1].astype(F32)).astype(BF))
    grad_tokens = None
    for i in range(images):
        s = st[i]
        s["dkv"], s["dh1"] = call(
            qkv_back_kernel,
            (shape(rows, 2 * half), shape(rows, width)),
            [
                pl.BlockSpec((1, rows, 2 * half), lambda i: (0, 0, 0)),
                pl.BlockSpec((1, rows, 2 * half), lambda i: (0, 0, 0)),
                whole(rows, 2 * half),
                act_half,
                rope_spec,
                qkv_spec,
            ],
            [whole(rows, 2 * half), act],
            name="qkv_back",
            flops=2 * rows * width * 3 * half,
            moved=6 * width * half + 10 * block_mb,
        )(s["keep"], s["recv"], s["far"], s["dq"], tables, full_qkv)
        s["dh1x"] = swap(s["dh1"])
    for i in range(images):
        s = st[i]
        again_buf = [] if grad_tokens is None else [grad_tokens]
        grad_tokens, s["dln1"] = call(
            tokens_back_kernel,
            (shape(images, rows, width), shape(1, width, dtype=F32)),
            [act, act, image_of(i, rows, width), line, act] + [ANY] * len(again_buf),
            [image_of(i, rows, width), line],
            name="tokens_back",
            moved=12 * block_mb,
            aliases={5: 0} if again_buf else None,
        )(s["dh1"], s["dh1x"], tokens, ln1, s["dx"], *again_buf)
    mixed = None
    for i in range(images):
        s = st[i]
        again_buf = [] if mixed is None else [mixed]
        mixed = call(
            mixed_kernel,
            shape(images, rows, width),
            [act, act, act] + [ANY] * len(again_buf),
            image_of(i, rows, width),
            name="mixed",
            moved=10 * block_mb,
            aliases={3: 0} if again_buf else None,
        )(s["x1"], s["out"], s["outx"], *again_buf)

    def stacked(name):
        return jnp.concatenate([s[name] for s in st], axis=0)

    def weight_grad(lhs, rhs):
        return dot_tn(lhs, rhs).astype(BF)

    query_pos = ctx * rows + jnp.arange(rows, dtype=jnp.int32)
    query_valid = query_pos[None, :] < lengths[:, None]
    dyb = jnp.where(query_valid[:, :, None], cotangent, jnp.zeros_like(cotangent)).reshape(images * rows, width)
    h2 = stacked("h2")
    grads_rest = jnp.concatenate(
        [
            weight_grad(stacked("dab"), stacked("a")),
            weight_grad(h2, stacked("dg")),
            weight_grad(h2, stacked("du")),
            weight_grad(dyb, stacked("m")),
        ],
        axis=1,
    )
    h1 = stacked("h1")
    grads_qkv = jnp.concatenate([weight_grad(h1, stacked("dq")), weight_grad(h1, stacked("dkv"))], axis=1)

    def reduce(value):
        own = lax.psum_scatter(value, both, scatter_dimension=0, tiled=True)
        return lax.all_gather(own, "ctx", axis=0, tiled=True).astype(F32)

    sum_rest = reduce(grads_rest)
    sum_qkv = reduce(grads_qkv)
    grad_proj = sum_rest[:, :half].T
    grad_pairs = jnp.stack(
        [sum_rest[:, half : half + ff], sum_rest[:, half + ffp : half + ffp + ff]]
    )
    grad_down = sum_rest[:, half + 2 * ffp : half + 2 * ffp + ff].T
    grad_qkv = jnp.stack([sum_qkv[:, j * half : (j + 1) * half] for j in range(3)])

    def gain(name):
        return sum(s[name] for s in st)[0]

    gain_ln1, gain_attn, gain_ln2, gain_ffn = lax.psum(
        (gain("dln1"), gain("dattn"), gain("dln2"), gain("dffn")), both
    )
    return (
        mixed,
        grad_tokens,
        gain_ln1,
        grad_qkv,
        gain_attn,
        grad_proj,
        gain_ln2,
        grad_pairs,
        gain_ffn[:ff],
        grad_down,
    )


def solution(mesh):
    tokens = P("shard", "ctx", None)
    matrix = P(None, "shard", "tp")
    flipped = P("tp", "shard")
    return jax.shard_map(
        local,
        mesh=mesh,
        in_specs=(
            tokens, tokens, P("shard"), P(), matrix, P("tp"), flipped, P(), matrix, P("tp"), flipped,
        ),
        out_specs=(tokens, tokens, P(), matrix, P("tp"), flipped, P(), matrix, P("tp"), flipped),
        check_vma=False,
    )
```

time: 1320 us -> 602 us (0.46)
  waiting for transfers between devices: 757 us -> 216 us
  matrix products: 230 us -> 23.8 us
  Pallas kernels: 0 us -> 159 us
  other arithmetic: 91.7 us -> 25.8 us
  local copies, waits for them, and re-layouts: 115 us -> 55.9 us
  blocking collectives: 93 us -> 67.3 us
  starting transfers between devices: 2.63 us -> 27.8 us
    reduce_scatter x7 -> x2, waiting for transfers between devices: 292 us -> 10.5 us  [reduce(): own = lax.psum_scatter(value, both, scatter_dimension=0, tiled=True)]
    all_gather x10 -> x3, waiting for transfers between devices: 256 us -> 39.3 us  [the longest x1 33.8 us: local(): full_qkv = lax.all_gather(qkv_part, both, axis=1, tiled=True)]
    dot_general x54 -> x6, matrix products: 230 us -> 23.8 us  [dot_tn(): lax.dot_general(a, b, (((0,), (0,)), ((), ())), preferred_element_type=F32)]
    psum x4 -> x0, waiting for transfers between devices: 206 us -> none  [the longest x1 97.5 us: local(): lax.psum(jnp.dot(entry_attn, full_proj, preferred_element_type=jnp.float3...]
    ppermute x0 -> x32, waiting for transfers between devices: none -> 166 us  [the longest x6 94.4 us: far(): return lax.ppermute(value, 'ctx', swap_far)]
    pallas_call x0 -> x27, Pallas kernels: none -> 159 us  [the longest x3 34.9 us: local(): call(attend_back_kernel, (shape(rows, half), shape(2, rows, 2 * half), sh...]
    psum x5 -> x1, blocking collectives: 93 us -> 59.9 us  [local(): lax.psum((gain('dln1'), gain('dattn'), gain('dln2'), gain('dffn')), both)]
    reduce_sum x16 -> x0, other arithmetic: 30.8 us -> none  [the longest x3 10.8 us: attend(): row_total = jnp.sum(exponent, axis=-1, keepdims=True)]
  transfers between devices with their start and end apart: 24 -> 37, of which waited for: 18 -> 16; matrix products, arithmetic and copies ran while one was open for 22% -> 8% of each run, Pallas kernels for 0% -> 26%
where the time goes in v1:
time: 602 us; the launch traced here: 592 us
  waiting for transfers between devices  216 us (36%)
  Pallas kernels  159 us (26%)
  blocking collectives  67.3 us (11%)
  local copies, waits for them, and re-layouts  55.9 us (9%)
  starting transfers between devices  27.8 us (5%)
  other arithmetic  25.8 us (4%)
  matrix products  23.8 us (4%)
  between operations  15.6 us (3%)
    ppermute x6, waiting for transfers between devices, far(): return lax.ppermute(value, 'ctx', swap_far)  94.4 us
    ppermute x17, waiting for transfers between devices, swap(): return lax.ppermute(value, 'tp', swap_tp)  71.7 us
    psum x1, blocking collectives, local(): lax.psum((gain('dln1'), gain('dattn'), gain('dln2'), gain('dffn')), both)  59.9 us
    unnamed x244, local copies, waits for them, and re-layouts  45 us
    pallas_call x3, Pallas kernels, local(): call(attend_back_kernel, (shape(rows, half), shape(2, rows, 2 * half), sh...  34.9 us
    all_gather x1, waiting for transfers between devices, local(): full_qkv = lax.all_gather(qkv_part, both, axis=1, tiled=True)  33.8 us
    pallas_call x3, Pallas kernels, local(): call(attend_kernel, (shape(rows, half), shape(8, 2 * rows, dtype=F32)), [...  28.2 us
    pallas_call x3, Pallas kernels, local(): call(middle_kernel, (shape(rows, width, dtype=F32), shape(rows, width), s...  27.6 us
  transfers between devices with their start and end apart: 37, of which 16 were waited for; matrix products, arithmetic and copies ran while one was open for 8% of the time, Pallas kernels for 26%

profile of v1, /device:TPU:0, one launch (start us, length us, event | category | flops | bytes accessed | tf_op | source)
XLA Modules:
  0.0 591.7 jit_solution(1629577227199401217)
XLA Ops:
  10.2 3.0 collective-permute-start.5
  22.0 3.2 broadcast_select_fusion
  25.2 33.8 %all-gather.4.cloned.1.call-done.w_ref = bf16[3,1024,512]{2,1,0:T(8,128)(2,1)} async-done(((bf16[3,64,512]{2,1,0:T(8,128)(2,1)}), bf16[3,1024,512]{2,1,0:T(8,128)(2,1)}) %all-gather.4.cloned.1.call-update) | async-done | bytes 3145744 | tf_op jit(solution)/shard_map/all_gather | solution.py:456
  58.9 3.5 qkv.3
  63.9 3.5 qkv.4
  69.8 3.5 qkv.5
  75.6 12.5 %collective-permute-done.1.kv2 = bf16[320,1024]{1,0:T(8,128)(2,1)S(1)} collective-permute-done((bf16[320,1024]{1,0:T(8,128)(2,1)S(1)}, bf16[320,1024]{1,0:T(8,128)(2,1)S(1)}, u32[]{:S(2)}, u32[]{:S(2)}) %collective-permute-start.1) | collective-permute-done | bytes 655392 | tf_op jit(solution)/shard_map/ppermute | solution.py:444
  90.0 12.1 %collective-permute-done.9.kv2 = bf16[320,1024]{1,0:T(8,128)(2,1)S(1)} collective-permute-done((bf16[320,1024]{1,0:T(8,128)(2,1)S(1)}, bf16[320,1024]{1,0:T(8,128)(2,1)S(1)}, u32[]{:S(2)}, u32[]{:S(2)}) %collective-permute-start.9) | collective-permute-done | bytes 655392 | tf_op jit(solution)/shard_map/ppermute | solution.py:444
  103.5 23.3 %collective-permute-done.15.kv2 = bf16[320,1024]{1,0:T(8,128)(2,1)S(1)} collective-permute-done((bf16[320,1024]{1,0:T(8,128)(2,1)S(1)}, bf16[320,1024]{1,0:T(8,128)(2,1)S(1)}, u32[]{:S(2)}, u32[]{:S(2)}) %collective-permute-start.15) | collective-permute-done | bytes 655392 | tf_op jit(solution)/shard_map/ppermute | solution.py:444
  126.8 6.1 %attend.3 = (bf16[320,512]{1,0:T(8,128)(2,1)S(1)}, f32[8,640]{1,0:T(8,128)S(1)}) custom-call(s32[4]{0:T(128)S(1)} %get-tuple-element.232.n_ref, bf16[320,512]{1,0:T(8,128)(2,1)S(1)} %get-tuple-element.100.q_ref, bf16[320,1024]{1,0:T(8,128)(2,1)S(1)} %get-tuple-element.101.kv0, bf16[320,1024]{1,0:T(8,128)(2,1)S(1)} %collective-permute-done.kv1, ...), custom_call_target="tpu_custom_call" | custom-call | flops 3355443200 | bytes 3932160 | tf_op jit(solution)/shard_map/attend/pallas_call | solution.py:508
  134.5 12.5 %attend.4 = (bf16[320,512]{1,0:T(8,128)(2,1)S(1)}, f32[8,640]{1,0:T(8,128)S(1)}) custom-call(s32[4]{0:T(128)S(1)} %get-tuple-element.231.n_ref, bf16[320,512]{1,0:T(8,128)(2,1)S(1)} %get-tuple-element.109.q_ref, bf16[320,1024]{1,0:T(8,128)(2,1)S(1)} %get-tuple-element.110.kv0, bf16[320,1024]{1,0:T(8,128)(2,1)S(1)} %collective-permute-done.8.kv1, ...), custom_call_target="tpu_custom_call" | custom-call | flops 3355443200 | bytes 3932160 | tf_op jit(solution)/shard_map/attend/pallas_call | solution.py:508
  148.6 9.7 %attend.5 = (bf16[320,512]{1,0:T(8,128)(2,1)S(1)}, f32[8,640]{1,0:T(8,128)S(1)}) custom-call(s32[4]{0:T(128)S(1)} %get-tuple-element.230.n_ref, bf16[320,512]{1,0:T(8,128)(2,1)S(1)} %get-tuple-element.118.q_ref, bf16[320,1024]{1,0:T(8,128)(2,1)S(1)} %get-tuple-element.119.kv0, bf16[320,1024]{1,0:T(8,128)(2,1)S(1)} %collective-permute-done.14.kv1, ...), custom_call_target="tpu_custom_call" | custom-call | flops 3355443200 | bytes 3932160 | tf_op jit(solution)/shard_map/attend/pallas_call | solution.py:508
  158.9 5.5 all-gather.6.cloned.1.call-done.w_ref
  164.4 9.1 %middle.3 = (f32[320,1024]{1,0:T(8,128)S(1)}, bf16[320,1024]{1,0:T(8,128)(2,1)S(1)}, bf16[320,1408]{1,0:T(8,128)(2,1)S(1)}, bf16[320,1408]{1,0:T(8,128)(2,1)S(1)...) custom-call(s32[2]{0:T(128)S(1)} %pad_add_fusion.sc_ref, ...), custom_call_target="tpu_custom_call" | custom-call | flops 3439329280 | bytes 17383424 | tf_op jit(solution)/shard_map/middle/pallas_call | solution.py:525
  175.7 9.2 %middle.4 = (f32[320,1024]{1,0:T(8,128)S(1)}, bf16[320,1024]{1,0:T(8,128)(2,1)S(1)}, bf16[320,1408]{1,0:T(8,128)(2,1)S(1)}, bf16[320,1408]{1,0:T(8,128)(2,1)S(1)...) custom-call(s32[2]{0:T(128)S(1)} %pad_add_fusion.1.sc_ref, ...), custom_call_target="tpu_custom_call" | custom-call | flops 3439329280 | bytes 17383424 | tf_op jit(solution)/shard_map/middle/pallas_call | solution.py:525
  186.8 9.4 %middle.5 = (f32[320,1024]{1,0:T(8,128)S(1)}, bf16[320,1024]{1,0:T(8,128)(2,1)S(1)}, bf16[320,1408]{1,0:T(8,128)(2,1)S(1)}, bf16[320,1408]{1,0:T(8,128)(2,1)S(1)...) custom-call(s32[2]{0:T(128)S(1)} %pad_add_fusion.2.sc_ref, ...), custom_call_target="tpu_custom_call" | custom-call | flops 3439329280 | bytes 17383424 | tf_op jit(solution)/shard_map/middle/pallas_call | solution.py:525
  200.0 7.3 %ffn.3 = (bf16[320,1408]{1,0:T(8,128)(2,1)S(1)}, bf16[320,1408]{1,0:T(8,128)(2,1)S(1)}, bf16[320,1408]{1,0:T(8,128)(2,1)S(1)}, bf16[320,1024]{1,0:T(8,128)(2,1)S...) custom-call(f32[8,384]{1,0:T(8,128)S(1)} %get-tuple-element.104.sa_ref, ...), custom_call_target="tpu_custom_call" | custom-call | flops 2768240640 | bytes 15368192 | tf_op jit(solution)/shard_map/ffn/pallas_call | solution.py:555
  212.0 7.3 %ffn.4 = (bf16[320,1408]{1,0:T(8,128)(2,1)S(1)}, bf16[320,1408]{1,0:T(8,128)(2,1)S(1)}, bf16[320,1408]{1,0:T(8,128)(2,1)S(1)}, bf16[320,1024]{1,0:T(8,128)(2,1)S...) custom-call(f32[8,384]{1,0:T(8,128)S(1)} %get-tuple-element.113.sa_ref, ...), custom_call_target="tpu_custom_call" | custom-call | flops 2768240640 | bytes 15368192 | tf_op jit(solution)/shard_map/ffn/pallas_call | solution.py:555
  223.2 7.4 %ffn.5 = (bf16[320,1408]{1,0:T(8,128)(2,1)S(1)}, bf16[320,1408]{1,0:T(8,128)(2,1)S(1)}, bf16[320,1408]{1,0:T(8,128)(2,1)S(1)}, bf16[320,1024]{1,0:T(8,128)(2,1)S...) custom-call(f32[8,384]{1,0:T(8,128)S(1)} %get-tuple-element.122.sa_ref, ...), custom_call_target="tpu_custom_call" | custom-call | flops 2768240640 | bytes 15368192 | tf_op jit(solution)/shard_map/ffn/pallas_call | solution.py:555
  232.6 7.0 %convolution_convert_fusion.1 = bf16[1024,1408]{1,0:T(8,128)(2,1)} fusion(bf16[960,1024]{1,0:T(8,128)(2,1)} %copy-done.110, bf16[320,1408]{1,0:T(8,128)(2,1)S(1)} %copy-done.52, bf16[320,1408]{1,0:T(8,128)(2,1)} %copy-done.57, bf16[320,1408]{1,0:T(8,128)(2,1)S(1)} %get-tuple-element.178), kind=kOutput, calls=%fused_computation.2 | convolution fusion | flops 2777792512 | bytes 7553024 | tf_op jit(solution)/shard_map/dot_general | solution.py:29
  239.6 4.9 convolution_convert_fusion.2
  244.6 4.9 convolution_convert_fusion
  251.4 5.2 attn_norm_back.3
  256.7 6.0 %attn_norm_back.4 = (f32[320,1024]{1,0:T(8,128)S(1)}, bf16[320,1024]{1,0:T(8,128)(2,1)S(1)}, bf16[320,512]{1,0:T(8,128)(2,1)S(1)}, f32[1,1024]{1,0:T(1,128)S(1)}, f32[1,512]{1,0:T(1,128)S(1)}) custom-call(s32[2]{0:T(128)S(1)} %pad_add_fusion.1.sc_ref, bf16[320,1024]{1,0:T(8,128)(2,1)S(1)} %get-tuple-element.135.dha_ref, ...), custom_call_target="tpu_custom_call" | custom-call | flops 671088640 | bytes 7340032 | tf_op jit(solution)/shard_map/attn_norm_back/pallas_call | solution.py:582
  264.6 5.3 attn_norm_back.5
  276.2 9.2 %pad_maximum_fusion = bf16[1024,4736]{1,0:T(8,128)(2,1)} fusion(bf16[1024,1408]{1,0:T(8,128)(2,1)} %convolution_convert_fusion, bf16[1024,1408]{1,0:T(8,128)(2,1)} %convolution_convert_fusion.1, bf16[1024,1408]{1,0:T(8,128)(2,1)} %convolution_convert_fusion.2, bf16[1024,512]{1,0:T(8,128)(2,1)} %copy.37), kind=kLoop, calls=%fused_computation | loop fusion | flops 38797312 | bytes 19398656 | tf_op jit(solution)/shard_map/concatenate | solution.py:672
  291.9 8.4 %attend_back.3 = (bf16[320,512]{1,0:T(8,128)(2,1)S(1)}, bf16[2,320,1024]{2,1,0:T(8,128)(2,1)S(1)}, bf16[2,320,1024]{2,1,0:T(8,128)(2,1)}) custom-call(s32[4]{0:T(128)S(1)} %get-tuple-element.232.n_ref, bf16[320,512]{1,0:T(8,128)(2,1)S(1)} %copy-done.89, bf16[320,1024]{1,0:T(8,128)(2,1)S(1)} %copy-done.69, bf16[320,1024]{1,0:T(8,128)(2,1)S(1)} %copy-done.73, ...), custom_call_target="tpu_custom_call" | custom-call | flops 8388608000 | bytes 6553600 | tf_op jit(solution)/shard_map/attend_back/pallas_call | solution.py:604
  300.5 14.2 %attend_back.4 = (bf16[320,512]{1,0:T(8,128)(2,1)S(1)}, bf16[2,320,1024]{2,1,0:T(8,128)(2,1)S(1)}, bf16[2,320,1024]{2,1,0:T(8,128)(2,1)}) custom-call(s32[4]{0:T(128)S(1)} %get-tuple-element.231.n_ref, bf16[320,512]{1,0:T(8,128)(2,1)S(1)} %copy-done.87, bf16[320,1024]{1,0:T(8,128)(2,1)S(1)} %copy-done.63, bf16[320,1024]{1,0:T(8,128)(2,1)S(1)} %copy-done.75, ...), custom_call_target="tpu_custom_call" | custom-call | flops 8388608000 | bytes 6553600 | tf_op jit(solution)/shard_map/attend_back/pallas_call | solution.py:604
  315.2 12.2 %attend_back.5 = (bf16[320,512]{1,0:T(8,128)(2,1)S(1)}, bf16[2,320,1024]{2,1,0:T(8,128)(2,1)S(1)}, bf16[2,320,1024]{2,1,0:T(8,128)(2,1)}) custom-call(s32[4]{0:T(128)S(1)} %get-tuple-element.230.n_ref, bf16[320,512]{1,0:T(8,128)(2,1)S(1)} %copy-done.85, bf16[320,1024]{1,0:T(8,128)(2,1)S(1)} %copy-done.61, bf16[320,1024]{1,0:T(8,128)(2,1)S(1)} %copy-done.81, ...), custom_call_target="tpu_custom_call" | custom-call | flops 8388608000 | bytes 6553600 | tf_op jit(solution)/shard_map/attend_back/pallas_call | solution.py:604
  333.4 13.3 %collective-permute-done.22.far_ref = bf16[320,1024]{1,0:T(8,128)(2,1)S(1)} collective-permute-done((bf16[320,1024]{1,0:T(8,128)(2,1)S(1)}, bf16[320,1024]{1,0:T(8,128)(2,1)S(1)}, u32[]{:S(2)}, u32[]{:S(2)}) %collective-permute-start.22) | collective-permute-done | bytes 655392 | tf_op jit(solution)/shard_map/ppermute | solution.py:444
  346.7 3.4 qkv_back.3
  351.0 17.2 %collective-permute-done.26.far_ref = bf16[320,1024]{1,0:T(8,128)(2,1)S(1)} collective-permute-done((bf16[320,1024]{1,0:T(8,128)(2,1)S(1)}, bf16[320,1024]{1,0:T(8,128)(2,1)S(1)}, u32[]{:S(2)}, u32[]{:S(2)}) %collective-permute-start.26) | collective-permute-done | bytes 655392 | tf_op jit(solution)/shard_map/ppermute | solution.py:444
  368.2 3.3 qkv_back.4
  371.5 16.0 %collective-permute-done.30.far_ref = bf16[320,1024]{1,0:T(8,128)(2,1)S(1)} collective-permute-done((bf16[320,1024]{1,0:T(8,128)(2,1)S(1)}, bf16[320,1024]{1,0:T(8,128)(2,1)S(1)}, u32[]{:S(2)}, u32[]{:S(2)}) %collective-permute-start.30) | collective-permute-done | bytes 655392 | tf_op jit(solution)/shard_map/ppermute | solution.py:444
  387.6 3.7 qkv_back.5
  391.3 2.4 fusion.27
  395.7 4.7 copy.41
  400.8 10.5 %reduce-scatter.5.cloned.1.call-done = bf16[64,4736]{1,0:T(8,128)(2,1)} async-done(((bf16[1024,4736]{1,0:T(8,128)(2,1)}), bf16[64,4736]{1,0:T(8,128)(2,1)}) %reduce-scatter.5.cloned.1.call-update) | async-done | bytes 606224 | tf_op jit(solution)/shard_map/reduce_scatter | solution.py:685
  416.9 12.3 %collective-permute-done.19.pb_ref = bf16[320,1024]{1,0:T(8,128)(2,1)S(1)} collective-permute-done((bf16[320,1024]{1,0:T(8,128)(2,1)}, bf16[320,1024]{1,0:T(8,128)(2,1)S(1)}, u32[]{:S(2)}, u32[]{:S(2)}) %collective-permute-start.19) | collective-permute-done | bytes 655392 | tf_op jit(solution)/shard_map/ppermute | solution.py:438
  432.9 10.4 %collective-permute-done.13.pb_ref = bf16[320,1024]{1,0:T(8,128)(2,1)S(1)} collective-permute-done((bf16[320,1024]{1,0:T(8,128)(2,1)}, bf16[320,1024]{1,0:T(8,128)(2,1)S(1)}, u32[]{:S(2)}, u32[]{:S(2)}) %collective-permute-start.13) | collective-permute-done | bytes 655392 | tf_op jit(solution)/shard_map/ppermute | solution.py:438
  444.4 13.0 %collective-permute-done.7.pb_ref = bf16[320,1024]{1,0:T(8,128)(2,1)S(1)} collective-permute-done((bf16[320,1024]{1,0:T(8,128)(2,1)S(1)}, bf16[320,1024]{1,0:T(8,128)(2,1)S(1)}, u32[]{:S(2)}, u32[]{:S(2)}) %collective-permute-start.7) | collective-permute-done | bytes 655392 | tf_op jit(solution)/shard_map/ppermute | solution.py:438
  458.4 13.0 %collective-permute-done.31.db_ref = bf16[320,1024]{1,0:T(8,128)(2,1)S(1)} collective-permute-done((bf16[320,1024]{1,0:T(8,128)(2,1)}, bf16[320,1024]{1,0:T(8,128)(2,1)S(1)}, u32[]{:S(2)}, u32[]{:S(2)}) %collective-permute-start.31) | collective-permute-done | bytes 655392 | tf_op jit(solution)/shard_map/ppermute | solution.py:438
  473.3 12.1 %collective-permute-done.27.db_ref = bf16[320,1024]{1,0:T(8,128)(2,1)S(1)} collective-permute-done((bf16[320,1024]{1,0:T(8,128)(2,1)}, bf16[320,1024]{1,0:T(8,128)(2,1)S(1)}, u32[]{:S(2)}, u32[]{:S(2)}) %collective-permute-start.27) | collective-permute-done | bytes 655392 | tf_op jit(solution)/shard_map/ppermute | solution.py:438
  487.4 10.8 %collective-permute-done.23.db_ref = bf16[320,1024]{1,0:T(8,128)(2,1)S(1)} collective-permute-done((bf16[320,1024]{1,0:T(8,128)(2,1)}, bf16[320,1024]{1,0:T(8,128)(2,1)S(1)}, u32[]{:S(2)}, u32[]{:S(2)}) %collective-permute-start.23) | collective-permute-done | bytes 655392 | tf_op jit(solution)/shard_map/ppermute | solution.py:438
  500.2 59.9 %all-reduce.4 = (f32[1024]{0:T(1024)}, f32[512]{0:T(512)}, f32[1024]{0:T(1024)}, f32[1408]{0:T(1024)}) all-reduce(f32[1024]{0:T(1024)S(1)} %bitcast.74, f32[512]{0:T(512)S(1)} %bitcast.75, f32[1024]{0:T(1024)S(1)} %bitcast.73, f32[1408]{0:T(1024)S(1)} %add_reduce_fusion), channel_id=1, replica_groups=mesh['shard'=4,'ctx'=4,'tp'=2] {'shard','ctx'}, use_global_device_ids=true, to_apply=%region_0.1 | all-reduce | flops 3968 | bytes 31744 | tf_op jit(solution)/shard_map/psum | solution.py:700
  560.1 7.4 %all_gather.14 = bf16[256,1536]{1,0:T(8,128)(2,1)S(1)} all-gather(bf16[64,1536]{1,0:T(8,128)(2,1)} %reduce-scatter.7.cloned.1.call-done), channel_id=1, replica_groups=mesh['shard'=4,'ctx'=4,'tp'=2] {'ctx'}, dimensions={0}, use_global_device_ids=true | all-gather | bytes 983040 | tf_op jit(solution)/shard_map/all_gather | solution.py:686
  574.1 3.6 pad_maximum_fusion.2
  577.6 5.6 copy.39
  (358 shorter events, 93.9 us)
Async XLA Ops:
  7.2 51.7 %all-gather.4.cloned.1.call-start = ((), (), s32[]{:S(2)}) async-start(), calls=%async_computation.2 | async-start | bytes 3342336 | tf_op jit(solution)/shard_map/all_gather | solution.py:456
  9.0 155.4 %all-gather.6.cloned.1.call-start = ((), (), s32[]{:S(2)}) async-start(), calls=%async_computation.3 | async-start | bytes 11419648 | tf_op jit(solution)/shard_map/all_gather | solution.py:469
  10.2 8.0 %collective-permute-start.5 = (bf16[64,512]{1,0:T(8,128)(2,1)S(1)}, bf16[64,512]{1,0:T(8,128)(2,1)S(1)}, u32[]{:S(2)}, u32[]{:S(2)}) collective-permute-start(bf16[64,512]{1,0:T(8,128)(2,1)S(1)} %bitcast.72), channel_id=1, source_target_pairs={{0,1},{1,0},{2,3},{3,2},{4,5},{5,4},{6,7},{7,6},{8,9},{9,8},{10,11... | collective-permute-start | bytes 196616 | tf_op jit(solution)/shard_map/ppermute | solution.py:438
  19.2 392.1 %reduce-scatter.5.cloned.1.call-start = ((), (), s32[]{:S(2)}) async-start(), calls=%async_computation.4 | async-start | bytes 10305536 | tf_op jit(solution)/shard_map/reduce_scatter | solution.py:685
  19.3 70.2 %collective-permute-start.4 = (f32[1,512]{1,0:T(1,128)S(1)}, f32[1,512]{1,0:T(1,128)S(1)}, u32[]{:S(2)}, u32[]{:S(2)}) collective-permute-start(f32[1,512]{1,0:T(1,128)S(1)} %bitcast.76), channel_id=1, source_target_pairs={{0,1},{1,0},{2,3},{3,2},{4,5},{5,4},{6,7},{7,6},{8,9},{9,8},{10,11... | collective-permute-start | bytes 6152 | tf_op jit(solution)/shard_map/ppermute | solution.py:438
  22.0 37.0 %copy-start.2 = (bf16[3,320,1024]{2,1,0:T(8,128)(2,1)S(1)}, bf16[3,320,1024]{2,1,0:T(8,128)(2,1)}, u32[]{:S(2)}) copy-start(bf16[3,320,1024]{2,1,0:T(8,128)(2,1)} %x_ref.17) | copy-start | bytes 5898244
  22.0 37.0 %copy-start.45 = (f32[1024]{0:T(1024)S(1)}, f32[1024]{0:T(1024)}, u32[]{:S(2)}) copy-start(f32[1024]{0:T(1024)} %param.14) | copy-start | bytes 12292
  63.3 63.5 %copy-start.68 = (bf16[320,1024]{1,0:T(8,128)(2,1)}, bf16[320,1024]{1,0:T(8,128)(2,1)S(1)}, u32[]{:S(2)}) copy-start(bf16[320,1024]{1,0:T(8,128)(2,1)S(1)} %get-tuple-element.101.kv0) | copy-start | bytes 1966084
  63.3 63.5 %copy-start.88 = (bf16[320,512]{1,0:T(8,128)(2,1)}, bf16[320,512]{1,0:T(8,128)(2,1)S(1)}, u32[]{:S(2)}) copy-start(bf16[320,512]{1,0:T(8,128)(2,1)S(1)} %get-tuple-element.100.q_ref) | copy-start | bytes 983044
  63.3 24.8 %collective-permute-start.1 = (bf16[320,1024]{1,0:T(8,128)(2,1)S(1)}, bf16[320,1024]{1,0:T(8,128)(2,1)S(1)}, u32[]{:S(2)}, u32[]{:S(2)}) collective-permute-start(bf16[320,1024]{1,0:T(8,128)(2,1)S(1)} %get-tuple-element.101.kv0), channel_id=1, source_target_pairs={{0,4},{2,6},{4,0},{6,2},{1,5},{3,7},{5,1},{7,3},{8,12},{10,14},{12... | collective-permute-start | bytes 1966088 | tf_op jit(solution)/shard_map/ppermute | solution.py:444
  68.3 66.2 %copy-start.62 = (bf16[320,1024]{1,0:T(8,128)(2,1)}, bf16[320,1024]{1,0:T(8,128)(2,1)S(1)}, u32[]{:S(2)}) copy-start(bf16[320,1024]{1,0:T(8,128)(2,1)S(1)} %get-tuple-element.110.kv0) | copy-start | bytes 1966084
  68.3 66.2 %copy-start.86 = (bf16[320,512]{1,0:T(8,128)(2,1)}, bf16[320,512]{1,0:T(8,128)(2,1)S(1)}, u32[]{:S(2)}) copy-start(bf16[320,512]{1,0:T(8,128)(2,1)S(1)} %get-tuple-element.109.q_ref) | copy-start | bytes 983044
  68.3 33.8 %collective-permute-start.9 = (bf16[320,1024]{1,0:T(8,128)(2,1)S(1)}, bf16[320,1024]{1,0:T(8,128)(2,1)S(1)}, u32[]{:S(2)}, u32[]{:S(2)}) collective-permute-start(bf16[320,1024]{1,0:T(8,128)(2,1)S(1)} %get-tuple-element.110.kv0), channel_id=1, source_target_pairs={{0,4},{2,6},{4,0},{6,2},{1,5},{3,7},{5,1},{7,3},{8,12},{10,14},{12... | collective-permute-start | bytes 1966088 | tf_op jit(solution)/shard_map/ppermute | solution.py:444
  69.8 33.1 %collective-permute-start = (bf16[320,1024]{1,0:T(8,128)(2,1)S(1)}, bf16[320,1024]{1,0:T(8,128)(2,1)S(1)}, u32[]{:S(2)}, u32[]{:S(2)}) collective-permute-start(bf16[320,1024]{1,0:T(8,128)(2,1)S(1)} %get-tuple-element.101.kv0), channel_id=1, source_target_pairs={{0,2},{2,0},{4,6},{6,4},{1,3},{3,1},{5,7},{7,5},{8,10},{10,8},{12,... | collective-permute-start | bytes 1966088 | tf_op jit(solution)/shard_map/ppermute | solution.py:441
  74.2 74.4 %copy-start.60 = (bf16[320,1024]{1,0:T(8,128)(2,1)}, bf16[320,1024]{1,0:T(8,128)(2,1)S(1)}, u32[]{:S(2)}) copy-start(bf16[320,1024]{1,0:T(8,128)(2,1)S(1)} %get-tuple-element.119.kv0) | copy-start | bytes 1966084
  74.2 74.4 %copy-start.84 = (bf16[320,512]{1,0:T(8,128)(2,1)}, bf16[320,512]{1,0:T(8,128)(2,1)S(1)}, u32[]{:S(2)}) copy-start(bf16[320,512]{1,0:T(8,128)(2,1)S(1)} %get-tuple-element.118.q_ref) | copy-start | bytes 983044
  74.2 52.5 %collective-permute-start.15 = (bf16[320,1024]{1,0:T(8,128)(2,1)S(1)}, bf16[320,1024]{1,0:T(8,128)(2,1)S(1)}, u32[]{:S(2)}, u32[]{:S(2)}) collective-permute-start(bf16[320,1024]{1,0:T(8,128)(2,1)S(1)} %get-tuple-element.119.kv0), channel_id=1, source_target_pairs={{0,4},{2,6},{4,0},{6,2},{1,5},{3,7},{5,1},{7,3},{8,12},{10,14},{12... | collective-permute-start | bytes 1966088 | tf_op jit(solution)/shard_map/ppermute | solution.py:444
  88.1 44.8 %copy-start.70 = (bf16[320,1024]{1,0:T(8,128)(2,1)}, bf16[320,1024]{1,0:T(8,128)(2,1)S(1)}, u32[]{:S(2)}) copy-start(bf16[320,1024]{1,0:T(8,128)(2,1)S(1)} %collective-permute-done.1.kv2) | copy-start | bytes 1966084
  88.1 38.7 %collective-permute-start.2 = (bf16[320,1024]{1,0:T(8,128)(2,1)S(1)}, bf16[320,1024]{1,0:T(8,128)(2,1)S(1)}, u32[]{:S(2)}, u32[]{:S(2)}) collective-permute-start(bf16[320,1024]{1,0:T(8,128)(2,1)S(1)} %collective-permute-done.1.kv2), channel_id=1, source_target_pairs={{0,2},{2,0},{4,6},{6,4},{1,3},{3,1},{5,7},{7,5},{8,10},{10,8},{12,... | collective-permute-start | bytes 1966088 | tf_op jit(solution)/shard_map/ppermute | solution.py:441
  89.5 45.0 %collective-permute-start.8 = (bf16[320,1024]{1,0:T(8,128)(2,1)S(1)}, bf16[320,1024]{1,0:T(8,128)(2,1)S(1)}, u32[]{:S(2)}, u32[]{:S(2)}) collective-permute-start(bf16[320,1024]{1,0:T(8,128)(2,1)S(1)} %get-tuple-element.110.kv0), channel_id=1, source_target_pairs={{0,2},{2,0},{4,6},{6,4},{1,3},{3,1},{5,7},{7,5},{8,10},{10,8},{12,... | collective-permute-start | bytes 1966088 | tf_op jit(solution)/shard_map/ppermute | solution.py:441
  102.1 32.4 %collective-permute-start.10 = (bf16[320,1024]{1,0:T(8,128)(2,1)S(1)}, bf16[320,1024]{1,0:T(8,128)(2,1)S(1)}, u32[]{:S(2)}, u32[]{:S(2)}) collective-permute-start(bf16[320,1024]{1,0:T(8,128)(2,1)S(1)} %collective-permute-done.9.kv2), channel_id=1, source_target_pairs={{0,2},{2,0},{4,6},{6,4},{1,3},{3,1},{5,7},{7,5},{8,10},{10,8},{12,... | collective-permute-start | bytes 1966088 | tf_op jit(solution)/shard_map/ppermute | solution.py:441
  102.9 45.6 %collective-permute-start.14 = (bf16[320,1024]{1,0:T(8,128)(2,1)S(1)}, bf16[320,1024]{1,0:T(8,128)(2,1)S(1)}, u32[]{:S(2)}, u32[]{:S(2)}) collective-permute-start(bf16[320,1024]{1,0:T(8,128)(2,1)S(1)} %get-tuple-element.119.kv0), channel_id=1, source_target_pairs={{0,2},{2,0},{4,6},{6,4},{1,3},{3,1},{5,7},{7,5},{8,10},{10,8},{12,... | collective-permute-start | bytes 1966088 | tf_op jit(solution)/shard_map/ppermute | solution.py:441
  126.8 21.8 %collective-permute-start.16 = (bf16[320,1024]{1,0:T(8,128)(2,1)S(1)}, bf16[320,1024]{1,0:T(8,128)(2,1)S(1)}, u32[]{:S(2)}, u32[]{:S(2)}) collective-permute-start(bf16[320,1024]{1,0:T(8,128)(2,1)S(1)} %collective-permute-done.15.kv2), channel_id=1, source_target_pairs={{0,2},{2,0},{4,6},{6,4},{1,3},{3,1},{5,7},{7,5},{8,10},{10,8},{12,... | collective-permute-start | bytes 1966088 | tf_op jit(solution)/shard_map/ppermute | solution.py:441
  132.9 26.0 %collective-permute-start.3 = (bf16[320,512]{1,0:T(8,128)(2,1)S(1)}, bf16[320,512]{1,0:T(8,128)(2,1)S(1)}, u32[]{:S(2)}, u32[]{:S(2)}) collective-permute-start(bf16[320,512]{1,0:T(8,128)(2,1)S(1)} %get-tuple-element.102.own_ref.o_ref), channel_id=1, source_target_pairs={{0,1},{1,0},{2,3},{3,2},{4,5},{5,4},{6,7},{7,6},{8,9},{9,8},{10,11... | collective-permute-start | bytes 983048 | tf_op jit(solution)/shard_map/ppermute | solution.py:438
  147.0 28.7 %collective-permute-start.11 = (bf16[320,512]{1,0:T(8,128)(2,1)S(1)}, bf16[320,512]{1,0:T(8,128)(2,1)}, u32[]{:S(2)}, u32[]{:S(2)}) collective-permute-start(bf16[320,512]{1,0:T(8,128)(2,1)S(1)} %get-tuple-element.111.own_ref.o_ref), channel_id=1, source_target_pairs={{0,1},{1,0},{2,3},{3,2},{4,5},{5,4},{6,7},{7,6},{8,9},{9,8},{10,11... | collective-permute-start | bytes 983048 | tf_op jit(solution)/shard_map/ppermute | solution.py:438
  158.3 28.5 %collective-permute-start.17 = (bf16[320,512]{1,0:T(8,128)(2,1)S(1)}, bf16[320,512]{1,0:T(8,128)(2,1)S(1)}, u32[]{:S(2)}, u32[]{:S(2)}) collective-permute-start(bf16[320,512]{1,0:T(8,128)(2,1)S(1)} %get-tuple-element.120.own_ref.o_ref), channel_id=1, source_target_pairs={{0,1},{1,0},{2,3},{3,2},{4,5},{5,4},{6,7},{7,6},{8,9},{9,8},{10,11... | collective-permute-start | bytes 983048 | tf_op jit(solution)/shard_map/ppermute | solution.py:438
  174.3 23.3 %collective-permute-start.6 = (f32[8,384]{1,0:T(8,128)S(1)}, f32[8,384]{1,0:T(8,128)S(1)}, u32[]{:S(2)}, u32[]{:S(2)}) collective-permute-start(f32[8,384]{1,0:T(8,128)S(1)} %get-tuple-element.104.sa_ref), channel_id=1, source_target_pairs={{0,1},{1,0},{2,3},{3,2},{4,5},{5,4},{6,7},{7,6},{8,9},{9,8},{10,11... | collective-permute-start | bytes 36872 | tf_op jit(solution)/shard_map/ppermute | solution.py:438
  185.8 70.9 %copy-start.4 = (f32[320,1024]{1,0:T(8,128)}, f32[320,1024]{1,0:T(8,128)S(1)}, u32[]{:S(2)}) copy-start(f32[320,1024]{1,0:T(8,128)S(1)} %get-tuple-element.112.x1_ref) | copy-start | bytes 3932164
  185.8 26.1 %collective-permute-start.12 = (f32[8,384]{1,0:T(8,128)S(1)}, f32[8,384]{1,0:T(8,128)S(1)}, u32[]{:S(2)}, u32[]{:S(2)}) collective-permute-start(f32[8,384]{1,0:T(8,128)S(1)} %get-tuple-element.113.sa_ref), channel_id=1, source_target_pairs={{0,1},{1,0},{2,3},{3,2},{4,5},{5,4},{6,7},{7,6},{8,9},{9,8},{10,11... | collective-permute-start | bytes 36872 | tf_op jit(solution)/shard_map/ppermute | solution.py:438
  196.2 68.4 %copy-start.6 = (f32[320,1024]{1,0:T(8,128)}, f32[320,1024]{1,0:T(8,128)S(1)}, u32[]{:S(2)}) copy-start(f32[320,1024]{1,0:T(8,128)S(1)} %get-tuple-element.121.x1_ref) | copy-start | bytes 3932164
  196.2 27.0 %collective-permute-start.18 = (f32[8,384]{1,0:T(8,128)S(1)}, f32[8,384]{1,0:T(8,128)S(1)}, u32[]{:S(2)}, u32[]{:S(2)}) collective-permute-start(f32[8,384]{1,0:T(8,128)S(1)} %get-tuple-element.122.sa_ref), channel_id=1, source_target_pairs={{0,1},{1,0},{2,3},{3,2},{4,5},{5,4},{6,7},{7,6},{8,9},{9,8},{10,11... | collective-permute-start | bytes 36872 | tf_op jit(solution)/shard_map/ppermute | solution.py:438
  210.9 38.6 %collective-permute-start.20 = (bf16[320,1024]{1,0:T(8,128)(2,1)S(1)}, bf16[320,1024]{1,0:T(8,128)(2,1)S(1)}, u32[]{:S(2)}, u32[]{:S(2)}) collective-permute-start(bf16[320,1024]{1,0:T(8,128)(2,1)S(1)} %get-tuple-element.127.dha_ref), channel_id=1, source_target_pairs={{0,1},{1,0},{2,3},{3,2},{4,5},{5,4},{6,7},{7,6},{8,9},{9,8},{10,11... | collective-permute-start | bytes 1966088 | tf_op jit(solution)/shard_map/ppermute | solution.py:438
  222.2 34.5 %collective-permute-start.24 = (bf16[320,1024]{1,0:T(8,128)(2,1)S(1)}, bf16[320,1024]{1,0:T(8,128)(2,1)}, u32[]{:S(2)}, u32[]{:S(2)}) collective-permute-start(bf16[320,1024]{1,0:T(8,128)(2,1)S(1)} %get-tuple-element.135.dha_ref), channel_id=1, source_target_pairs={{0,1},{1,0},{2,3},{3,2},{4,5},{5,4},{6,7},{7,6},{8,9},{9,8},{10,11... | collective-permute-start | bytes 1966088 | tf_op jit(solution)/shard_map/ppermute | solution.py:438
  231.6 33.0 %collective-permute-start.28 = (bf16[320,1024]{1,0:T(8,128)(2,1)S(1)}, bf16[320,1024]{1,0:T(8,128)(2,1)S(1)}, u32[]{:S(2)}, u32[]{:S(2)}) collective-permute-start(bf16[320,1024]{1,0:T(8,128)(2,1)S(1)} %get-tuple-element.143.dha_ref), channel_id=1, source_target_pairs={{0,1},{1,0},{2,3},{3,2},{4,5},{5,4},{6,7},{7,6},{8,9},{9,8},{10,11... | collective-permute-start | bytes 1966088 | tf_op jit(solution)/shard_map/ppermute | solution.py:438
  285.5 274.6 %reduce-scatter.7.cloned.1.call-start = ((), (), s32[]{:S(2)}) async-start(), calls=%async_computation.6 | async-start | bytes 3342336 | tf_op jit(solution)/shard_map/reduce_scatter | solution.py:685
  300.3 27.5 %collective-permute-start.21 = (bf16[2,320,1024]{2,1,0:T(8,128)(2,1)}, bf16[2,320,1024]{2,1,0:T(8,128)(2,1)S(1)}, u32[]{:S(2)}, u32[]{:S(2)}) collective-permute-start(bf16[2,320,1024]{2,1,0:T(8,128)(2,1)} %get-tuple-element.131), channel_id=1, source_target_pairs={{0,2},{2,0},{4,6},{6,4},{1,3},{3,1},{5,7},{7,5},{8,10},{10,8},{12,... | collective-permute-start | bytes 3932168 | tf_op jit(solution)/shard_map/ppermute | solution.py:441
  314.7 13.5 %collective-permute-start.25 = (bf16[2,320,1024]{2,1,0:T(8,128)(2,1)}, bf16[2,320,1024]{2,1,0:T(8,128)(2,1)S(1)}, u32[]{:S(2)}, u32[]{:S(2)}) collective-permute-start(bf16[2,320,1024]{2,1,0:T(8,128)(2,1)} %get-tuple-element.139), channel_id=1, source_target_pairs={{0,2},{2,0},{4,6},{6,4},{1,3},{3,1},{5,7},{7,5},{8,10},{10,8},{12,... | collective-permute-start | bytes 3932168 | tf_op jit(solution)/shard_map/ppermute | solution.py:441
  327.4 3.2 collective-permute-start.29
  328.1 18.6 %collective-permute-start.22 = (bf16[320,1024]{1,0:T(8,128)(2,1)S(1)}, bf16[320,1024]{1,0:T(8,128)(2,1)S(1)}, u32[]{:S(2)}, u32[]{:S(2)}) collective-permute-start(bf16[320,1024]{1,0:T(8,128)(2,1)S(1)} %fusion.43), channel_id=1, source_target_pairs={{0,4},{2,6},{4,0},{6,2},{1,5},{3,7},{5,1},{7,3},{8,12},{10,14},{12... | collective-permute-start | bytes 1966088 | tf_op jit(solution)/shard_map/ppermute | solution.py:444
  328.5 39.7 %collective-permute-start.26 = (bf16[320,1024]{1,0:T(8,128)(2,1)S(1)}, bf16[320,1024]{1,0:T(8,128)(2,1)S(1)}, u32[]{:S(2)}, u32[]{:S(2)}) collective-permute-start(bf16[320,1024]{1,0:T(8,128)(2,1)S(1)} %fusion.44), channel_id=1, source_target_pairs={{0,4},{2,6},{4,0},{6,2},{1,5},{3,7},{5,1},{7,3},{8,12},{10,14},{12... | collective-permute-start | bytes 1966088 | tf_op jit(solution)/shard_map/ppermute | solution.py:444
  330.9 56.6 %collective-permute-start.30 = (bf16[320,1024]{1,0:T(8,128)(2,1)S(1)}, bf16[320,1024]{1,0:T(8,128)(2,1)S(1)}, u32[]{:S(2)}, u32[]{:S(2)}) collective-permute-start(bf16[320,1024]{1,0:T(8,128)(2,1)S(1)} %fusion.45), channel_id=1, source_target_pairs={{0,4},{2,6},{4,0},{6,2},{1,5},{3,7},{5,1},{7,3},{8,12},{10,14},{12... | collective-permute-start | bytes 1966088 | tf_op jit(solution)/shard_map/ppermute | solution.py:444
  400.5 168.6 %all-gather.8.cloned.1.call-start = ((), (), s32[]{:S(2)}) async-start(), calls=%async_computation.5 | async-start | bytes 3031040 | tf_op jit(solution)/shard_map/all_gather | solution.py:686
  411.4 17.9 %collective-permute-start.19 = (bf16[320,1024]{1,0:T(8,128)(2,1)}, bf16[320,1024]{1,0:T(8,128)(2,1)S(1)}, u32[]{:S(2)}, u32[]{:S(2)}) collective-permute-start(bf16[320,1024]{1,0:T(8,128)(2,1)} %copy-done.29), channel_id=1, source_target_pairs={{0,1},{1,0},{2,3},{3,2},{4,5},{5,4},{6,7},{7,6},{8,9},{9,8},{10,11... | collective-permute-start | bytes 1966088 | tf_op jit(solution)/shard_map/ppermute | solution.py:438
  412.9 30.4 %collective-permute-start.13 = (bf16[320,1024]{1,0:T(8,128)(2,1)}, bf16[320,1024]{1,0:T(8,128)(2,1)S(1)}, u32[]{:S(2)}, u32[]{:S(2)}) collective-permute-start(bf16[320,1024]{1,0:T(8,128)(2,1)} %copy-done.27), channel_id=1, source_target_pairs={{0,1},{1,0},{2,3},{3,2},{4,5},{5,4},{6,7},{7,6},{8,9},{9,8},{10,11... | collective-permute-start | bytes 1966088 | tf_op jit(solution)/shard_map/ppermute | solution.py:438
  413.5 43.9 %collective-permute-start.7 = (bf16[320,1024]{1,0:T(8,128)(2,1)S(1)}, bf16[320,1024]{1,0:T(8,128)(2,1)S(1)}, u32[]{:S(2)}, u32[]{:S(2)}) collective-permute-start(bf16[320,1024]{1,0:T(8,128)(2,1)S(1)} %copy-done.26), channel_id=1, source_target_pairs={{0,1},{1,0},{2,3},{3,2},{4,5},{5,4},{6,7},{7,6},{8,9},{9,8},{10,11... | collective-permute-start | bytes 1966088 | tf_op jit(solution)/shard_map/ppermute | solution.py:438
  414.9 56.5 %collective-permute-start.31 = (bf16[320,1024]{1,0:T(8,128)(2,1)}, bf16[320,1024]{1,0:T(8,128)(2,1)S(1)}, u32[]{:S(2)}, u32[]{:S(2)}) collective-permute-start(bf16[320,1024]{1,0:T(8,128)(2,1)} %copy-done.43), channel_id=1, source_target_pairs={{0,1},{1,0},{2,3},{3,2},{4,5},{5,4},{6,7},{7,6},{8,9},{9,8},{10,11... | collective-permute-start | bytes 1966088 | tf_op jit(solution)/shard_map/ppermute | solution.py:438
  415.5 70.0 %collective-permute-start.27 = (bf16[320,1024]{1,0:T(8,128)(2,1)}, bf16[320,1024]{1,0:T(8,128)(2,1)S(1)}, u32[]{:S(2)}, u32[]{:S(2)}) collective-permute-start(bf16[320,1024]{1,0:T(8,128)(2,1)} %copy-done.41), channel_id=1, source_target_pairs={{0,1},{1,0},{2,3},{3,2},{4,5},{5,4},{6,7},{7,6},{8,9},{9,8},{10,11... | collective-permute-start | bytes 1966088 | tf_op jit(solution)/shard_map/ppermute | solution.py:438
  429.3 69.0 %collective-permute-start.23 = (bf16[320,1024]{1,0:T(8,128)(2,1)}, bf16[320,1024]{1,0:T(8,128)(2,1)S(1)}, u32[]{:S(2)}, u32[]{:S(2)}) collective-permute-start(bf16[320,1024]{1,0:T(8,128)(2,1)} %copy-done.39), channel_id=1, source_target_pairs={{0,1},{1,0},{2,3},{3,2},{4,5},{5,4},{6,7},{7,6},{8,9},{9,8},{10,11... | collective-permute-start | bytes 1966088 | tf_op jit(solution)/shard_map/ppermute | solution.py:438
  (104 other events, 838.7 us)
Sparse Core Ops, SparseCore 0:
  10.8 48.0 all-gather.3
  61.8 102.5 all-gather.5
  285.6 125.6 reduce-scatter.4
  415.5 65.9 reduce-scatter.6
  483.0 23.3 all-gather.7

commit v2 on v1

--- a/solution.py
+++ b/solution.py
@@ -208,49 +208,69 @@
 
 
 def middle_kernel(
-    sc_ref, x_ref, cot_ref, own_ref, other_ref, again_ref, ln2_ref, fgain_ref, w_ref,
+    sc_ref, x_ref, cot_ref, own_ref0, own_ref1, own_ref2, other_ref0, other_ref1, other_ref2,
+    again_ref, ln2_ref, fgain_ref, wp_ref, ws_ref,
     x1_ref, h2_ref, g_ref, u_ref, dm_ref, a_ref, st_ref,
     pj_s, gw_s, uw_s, dw_s, o_s, a_s, st_s, sem,
 ):
+    image = pl.program_id(0)
     width = x_ref.shape[2]
-    half = own_ref.shape[1]
-    rows = own_ref.shape[0]
-    ff = g_ref.shape[1]
-    loads = []
-    at = 0
-    for slot, dst in enumerate((pj_s, gw_s, uw_s, dw_s)):
-        loads.append(
-            pltpu.make_async_copy(w_ref.at[:, pl.ds(at, dst.shape[1])], dst, sem.at[slot])
-        )
-        at += dst.shape[1]
-    for load in loads:
-        load.start()
-    tp = sc_ref[1]
-    merge_heads(o_s, own_ref, other_ref, tp, half)
+    half = own_ref0.shape[1]
+    rows = own_ref0.shape[0]
+    ff = g_ref.shape[2]
+    loads = [
+        pltpu.make_async_copy(ws_ref.at[:, pl.ds(0, width)], pj_s, sem.at[0]),
+        pltpu.make_async_copy(wp_ref.at[:, pl.ds(0, ff)], gw_s, sem.at[1]),
+        pltpu.make_async_copy(wp_ref.at[:, pl.ds(ff, ff)], uw_s, sem.at[2]),
+        pltpu.make_async_copy(ws_ref.at[:, pl.ds(width, ff)], dw_s, sem.at[3]),
+    ]
+
+    @pl.when(image == 0)
+    def _():
+        for load in loads:
+            load.start()
+
+    tp = sc_ref[3]
+    for at, (own_ref, other_ref) in enumerate(
+        ((own_ref0, other_ref0), (own_ref1, other_ref1), (own_ref2, other_ref2))
+    ):
+
+        @pl.when(image == at)
+        def _():
+            merge_heads(o_s, own_ref, other_ref, tp, half)
+
     normed, _ = row_norm(o_s[...].astype(F32), width)
     a_s[...] = (normed * again_ref[...]).astype(BF)
-    a_ref[...] = a_s[:, pl.ds(pl.multiple_of(tp * half, half), half)]
-    loads[0].wait()
+    a_ref[0] = a_s[:, pl.ds(pl.multiple_of(tp * half, half), half)]
+
+    @pl.when(image == 0)
+    def _():
+        loads[0].wait()
+
     a = a_s[...]
     for at, size in tiles(width):
-        x1_ref[:, at : at + size] = x_ref[0, :, at : at + size].astype(F32) + dot_nt(
+        x1_ref[0, :, at : at + size] = x_ref[0, :, at : at + size].astype(F32) + dot_nt(
             a, pj_s[at : at + size, :]
         )
-    normed, _ = row_norm(x1_ref[...], width)
-    h2_ref[...] = (normed * ln2_ref[...]).astype(BF)
-    h2 = h2_ref[...]
-    dyb = valid_rows(cot_ref[0], sc_ref[0])
-    for load in loads[1:]:
-        load.wait()
+    normed, _ = row_norm(x1_ref[0], width)
+    h2_ref[0] = (normed * ln2_ref[...]).astype(BF)
+    h2 = h2_ref[0]
+    dyb = valid_rows(cot_ref[0], sc_ref[image])
+
+    @pl.when(image == 0)
+    def _():
+        for load in loads[1:]:
+            load.wait()
+
     sums = [jnp.zeros((rows, LANES), F32) for _ in range(4)]
     for at, size in tiles(ff):
         span = slice(at, at + size)
         g = dot_nn(h2, gw_s[:, span]).astype(BF)
         u = dot_nn(h2, uw_s[:, span]).astype(BF)
         dm = dot_nn(dyb, dw_s[:, span]).astype(BF)
-        g_ref[:, span] = g
-        u_ref[:, span] = u
-        dm_ref[:, span] = dm
+        g_ref[0, :, span] = g
+        u_ref[0, :, span] = u
+        dm_ref[0, :, span] = dm
         gf = g.astype(F32)
         z = gf * jax.nn.sigmoid(gf) * u.astype(F32)
         e = dm.astype(F32) * fgain_ref[:, span]
@@ -264,27 +284,25 @@
         packed = jnp.where(lane == slot, jnp.sum(part, axis=1, keepdims=True), packed)
     st_s[...] = jnp.zeros(st_s.shape, F32)
     st_s[:rows, :] = packed
-    st_ref[...] = st_s[...].T[:8, :]
+    st_ref[0] = st_s[...].T[:8, :]
 
 
 def ffn_kernel(
-    sa_ref, sb_ref, g_ref, u_ref, dm_ref, fgain_ref, w_ref,
+    sa_ref, sb_ref, g_ref, u_ref, dm_ref, fgain_ref, wp_ref, ws_ref,
     m_ref, dg_ref, du_ref, out_ref, dh_ref, dgain_ref,
     gw_s, uw_s, dw_s, st_s, sem, *, total,
 ):
-    rows, ff = g_ref.shape
-    width = w_ref.shape[0]
-    loads = []
-    at = width
-    for slot, dst in enumerate((gw_s, uw_s, dw_s)):
-        loads.append(
-            pltpu.make_async_copy(w_ref.at[:, pl.ds(at, dst.shape[1])], dst, sem.at[slot])
-        )
-        at += dst.shape[1]
+    _, rows, ff = g_ref.shape
+    width = wp_ref.shape[0]
+    loads = [
+        pltpu.make_async_copy(wp_ref.at[:, pl.ds(0, ff)], gw_s, sem.at[0]),
+        pltpu.make_async_copy(wp_ref.at[:, pl.ds(ff, ff)], uw_s, sem.at[1]),
+        pltpu.make_async_copy(ws_ref.at[:, pl.ds(width, ff)], dw_s, sem.at[2]),
+    ]
     for load in loads:
         load.start()
     st_s[...] = jnp.zeros(st_s.shape, F32)
-    st_s[:8, :] = sa_ref[...] + sb_ref[...]
+    st_s[:8, :] = sa_ref[0] + sb_ref[0]
     st = st_s[...].T[:rows, :]
     lane = lax.broadcasted_iota(jnp.int32, st.shape, 1)
 
@@ -297,9 +315,9 @@
     second = inv * (column(3) - mean * first)
     for at, size in tiles(ff):
         span = slice(at, at + size)
-        g = g_ref[:, span].astype(F32)
-        u = u_ref[:, span].astype(F32)
-        dm = dm_ref[:, span].astype(F32)
+        g = g_ref[0, :, span].astype(F32)
+        u = u_ref[0, :, span].astype(F32)
+        dm = dm_ref[0, :, span].astype(F32)
         gain = fgain_ref[:, span]
         sig = jax.nn.sigmoid(g)
         act = g * sig
@@ -328,13 +346,13 @@
     dx_ref, dab_ref, do_ref, dln2_ref, dgain_ref,
     pj_s, o_s, e_s, f_s, sem,
 ):
-    width = x1_ref.shape[1]
+    width = x1_ref.shape[2]
     half = own_ref.shape[1]
     load = pltpu.make_async_copy(w_ref.at[:, pl.ds(0, width)], pj_s, sem.at[0])
     load.start()
     tp = sc_ref[1]
     dh = dha_ref[...].astype(F32) + dhb_ref[...].astype(F32)
-    normed, inv = row_norm(x1_ref[...], width)
+    normed, inv = row_norm(x1_ref[0], width)
     dln2_ref[...] = jnp.sum(dh * normed, axis=0, keepdims=True)
     dy = valid_rows(cot_ref[0].astype(F32), sc_ref[0])
     dx = dy + row_norm_back(dh * ln2_ref[...], normed, inv, width)
@@ -381,7 +399,67 @@
 
 def mixed_kernel(x1_ref, pa_ref, pb_ref, *rest):
     out_ref = rest[-1]
-    out_ref[0] = (x1_ref[...] + (pa_ref[...].astype(F32) + pb_ref[...].astype(F32))).astype(BF)
+    out_ref[0] = (x1_ref[0] + (pa_ref[...].astype(F32) + pb_ref[...].astype(F32))).astype(BF)
+
+
+def place_kernel(at_ref, *refs, part):
+    *pieces, out_ref, sem = refs
+    copies = []
+    for slot, piece in enumerate(pieces):
+        row = pl.multiple_of(at_ref[slot], part)
+        copies.append(
+            pltpu.make_async_copy(piece, out_ref.at[pl.ds(row, piece.shape[0]), :], sem.at[slot])
+        )
+    for copy in copies:
+        copy.start()
+    for copy in copies:
+        copy.wait()
+
+
+def grads_kernel(n_ref, *refs, plan):
+    out_ref, flip_s, out_s, sem = refs[-4:]
+    refs = list(refs[:-4])
+
+    def take(count):
+        mine = refs[:count]
+        del refs[:count]
+        return mine
+
+    def joined(mine, cols):
+        if len(mine) == 1:
+            block = mine[0][:, :, cols]
+            return block.reshape(block.shape[0] * block.shape[1], block.shape[2])
+        return jnp.concatenate([ref[:, cols] for ref in mine], axis=0)
+
+    copies = []
+    column = 0
+    for group, (masked, left, rights) in enumerate(plan):
+        mine = take(left)
+        if masked:
+            parts = [valid_rows(mine[0][i], n_ref[i]) for i in range(mine[0].shape[0])]
+            flip_s[...] = jnp.concatenate(parts, axis=0).T
+        else:
+            flip_s[...] = joined(mine, slice(None)).T
+        flipped = flip_s[...]
+        start = column
+        for right in rights:
+            mine = take(right)
+            span = mine[0].shape[-1]
+            for at, size in tiles(span):
+                out_s[:, column + at : column + at + size] = dot_nn(
+                    flipped, joined(mine, slice(at, at + size))
+                ).astype(BF)
+            column += span
+        copies.append(
+            pltpu.make_async_copy(
+                out_s.at[:, pl.ds(start, column - start)],
+                out_ref.at[:, pl.ds(start, column - start)],
+                sem.at[group],
+            )
+        )
+        copies[-1].start()
+    for copy in copies:
+        copy.wait()
 
 
 VMEM = pl.BlockSpec(memory_space=pltpu.VMEM)
@@ -393,13 +471,13 @@
     return jax.ShapeDtypeStruct(dims, dtype)
 
 
-def call(kernel, out_shape, in_specs, out_specs, scratch=(), name=None, flops=0, moved=0, aliases=None, mib=48):
+def call(kernel, out_shape, in_specs, out_specs, scratch=(), name=None, flops=0, moved=0, aliases=None, mib=48, grid=1):
     return pl.pallas_call(
         kernel,
         out_shape=out_shape,
         in_specs=in_specs,
         out_specs=out_specs,
-        grid=(1,),
+        grid=(grid,),
         scratch_shapes=list(scratch),
         input_output_aliases=aliases or {},
         name=name,
@@ -454,20 +532,46 @@
     first = ctx * part
     qkv_part = lax.dynamic_slice_in_dim(qkv_weight, first, part, axis=1)
     full_qkv = lax.all_gather(qkv_part, both, axis=1, tiled=True)
-    proj_part = lax.dynamic_slice_in_dim(proj_weight, first, part, axis=1).T
     pairs_part = lax.dynamic_slice_in_dim(gate_up, first, part, axis=1)
-    down_part = lax.dynamic_slice_in_dim(down_weight, first, part, axis=1).T
-    rest_part = jnp.concatenate(
+    shards = lax.axis_size("shard")
+    shard = lax.axis_index("shard")
+
+    def shift(value, by):
+        return lax.ppermute(value, "shard", [(at, (at + by) % shards) for at in range(shards)])
+
+    low_half = ctx % 2
+    half_part = 2 * part
+    side_part = jnp.concatenate(
         [
-            ordered(proj_part, 1),
-            jnp.pad(pairs_part[0], ((0, 0), (0, pad))),
-            jnp.pad(pairs_part[1], ((0, 0), (0, pad))),
-            jnp.pad(down_part, ((0, 0), (0, pad))),
+            ordered(lax.dynamic_slice_in_dim(proj_weight, low_half * half_part, half_part, axis=1).T, 1),
+            jnp.pad(
+                lax.dynamic_slice_in_dim(down_weight, low_half * half_part, half_part, axis=1).T,
+                ((0, 0), (0, pad)),
+            ),
         ],
         axis=1,
     )
-    rest = lax.all_gather(rest_part, both, axis=0, tiled=True)
-    rest_width = rest.shape[1]
+    pieces, rows_at = [], []
+    for by in range(shards):
+        own = side_part if by == 0 else shift(side_part, by)
+        base = (shard + shards - by) % shards * depth
+        for flip, piece in enumerate((own, near(own))):
+            pieces.append(piece)
+            rows_at.append(base + (low_half ^ flip) * half_part)
+    side = call(
+        functools.partial(place_kernel, part=half_part),
+        shape(width, width + ffp),
+        [SMEM] + [ANY] * len(pieces),
+        ANY,
+        [pltpu.SemaphoreType.DMA((len(pieces),))],
+        name="place",
+        moved=4 * width * (width + ffp),
+        mib=8,
+    )(jnp.stack(rows_at).astype(jnp.int32), *pieces)
+    pairs_part = jnp.concatenate(
+        [jnp.pad(pairs_part[at], ((0, 0), (0, pad))) for at in range(2)], axis=1
+    )
+    pairs = lax.all_gather(pairs_part, both, axis=0, tiled=True)
 
     ln1 = ln1_gain[None, :]
     ln2 = ln2_gain[None, :]
@@ -497,6 +601,7 @@
             [image_of(i, rows, width), line, qkv_spec, rope_spec],
             [act, act_half, whole(rows, 2 * half)],
             name="qkv",
+            mib=24,
             flops=2 * rows * width * 3 * half,
             moved=6 * width * half + 8 * block_mb,
         )(tokens, ln1, full_qkv, tables)
@@ -516,40 +621,49 @@
                 pltpu.VMEM((LANES, 2 * rows), F32),
             ],
             name="attend",
+            mib=24,
             flops=16 * rows * 4 * rows * half,
             moved=12 * block_mb,
         )(s["n"], s["q"], s["kv"], s["kvc"], s["kvf"], s["kvx"])
         s["ox"] = swap(s["o"])
-    for i in range(images):
-        s = st[i]
-        s["x1"], s["h2"], s["g"], s["u"], s["dm"], s["a"], s["st"] = call(
-            middle_kernel,
-            (
-                shape(rows, width, dtype=F32),
-                shape(rows, width),
-                shape(rows, ffp),
-                shape(rows, ffp),
-                shape(rows, ffp),
-                shape(rows, half),
-                shape(8, 384, dtype=F32),
-            ),
-            [SMEM, image_of(i, rows, width), image_of(i, rows, width), act_half, act_half, line, line, line_ff, ANY],
-            [act, act, act_ff, act_ff, act_ff, act_half, whole(8, 384)],
-            [
-                pltpu.VMEM((width, width), BF),
-                pltpu.VMEM((width, ffp), BF),
-                pltpu.VMEM((width, ffp), BF),
-                pltpu.VMEM((width, ffp), BF),
-                pltpu.VMEM((rows, width), BF),
-                pltpu.VMEM((rows, width), BF),
-                pltpu.VMEM((384, LANES), F32),
-                pltpu.SemaphoreType.DMA((4,)),
-            ],
-            name="middle",
-            flops=2 * rows * width * (width + 3 * ffp),
-            moved=2 * width * rest_width + 12 * block_mb + 6 * rows * ffp,
-        )(s["sc"], tokens, cotangent, s["o"], s["ox"], again, ln2, fgain, rest)
-        s["stx"] = swap(s["st"])
+    valid = jnp.concatenate([counts[:, 0], tp.astype(jnp.int32)[None]])
+
+    def each(*dims):
+        return pl.BlockSpec((1,) + dims, lambda i: (i,) + (0,) * len(dims))
+
+    x1, h2, gate, up, dm, attn_in, stats = call(
+        middle_kernel,
+        (
+            shape(images, rows, width, dtype=F32),
+            shape(images, rows, width),
+            shape(images, rows, ffp),
+            shape(images, rows, ffp),
+            shape(images, rows, ffp),
+            shape(images, rows, half),
+            shape(images, 8, 384, dtype=F32),
+        ),
+        [SMEM, each(rows, width), each(rows, width)] + [act_half] * 6 + [line, line, line_ff, ANY, ANY],
+        [
+            each(rows, width), each(rows, width), each(rows, ffp), each(rows, ffp), each(rows, ffp),
+            each(rows, half), each(8, 384),
+        ],
+        [
+            pltpu.VMEM((width, width), BF),
+            pltpu.VMEM((width, ffp), BF),
+            pltpu.VMEM((width, ffp), BF),
+            pltpu.VMEM((width, ffp), BF),
+            pltpu.VMEM((rows, width), BF),
+            pltpu.VMEM((rows, width), BF),
+            pltpu.VMEM((384, LANES), F32),
+            pltpu.SemaphoreType.DMA((4,)),
+        ],
+        name="middle",
+        mib=48,
+        grid=images,
+        flops=2 * images * rows * width * (width + 3 * ffp),
+        moved=2 * width * (width + 3 * ffp) + images * (12 * block_mb + 6 * rows * ffp),
+    )(valid, tokens, cotangent, *[s["o"] for s in st], *[s["ox"] for s in st], again, ln2, fgain, pairs, side)
+    stats_x = swap(stats)
     for i in range(images):
         s = st[i]
         s["m"], s["dg"], s["du"], s["out"], s["dh2"], s["dffn"] = call(
@@ -562,7 +676,7 @@
                 shape(rows, width),
                 shape(1, ffp, dtype=F32),
             ),
-            [whole(8, 384), whole(8, 384), act_ff, act_ff, act_ff, line_ff, ANY],
+            [image_of(i, 8, 384)] * 2 + [image_of(i, rows, ffp)] * 3 + [line_ff, ANY, ANY],
             [act_ff, act_ff, act_ff, act, act, line_ff],
             [
                 pltpu.VMEM((width, ffp), BF),
@@ -572,11 +686,38 @@
                 pltpu.SemaphoreType.DMA((3,)),
             ],
             name="ffn",
+            mib=36,
             flops=2 * rows * width * 3 * ffp,
             moved=6 * width * ffp + 12 * rows * ffp + 4 * block_mb,
-        )(s["st"], s["stx"], s["g"], s["u"], s["dm"], fgain, rest)
+        )(stats, stats_x, gate, up, dm, fgain, pairs, side)
         s["dh2x"] = swap(s["dh2"])
         s["outx"] = swap(s["out"])
+    def weight_grads(groups, tag):
+        plan = [(masked, len(left), [len(right) for right in rights]) for masked, left, rights in groups]
+        flat = [v for _, left, rights in groups for v in left + [w for right in rights for w in right]]
+        columns = sum(right[0].shape[-1] for _, _, rights in groups for right in rights)
+        return call(
+            functools.partial(grads_kernel, plan=plan),
+            shape(width, columns),
+            [SMEM] + [whole(*v.shape) for v in flat],
+            ANY,
+            [
+                pltpu.VMEM((width, images * rows), BF),
+                pltpu.VMEM((width, columns), BF),
+                pltpu.SemaphoreType.DMA((len(groups),)),
+            ],
+            name=tag,
+            flops=2 * images * rows * width * columns,
+            moved=4 * width * columns,
+            mib=50 if columns > 2 * width else 36,
+        )(counts[:, 0], *flat)
+
+    def of(key):
+        return [s[key] for s in st]
+
+    grads_ffn = weight_grads(
+        [(False, [h2], [of("dg"), of("du")]), (True, [cotangent], [of("m")])], "grads_ffn"
+    )
     for i in range(images):
         s = st[i]
         s["dx"], s["dab"], s["do"], s["dln2"], s["dattn"] = call(
@@ -588,7 +729,7 @@
                 shape(1, width, dtype=F32),
                 shape(1, half, dtype=F32),
             ),
-            [SMEM, act, act, act, image_of(i, rows, width), line, act_half, act_half, line, ANY],
+            [SMEM, act, act, image_of(i, rows, width), image_of(i, rows, width), line, act_half, act_half, line, ANY],
             [act, act, act_half, line, whole(1, half)],
             [
                 pltpu.VMEM((width, width), BF),
@@ -598,9 +739,14 @@
                 pltpu.SemaphoreType.DMA((1,)),
             ],
             name="attn_norm_back",
+            mib=28,
             flops=2 * rows * width * width,
             moved=2 * width * width + 16 * block_mb,
-        )(s["sc"], s["dh2"], s["dh2x"], s["x1"], cotangent, ln2, s["o"], s["ox"], again, rest)
+        )(s["sc"], s["dh2"], s["dh2x"], x1, cotangent, ln2, s["o"], s["ox"], again, side)
+        if i == 0:
+            s["do"], grads_ffn = lax.optimization_barrier((s["do"], grads_ffn))
+        else:
+            s["do"], st[i - 1]["outx"] = lax.optimization_barrier((s["do"], st[i - 1]["outx"]))
         s["dq"], s["keep"], s["send"] = call(
             attend_back_kernel,
             (shape(rows, half), shape(2, rows, 2 * half), shape(2, rows, 2 * half)),
@@ -608,11 +754,27 @@
             [act_half, whole(2, rows, 2 * half), whole(2, rows, 2 * half)],
             [pltpu.VMEM((LANES, 2 * rows), F32)],
             name="attend_back",
+            mib=28,
             flops=40 * rows * 4 * rows * half,
             moved=20 * block_mb,
         )(s["n"], s["q"], s["kv"], s["kvc"], s["kvf"], s["kvx"], s["o"], s["do"], s["lse"], tables)
         s["recv"] = near(s["send"])
         s["far"] = far((s["keep"][1].astype(F32) + s["recv"][1].astype(F32)).astype(BF))
+    mixed = None
+    for i in range(images):
+        s = st[i]
+        again_buf = [] if mixed is None else [mixed]
+        mixed = call(
+            mixed_kernel,
+            shape(images, rows, width),
+            [image_of(i, rows, width), act, act] + [ANY] * len(again_buf),
+            image_of(i, rows, width),
+            name="mixed",
+            mib=12,
+            moved=10 * block_mb,
+            aliases={3: 0} if again_buf else None,
+        )(x1, s["out"], s["outx"], *again_buf)
+    st[0]["dq"], mixed = lax.optimization_barrier((st[0]["dq"], mixed))
     grad_tokens = None
     for i in range(images):
         s = st[i]
@@ -629,6 +791,7 @@
             ],
             [whole(rows, 2 * half), act],
             name="qkv_back",
+            mib=24,
             flops=2 * rows * width * 3 * half,
             moved=6 * width * half + 10 * block_mb,
         )(s["keep"], s["recv"], s["far"], s["dq"], tables, full_qkv)
@@ -642,64 +805,49 @@
             [act, act, image_of(i, rows, width), line, act] + [ANY] * len(again_buf),
             [image_of(i, rows, width), line],
             name="tokens_back",
+            mib=16,
             moved=12 * block_mb,
             aliases={5: 0} if again_buf else None,
         )(s["dh1"], s["dh1x"], tokens, ln1, s["dx"], *again_buf)
-    mixed = None
-    for i in range(images):
-        s = st[i]
-        again_buf = [] if mixed is None else [mixed]
-        mixed = call(
-            mixed_kernel,
-            shape(images, rows, width),
-            [act, act, act] + [ANY] * len(again_buf),
-            image_of(i, rows, width),
-            name="mixed",
-            moved=10 * block_mb,
-            aliases={3: 0} if again_buf else None,
-        )(s["x1"], s["out"], s["outx"], *again_buf)
-
-    def stacked(name):
-        return jnp.concatenate([s[name] for s in st], axis=0)
-
-    def weight_grad(lhs, rhs):
-        return dot_tn(lhs, rhs).astype(BF)
-
-    query_pos = ctx * rows + jnp.arange(rows, dtype=jnp.int32)
-    query_valid = query_pos[None, :] < lengths[:, None]
-    dyb = jnp.where(query_valid[:, :, None], cotangent, jnp.zeros_like(cotangent)).reshape(images * rows, width)
-    h2 = stacked("h2")
-    grads_rest = jnp.concatenate(
-        [
-            weight_grad(stacked("dab"), stacked("a")),
-            weight_grad(h2, stacked("dg")),
-            weight_grad(h2, stacked("du")),
-            weight_grad(dyb, stacked("m")),
-        ],
-        axis=1,
+    own_ffn = lax.psum_scatter(grads_ffn, both, scatter_dimension=0, tiled=True)
+
+    def around(own):
+        beyond = far(own)
+        held = [own, near(own), beyond, near(beyond)]
+        return jnp.concatenate([lax.select_n(ctx ^ at, *held) for at in range(4)], axis=0)
+
+    grads_qkv = weight_grads(
+        [(False, of("h1"), [of("dq"), of("dkv")]), (False, of("dab"), [[attn_in]])], "grads_qkv"
     )
-    h1 = stacked("h1")
-    grads_qkv = jnp.concatenate([weight_grad(h1, stacked("dq")), weight_grad(h1, stacked("dkv"))], axis=1)
-
-    def reduce(value):
-        own = lax.psum_scatter(value, both, scatter_dimension=0, tiled=True)
-        return lax.all_gather(own, "ctx", axis=0, tiled=True).astype(F32)
-
-    sum_rest = reduce(grads_rest)
-    sum_qkv = reduce(grads_qkv)
-    grad_proj = sum_rest[:, :half].T
-    grad_pairs = jnp.stack(
-        [sum_rest[:, half : half + ff], sum_rest[:, half + ffp : half + ffp + ff]]
-    )
-    grad_down = sum_rest[:, half + 2 * ffp : half + 2 * ffp + ff].T
+    grads_qkv, own_ffn = lax.optimization_barrier((grads_qkv, own_ffn))
+    own_qkv = lax.psum_scatter(grads_qkv, both, scatter_dimension=0, tiled=True)
+    sum_ffn = around(own_ffn).astype(F32)
+    own_qkv, grad_tokens, st[0]["dln1"] = lax.optimization_barrier((own_qkv, grad_tokens, st[0]["dln1"]))
+    sum_qkv = lax.all_gather(own_qkv, "ctx", axis=0, tiled=True).astype(F32)
+    grad_proj = sum_qkv[:, 3 * half :].T
+    grad_pairs = jnp.stack([sum_ffn[:, :ff], sum_ffn[:, ffp : ffp + ff]])
+    grad_down = sum_ffn[:, 2 * ffp : 2 * ffp + ff].T
     grad_qkv = jnp.stack([sum_qkv[:, j * half : (j + 1) * half] for j in range(3)])
+
+    def everywhere(value):
+        step = 1
+        while step < ctx_size:
+            value = value + lax.ppermute(value, "ctx", pair_perm(ctx_size, step))
+            step *= 2
+        step = 1
+        while step < shards:
+            value = value + lax.ppermute(value, "shard", pair_perm(shards, step))
+            step *= 2
+        return value
 
     def gain(name):
         return sum(s[name] for s in st)[0]
 
-    gain_ln1, gain_attn, gain_ln2, gain_ffn = lax.psum(
-        (gain("dln1"), gain("dattn"), gain("dln2"), gain("dffn")), both
-    )
+    packed = everywhere(jnp.concatenate([gain("dffn"), gain("dln2"), gain("dattn")]))
+    gain_ffn = packed[:ff]
+    gain_ln2 = packed[ffp : ffp + width]
+    gain_attn = packed[ffp + width :]
+    gain_ln1 = everywhere(gain("dln1"))
     return (
         mixed,
         grad_tokens,
@@ -709,7 +857,7 @@
         grad_proj,
         gain_ln2,
         grad_pairs,
-        gain_ffn[:ff],
+        gain_ffn,
         grad_down,
     )
 

time: 602 us -> 549 us (0.912)
  blocking collectives: 67.3 us -> 0 us
  local copies, waits for them, and re-layouts: 55.9 us -> 82.3 us
  matrix products: 23.8 us -> 0 us
  other arithmetic: 25.8 us -> 13.4 us
  Pallas kernels: 159 us -> 171 us
  starting transfers between devices: 27.8 us -> 37.3 us
    ppermute x0 -> x11, waiting for transfers between devices: none -> 70.5 us  [the longest x3 47.6 us: shift(): lax.ppermute(value, 'shard', [(at, (at + by) % shards) for at in range(sh...]
    ppermute x6 -> x7, waiting for transfers between devices: 94.4 us -> 30.6 us  [far(): return lax.ppermute(value, 'ctx', swap_far)]
    psum x1 -> x0, blocking collectives: 59.9 us -> none  [local(): lax.psum((gain('dln1'), gain('dattn'), gain('dln2'), gain('dffn')), both)]
    unnamed x244 -> x223, local copies, waits for them, and re-layouts: 45 us -> 74.3 us
    dot_general x6 -> x0, matrix products: 23.8 us -> none  [dot_tn(): lax.dot_general(a, b, (((0,), (0,)), ((), ())), preferred_element_type=F32)]
    pallas_call x6 -> x7, Pallas kernels: 30.7 us -> 48.7 us  [the longest x1 22.1 us: local(): call(middle_kernel, (shape(images, rows, width, dtype=F32), shape(images,...]
    ppermute x17 -> x15, waiting for transfers between devices: 71.7 us -> 61.4 us  [swap(): return lax.ppermute(value, 'tp', swap_tp)]
    concatenate x2 -> x4, other arithmetic: 11.2 us -> 0.89 us  [the longest x1 0.76 us: local(): jnp.concatenate([jnp.pad(pairs_part[at], ((0, 0), (0, pad))) for at in ra...]
  transfers between devices with their start and end apart: 37 -> 53, of which waited for: 16 -> 25; matrix products, arithmetic and copies ran while one was open for 8% -> 5% of each run, Pallas kernels for 26% -> 26%
where the time goes in v2:
time: 549 us; the launch traced here: 538 us
  waiting for transfers between devices  219 us (40%)
  Pallas kernels  171 us (31%)
  local copies, waits for them, and re-layouts  82.3 us (15%)
  starting transfers between devices  37.3 us (7%)
  between operations  15 us (3%)
  other arithmetic  13.4 us (2%)
    unnamed x223, local copies, waits for them, and re-layouts  74.3 us
    ppermute x15, waiting for transfers between devices, swap(): return lax.ppermute(value, 'tp', swap_tp)  61.4 us
    ppermute x3, waiting for transfers between devices, shift(): lax.ppermute(value, 'shard', [(at, (at + by) % shards) for at in range(sh...  47.6 us
    pallas_call x3, Pallas kernels, local(): call(attend_back_kernel, (shape(rows, half), shape(2, rows, 2 * half), sh...  40 us
    all_gather x1, waiting for transfers between devices, local(): full_qkv = lax.all_gather(qkv_part, both, axis=1, tiled=True)  35.5 us
    pallas_call x3, Pallas kernels, local(): call(attend_kernel, (shape(rows, half), shape(8, 2 * rows, dtype=F32)), [...  31.8 us
    ppermute x7, waiting for transfers between devices, far(): return lax.ppermute(value, 'ctx', swap_far)  30.6 us
    pallas_call x1, Pallas kernels, local(): call(middle_kernel, (shape(images, rows, width, dtype=F32), shape(images,...  22.1 us
  transfers between devices with their start and end apart: 53, of which 25 were waited for; matrix products, arithmetic and copies ran while one was open for 5% of the time, Pallas kernels for 26%

profile of v2, /device:TPU:0, one launch (start us, length us, event | category | flops | bytes accessed | tf_op | source)
XLA Modules:
  0.0 538.3 jit_solution(11082802563715191120)
XLA Ops:
  9.1 3.0 constant_dynamic-slice_fusion
  15.5 2.9 collective-permute-start.13
  23.2 35.5 %all-gather.4.cloned.1.call-done.w_ref = bf16[3,1024,512]{2,1,0:T(8,128)(2,1)} async-done(((bf16[3,64,512]{2,1,0:T(8,128)(2,1)}), bf16[3,1024,512]{2,1,0:T(8,128)(2,1)}) %all-gather.4.cloned.1.call-update) | async-done | bytes 3145744 | tf_op jit(solution)/shard_map/all_gather | solution.py:534
  65.8 2.5 qkv.4
  72.2 2.5 qkv.3
  76.2 15.6 %collective-permute-done.15.refs_2_ = bf16[128,2432]{1,0:T(8,128)(2,1)S(1)} collective-permute-done((bf16[128,2432]{1,0:T(8,128)(2,1)S(1)}, bf16[128,2432]{1,0:T(8,128)(2,1)S(1)}, u32[]{:S(2)}, u32[]{:S(2)}) %collective-permute-start.15) | collective-permute-done | bytes 622624 | tf_op jit(solution)/shard_map/ppermute | solution.py:540
  94.0 28.4 %collective-permute-done.17.refs_4_ = bf16[128,2432]{1,0:T(8,128)(2,1)S(1)} collective-permute-done((bf16[128,2432]{1,0:T(8,128)(2,1)S(1)}, bf16[128,2432]{1,0:T(8,128)(2,1)S(1)}, u32[]{:S(2)}, u32[]{:S(2)}) %collective-permute-start.17) | collective-permute-done | bytes 622624 | tf_op jit(solution)/shard_map/ppermute | solution.py:540
  124.9 3.4 collective-permute-start.19
  131.5 10.9 %attend.5 = (bf16[320,512]{1,0:T(8,128)(2,1)S(1)}, f32[8,640]{1,0:T(8,128)S(1)}) custom-call(s32[4]{0:T(128)S(1)} %get-tuple-element.234.n_ref, bf16[320,512]{1,0:T(8,128)(2,1)S(1)} %copy-done.91, bf16[320,1024]{1,0:T(8,128)(2,1)S(1)} %copy-done.74, bf16[320,1024]{1,0:T(8,128)(2,1)S(1)} %copy-done.80, bf16[320,1024]{1,0:T(8,128)(2,1)} %collective-permute-done.7.kv2, ...), custom_call_target="tpu_custom_call" | custom-call | flops 3355443200 | bytes 3932160 | tf_op jit(solution)/shard_map/attend/pallas_call | solution.py:613
  145.0 8.1 %attend.4 = (bf16[320,512]{1,0:T(8,128)(2,1)S(1)}, f32[8,640]{1,0:T(8,128)S(1)}) custom-call(s32[4]{0:T(128)S(1)} %get-tuple-element.235.n_ref, bf16[320,512]{1,0:T(8,128)(2,1)S(1)} %copy-done.88, bf16[320,1024]{1,0:T(8,128)(2,1)} %get-tuple-element.103.kv0, bf16[320,1024]{1,0:T(8,128)(2,1)S(1)} %copy-done.77, bf16[320,1024]{1,0:T(8,128)(2,1)} %collective-permute-done.4.kv2, ...), custom_call_target="tpu_custom_call" | custom-call | flops 3355443200 | bytes 3932160 | tf_op jit(solution)/shard_map/attend/pallas_call | solution.py:613
  153.1 3.6 collective-permute-done.19.refs_6_
  158.7 12.9 %attend.3 = (bf16[320,512]{1,0:T(8,128)(2,1)S(1)}, f32[8,640]{1,0:T(8,128)S(1)}) custom-call(s32[4]{0:T(128)S(1)} %get-tuple-element.236.n_ref, bf16[320,512]{1,0:T(8,128)(2,1)S(1)} %copy-done.85, bf16[320,1024]{1,0:T(8,128)(2,1)} %get-tuple-element.100.kv0, bf16[320,1024]{1,0:T(8,128)(2,1)} %collective-permute-done.kv1, ...), custom_call_target="tpu_custom_call" | custom-call | flops 3355443200 | bytes 3932160 | tf_op jit(solution)/shard_map/attend/pallas_call | solution.py:613
  178.4 3.8 collective-permute-done.11.other_ref2.other_ref
  182.2 7.0 %collective-permute-done.10.other_ref1.other_ref = bf16[320,512]{1,0:T(8,128)(2,1)S(1)} collective-permute-done((bf16[320,512]{1,0:T(8,128)(2,1)S(1)}, bf16[320,512]{1,0:T(8,128)(2,1)S(1)}, u32[]{:S(2)}, u32[]{:S(2)}) %collective-permute-start.10) | collective-permute-done | bytes 327712 | tf_op jit(solution)/shard_map/ppermute | solution.py:516
  189.2 6.1 %collective-permute-done.9.other_ref0.other_ref = bf16[320,512]{1,0:T(8,128)(2,1)S(1)} collective-permute-done((bf16[320,512]{1,0:T(8,128)(2,1)S(1)}, bf16[320,512]{1,0:T(8,128)(2,1)S(1)}, u32[]{:S(2)}, u32[]{:S(2)}) %collective-permute-start.9) | collective-permute-done | bytes 327712 | tf_op jit(solution)/shard_map/ppermute | solution.py:516
  195.4 22.1 %middle.1 = (f32[3,320,1024]{2,1,0:T(8,128)}, bf16[3,320,1024]{2,1,0:T(8,128)(2,1)S(1)}, bf16[3,320,1408]{2,1,0:T(8,128)(2,1)}, bf16[3,320,1408]{2,1,0:T(8,128)(...) custom-call(s32[4]{0:T(128)S(1)} %pad_add_fusion.1.sc_ref, ...), custom_call_target="tpu_custom_call" | custom-call | flops 10317987840 | bytes 30654464 | tf_op jit(solution)/shard_map/middle/pallas_call | solution.py:634
  221.1 2.6 collective-permute-done.21.sb_ref
  229.1 6.1 %ffn.3 = (bf16[320,1408]{1,0:T(8,128)(2,1)S(1)}, bf16[320,1408]{1,0:T(8,128)(2,1)S(1)}, bf16[320,1408]{1,0:T(8,128)(2,1)S(1)}, bf16[320,1024]{1,0:T(8,128)(2,1)S...) custom-call(f32[3,8,384]{2,1,0:T(8,128)S(1)} %get-tuple-element.108.sa_ref, ...), custom_call_target="tpu_custom_call" | custom-call | flops 2768240640 | bytes 15368192 | tf_op jit(solution)/shard_map/ffn/pallas_call | solution.py:669
  239.4 6.1 %ffn.5 = (bf16[320,1408]{1,0:T(8,128)(2,1)S(1)}, bf16[320,1408]{1,0:T(8,128)(2,1)S(1)}, bf16[320,1408]{1,0:T(8,128)(2,1)S(1)}, bf16[320,1024]{1,0:T(8,128)(2,1)S...) custom-call(f32[3,8,384]{2,1,0:T(8,128)S(1)} %get-tuple-element.108.sa_ref, ...), custom_call_target="tpu_custom_call" | custom-call | flops 2768240640 | bytes 15368192 | tf_op jit(solution)/shard_map/ffn/pallas_call | solution.py:669
  249.3 6.2 %ffn.4 = (bf16[320,1408]{1,0:T(8,128)(2,1)S(1)}, bf16[320,1408]{1,0:T(8,128)(2,1)S(1)}, bf16[320,1408]{1,0:T(8,128)(2,1)S(1)}, bf16[320,1024]{1,0:T(8,128)(2,1)S...) custom-call(f32[3,8,384]{2,1,0:T(8,128)S(1)} %get-tuple-element.108.sa_ref, ...), custom_call_target="tpu_custom_call" | custom-call | flops 2768240640 | bytes 15368192 | tf_op jit(solution)/shard_map/ffn/pallas_call | solution.py:669
  264.8 15.1 %grads_ffn.1 = bf16[1024,4224]{1,0:T(8,128)(2,1)} custom-call(s32[3]{0:T(128)S(1)} %slice_reduce_fusion.n_ref, bf16[3,320,1024]{2,1,0:T(8,128)(2,1)} %copy-done.97, bf16[320,1408]{1,0:T(8,128)(2,1)S(1)} %copy-done.54, bf16[320,1408]{1,0:T(8,128)(2,1)S(1)} %copy-done.63, bf16[320,1408]{1,0:T(8,128)(2,1)S(1)} %copy-done.59, bf16[320,1408]{1,0:T(8,128)(2,1)S(1)} %copy-done.56, ...), custom_call_target="tpu_custom_call" | custom-call | flops 8304721920 | bytes 17301504 | tf_op jit(solution)/shard_map/grads_ffn/pallas_call | solution.py:699
  286.4 4.4 attn_norm_back.3
  298.9 12.5 %collective-permute-done.24.dhb_ref = bf16[320,1024]{1,0:T(8,128)(2,1)S(1)} collective-permute-done((bf16[320,1024]{1,0:T(8,128)(2,1)}, bf16[320,1024]{1,0:T(8,128)(2,1)S(1)}, u32[]{:S(2)}, u32[]{:S(2)}) %collective-permute-start.24) | collective-permute-done | bytes 655392 | tf_op jit(solution)/shard_map/ppermute | solution.py:516
  311.4 2.8 copy-done.4
  319.5 3.5 attn_norm_back.4
  323.0 2.5 collective-permute-done.25.pb_ref
  325.5 15.7 %attend_back.5 = (bf16[320,512]{1,0:T(8,128)(2,1)S(1)}, bf16[2,320,1024]{2,1,0:T(8,128)(2,1)S(1)}, bf16[2,320,1024]{2,1,0:T(8,128)(2,1)S(1)}) custom-call(s32[4]{0:T(128)S(1)} %get-tuple-element.234.n_ref, bf16[320,512]{1,0:T(8,128)(2,1)S(1)} %copy-done.92, bf16[320,1024]{1,0:T(8,128)(2,1)S(1)} %copy-done.75, bf16[320,1024]{1,0:T(8,128)(2,1)S(1)} %copy-done.81, ...), custom_call_target="tpu_custom_call" | custom-call | flops 8388608000 | bytes 6553600 | tf_op jit(solution)/shard_map/attend_back/pallas_call | solution.py:750
  341.4 3.5 attn_norm_back.5
  345.9 4.4 collective-permute-done.27.pb_ref
  350.4 9.7 %attend_back.4 = (bf16[320,512]{1,0:T(8,128)(2,1)S(1)}, bf16[2,320,1024]{2,1,0:T(8,128)(2,1)S(1)}, bf16[2,320,1024]{2,1,0:T(8,128)(2,1)S(1)}) custom-call(s32[4]{0:T(128)S(1)} %get-tuple-element.235.n_ref, bf16[320,512]{1,0:T(8,128)(2,1)S(1)} %copy-done.89, bf16[320,1024]{1,0:T(8,128)(2,1)} %get-tuple-element.103.kv0, bf16[320,1024]{1,0:T(8,128)(2,1)S(1)} %copy-done.78, ...), custom_call_target="tpu_custom_call" | custom-call | flops 8388608000 | bytes 6553600 | tf_op jit(solution)/shard_map/attend_back/pallas_call | solution.py:750
  360.2 14.6 %attend_back.3 = (bf16[320,512]{1,0:T(8,128)(2,1)S(1)}, bf16[2,320,1024]{2,1,0:T(8,128)(2,1)S(1)}, bf16[2,320,1024]{2,1,0:T(8,128)(2,1)S(1)}) custom-call(s32[4]{0:T(128)S(1)} %get-tuple-element.236.n_ref, bf16[320,512]{1,0:T(8,128)(2,1)S(1)} %copy-done.86, bf16[320,1024]{1,0:T(8,128)(2,1)} %get-tuple-element.100.kv0, ...), custom_call_target="tpu_custom_call" | custom-call | flops 8388608000 | bytes 6553600 | tf_op jit(solution)/shard_map/attend_back/pallas_call | solution.py:750
  382.7 9.4 %collective-permute-done.23.pb_ref = bf16[320,1024]{1,0:T(8,128)(2,1)S(1)} collective-permute-done((bf16[320,1024]{1,0:T(8,128)(2,1)S(1)}, bf16[320,1024]{1,0:T(8,128)(2,1)S(1)}, u32[]{:S(2)}, u32[]{:S(2)}) %collective-permute-start.23) | collective-permute-done | bytes 655392 | tf_op jit(solution)/shard_map/ppermute | solution.py:516
  393.1 6.8 %collective-permute-done.33.far_ref = bf16[320,1024]{1,0:T(8,128)(2,1)S(1)} collective-permute-done((bf16[320,1024]{1,0:T(8,128)(2,1)S(1)}, bf16[320,1024]{1,0:T(8,128)(2,1)S(1)}, u32[]{:S(2)}, u32[]{:S(2)}) %collective-permute-start.33) | collective-permute-done | bytes 655392 | tf_op jit(solution)/shard_map/ppermute | solution.py:522
  401.3 12.6 %collective-permute-done.31.far_ref = bf16[320,1024]{1,0:T(8,128)(2,1)S(1)} collective-permute-done((bf16[320,1024]{1,0:T(8,128)(2,1)S(1)}, bf16[320,1024]{1,0:T(8,128)(2,1)S(1)}, u32[]{:S(2)}, u32[]{:S(2)}) %collective-permute-start.31) | collective-permute-done | bytes 655392 | tf_op jit(solution)/shard_map/ppermute | solution.py:522
  416.2 11.2 %collective-permute-done.29.far_ref = bf16[320,1024]{1,0:T(8,128)(2,1)S(1)} collective-permute-done((bf16[320,1024]{1,0:T(8,128)(2,1)S(1)}, bf16[320,1024]{1,0:T(8,128)(2,1)S(1)}, u32[]{:S(2)}, u32[]{:S(2)}) %collective-permute-start.29) | collective-permute-done | bytes 655392 | tf_op jit(solution)/shard_map/ppermute | solution.py:522
  429.7 6.3 %grads_qkv.1 = bf16[1024,2048]{1,0:T(8,128)(2,1)S(1)} custom-call(s32[3]{0:T(128)S(1)} %slice_reduce_fusion.n_ref, bf16[320,1024]{1,0:T(8,128)(2,1)S(1)} %copy-done.70, bf16[320,1024]{1,0:T(8,128)(2,1)S(1)} %copy-done.68, bf16[320,1024]{1,0:T(8,128)(2,1)S(1)} %copy-done.66, bf16[320,512]{1,0:T(8,128)(2,1)S(1)} %get-tuple-element.141.dq_ref.refs_3_, ...), custom_call_target="tpu_custom_call" | custom-call | flops 4026531840 | bytes 8388608 | tf_op jit(solution)/shard_map/grads_qkv/pallas_call | solution.py:699
  444.4 8.3 %collective-permute-done.42 = f32[2944]{0:T(1024)S(1)} collective-permute-done((f32[2944]{0:T(1024)S(1)}, f32[2944]{0:T(1024)S(1)}, u32[]{:S(2)}, u32[]{:S(2)}) %collective-permute-start.42) | collective-permute-done | bytes 11808 | tf_op jit(solution)/shard_map/ppermute | solution.py:835
  452.7 3.7 collective-permute-done.43
  456.4 4.6 collective-permute-done.44
  464.7 3.1 tokens_back.3
  467.8 3.4 collective-permute-done.35.db_ref
  471.2 3.3 tokens_back.4
  474.5 9.3 %collective-permute-done.34.db_ref = bf16[320,1024]{1,0:T(8,128)(2,1)} collective-permute-done((bf16[320,1024]{1,0:T(8,128)(2,1)S(1)}, bf16[320,1024]{1,0:T(8,128)(2,1)}, u32[]{:S(2)}, u32[]{:S(2)}) %collective-permute-start.34) | collective-permute-done | bytes 655392 | tf_op jit(solution)/shard_map/ppermute | solution.py:516
  483.8 3.0 tokens_back.5
  486.8 20.7 %reduce-scatter.5.cloned.1.call-done = bf16[64,2048]{1,0:T(8,128)(2,1)} async-done(((bf16[1024,2048]{1,0:T(8,128)(2,1)}), bf16[64,2048]{1,0:T(8,128)(2,1)}) %reduce-scatter.5.cloned.1.call-update) | async-done | bytes 262160 | tf_op jit(solution)/shard_map/reduce_scatter | solution.py:823
  510.5 2.7 collective-permute-done.38
  514.3 2.5 collective-permute-done.39
  519.9 5.5 %copy.35 = f32[2,256,1365]{1,0,2:T(2,128)} copy(f32[2,256,1365]{2,1,0:T(8,128)} %pad_maximum_fusion) | data formatting | bytes 5591040
  (371 shorter events, 128.8 us)
Async XLA Ops:
  7.2 51.5 %all-gather.4.cloned.1.call-start = ((), (), s32[]{:S(2)}) async-start(), calls=%async_computation.2 | async-start | bytes 3342336 | tf_op jit(solution)/shard_map/all_gather | solution.py:534
  9.0 186.3 %all-gather.6.cloned.1.call-start = ((), (), s32[]{:S(2)}) async-start(), calls=%async_computation.3 | async-start | bytes 6127616 | tf_op jit(solution)/shard_map/all_gather | solution.py:574
  14.6 423.5 %reduce-scatter.3.cloned.1.call-start = ((), (), s32[]{:S(2)}) async-start(), calls=%async_computation.4 | async-start | bytes 9191424 | tf_op jit(solution)/shard_map/reduce_scatter | solution.py:812
  15.5 6.7 %collective-permute-start.13 = (bf16[128,512]{1,0:T(8,128)(2,1)}, bf16[128,512]{1,0:T(8,128)(2,1)}, u32[]{:S(2)}, u32[]{:S(2)}) collective-permute-start(bf16[128,512]{1,0:T(8,128)(2,1)} %bitcast.21), channel_id=1, source_target_pairs={{0,1},{1,0},{2,3},{3,2},{4,5},{5,4},{6,7},{7,6},{8,9},{9,8},{10,11... | collective-permute-start | bytes 393224 | tf_op jit(solution)/shard_map/ppermute | solution.py:516
  63.2 30.1 %collective-permute-start.7 = (bf16[320,1024]{1,0:T(8,128)(2,1)S(1)}, bf16[320,1024]{1,0:T(8,128)(2,1)}, u32[]{:S(2)}, u32[]{:S(2)}) collective-permute-start(bf16[320,1024]{1,0:T(8,128)(2,1)S(1)} %get-tuple-element.106.kv0), channel_id=1, source_target_pairs={{0,4},{2,6},{4,0},{6,2},{1,5},{3,7},{5,1},{7,3},{8,12},{10,14},{12... | collective-permute-start | bytes 1966088 | tf_op jit(solution)/shard_map/ppermute | solution.py:522
  63.9 28.0 %collective-permute-start.15 = (bf16[128,2432]{1,0:T(8,128)(2,1)S(1)}, bf16[128,2432]{1,0:T(8,128)(2,1)S(1)}, u32[]{:S(2)}, u32[]{:S(2)}) collective-permute-start(bf16[128,2432]{1,0:T(8,128)(2,1)S(1)} %fusion.6.refs_0_), channel_id=1, source_target_pairs={{0,8},{8,16},{16,24},{24,0},{1,9},{9,17},{17,25},{25,1},{2,10},{10... | collective-permute-start | bytes 1867784 | tf_op jit(solution)/shard_map/ppermute | solution.py:540
  69.8 53.4 %collective-permute-start.4 = (bf16[320,1024]{1,0:T(8,128)(2,1)}, bf16[320,1024]{1,0:T(8,128)(2,1)}, u32[]{:S(2)}, u32[]{:S(2)}) collective-permute-start(bf16[320,1024]{1,0:T(8,128)(2,1)} %get-tuple-element.103.kv0), channel_id=1, source_target_pairs={{0,4},{2,6},{4,0},{6,2},{1,5},{3,7},{5,1},{7,3},{8,12},{10,14},{12... | collective-permute-start | bytes 1966088 | tf_op jit(solution)/shard_map/ppermute | solution.py:522
  71.3 51.1 %collective-permute-start.17 = (bf16[128,2432]{1,0:T(8,128)(2,1)S(1)}, bf16[128,2432]{1,0:T(8,128)(2,1)S(1)}, u32[]{:S(2)}, u32[]{:S(2)}) collective-permute-start(bf16[128,2432]{1,0:T(8,128)(2,1)S(1)} %fusion.6.refs_0_), channel_id=1, source_target_pairs={{0,16},{8,24},{16,0},{24,8},{1,17},{9,25},{17,1},{25,9},{2,18},{10... | collective-permute-start | bytes 1867784 | tf_op jit(solution)/shard_map/ppermute | solution.py:540
  72.1 51.2 %collective-permute-start.6 = (bf16[320,1024]{1,0:T(8,128)(2,1)S(1)}, bf16[320,1024]{1,0:T(8,128)(2,1)S(1)}, u32[]{:S(2)}, u32[]{:S(2)}) collective-permute-start(bf16[320,1024]{1,0:T(8,128)(2,1)S(1)} %get-tuple-element.106.kv0), channel_id=1, source_target_pairs={{0,2},{2,0},{4,6},{6,4},{1,3},{3,1},{5,7},{7,5},{8,10},{10,8},{12,... | collective-permute-start | bytes 1966088 | tf_op jit(solution)/shard_map/ppermute | solution.py:519
  91.8 32.8 %collective-permute-start.1 = (bf16[320,1024]{1,0:T(8,128)(2,1)}, bf16[320,1024]{1,0:T(8,128)(2,1)S(1)}, u32[]{:S(2)}, u32[]{:S(2)}) collective-permute-start(bf16[320,1024]{1,0:T(8,128)(2,1)} %get-tuple-element.100.kv0), channel_id=1, source_target_pairs={{0,4},{2,6},{4,0},{6,2},{1,5},{3,7},{5,1},{7,3},{8,12},{10,14},{12... | collective-permute-start | bytes 1966088 | tf_op jit(solution)/shard_map/ppermute | solution.py:522
  93.3 31.6 %collective-permute-start.8 = (bf16[320,1024]{1,0:T(8,128)(2,1)}, bf16[320,1024]{1,0:T(8,128)(2,1)}, u32[]{:S(2)}, u32[]{:S(2)}) collective-permute-start(bf16[320,1024]{1,0:T(8,128)(2,1)} %collective-permute-done.7.kv2), channel_id=1, source_target_pairs={{0,2},{2,0},{4,6},{6,4},{1,3},{3,1},{5,7},{7,5},{8,10},{10,8},{12,... | collective-permute-start | bytes 1966088 | tf_op jit(solution)/shard_map/ppermute | solution.py:519
  122.4 20.0 %collective-permute-start.3 = (bf16[320,1024]{1,0:T(8,128)(2,1)}, bf16[320,1024]{1,0:T(8,128)(2,1)S(1)}, u32[]{:S(2)}, u32[]{:S(2)}) collective-permute-start(bf16[320,1024]{1,0:T(8,128)(2,1)} %get-tuple-element.103.kv0), channel_id=1, source_target_pairs={{0,2},{2,0},{4,6},{6,4},{1,3},{3,1},{5,7},{7,5},{8,10},{10,8},{12,... | collective-permute-start | bytes 1966088 | tf_op jit(solution)/shard_map/ppermute | solution.py:519
  123.2 20.3 %collective-permute-start.5 = (bf16[320,1024]{1,0:T(8,128)(2,1)}, bf16[320,1024]{1,0:T(8,128)(2,1)}, u32[]{:S(2)}, u32[]{:S(2)}) collective-permute-start(bf16[320,1024]{1,0:T(8,128)(2,1)} %collective-permute-done.4.kv2), channel_id=1, source_target_pairs={{0,2},{2,0},{4,6},{6,4},{1,3},{3,1},{5,7},{7,5},{8,10},{10,8},{12,... | collective-permute-start | bytes 1966088 | tf_op jit(solution)/shard_map/ppermute | solution.py:519
  124.2 34.0 %collective-permute-start = (bf16[320,1024]{1,0:T(8,128)(2,1)}, bf16[320,1024]{1,0:T(8,128)(2,1)}, u32[]{:S(2)}, u32[]{:S(2)}) collective-permute-start(bf16[320,1024]{1,0:T(8,128)(2,1)} %get-tuple-element.100.kv0), channel_id=1, source_target_pairs={{0,2},{2,0},{4,6},{6,4},{1,3},{3,1},{5,7},{7,5},{8,10},{10,8},{12,... | collective-permute-start | bytes 1966088 | tf_op jit(solution)/shard_map/ppermute | solution.py:519
  124.7 33.5 %collective-permute-start.2 = (bf16[320,1024]{1,0:T(8,128)(2,1)S(1)}, bf16[320,1024]{1,0:T(8,128)(2,1)}, u32[]{:S(2)}, u32[]{:S(2)}) collective-permute-start(bf16[320,1024]{1,0:T(8,128)(2,1)S(1)} %collective-permute-done.1.kv2), channel_id=1, source_target_pairs={{0,2},{2,0},{4,6},{6,4},{1,3},{3,1},{5,7},{7,5},{8,10},{10,8},{12,... | collective-permute-start | bytes 1966088 | tf_op jit(solution)/shard_map/ppermute | solution.py:519
  124.9 31.8 %collective-permute-start.19 = (bf16[128,2432]{1,0:T(8,128)(2,1)S(1)}, bf16[128,2432]{1,0:T(8,128)(2,1)S(1)}, u32[]{:S(2)}, u32[]{:S(2)}) collective-permute-start(bf16[128,2432]{1,0:T(8,128)(2,1)S(1)} %fusion.6.refs_0_), channel_id=1, source_target_pairs={{0,24},{8,0},{16,8},{24,16},{1,25},{9,1},{17,9},{25,17},{2,26},{10... | collective-permute-start | bytes 1867784 | tf_op jit(solution)/shard_map/ppermute | solution.py:540
  143.3 28.8 %collective-permute-start.14 = (bf16[128,2432]{1,0:T(8,128)(2,1)S(1)}, bf16[128,2432]{1,0:T(8,128)(2,1)S(1)}, u32[]{:S(2)}, u32[]{:S(2)}) collective-permute-start(bf16[128,2432]{1,0:T(8,128)(2,1)S(1)} %fusion.6.refs_0_), channel_id=1, source_target_pairs={{0,2},{2,0},{4,6},{6,4},{1,3},{3,1},{5,7},{7,5},{8,10},{10,8},{12,... | collective-permute-start | bytes 1867784 | tf_op jit(solution)/shard_map/ppermute | solution.py:519
  143.5 30.1 %collective-permute-start.16 = (bf16[128,2432]{1,0:T(8,128)(2,1)S(1)}, bf16[128,2432]{1,0:T(8,128)(2,1)S(1)}, u32[]{:S(2)}, u32[]{:S(2)}) collective-permute-start(bf16[128,2432]{1,0:T(8,128)(2,1)S(1)} %copy-done.33), channel_id=1, source_target_pairs={{0,2},{2,0},{4,6},{6,4},{1,3},{3,1},{5,7},{7,5},{8,10},{10,8},{12,... | collective-permute-start | bytes 1867784 | tf_op jit(solution)/shard_map/ppermute | solution.py:519
  156.7 14.9 %collective-permute-start.12 = (f32[1,512]{1,0:T(1,128)S(1)}, f32[1,512]{1,0:T(1,128)S(1)}, u32[]{:S(2)}, u32[]{:S(2)}) collective-permute-start(f32[1,512]{1,0:T(1,128)S(1)} %bitcast.79), channel_id=1, source_target_pairs={{0,1},{1,0},{2,3},{3,2},{4,5},{5,4},{6,7},{7,6},{8,9},{9,8},{10,11... | collective-permute-start | bytes 6152 | tf_op jit(solution)/shard_map/ppermute | solution.py:516
  158.2 16.1 %collective-permute-start.18 = (bf16[128,2432]{1,0:T(8,128)(2,1)S(1)}, bf16[128,2432]{1,0:T(8,128)(2,1)S(1)}, u32[]{:S(2)}, u32[]{:S(2)}) collective-permute-start(bf16[128,2432]{1,0:T(8,128)(2,1)S(1)} %copy-done.35), channel_id=1, source_target_pairs={{0,2},{2,0},{4,6},{6,4},{1,3},{3,1},{5,7},{7,5},{8,10},{10,8},{12,... | collective-permute-start | bytes 1867784 | tf_op jit(solution)/shard_map/ppermute | solution.py:519
  158.2 16.1 %collective-permute-start.20 = (bf16[128,2432]{1,0:T(8,128)(2,1)S(1)}, bf16[128,2432]{1,0:T(8,128)(2,1)S(1)}, u32[]{:S(2)}, u32[]{:S(2)}) collective-permute-start(bf16[128,2432]{1,0:T(8,128)(2,1)S(1)} %collective-permute-done.19.refs_6_), channel_id=1, source_target_pairs={{0,2},{2,0},{4,6},{6,4},{1,3},{3,1},{5,7},{7,5},{8,10},{10,8},{12,... | collective-permute-start | bytes 1867784 | tf_op jit(solution)/shard_map/ppermute | solution.py:519
  171.6 10.6 %collective-permute-start.11 = (bf16[320,512]{1,0:T(8,128)(2,1)S(1)}, bf16[320,512]{1,0:T(8,128)(2,1)S(1)}, u32[]{:S(2)}, u32[]{:S(2)}) collective-permute-start(bf16[320,512]{1,0:T(8,128)(2,1)S(1)} %get-tuple-element.107.own_ref2.own_ref.o_ref), channel_id=1, source_target_pairs={{0,1},{1,0},{2,3},{3,2},{4,5},{5,4},{6,7},{7,6},{8,9},{9,8},{10,11... | collective-permute-start | bytes 983048 | tf_op jit(solution)/shard_map/ppermute | solution.py:516
  172.2 17.1 %collective-permute-start.10 = (bf16[320,512]{1,0:T(8,128)(2,1)S(1)}, bf16[320,512]{1,0:T(8,128)(2,1)S(1)}, u32[]{:S(2)}, u32[]{:S(2)}) collective-permute-start(bf16[320,512]{1,0:T(8,128)(2,1)S(1)} %get-tuple-element.104.own_ref1.own_ref.o_ref), channel_id=1, source_target_pairs={{0,1},{1,0},{2,3},{3,2},{4,5},{5,4},{6,7},{7,6},{8,9},{9,8},{10,11... | collective-permute-start | bytes 983048 | tf_op jit(solution)/shard_map/ppermute | solution.py:516
  173.7 21.7 %collective-permute-start.9 = (bf16[320,512]{1,0:T(8,128)(2,1)S(1)}, bf16[320,512]{1,0:T(8,128)(2,1)S(1)}, u32[]{:S(2)}, u32[]{:S(2)}) collective-permute-start(bf16[320,512]{1,0:T(8,128)(2,1)S(1)} %get-tuple-element.101.own_ref0.own_ref.o_ref), channel_id=1, source_target_pairs={{0,1},{1,0},{2,3},{3,2},{4,5},{5,4},{6,7},{7,6},{8,9},{9,8},{10,11... | collective-permute-start | bytes 983048 | tf_op jit(solution)/shard_map/ppermute | solution.py:516
  219.8 4.0 collective-permute-start.21
  238.8 41.1 %collective-permute-start.22 = (bf16[320,1024]{1,0:T(8,128)(2,1)}, bf16[320,1024]{1,0:T(8,128)(2,1)}, u32[]{:S(2)}, u32[]{:S(2)}) collective-permute-start(bf16[320,1024]{1,0:T(8,128)(2,1)} %get-tuple-element.112.dha_ref), channel_id=1, source_target_pairs={{0,1},{1,0},{2,3},{3,2},{4,5},{5,4},{6,7},{7,6},{8,9},{9,8},{10,11... | collective-permute-start | bytes 1966088 | tf_op jit(solution)/shard_map/ppermute | solution.py:516
  293.4 214.1 %reduce-scatter.5.cloned.1.call-start = ((), (), s32[]{:S(2)}) async-start(), calls=%async_computation.5 | async-start | bytes 4456448 | tf_op jit(solution)/shard_map/reduce_scatter | solution.py:823
  293.5 17.9 %collective-permute-start.24 = (bf16[320,1024]{1,0:T(8,128)(2,1)}, bf16[320,1024]{1,0:T(8,128)(2,1)S(1)}, u32[]{:S(2)}, u32[]{:S(2)}) collective-permute-start(bf16[320,1024]{1,0:T(8,128)(2,1)} %copy-done.26), channel_id=1, source_target_pairs={{0,1},{1,0},{2,3},{3,2},{4,5},{5,4},{6,7},{7,6},{8,9},{9,8},{10,11... | collective-permute-start | bytes 1966088 | tf_op jit(solution)/shard_map/ppermute | solution.py:516
  295.0 30.5 %collective-permute-start.25 = (bf16[320,1024]{1,0:T(8,128)(2,1)}, bf16[320,1024]{1,0:T(8,128)(2,1)S(1)}, u32[]{:S(2)}, u32[]{:S(2)}) collective-permute-start(bf16[320,1024]{1,0:T(8,128)(2,1)} %copy-done.22), channel_id=1, source_target_pairs={{0,1},{1,0},{2,3},{3,2},{4,5},{5,4},{6,7},{7,6},{8,9},{9,8},{10,11... | collective-permute-start | bytes 1966088 | tf_op jit(solution)/shard_map/ppermute | solution.py:516
  296.9 44.4 %collective-permute-start.26 = (bf16[320,1024]{1,0:T(8,128)(2,1)}, bf16[320,1024]{1,0:T(8,128)(2,1)S(1)}, u32[]{:S(2)}, u32[]{:S(2)}) collective-permute-start(bf16[320,1024]{1,0:T(8,128)(2,1)} %copy-done.24), channel_id=1, source_target_pairs={{0,1},{1,0},{2,3},{3,2},{4,5},{5,4},{6,7},{7,6},{8,9},{9,8},{10,11... | collective-permute-start | bytes 1966088 | tf_op jit(solution)/shard_map/ppermute | solution.py:516
  298.4 52.0 %collective-permute-start.27 = (bf16[320,1024]{1,0:T(8,128)(2,1)}, bf16[320,1024]{1,0:T(8,128)(2,1)S(1)}, u32[]{:S(2)}, u32[]{:S(2)}) collective-permute-start(bf16[320,1024]{1,0:T(8,128)(2,1)} %copy-done.28), channel_id=1, source_target_pairs={{0,1},{1,0},{2,3},{3,2},{4,5},{5,4},{6,7},{7,6},{8,9},{9,8},{10,11... | collective-permute-start | bytes 1966088 | tf_op jit(solution)/shard_map/ppermute | solution.py:516
  341.2 35.3 %collective-permute-start.32 = (bf16[2,320,1024]{2,1,0:T(8,128)(2,1)S(1)}, bf16[2,320,1024]{2,1,0:T(8,128)(2,1)S(1)}, u32[]{:S(2)}, u32[]{:S(2)}) collective-permute-start(bf16[2,320,1024]{2,1,0:T(8,128)(2,1)S(1)} %get-tuple-element.155), channel_id=1, source_target_pairs={{0,2},{2,0},{4,6},{6,4},{1,3},{3,1},{5,7},{7,5},{8,10},{10,8},{12,... | collective-permute-start | bytes 3932168 | tf_op jit(solution)/shard_map/ppermute | solution.py:519
  360.1 17.8 %collective-permute-start.30 = (bf16[2,320,1024]{2,1,0:T(8,128)(2,1)S(1)}, bf16[2,320,1024]{2,1,0:T(8,128)(2,1)S(1)}, u32[]{:S(2)}, u32[]{:S(2)}) collective-permute-start(bf16[2,320,1024]{2,1,0:T(8,128)(2,1)S(1)} %get-tuple-element.152), channel_id=1, source_target_pairs={{0,2},{2,0},{4,6},{6,4},{1,3},{3,1},{5,7},{7,5},{8,10},{10,8},{12,... | collective-permute-start | bytes 3932168 | tf_op jit(solution)/shard_map/ppermute | solution.py:519
  374.8 4.4 collective-permute-start.28
  375.1 16.9 %collective-permute-start.23 = (bf16[320,1024]{1,0:T(8,128)(2,1)S(1)}, bf16[320,1024]{1,0:T(8,128)(2,1)S(1)}, u32[]{:S(2)}, u32[]{:S(2)}) collective-permute-start(bf16[320,1024]{1,0:T(8,128)(2,1)S(1)} %get-tuple-element.128.pa_ref), channel_id=1, source_target_pairs={{0,1},{1,0},{2,3},{3,2},{4,5},{5,4},{6,7},{7,6},{8,9},{9,8},{10,11... | collective-permute-start | bytes 1966088 | tf_op jit(solution)/shard_map/ppermute | solution.py:516
  376.8 23.1 %collective-permute-start.33 = (bf16[320,1024]{1,0:T(8,128)(2,1)S(1)}, bf16[320,1024]{1,0:T(8,128)(2,1)S(1)}, u32[]{:S(2)}, u32[]{:S(2)}) collective-permute-start(bf16[320,1024]{1,0:T(8,128)(2,1)S(1)} %fusion.5), channel_id=1, source_target_pairs={{0,4},{2,6},{4,0},{6,2},{1,5},{3,7},{5,1},{7,3},{8,12},{10,14},{12... | collective-permute-start | bytes 1966088 | tf_op jit(solution)/shard_map/ppermute | solution.py:522
  378.2 35.7 %collective-permute-start.31 = (bf16[320,1024]{1,0:T(8,128)(2,1)S(1)}, bf16[320,1024]{1,0:T(8,128)(2,1)S(1)}, u32[]{:S(2)}, u32[]{:S(2)}) collective-permute-start(bf16[320,1024]{1,0:T(8,128)(2,1)S(1)} %fusion.4), channel_id=1, source_target_pairs={{0,4},{2,6},{4,0},{6,2},{1,5},{3,7},{5,1},{7,3},{8,12},{10,14},{12... | collective-permute-start | bytes 1966088 | tf_op jit(solution)/shard_map/ppermute | solution.py:522
  379.5 47.9 %collective-permute-start.29 = (bf16[320,1024]{1,0:T(8,128)(2,1)S(1)}, bf16[320,1024]{1,0:T(8,128)(2,1)S(1)}, u32[]{:S(2)}, u32[]{:S(2)}) collective-permute-start(bf16[320,1024]{1,0:T(8,128)(2,1)S(1)} %fusion.3), channel_id=1, source_target_pairs={{0,4},{2,6},{4,0},{6,2},{1,5},{3,7},{5,1},{7,3},{8,12},{10,14},{12... | collective-permute-start | bytes 1966088 | tf_op jit(solution)/shard_map/ppermute | solution.py:522
  438.1 89.4 %all-gather.8.cloned.1.call-start = ((), (), s32[]{:S(2)}) async-start(), calls=%async_computation.6 | async-start | bytes 1310720 | tf_op jit(solution)/shard_map/all_gather | solution.py:826
  438.4 22.6 %collective-permute-start.46 = (bf16[64,4224]{1,0:T(8,128)(2,1)}, bf16[64,4224]{1,0:T(8,128)(2,1)}, u32[]{:S(2)}, u32[]{:S(2)}) collective-permute-start(bf16[64,4224]{1,0:T(8,128)(2,1)} %reduce-scatter.3.cloned.1.call-done), channel_id=1, source_target_pairs={{0,4},{2,6},{4,0},{6,2},{1,5},{3,7},{5,1},{7,3},{8,12},{10,14},{12... | collective-permute-start | bytes 1622024 | tf_op jit(solution)/shard_map/ppermute | solution.py:522
  439.3 23.9 %collective-permute-start.36 = (bf16[320,1024]{1,0:T(8,128)(2,1)S(1)}, bf16[320,1024]{1,0:T(8,128)(2,1)}, u32[]{:S(2)}, u32[]{:S(2)}) collective-permute-start(bf16[320,1024]{1,0:T(8,128)(2,1)S(1)} %copy-done.31), channel_id=1, source_target_pairs={{0,1},{1,0},{2,3},{3,2},{4,5},{5,4},{6,7},{7,6},{8,9},{9,8},{10,11... | collective-permute-start | bytes 1966088 | tf_op jit(solution)/shard_map/ppermute | solution.py:516
  440.0 31.2 %collective-permute-start.35 = (bf16[320,1024]{1,0:T(8,128)(2,1)}, bf16[320,1024]{1,0:T(8,128)(2,1)}, u32[]{:S(2)}, u32[]{:S(2)}) collective-permute-start(bf16[320,1024]{1,0:T(8,128)(2,1)} %get-tuple-element.165.da_ref), channel_id=1, source_target_pairs={{0,1},{1,0},{2,3},{3,2},{4,5},{5,4},{6,7},{7,6},{8,9},{9,8},{10,11... | collective-permute-start | bytes 1966088 | tf_op jit(solution)/shard_map/ppermute | solution.py:516
  441.4 42.4 %collective-permute-start.34 = (bf16[320,1024]{1,0:T(8,128)(2,1)S(1)}, bf16[320,1024]{1,0:T(8,128)(2,1)}, u32[]{:S(2)}, u32[]{:S(2)}) collective-permute-start(bf16[320,1024]{1,0:T(8,128)(2,1)S(1)} %get-tuple-element.163.da_ref), channel_id=1, source_target_pairs={{0,1},{1,0},{2,3},{3,2},{4,5},{5,4},{6,7},{7,6},{8,9},{9,8},{10,11... | collective-permute-start | bytes 1966088 | tf_op jit(solution)/shard_map/ppermute | solution.py:516
  443.3 9.4 %collective-permute-start.42 = (f32[2944]{0:T(1024)S(1)}, f32[2944]{0:T(1024)S(1)}, u32[]{:S(2)}, u32[]{:S(2)}) collective-permute-start(f32[2944]{0:T(1024)S(1)} %fusion.18), channel_id=1, source_target_pairs={{0,4},{2,6},{4,0},{6,2},{1,5},{3,7},{5,1},{7,3},{8,12},{10,14},{12... | collective-permute-start | bytes 35336 | tf_op jit(solution)/shard_map/ppermute | solution.py:835
  456.4 4.6 collective-permute-start.44
  461.0 46.6 %collective-permute-start.45 = (bf16[64,4224]{1,0:T(8,128)(2,1)}, bf16[64,4224]{1,0:T(8,128)(2,1)}, u32[]{:S(2)}, u32[]{:S(2)}) collective-permute-start(bf16[64,4224]{1,0:T(8,128)(2,1)} %reduce-scatter.3.cloned.1.call-done), channel_id=1, source_target_pairs={{0,2},{2,0},{4,6},{6,4},{1,3},{3,1},{5,7},{7,5},{8,10},{10,8},{12,... | collective-permute-start | bytes 1622024 | tf_op jit(solution)/shard_map/ppermute | solution.py:519
  461.0 46.6 %collective-permute-start.47 = (bf16[64,4224]{1,0:T(8,128)(2,1)}, bf16[64,4224]{1,0:T(8,128)(2,1)}, u32[]{:S(2)}, u32[]{:S(2)}) collective-permute-start(bf16[64,4224]{1,0:T(8,128)(2,1)} %collective-permute-done.46), channel_id=1, source_target_pairs={{0,2},{2,0},{4,6},{6,4},{1,3},{3,1},{5,7},{7,5},{8,10},{10,8},{12,... | collective-permute-start | bytes 1622024 | tf_op jit(solution)/shard_map/ppermute | solution.py:519
  516.8 10.1 %collective-permute-start.40 = (f32[1024]{0:T(1024)S(1)}, f32[1024]{0:T(1024)S(1)}, u32[]{:S(2)}, u32[]{:S(2)}) collective-permute-start(f32[1024]{0:T(1024)S(1)} %add.197), channel_id=1, source_target_pairs={{0,16},{8,24},{16,0},{24,8},{1,17},{9,25},{17,1},{25,9},{2,18},{10... | collective-permute-start | bytes 12296 | tf_op jit(solution)/shard_map/ppermute | solution.py:839
  (113 other events, 979.1 us)
Sparse Core Ops, SparseCore 0:
  10.8 47.9 all-gather.3
  61.6 90.9 all-gather.5
  293.6 109.9 reduce-scatter.2
  438.2 69.2 reduce-scatter.4
  509.6 15.8 all-gather.7

commit v3 on v2

--- a/solution.py
+++ b/solution.py
@@ -94,8 +94,9 @@
             q_ref[:, at + off : at + off + LANES] = (
                 turn(q[:, cols], rope_ref, 1.0) * HEAD ** (-0.5)
             ).astype(BF)
-            kv_ref[:, at + off : at + off + LANES] = turn(k[:, cols], rope_ref, 1.0).astype(BF)
-        kv_ref[:, width + at : width + at + size] = v.astype(BF)
+            pair = 2 * (at + off)
+            kv_ref[:, pair : pair + LANES] = turn(k[:, cols], rope_ref, 1.0).astype(BF)
+            kv_ref[:, pair + LANES : pair + 2 * LANES] = v[:, cols].astype(BF)
 
 
 def split_pair(values):
@@ -113,93 +114,84 @@
 
 
 def attend_kernel(n_ref, q_ref, kv0, kv1, kv2, kv3, o_ref, lse_ref, m_s, l_s, acc_s):
-    rows, width = q_ref.shape
-    for pair in range(width // LANES):
-        cols = slice(pair * LANES, (pair + 1) * LANES)
-        vcols = slice(width + pair * LANES, width + (pair + 1) * LANES)
-        qb = split_pair(q_ref[:, cols])
-        m_s[...] = jnp.full(m_s.shape, -1e30, F32)
-        l_s[...] = jnp.zeros(l_s.shape, F32)
-        acc_s[...] = jnp.zeros(acc_s.shape, F32)
-
-        def step(kv_ref, count, size):
-            s = dot_nt(kv_ref[:size, cols], qb)
-            key = lax.broadcasted_iota(jnp.int32, s.shape, 0)
-            s = jnp.where(key < count, s, -1e30)
-            m_old = m_s[...]
-            m_new = jnp.maximum(m_old, jnp.max(s, axis=0, keepdims=True))
-            scale = jnp.exp(m_old - m_new)
-            e = jnp.exp(s - m_new)
-            m_s[...] = m_new
-            l_s[...] = l_s[...] * scale + jnp.sum(e, axis=0, keepdims=True)
-            acc_s[...] = acc_s[...] * scale + dot_tn(kv_ref[:size, vcols], e.astype(BF))
-
-        for at, kv_ref in enumerate((kv0, kv1, kv2, kv3)):
-            count = n_ref[at]
-
-            @pl.when(count > TAIL)
-            def _():
-                step(kv_ref, count, kv_ref.shape[0])
-
-            @pl.when((count > 0) & (count <= TAIL))
-            def _():
-                step(kv_ref, count, TAIL)
-
-        total = l_s[...]
-        out = acc_s[...] * (1.0 / total)
-        o_ref[:, cols] = join_pair(out.T).astype(BF)
-        lse_ref[pair : pair + 1, :] = m_s[...] + jnp.log(total)
+    qb = split_pair(q_ref[...])
+    m_s[...] = jnp.full(m_s.shape, -1e30, F32)
+    l_s[...] = jnp.zeros(l_s.shape, F32)
+    acc_s[...] = jnp.zeros(acc_s.shape, F32)
+
+    def step(kv_ref, count, size):
+        s = dot_nt(kv_ref[:size, :LANES], qb)
+        key = lax.broadcasted_iota(jnp.int32, s.shape, 0)
+        s = jnp.where(key < count, s, -1e30)
+        m_old = m_s[...]
+        m_new = jnp.maximum(m_old, jnp.max(s, axis=0, keepdims=True))
+        scale = jnp.exp(m_old - m_new)
+        e = jnp.exp(s - m_new)
+        m_s[...] = m_new
+        l_s[...] = l_s[...] * scale + jnp.sum(e, axis=0, keepdims=True)
+        acc_s[...] = acc_s[...] * scale + dot_tn(kv_ref[:size, LANES:], e.astype(BF))
+
+    for at, kv_ref in enumerate((kv0, kv1, kv2, kv3)):
+        count = n_ref[at]
+
+        @pl.when(count > TAIL)
+        def _():
+            step(kv_ref, count, kv_ref.shape[0])
+
+        @pl.when((count > 0) & (count <= TAIL))
+        def _():
+            step(kv_ref, count, TAIL)
+
+    total = l_s[...]
+    out = acc_s[...] * (1.0 / total)
+    o_ref[...] = join_pair(out.T).astype(BF)
+    lse_ref[0] = m_s[...] + jnp.log(total)
 
 
 def attend_back_kernel(
     n_ref, q_ref, kv0, kv1, kv2, kv3, o_ref, do_ref, lse_ref, rope_ref, dq_ref, keep_ref, send_ref, dq_s
 ):
-    rows, width = q_ref.shape
-    for pair in range(width // LANES):
-        cols = slice(pair * LANES, (pair + 1) * LANES)
-        vcols = slice(width + pair * LANES, width + (pair + 1) * LANES)
-        qb = split_pair(q_ref[:, cols])
-        do = do_ref[:, cols]
-        dob = split_pair(do)
-        prod = split_pair(do.astype(F32) * o_ref[:, cols].astype(F32))
-        delta = jnp.sum(prod.T, axis=0, keepdims=True)
-        lse = lse_ref[pair : pair + 1, :]
-        dq_s[...] = jnp.zeros(dq_s.shape, F32)
-
-        def step(kv_ref, out_ref, slot, count, size):
-            k = kv_ref[:size, cols]
-            s = dot_nt(k, qb)
-            key = lax.broadcasted_iota(jnp.int32, s.shape, 0)
-            p = jnp.where(key < count, jnp.exp(s - lse), 0.0)
-            dp = dot_nt(kv_ref[:size, vcols], dob)
-            ds = (p * (dp - delta)).astype(BF)
-            out_ref[slot, :size, vcols] = dot_nn(p.astype(BF), dob).astype(BF)
-            out_ref[slot, :size, cols] = dot_nn(ds, qb).astype(BF)
-            dq_s[...] += dot_tn(k, ds)
-            if size < rows:
-                out_ref[slot, size:, vcols] = jnp.zeros((rows - size, LANES), BF)
-                out_ref[slot, size:, cols] = jnp.zeros((rows - size, LANES), BF)
-
-        for at, kv_ref in enumerate((kv0, kv1, kv2, kv3)):
-            count = n_ref[at]
-            out_ref = (keep_ref, send_ref)[at % 2]
-            slot = at // 2
-
-            @pl.when(count > TAIL)
-            def _():
-                step(kv_ref, out_ref, slot, count, kv_ref.shape[0])
-
-            @pl.when((count > 0) & (count <= TAIL))
-            def _():
-                step(kv_ref, out_ref, slot, count, TAIL)
-
-            @pl.when(count <= 0)
-            def _():
-                out_ref[slot, :, vcols] = jnp.zeros((rows, LANES), BF)
-                out_ref[slot, :, cols] = jnp.zeros((rows, LANES), BF)
-
-        dq = join_pair(dq_s[...].T) * HEAD ** (-0.5)
-        dq_ref[:, cols] = turn(dq, rope_ref, -1.0).astype(BF)
+    rows = q_ref.shape[0]
+    qb = split_pair(q_ref[...])
+    do = do_ref[...]
+    dob = split_pair(do)
+    prod = split_pair(do.astype(F32) * o_ref[...].astype(F32))
+    delta = jnp.sum(prod.T, axis=0, keepdims=True)
+    lse = lse_ref[0]
+    dq_s[...] = jnp.zeros(dq_s.shape, F32)
+
+    def step(kv_ref, out_ref, slot, count, size):
+        k = kv_ref[:size, :LANES]
+        s = dot_nt(k, qb)
+        key = lax.broadcasted_iota(jnp.int32, s.shape, 0)
+        p = jnp.where(key < count, jnp.exp(s - lse), 0.0)
+        dp = dot_nt(kv_ref[:size, LANES:], dob)
+        ds = (p * (dp - delta)).astype(BF)
+        out_ref[slot, :size, LANES:] = dot_nn(p.astype(BF), dob).astype(BF)
+        out_ref[slot, :size, :LANES] = dot_nn(ds, qb).astype(BF)
+        dq_s[...] += dot_tn(k, ds)
+        if size < rows:
+            out_ref[slot, size:, :] = jnp.zeros((rows - size, 2 * LANES), BF)
+
+    for at, kv_ref in enumerate((kv0, kv1, kv2, kv3)):
+        count = n_ref[at]
+        out_ref = (keep_ref, send_ref)[at % 2]
+        slot = at // 2
+
+        @pl.when(count > TAIL)
+        def _():
+            step(kv_ref, out_ref, slot, count, kv_ref.shape[0])
+
+        @pl.when((count > 0) & (count <= TAIL))
+        def _():
+            step(kv_ref, out_ref, slot, count, TAIL)
+
+        @pl.when(count <= 0)
+        def _():
+            out_ref[slot] = jnp.zeros((rows, 2 * LANES), BF)
+
+    dq = join_pair(dq_s[...].T) * HEAD ** (-0.5)
+    dq_ref[...] = turn(dq, rope_ref, -1.0).astype(BF)
 
 
 def merge_heads(dst, own_ref, other_ref, tp, half):
@@ -209,7 +201,7 @@
 
 def middle_kernel(
     sc_ref, x_ref, cot_ref, own_ref0, own_ref1, own_ref2, other_ref0, other_ref1, other_ref2,
-    again_ref, ln2_ref, fgain_ref, wp_ref, ws_ref,
+    again_ref, ln2_ref, fgain_ref, w_ref,
     x1_ref, h2_ref, g_ref, u_ref, dm_ref, a_ref, st_ref,
     pj_s, gw_s, uw_s, dw_s, o_s, a_s, st_s, sem,
 ):
@@ -219,10 +211,10 @@
     rows = own_ref0.shape[0]
     ff = g_ref.shape[2]
     loads = [
-        pltpu.make_async_copy(ws_ref.at[:, pl.ds(0, width)], pj_s, sem.at[0]),
-        pltpu.make_async_copy(wp_ref.at[:, pl.ds(0, ff)], gw_s, sem.at[1]),
-        pltpu.make_async_copy(wp_ref.at[:, pl.ds(ff, ff)], uw_s, sem.at[2]),
-        pltpu.make_async_copy(ws_ref.at[:, pl.ds(width, ff)], dw_s, sem.at[3]),
+        pltpu.make_async_copy(w_ref.at[:, pl.ds(0, width)], pj_s, sem.at[0]),
+        pltpu.make_async_copy(w_ref.at[:, pl.ds(width + ff, ff)], gw_s, sem.at[1]),
+        pltpu.make_async_copy(w_ref.at[:, pl.ds(width + 2 * ff, ff)], uw_s, sem.at[2]),
+        pltpu.make_async_copy(w_ref.at[:, pl.ds(width, ff)], dw_s, sem.at[3]),
     ]
 
     @pl.when(image == 0)
@@ -288,16 +280,16 @@
 
 
 def ffn_kernel(
-    sa_ref, sb_ref, g_ref, u_ref, dm_ref, fgain_ref, wp_ref, ws_ref,
+    sa_ref, sb_ref, g_ref, u_ref, dm_ref, fgain_ref, w_ref,
     m_ref, dg_ref, du_ref, out_ref, dh_ref, dgain_ref,
     gw_s, uw_s, dw_s, st_s, sem, *, total,
 ):
     _, rows, ff = g_ref.shape
-    width = wp_ref.shape[0]
+    width = w_ref.shape[0]
     loads = [
-        pltpu.make_async_copy(wp_ref.at[:, pl.ds(0, ff)], gw_s, sem.at[0]),
-        pltpu.make_async_copy(wp_ref.at[:, pl.ds(ff, ff)], uw_s, sem.at[1]),
-        pltpu.make_async_copy(ws_ref.at[:, pl.ds(width, ff)], dw_s, sem.at[2]),
+        pltpu.make_async_copy(w_ref.at[:, pl.ds(width + ff, ff)], gw_s, sem.at[0]),
+        pltpu.make_async_copy(w_ref.at[:, pl.ds(width + 2 * ff, ff)], uw_s, sem.at[1]),
+        pltpu.make_async_copy(w_ref.at[:, pl.ds(width, ff)], dw_s, sem.at[2]),
     ]
     for load in loads:
         load.start()
@@ -376,8 +368,9 @@
     rows, half = dq_ref.shape
     total = keep_ref[0].astype(F32) + recv_ref[0].astype(F32) + far_ref[...].astype(F32)
     for at in range(0, half, LANES):
-        dkv_ref[:, at : at + LANES] = turn(total[:, at : at + LANES], rope_ref, -1.0).astype(BF)
-    dkv_ref[:, half:] = total[:, half:].astype(BF)
+        pair = total[:, 2 * at : 2 * at + 2 * LANES]
+        dkv_ref[:, at : at + LANES] = turn(pair[:, :LANES], rope_ref, -1.0).astype(BF)
+        dkv_ref[:, half + at : half + at + LANES] = pair[:, LANES:].astype(BF)
     dq = dq_ref[...]
     dk = dkv_ref[:, :half]
     dv = dkv_ref[:, half:]
@@ -402,18 +395,18 @@
     out_ref[0] = (x1_ref[0] + (pa_ref[...].astype(F32) + pb_ref[...].astype(F32))).astype(BF)
 
 
-def place_kernel(at_ref, *refs, part):
-    *pieces, out_ref, sem = refs
-    copies = []
-    for slot, piece in enumerate(pieces):
-        row = pl.multiple_of(at_ref[slot], part)
-        copies.append(
-            pltpu.make_async_copy(piece, out_ref.at[pl.ds(row, piece.shape[0]), :], sem.at[slot])
-        )
-    for copy in copies:
-        copy.start()
-    for copy in copies:
-        copy.wait()
+def finish_kernel(sum_ref, pairs_ref, down_ref):
+    ff = down_ref.shape[0]
+    ffp = sum_ref.shape[1] // 3
+    for at in range(0, ff, LANES):
+        size = min(LANES, ff - at)
+        for slot in range(3):
+            cols = slice(slot * ffp + at, slot * ffp + at + LANES)
+            flipped = sum_ref[:, cols].astype(F32).T[:size]
+            if slot < 2:
+                pairs_ref[at : at + size, slot, :] = flipped
+            else:
+                down_ref[at : at + size, :] = flipped
 
 
 def grads_kernel(n_ref, *refs, plan):
@@ -465,6 +458,7 @@
 VMEM = pl.BlockSpec(memory_space=pltpu.VMEM)
 SMEM = pl.BlockSpec(memory_space=pltpu.SMEM)
 ANY = pl.BlockSpec(memory_space=pl.ANY)
+HBM = pl.BlockSpec(memory_space=pltpu.HBM)
 
 
 def shape(*dims, dtype=BF):
@@ -481,7 +475,7 @@
         scratch_shapes=list(scratch),
         input_output_aliases=aliases or {},
         name=name,
-        cost_estimate=pl.CostEstimate(flops=flops, bytes_accessed=moved, transcendentals=0),
+        cost_estimate=pl.CostEstimate(flops=flops // 16, bytes_accessed=moved // 16, transcendentals=0),
         compiler_params=pltpu.CompilerParams(vmem_limit_bytes=mib << 20),
     )
 
@@ -492,6 +486,10 @@
 
 def image_of(index, rows, width):
     return pl.BlockSpec((1, rows, width), lambda i: (index, 0, 0))
+
+
+def in_hbm(value):
+    return pltpu.with_memory_space_constraint(value, pltpu.HBM)
 
 
 def local(
@@ -532,46 +530,21 @@
     first = ctx * part
     qkv_part = lax.dynamic_slice_in_dim(qkv_weight, first, part, axis=1)
     full_qkv = lax.all_gather(qkv_part, both, axis=1, tiled=True)
+    proj_part = lax.dynamic_slice_in_dim(proj_weight, first, part, axis=1).T
+    down_part = lax.dynamic_slice_in_dim(down_weight, first, part, axis=1).T
     pairs_part = lax.dynamic_slice_in_dim(gate_up, first, part, axis=1)
     shards = lax.axis_size("shard")
-    shard = lax.axis_index("shard")
-
-    def shift(value, by):
-        return lax.ppermute(value, "shard", [(at, (at + by) % shards) for at in range(shards)])
-
-    low_half = ctx % 2
-    half_part = 2 * part
-    side_part = jnp.concatenate(
+    rest_part = jnp.concatenate(
         [
-            ordered(lax.dynamic_slice_in_dim(proj_weight, low_half * half_part, half_part, axis=1).T, 1),
-            jnp.pad(
-                lax.dynamic_slice_in_dim(down_weight, low_half * half_part, half_part, axis=1).T,
-                ((0, 0), (0, pad)),
-            ),
+            ordered(proj_part, 1),
+            jnp.pad(down_part, ((0, 0), (0, pad))),
+            jnp.pad(pairs_part[0], ((0, 0), (0, pad))),
+            jnp.pad(pairs_part[1], ((0, 0), (0, pad))),
         ],
         axis=1,
     )
-    pieces, rows_at = [], []
-    for by in range(shards):
-        own = side_part if by == 0 else shift(side_part, by)
-        base = (shard + shards - by) % shards * depth
-        for flip, piece in enumerate((own, near(own))):
-            pieces.append(piece)
-            rows_at.append(base + (low_half ^ flip) * half_part)
-    side = call(
-        functools.partial(place_kernel, part=half_part),
-        shape(width, width + ffp),
-        [SMEM] + [ANY] * len(pieces),
-        ANY,
-        [pltpu.SemaphoreType.DMA((len(pieces),))],
-        name="place",
-        moved=4 * width * (width + ffp),
-        mib=8,
-    )(jnp.stack(rows_at).astype(jnp.int32), *pieces)
-    pairs_part = jnp.concatenate(
-        [jnp.pad(pairs_part[at], ((0, 0), (0, pad))) for at in range(2)], axis=1
-    )
-    pairs = lax.all_gather(pairs_part, both, axis=0, tiled=True)
+    rest = lax.all_gather(rest_part, both, axis=0, tiled=True)
+    rest = pltpu.with_memory_space_constraint(rest, pltpu.HBM)
 
     ln1 = ln1_gain[None, :]
     ln2 = ln2_gain[None, :]
@@ -588,6 +561,10 @@
     line_ff = whole(1, ffp)
     rope_spec = whole(3, rows, LANES)
     qkv_spec = whole(3, width, half)
+    pair_half = pl.BlockSpec((rows, LANES), lambda i: (0, i))
+    pair_kv = pl.BlockSpec((rows, 2 * LANES), lambda i: (0, i))
+    pair_kv2 = pl.BlockSpec((2, rows, 2 * LANES), lambda i: (0, 0, i))
+    pair_line = pl.BlockSpec((1, 1, 2 * rows), lambda i: (i, 0, 0))
     block_mb = rows * width
 
     st = [dict() for _ in range(images)]
@@ -605,23 +582,28 @@
             flops=2 * rows * width * 3 * half,
             moved=6 * width * half + 8 * block_mb,
         )(tokens, ln1, full_qkv, tables)
-        s["kvc"] = near(s["kv"])
+        s["kvc"] = in_hbm(near(s["kv"]))
         s["kvf"] = far(s["kv"])
-        s["kvx"] = near(s["kvf"])
+        s["q"] = in_hbm(s["q"])
     for i in range(images):
         s = st[i]
+        if i == images - 1:
+            s["kvf"], st[0]["o"] = lax.optimization_barrier((s["kvf"], st[0]["o"]))
+        s["kvx"] = in_hbm(near(s["kvf"]))
+        s["kvf"], s["kv"] = in_hbm(s["kvf"]), in_hbm(s["kv"])
         s["o"], s["lse"] = call(
             attend_kernel,
-            (shape(rows, half), shape(8, 2 * rows, dtype=F32)),
-            [SMEM, act_half] + [whole(rows, 2 * half)] * 4,
-            [act_half, whole(8, 2 * rows)],
+            (shape(rows, half), shape(half // LANES, 1, 2 * rows, dtype=F32)),
+            [SMEM, pair_half] + [pair_kv] * 4,
+            [pair_half, pair_line],
             [
                 pltpu.VMEM((1, 2 * rows), F32),
                 pltpu.VMEM((1, 2 * rows), F32),
                 pltpu.VMEM((LANES, 2 * rows), F32),
             ],
             name="attend",
-            mib=24,
+            mib=20,
+            grid=half // LANES,
             flops=16 * rows * 4 * rows * half,
             moved=12 * block_mb,
         )(s["n"], s["q"], s["kv"], s["kvc"], s["kvf"], s["kvx"])
@@ -642,7 +624,7 @@
             shape(images, rows, half),
             shape(images, 8, 384, dtype=F32),
         ),
-        [SMEM, each(rows, width), each(rows, width)] + [act_half] * 6 + [line, line, line_ff, ANY, ANY],
+        [SMEM, each(rows, width), each(rows, width)] + [act_half] * 6 + [line, line, line_ff, HBM],
         [
             each(rows, width), each(rows, width), each(rows, ffp), each(rows, ffp), each(rows, ffp),
             each(rows, half), each(8, 384),
@@ -662,7 +644,7 @@
         grid=images,
         flops=2 * images * rows * width * (width + 3 * ffp),
         moved=2 * width * (width + 3 * ffp) + images * (12 * block_mb + 6 * rows * ffp),
-    )(valid, tokens, cotangent, *[s["o"] for s in st], *[s["ox"] for s in st], again, ln2, fgain, pairs, side)
+    )(valid, tokens, cotangent, *[s["o"] for s in st], *[s["ox"] for s in st], again, ln2, fgain, rest)
     stats_x = swap(stats)
     for i in range(images):
         s = st[i]
@@ -676,7 +658,7 @@
                 shape(rows, width),
                 shape(1, ffp, dtype=F32),
             ),
-            [image_of(i, 8, 384)] * 2 + [image_of(i, rows, ffp)] * 3 + [line_ff, ANY, ANY],
+            [image_of(i, 8, 384)] * 2 + [image_of(i, rows, ffp)] * 3 + [line_ff, HBM],
             [act_ff, act_ff, act_ff, act, act, line_ff],
             [
                 pltpu.VMEM((width, ffp), BF),
@@ -689,9 +671,8 @@
             mib=36,
             flops=2 * rows * width * 3 * ffp,
             moved=6 * width * ffp + 12 * rows * ffp + 4 * block_mb,
-        )(stats, stats_x, gate, up, dm, fgain, pairs, side)
+        )(stats, stats_x, gate, up, dm, fgain, rest)
         s["dh2x"] = swap(s["dh2"])
-        s["outx"] = swap(s["out"])
     def weight_grads(groups, tag):
         plan = [(masked, len(left), [len(right) for right in rights]) for masked, left, rights in groups]
         flat = [v for _, left, rights in groups for v in left + [w for right in rights for w in right]]
@@ -718,7 +699,7 @@
     grads_ffn = weight_grads(
         [(False, [h2], [of("dg"), of("du")]), (True, [cotangent], [of("m")])], "grads_ffn"
     )
-    for i in range(images):
+    def norm_back(i):
         s = st[i]
         s["dx"], s["dab"], s["do"], s["dln2"], s["dattn"] = call(
             attn_norm_back_kernel,
@@ -729,7 +710,7 @@
                 shape(1, width, dtype=F32),
                 shape(1, half, dtype=F32),
             ),
-            [SMEM, act, act, image_of(i, rows, width), image_of(i, rows, width), line, act_half, act_half, line, ANY],
+            [SMEM, act, act, image_of(i, rows, width), image_of(i, rows, width), line, act_half, act_half, line, HBM],
             [act, act, act_half, line, whole(1, half)],
             [
                 pltpu.VMEM((width, width), BF),
@@ -742,41 +723,26 @@
             mib=28,
             flops=2 * rows * width * width,
             moved=2 * width * width + 16 * block_mb,
-        )(s["sc"], s["dh2"], s["dh2x"], x1, cotangent, ln2, s["o"], s["ox"], again, side)
-        if i == 0:
-            s["do"], grads_ffn = lax.optimization_barrier((s["do"], grads_ffn))
-        else:
-            s["do"], st[i - 1]["outx"] = lax.optimization_barrier((s["do"], st[i - 1]["outx"]))
+        )(s["sc"], s["dh2"], s["dh2x"], x1, cotangent, ln2, s["o"], s["ox"], again, rest)
+
+    def attention_back(i):
+        s = st[i]
         s["dq"], s["keep"], s["send"] = call(
             attend_back_kernel,
             (shape(rows, half), shape(2, rows, 2 * half), shape(2, rows, 2 * half)),
-            [SMEM, act_half] + [whole(rows, 2 * half)] * 4 + [act_half, act_half, whole(8, 2 * rows), rope_spec],
-            [act_half, whole(2, rows, 2 * half), whole(2, rows, 2 * half)],
+            [SMEM, pair_half] + [pair_kv] * 4 + [pair_half, pair_half, pair_line, rope_spec],
+            [pair_half, pair_kv2, pair_kv2],
             [pltpu.VMEM((LANES, 2 * rows), F32)],
+            grid=half // LANES,
             name="attend_back",
-            mib=28,
+            mib=20,
             flops=40 * rows * 4 * rows * half,
             moved=20 * block_mb,
         )(s["n"], s["q"], s["kv"], s["kvc"], s["kvf"], s["kvx"], s["o"], s["do"], s["lse"], tables)
         s["recv"] = near(s["send"])
-        s["far"] = far((s["keep"][1].astype(F32) + s["recv"][1].astype(F32)).astype(BF))
-    mixed = None
-    for i in range(images):
-        s = st[i]
-        again_buf = [] if mixed is None else [mixed]
-        mixed = call(
-            mixed_kernel,
-            shape(images, rows, width),
-            [image_of(i, rows, width), act, act] + [ANY] * len(again_buf),
-            image_of(i, rows, width),
-            name="mixed",
-            mib=12,
-            moved=10 * block_mb,
-            aliases={3: 0} if again_buf else None,
-        )(x1, s["out"], s["outx"], *again_buf)
-    st[0]["dq"], mixed = lax.optimization_barrier((st[0]["dq"], mixed))
-    grad_tokens = None
-    for i in range(images):
+        s["mid"] = (s["keep"][1].astype(F32) + s["recv"][1].astype(F32)).astype(BF)
+
+    def qkv_back(i):
         s = st[i]
         s["dkv"], s["dh1"] = call(
             qkv_back_kernel,
@@ -796,7 +762,23 @@
             moved=6 * width * half + 10 * block_mb,
         )(s["keep"], s["recv"], s["far"], s["dq"], tables, full_qkv)
         s["dh1x"] = swap(s["dh1"])
-    for i in range(images):
+
+    def mixed_part(i, mixed):
+        s = st[i]
+        again_buf = [] if mixed is None else [mixed]
+        mixed = call(
+            mixed_kernel,
+            shape(images, rows, width),
+            [image_of(i, rows, width), act, act] + [ANY] * len(again_buf),
+            image_of(i, rows, width),
+            name="mixed",
+            mib=12,
+            moved=10 * block_mb,
+            aliases={3: 0} if again_buf else None,
+        )(x1, s["out"], s["outx"], *again_buf)
+        return mixed
+
+    def tokens_part(i, grad_tokens):
         s = st[i]
         again_buf = [] if grad_tokens is None else [grad_tokens]
         grad_tokens, s["dln1"] = call(
@@ -809,6 +791,41 @@
             moved=12 * block_mb,
             aliases={5: 0} if again_buf else None,
         )(s["dh1"], s["dh1x"], tokens, ln1, s["dx"], *again_buf)
+        return grad_tokens
+
+    def tie(*values):
+        return lax.optimization_barrier(values)
+
+    mixed = grad_tokens = None
+    norm_back(0)
+    late = [st[1], st[2]]
+    tied = tie(st[0]["do"], *[s["out"] for s in st], *[s["dh2x"] for s in late], grads_ffn)
+    st[0]["do"], grads_ffn = tied[0], tied[-1]
+    for i, s in enumerate(st):
+        s["out"] = tied[1 + i]
+        s["outx"] = swap(s["out"])
+    for i, s in enumerate(late):
+        s["dh2x"] = tied[1 + images + i]
+    attention_back(0)
+    norm_back(1)
+    st[1]["do"], st[0]["mid"] = tie(st[1]["do"], st[0]["mid"])
+    st[0]["far"] = far(st[0]["mid"])
+    attention_back(1)
+    norm_back(2)
+    st[2]["do"], st[0]["far"] = tie(st[2]["do"], st[0]["far"])
+    st[1]["far"] = far(st[1]["mid"])
+    qkv_back(0)
+    attention_back(2)
+    st[2]["far"] = far(st[2]["mid"])
+    qkv_back(1)
+    st[2]["far"], st[1]["dkv"], st[0]["outx"], st[0]["dh1x"] = tie(
+        st[2]["far"], st[1]["dkv"], st[0]["outx"], st[0]["dh1x"]
+    )
+    qkv_back(2)
+    for i in range(images):
+        mixed = mixed_part(i, mixed)
+    for i in range(images):
+        grad_tokens = tokens_part(i, grad_tokens)
     own_ffn = lax.psum_scatter(grads_ffn, both, scatter_dimension=0, tiled=True)
 
     def around(own):
@@ -821,13 +838,15 @@
     )
     grads_qkv, own_ffn = lax.optimization_barrier((grads_qkv, own_ffn))
     own_qkv = lax.psum_scatter(grads_qkv, both, scatter_dimension=0, tiled=True)
-    sum_ffn = around(own_ffn).astype(F32)
-    own_qkv, grad_tokens, st[0]["dln1"] = lax.optimization_barrier((own_qkv, grad_tokens, st[0]["dln1"]))
-    sum_qkv = lax.all_gather(own_qkv, "ctx", axis=0, tiled=True).astype(F32)
-    grad_proj = sum_qkv[:, 3 * half :].T
-    grad_pairs = jnp.stack([sum_ffn[:, :ff], sum_ffn[:, ffp : ffp + ff]])
-    grad_down = sum_ffn[:, 2 * ffp : 2 * ffp + ff].T
-    grad_qkv = jnp.stack([sum_qkv[:, j * half : (j + 1) * half] for j in range(3)])
+    grad_pairs, grad_down = call(
+        finish_kernel,
+        (shape(ff, 2, depth, dtype=F32), shape(ff, depth, dtype=F32)),
+        [whole(depth, 3 * ffp)],
+        [whole(ff, 2, depth), whole(ff, depth)],
+        name="finish",
+        mib=20,
+        moved=18 * ff * depth,
+    )(around(own_ffn))
 
     def everywhere(value):
         step = 1
@@ -848,6 +867,14 @@
     gain_ln2 = packed[ffp : ffp + width]
     gain_attn = packed[ffp + width :]
     gain_ln1 = everywhere(gain("dln1"))
+    own_qkv, grad_tokens, mixed, gain_ln1, gain_ffn, grad_pairs, grad_down = tie(
+        own_qkv, grad_tokens, mixed, gain_ln1, gain_ffn, grad_pairs, grad_down
+    )
+    grad_pairs = jnp.transpose(grad_pairs, (1, 2, 0))
+    sum_qkv = lax.all_gather(own_qkv[:, : 3 * half], "ctx", axis=0, tiled=True).astype(F32)
+    grad_proj = around(own_qkv[:, 3 * half :]).astype(F32).T
+    grad_qkv = jnp.stack([sum_qkv[:, j * half : (j + 1) * half] for j in range(3)])
+
     return (
         mixed,
         grad_tokens,

time: 549 us -> 480 us (0.87)
  waiting for transfers between devices: 219 us -> 181 us
  local copies, waits for them, and re-layouts: 82.3 us -> 56.1 us
  blocking collectives: 0 us -> 8.88 us
  starting transfers between devices: 37.3 us -> 31.6 us
    ppermute x7 -> x8, waiting for transfers between devices: 30.6 us -> 86.4 us  [far(): return lax.ppermute(value, 'ctx', swap_far)]
    ppermute x3 -> x0, waiting for transfers between devices: 47.6 us -> none  [shift(): lax.ppermute(value, 'shard', [(at, (at + by) % shards) for at in range(sh...]
    ppermute x15, waiting for transfers between devices: 61.4 us -> 31.4 us  [swap(): return lax.ppermute(value, 'tp', swap_tp)]
    unnamed x223 -> x177, local copies, waits for them, and re-layouts: 74.3 us -> 45.8 us
    reduce_scatter x1, waiting for transfers between devices: 20.7 us -> 1.99 us  [local(): own_qkv = lax.psum_scatter(grads_qkv, both, scatter_dimension=0, tiled=True)]
    all_gather x0 -> x1, blocking collectives: none -> 8.88 us  [local(): lax.all_gather(own_qkv[:, :3 * half], 'ctx', axis=0, tiled=True).astype(F32)]
    ppermute x3 -> x0, starting transfers between devices: 6.13 us -> none  [shift(): lax.ppermute(value, 'shard', [(at, (at + by) % shards) for at in range(sh...]
  transfers between devices with their start and end apart: 53 -> 48, of which waited for: 25 -> 20; matrix products, arithmetic and copies ran while one was open for 5% -> 4% of each run, Pallas kernels for 26% -> 30%
where the time goes in v3:
time: 480 us; the launch traced here: 471 us
  waiting for transfers between devices  181 us (38%)
  Pallas kernels  169 us (35%)
  local copies, waits for them, and re-layouts  56.1 us (12%)
  starting transfers between devices  31.6 us (7%)
  between operations  15.1 us (3%)
  other arithmetic  9.29 us (2%)
  blocking collectives  8.88 us (2%)
    ppermute x8, waiting for transfers between devices, far(): return lax.ppermute(value, 'ctx', swap_far)  86.4 us
    unnamed x177, local copies, waits for them, and re-layouts  45.8 us
    all_gather x1, waiting for transfers between devices, local(): full_qkv = lax.all_gather(qkv_part, both, axis=1, tiled=True)  37 us
    pallas_call x3, Pallas kernels, attention_back(): call(attend_back_kernel, (shape(rows, half), shape(2, rows, 2 * half), sh...  36.6 us
    ppermute x15, waiting for transfers between devices, swap(): return lax.ppermute(value, 'tp', swap_tp)  31.4 us
    pallas_call x3, Pallas kernels, local(): call(attend_kernel, (shape(rows, half), shape(half // LANES, 1, 2 * rows,...  29.8 us
    pallas_call x2, Pallas kernels, weight_grads(): call(functools.partial(grads_kernel, plan=plan), shape(width, columns), [...  21.8 us
    pallas_call x1, Pallas kernels, local(): call(middle_kernel, (shape(images, rows, width, dtype=F32), shape(images,...  21.3 us
  transfers between devices with their start and end apart: 48, of which 20 were waited for; matrix products, arithmetic and copies ran while one was open for 4% of the time, Pallas kernels for 30%

profile of v3, /device:TPU:0, one launch (start us, length us, event | category | flops | bytes accessed | tf_op | source)
XLA Modules:
  0.0 471.0 jit_solution(2169928641632142692)
XLA Ops:
  10.2 3.0 collective-permute-start.13
  14.4 1.9 constant_dynamic-slice_fusion.1
  21.8 37.0 %all-gather.3.cloned.1.call-done.w_ref = bf16[3,1024,512]{2,1,0:T(8,128)(2,1)} async-done(((bf16[3,64,512]{2,1,0:T(8,128)(2,1)}), bf16[3,1024,512]{2,1,0:T(8,128)(2,1)}) %all-gather.3.cloned.1.call-update) | async-done | bytes 3145744 | tf_op jit(solution)/shard_map/all_gather | solution.py:532
  58.8 1.9 copy-done.5
  69.1 19.5 %collective-permute-done.1.kv2 = bf16[320,1024]{1,0:T(8,128)(2,1)S(1)} collective-permute-done((bf16[320,1024]{1,0:T(8,128)(2,1)S(1)}, bf16[320,1024]{1,0:T(8,128)(2,1)S(1)}, u32[]{:S(2)}, u32[]{:S(2)}) %collective-permute-start.1) | collective-permute-done | bytes 655392 | tf_op jit(solution)/shard_map/ppermute | solution.py:520
  91.6 11.0 %collective-permute-done.5.kv2 = bf16[320,1024]{1,0:T(8,128)(2,1)S(1)} collective-permute-done((bf16[320,1024]{1,0:T(8,128)(2,1)S(1)}, bf16[320,1024]{1,0:T(8,128)(2,1)S(1)}, u32[]{:S(2)}, u32[]{:S(2)}) %collective-permute-start.5) | collective-permute-done | bytes 655392 | tf_op jit(solution)/shard_map/ppermute | solution.py:520
  103.6 12.6 %attend.3 = (bf16[320,512]{1,0:T(8,128)(2,1)S(1)}, f32[4,1,640]{2,1,0:T(1,128)S(1)}) custom-call(s32[4]{0:T(128)S(1)} %get-tuple-element.264.n_ref, bf16[320,512]{1,0:T(8,128)(2,1)} %copy-done.29, bf16[320,1024]{1,0:T(8,128)(2,1)} %copy-done.19, bf16[320,1024]{1,0:T(8,128)(2,1)} %copy-done.75, bf16[320,1024]{1,0:T(8,128)(2,1)} %copy-done.74, ...), custom_call_target="tpu_custom_call" | custom-call | flops 209715200 | bytes 245760 | tf_op jit(solution)/shard_map/attend/pallas_call | solution.py:594
  116.2 11.9 %collective-permute-done.3.kv2 = bf16[320,1024]{1,0:T(8,128)(2,1)S(1)} collective-permute-done((bf16[320,1024]{1,0:T(8,128)(2,1)S(1)}, bf16[320,1024]{1,0:T(8,128)(2,1)S(1)}, u32[]{:S(2)}, u32[]{:S(2)}) %collective-permute-start.3) | collective-permute-done | bytes 655392 | tf_op jit(solution)/shard_map/ppermute | solution.py:520
  131.2 9.5 %attend.4 = (bf16[320,512]{1,0:T(8,128)(2,1)S(1)}, f32[4,1,640]{2,1,0:T(1,128)S(1)}) custom-call(s32[4]{0:T(128)S(1)} %get-tuple-element.263.n_ref, bf16[320,512]{1,0:T(8,128)(2,1)} %copy-done.28, bf16[320,1024]{1,0:T(8,128)(2,1)} %copy-done.18, bf16[320,1024]{1,0:T(8,128)(2,1)} %copy-done.76, bf16[320,1024]{1,0:T(8,128)(2,1)} %copy-done.72, ...), custom_call_target="tpu_custom_call" | custom-call | flops 209715200 | bytes 245760 | tf_op jit(solution)/shard_map/attend/pallas_call | solution.py:594
  143.4 7.7 %attend.5 = (bf16[320,512]{1,0:T(8,128)(2,1)S(1)}, f32[4,1,640]{2,1,0:T(1,128)S(1)}) custom-call(s32[4]{0:T(128)S(1)} %get-tuple-element.262.n_ref, bf16[320,512]{1,0:T(8,128)(2,1)} %copy-done.27, bf16[320,1024]{1,0:T(8,128)(2,1)} %copy-done.17, bf16[320,1024]{1,0:T(8,128)(2,1)} %copy-done.71, bf16[320,1024]{1,0:T(8,128)(2,1)} %copy-done.70, ...), custom_call_target="tpu_custom_call" | custom-call | flops 209715200 | bytes 245760 | tf_op jit(solution)/shard_map/attend/pallas_call | solution.py:594
  151.8 8.6 %collective-permute-done.11.other_ref2.other_ref = bf16[320,512]{1,0:T(8,128)(2,1)S(1)} collective-permute-done((bf16[320,512]{1,0:T(8,128)(2,1)S(1)}, bf16[320,512]{1,0:T(8,128)(2,1)S(1)}, u32[]{:S(2)}, u32[]{:S(2)}) %collective-permute-start.11) | collective-permute-done | bytes 327712 | tf_op jit(solution)/shard_map/ppermute | solution.py:514
  160.5 4.5 all-gather.5.cloned.1.call-done.w_ref
  165.0 21.3 %middle.1 = (f32[3,320,1024]{2,1,0:T(8,128)}, bf16[3,320,1024]{2,1,0:T(8,128)(2,1)S(1)}, bf16[3,320,1408]{2,1,0:T(8,128)(2,1)}, bf16[3,320,1408]{2,1,0:T(8,128)(...) custom-call(s32[4]{0:T(128)S(1)} %pad_add_fusion.1.sc_ref, ...), custom_call_target="tpu_custom_call" | custom-call | flops 644874240 | bytes 1915904 | tf_op jit(solution)/shard_map/middle/pallas_call | solution.py:616
  187.9 2.5 collective-permute-done.14.sb_ref
  190.4 1.8 copy-done.10
  195.6 6.2 %ffn.5 = (bf16[320,1408]{1,0:T(8,128)(2,1)S(1)}, bf16[320,1408]{1,0:T(8,128)(2,1)S(1)}, bf16[320,1408]{1,0:T(8,128)(2,1)S(1)}, bf16[320,1024]{1,0:T(8,128)(2,1)S...) custom-call(f32[3,8,384]{2,1,0:T(8,128)S(1)} %get-tuple-element.128.sa_ref, ...), custom_call_target="tpu_custom_call" | custom-call | flops 173015040 | bytes 960512 | tf_op jit(solution)/shard_map/ffn/pallas_call | solution.py:651
  205.2 6.2 %ffn.3 = (bf16[320,1408]{1,0:T(8,128)(2,1)S(1)}, bf16[320,1408]{1,0:T(8,128)(2,1)S(1)}, bf16[320,1408]{1,0:T(8,128)(2,1)S(1)}, bf16[320,1024]{1,0:T(8,128)(2,1)S...) custom-call(f32[3,8,384]{2,1,0:T(8,128)S(1)} %get-tuple-element.128.sa_ref, ...), custom_call_target="tpu_custom_call" | custom-call | flops 173015040 | bytes 960512 | tf_op jit(solution)/shard_map/ffn/pallas_call | solution.py:651
  212.8 7.2 %ffn.4 = (bf16[320,1408]{1,0:T(8,128)(2,1)S(1)}, bf16[320,1408]{1,0:T(8,128)(2,1)S(1)}, bf16[320,1408]{1,0:T(8,128)(2,1)S(1)}, bf16[320,1024]{1,0:T(8,128)(2,1)}...) custom-call(f32[3,8,384]{2,1,0:T(8,128)S(1)} %get-tuple-element.128.sa_ref, ...), custom_call_target="tpu_custom_call" | custom-call | flops 173015040 | bytes 960512 | tf_op jit(solution)/shard_map/ffn/pallas_call | solution.py:651
  224.6 15.2 %grads_ffn.1 = bf16[1024,4224]{1,0:T(8,128)(2,1)} custom-call(s32[3]{0:T(128)S(1)} %slice_reduce_fusion.n_ref, bf16[3,320,1024]{2,1,0:T(8,128)(2,1)} %copy-done.20, bf16[320,1408]{1,0:T(8,128)(2,1)S(1)} %get-tuple-element.141.refs_1_, bf16[320,1408]{1,0:T(8,128)(2,1)S(1)} %get-tuple-element.142.refs_2_, bf16[320,1408]{1,0:T(8,128)(2,1)S(1)} %get-tuple-element.143.refs_3_, ...), custom_call_target="tpu_custom_call" | custom-call | flops 519045120 | bytes 1081344 | tf_op jit(solution)/shard_map/grads_ffn/pallas_call | solution.py:680
  239.9 2.1 copy-done.2
  243.9 5.4 %attn_norm_back.3 = (f32[320,1024]{1,0:T(8,128)S(1)}, bf16[320,1024]{1,0:T(8,128)(2,1)S(1)}, bf16[320,512]{1,0:T(8,128)(2,1)S(1)}, f32[1,1024]{1,0:T(1,128)S(1)}, f32[1,512]{1,0:T(1,128)S(1)}) custom-call(s32[2]{0:T(128)S(1)} %pad_add_fusion.sc_ref, bf16[320,1024]{1,0:T(8,128)(2,1)} %get-tuple-element.132.dha_ref, ...), custom_call_target="tpu_custom_call" | custom-call | flops 41943040 | bytes 458752 | tf_op jit(solution)/shard_map/attn_norm_back/pallas_call | solution.py:704
  254.0 14.8 %attend_back.3 = (bf16[320,512]{1,0:T(8,128)(2,1)S(1)}, bf16[2,320,1024]{2,1,0:T(8,128)(2,1)S(1)}, bf16[2,320,1024]{2,1,0:T(8,128)(2,1)S(1)}) custom-call(s32[4]{0:T(128)S(1)} %get-tuple-element.264.n_ref, bf16[320,512]{1,0:T(8,128)(2,1)} %copy-done.29, bf16[320,1024]{1,0:T(8,128)(2,1)} %copy-done.19, bf16[320,1024]{1,0:T(8,128)(2,1)} %copy-done.75, ...), custom_call_target="tpu_custom_call" | custom-call | flops 524288000 | bytes 409600 | tf_op jit(solution)/shard_map/attend_back/pallas_call | solution.py:730
  270.7 5.7 %attn_norm_back.4 = (f32[320,1024]{1,0:T(8,128)S(1)}, bf16[320,1024]{1,0:T(8,128)(2,1)S(1)}, bf16[320,512]{1,0:T(8,128)(2,1)S(1)}, f32[1,1024]{1,0:T(1,128)S(1)}, f32[1,512]{1,0:T(1,128)S(1)}) custom-call(s32[2]{0:T(128)S(1)} %pad_add_fusion.2.sc_ref, bf16[320,1024]{1,0:T(8,128)(2,1)} %get-tuple-element.138.dha_ref, ...), custom_call_target="tpu_custom_call" | custom-call | flops 41943040 | bytes 458752 | tf_op jit(solution)/shard_map/attn_norm_back/pallas_call | solution.py:704
  277.3 11.6 %attend_back.4 = (bf16[320,512]{1,0:T(8,128)(2,1)S(1)}, bf16[2,320,1024]{2,1,0:T(8,128)(2,1)S(1)}, bf16[2,320,1024]{2,1,0:T(8,128)(2,1)S(1)}) custom-call(s32[4]{0:T(128)S(1)} %get-tuple-element.263.n_ref, bf16[320,512]{1,0:T(8,128)(2,1)} %copy-done.28, bf16[320,1024]{1,0:T(8,128)(2,1)} %copy-done.18, bf16[320,1024]{1,0:T(8,128)(2,1)} %copy-done.76, ...), custom_call_target="tpu_custom_call" | custom-call | flops 524288000 | bytes 409600 | tf_op jit(solution)/shard_map/attend_back/pallas_call | solution.py:730
  289.9 5.4 %attn_norm_back.5 = (f32[320,1024]{1,0:T(8,128)S(1)}, bf16[320,1024]{1,0:T(8,128)(2,1)S(1)}, bf16[320,512]{1,0:T(8,128)(2,1)S(1)}, f32[1,1024]{1,0:T(1,128)S(1)}, f32[1,512]{1,0:T(1,128)S(1)}) custom-call(s32[2]{0:T(128)S(1)} %pad_add_fusion.3.sc_ref, bf16[320,1024]{1,0:T(8,128)(2,1)} %get-tuple-element.139.dha_ref, ...), custom_call_target="tpu_custom_call" | custom-call | flops 41943040 | bytes 458752 | tf_op jit(solution)/shard_map/attn_norm_back/pallas_call | solution.py:704
  296.3 4.9 %collective-permute-done.19.far_ref = bf16[320,1024]{1,0:T(8,128)(2,1)S(1)} collective-permute-done((bf16[320,1024]{1,0:T(8,128)(2,1)S(1)}, bf16[320,1024]{1,0:T(8,128)(2,1)S(1)}, u32[]{:S(2)}, u32[]{:S(2)}) %collective-permute-start.19) | collective-permute-done | bytes 655392 | tf_op jit(solution)/shard_map/ppermute | solution.py:520
  301.2 10.1 %attend_back.5 = (bf16[320,512]{1,0:T(8,128)(2,1)S(1)}, bf16[2,320,1024]{2,1,0:T(8,128)(2,1)S(1)}, bf16[2,320,1024]{2,1,0:T(8,128)(2,1)S(1)}) custom-call(s32[4]{0:T(128)S(1)} %get-tuple-element.262.n_ref, bf16[320,512]{1,0:T(8,128)(2,1)} %copy-done.27, bf16[320,1024]{1,0:T(8,128)(2,1)} %copy-done.17, bf16[320,1024]{1,0:T(8,128)(2,1)} %copy-done.71, ...), custom_call_target="tpu_custom_call" | custom-call | flops 524288000 | bytes 409600 | tf_op jit(solution)/shard_map/attend_back/pallas_call | solution.py:730
  313.0 2.1 collective-permute-start.25
  317.8 25.1 %collective-permute-done.23.far_ref = bf16[320,1024]{1,0:T(8,128)(2,1)S(1)} collective-permute-done((bf16[320,1024]{1,0:T(8,128)(2,1)S(1)}, bf16[320,1024]{1,0:T(8,128)(2,1)S(1)}, u32[]{:S(2)}, u32[]{:S(2)}) %collective-permute-start.23) | collective-permute-done | bytes 655392 | tf_op jit(solution)/shard_map/ppermute | solution.py:520
  346.9 14.0 %collective-permute-done.21.far_ref = bf16[320,1024]{1,0:T(8,128)(2,1)S(1)} collective-permute-done((bf16[320,1024]{1,0:T(8,128)(2,1)S(1)}, bf16[320,1024]{1,0:T(8,128)(2,1)S(1)}, u32[]{:S(2)}, u32[]{:S(2)}) %collective-permute-start.21) | collective-permute-done | bytes 655392 | tf_op jit(solution)/shard_map/ppermute | solution.py:520
  363.3 6.6 %grads_qkv.1 = bf16[1024,2048]{1,0:T(8,128)(2,1)S(1)} custom-call(s32[3]{0:T(128)S(1)} %slice_reduce_fusion.n_ref, bf16[320,1024]{1,0:T(8,128)(2,1)S(1)} %copy-done.46, bf16[320,1024]{1,0:T(8,128)(2,1)S(1)} %copy-done.48, bf16[320,1024]{1,0:T(8,128)(2,1)S(1)} %copy-done.50, bf16[320,512]{1,0:T(8,128)(2,1)S(1)} %get-tuple-element.152.dq_ref.refs_3_, ...), custom_call_target="tpu_custom_call" | custom-call | flops 251658240 | bytes 524288 | tf_op jit(solution)/shard_map/grads_qkv/pallas_call | solution.py:680
  369.8 2.0 copy-done.13
  378.2 13.0 %collective-permute-done.27.db_ref = bf16[320,1024]{1,0:T(8,128)(2,1)S(1)} collective-permute-done((bf16[320,1024]{1,0:T(8,128)(2,1)}, bf16[320,1024]{1,0:T(8,128)(2,1)S(1)}, u32[]{:S(2)}, u32[]{:S(2)}) %collective-permute-start.27) | collective-permute-done | bytes 655392 | tf_op jit(solution)/shard_map/ppermute | solution.py:514
  394.3 1.9 tokens_back.3
  396.2 1.9 tokens_back.4
  398.0 7.2 %collective-permute-done.26.db_ref = bf16[320,1024]{1,0:T(8,128)(2,1)S(1)} collective-permute-done((bf16[320,1024]{1,0:T(8,128)(2,1)}, bf16[320,1024]{1,0:T(8,128)(2,1)S(1)}, u32[]{:S(2)}, u32[]{:S(2)}) %collective-permute-start.26) | collective-permute-done | bytes 655392 | tf_op jit(solution)/shard_map/ppermute | solution.py:514
  405.3 1.9 tokens_back.5
  409.2 3.3 collective-permute-done.35
  413.1 3.0 collective-permute-done.31
  417.0 3.0 collective-permute-done.36
  420.8 3.3 collective-permute-done.32
  424.8 4.8 %collective-permute-done.37 = f32[2944]{0:T(1024)S(1)} collective-permute-done((f32[2944]{0:T(1024)S(1)}, f32[2944]{0:T(1024)S(1)}, u32[]{:S(2)}, u32[]{:S(2)}) %collective-permute-start.37) | collective-permute-done | bytes 11808 | tf_op jit(solution)/shard_map/ppermute | solution.py:858
  431.4 2.1 copy-done.4
  436.8 2.3 mixed.4.rest_0_
  439.1 2.2 mixed.5
  443.8 3.0 finish.1
  446.9 2.0 reduce-scatter.5.cloned.1.call-done
  451.3 8.9 %all_gather.11 = bf16[256,1536]{1,0:T(8,128)(2,1)S(1)} all-gather(bf16[64,1536]{1,0:T(8,128)(2,1)S(1)} %slice.87), channel_id=1, replica_groups=mesh['shard'=4,'ctx'=4,'tp'=2] {'ctx'}, dimensions={0}, use_global_device_ids=true | all-gather | bytes 983040 | tf_op jit(solution)/shard_map/all_gather | solution.py:874
  (314 shorter events, 92.9 us)
Async XLA Ops:
  7.2 51.5 %all-gather.3.cloned.1.call-start = ((), (), s32[]{:S(2)}) async-start(), calls=%async_computation.2 | async-start | bytes 3342336 | tf_op jit(solution)/shard_map/all_gather | solution.py:532
  9.0 155.9 %all-gather.5.cloned.1.call-start = ((), (), s32[]{:S(2)}) async-start(), calls=%async_computation.3 | async-start | bytes 11419648 | tf_op jit(solution)/shard_map/all_gather | solution.py:546
  10.2 8.0 %collective-permute-start.13 = (bf16[64,512]{1,0:T(8,128)(2,1)S(1)}, bf16[64,512]{1,0:T(8,128)(2,1)S(1)}, u32[]{:S(2)}, u32[]{:S(2)}) collective-permute-start(bf16[64,512]{1,0:T(8,128)(2,1)S(1)} %bitcast.56), channel_id=1, source_target_pairs={{0,1},{1,0},{2,3},{3,2},{4,5},{5,4},{6,7},{7,6},{8,9},{9,8},{10,11... | collective-permute-start | bytes 196616 | tf_op jit(solution)/shard_map/ppermute | solution.py:514
  19.2 354.1 %reduce-scatter.3.cloned.1.call-start = ((), (), s32[]{:S(2)}) async-start(), calls=%async_computation.4 | async-start | bytes 9191424 | tf_op jit(solution)/shard_map/reduce_scatter | solution.py:829
  63.9 24.8 %collective-permute-start.1 = (bf16[320,1024]{1,0:T(8,128)(2,1)S(1)}, bf16[320,1024]{1,0:T(8,128)(2,1)S(1)}, u32[]{:S(2)}, u32[]{:S(2)}) collective-permute-start(bf16[320,1024]{1,0:T(8,128)(2,1)S(1)} %get-tuple-element.118.kv0), channel_id=1, source_target_pairs={{0,4},{2,6},{4,0},{6,2},{1,5},{3,7},{5,1},{7,3},{8,12},{10,14},{12... | collective-permute-start | bytes 1966088 | tf_op jit(solution)/shard_map/ppermute | solution.py:520
  64.4 26.9 %collective-permute-start = (bf16[320,1024]{1,0:T(8,128)(2,1)S(1)}, bf16[320,1024]{1,0:T(8,128)(2,1)S(1)}, u32[]{:S(2)}, u32[]{:S(2)}) collective-permute-start(bf16[320,1024]{1,0:T(8,128)(2,1)S(1)} %get-tuple-element.118.kv0), channel_id=1, source_target_pairs={{0,2},{2,0},{4,6},{6,4},{1,3},{3,1},{5,7},{7,5},{8,10},{10,8},{12,... | collective-permute-start | bytes 1966088 | tf_op jit(solution)/shard_map/ppermute | solution.py:517
  67.6 35.0 %collective-permute-start.5 = (bf16[320,1024]{1,0:T(8,128)(2,1)S(1)}, bf16[320,1024]{1,0:T(8,128)(2,1)S(1)}, u32[]{:S(2)}, u32[]{:S(2)}) collective-permute-start(bf16[320,1024]{1,0:T(8,128)(2,1)S(1)} %get-tuple-element.123.kv0), channel_id=1, source_target_pairs={{0,4},{2,6},{4,0},{6,2},{1,5},{3,7},{5,1},{7,3},{8,12},{10,14},{12... | collective-permute-start | bytes 1966088 | tf_op jit(solution)/shard_map/ppermute | solution.py:520
  88.6 14.1 %collective-permute-start.2 = (bf16[320,1024]{1,0:T(8,128)(2,1)S(1)}, bf16[320,1024]{1,0:T(8,128)(2,1)S(1)}, u32[]{:S(2)}, u32[]{:S(2)}) collective-permute-start(bf16[320,1024]{1,0:T(8,128)(2,1)S(1)} %collective-permute-done.1.kv2), channel_id=1, source_target_pairs={{0,2},{2,0},{4,6},{6,4},{1,3},{3,1},{5,7},{7,5},{8,10},{10,8},{12,... | collective-permute-start | bytes 1966088 | tf_op jit(solution)/shard_map/ppermute | solution.py:517
  90.3 37.7 %collective-permute-start.3 = (bf16[320,1024]{1,0:T(8,128)(2,1)S(1)}, bf16[320,1024]{1,0:T(8,128)(2,1)S(1)}, u32[]{:S(2)}, u32[]{:S(2)}) collective-permute-start(bf16[320,1024]{1,0:T(8,128)(2,1)S(1)} %get-tuple-element.119.kv0), channel_id=1, source_target_pairs={{0,4},{2,6},{4,0},{6,2},{1,5},{3,7},{5,1},{7,3},{8,12},{10,14},{12... | collective-permute-start | bytes 1966088 | tf_op jit(solution)/shard_map/ppermute | solution.py:520
  91.1 51.2 %collective-permute-start.7 = (bf16[320,1024]{1,0:T(8,128)(2,1)S(1)}, bf16[320,1024]{1,0:T(8,128)(2,1)S(1)}, u32[]{:S(2)}, u32[]{:S(2)}) collective-permute-start(bf16[320,1024]{1,0:T(8,128)(2,1)S(1)} %get-tuple-element.119.kv0), channel_id=1, source_target_pairs={{0,2},{2,0},{4,6},{6,4},{1,3},{3,1},{5,7},{7,5},{8,10},{10,8},{12,... | collective-permute-start | bytes 1966088 | tf_op jit(solution)/shard_map/ppermute | solution.py:517
  91.3 38.5 %collective-permute-start.4 = (bf16[320,1024]{1,0:T(8,128)(2,1)S(1)}, bf16[320,1024]{1,0:T(8,128)(2,1)S(1)}, u32[]{:S(2)}, u32[]{:S(2)}) collective-permute-start(bf16[320,1024]{1,0:T(8,128)(2,1)S(1)} %get-tuple-element.123.kv0), channel_id=1, source_target_pairs={{0,2},{2,0},{4,6},{6,4},{1,3},{3,1},{5,7},{7,5},{8,10},{10,8},{12,... | collective-permute-start | bytes 1966088 | tf_op jit(solution)/shard_map/ppermute | solution.py:517
  102.7 27.7 %collective-permute-start.6 = (bf16[320,1024]{1,0:T(8,128)(2,1)S(1)}, bf16[320,1024]{1,0:T(8,128)(2,1)S(1)}, u32[]{:S(2)}, u32[]{:S(2)}) collective-permute-start(bf16[320,1024]{1,0:T(8,128)(2,1)S(1)} %collective-permute-done.5.kv2), channel_id=1, source_target_pairs={{0,2},{2,0},{4,6},{6,4},{1,3},{3,1},{5,7},{7,5},{8,10},{10,8},{12,... | collective-permute-start | bytes 1966088 | tf_op jit(solution)/shard_map/ppermute | solution.py:517
  128.1 14.2 %collective-permute-start.8 = (bf16[320,1024]{1,0:T(8,128)(2,1)S(1)}, bf16[320,1024]{1,0:T(8,128)(2,1)S(1)}, u32[]{:S(2)}, u32[]{:S(2)}) collective-permute-start(bf16[320,1024]{1,0:T(8,128)(2,1)S(1)} %collective-permute-done.3.kv2), channel_id=1, source_target_pairs={{0,2},{2,0},{4,6},{6,4},{1,3},{3,1},{5,7},{7,5},{8,10},{10,8},{12,... | collective-permute-start | bytes 1966088 | tf_op jit(solution)/shard_map/ppermute | solution.py:517
  128.1 23.7 %collective-permute-start.12 = (f32[1,512]{1,0:T(1,128)S(1)}, f32[1,512]{1,0:T(1,128)S(1)}, u32[]{:S(2)}, u32[]{:S(2)}) collective-permute-start(f32[1,512]{1,0:T(1,128)S(1)} %bitcast.63), channel_id=1, source_target_pairs={{0,1},{1,0},{2,3},{3,2},{4,5},{5,4},{6,7},{7,6},{8,9},{9,8},{10,11... | collective-permute-start | bytes 6152 | tf_op jit(solution)/shard_map/ppermute | solution.py:514
  129.8 22.0 %collective-permute-start.9 = (bf16[320,512]{1,0:T(8,128)(2,1)S(1)}, bf16[320,512]{1,0:T(8,128)(2,1)S(1)}, u32[]{:S(2)}, u32[]{:S(2)}) collective-permute-start(bf16[320,512]{1,0:T(8,128)(2,1)S(1)} %get-tuple-element.121.own_ref0.own_ref.o_ref), channel_id=1, source_target_pairs={{0,1},{1,0},{2,3},{3,2},{4,5},{5,4},{6,7},{7,6},{8,9},{9,8},{10,11... | collective-permute-start | bytes 983048 | tf_op jit(solution)/shard_map/ppermute | solution.py:514
  140.7 11.1 %collective-permute-start.10 = (bf16[320,512]{1,0:T(8,128)(2,1)S(1)}, bf16[320,512]{1,0:T(8,128)(2,1)S(1)}, u32[]{:S(2)}, u32[]{:S(2)}) collective-permute-start(bf16[320,512]{1,0:T(8,128)(2,1)S(1)} %get-tuple-element.124.own_ref1.own_ref.o_ref), channel_id=1, source_target_pairs={{0,1},{1,0},{2,3},{3,2},{4,5},{5,4},{6,7},{7,6},{8,9},{9,8},{10,11... | collective-permute-start | bytes 983048 | tf_op jit(solution)/shard_map/ppermute | solution.py:514
  151.1 9.3 %collective-permute-start.11 = (bf16[320,512]{1,0:T(8,128)(2,1)S(1)}, bf16[320,512]{1,0:T(8,128)(2,1)S(1)}, u32[]{:S(2)}, u32[]{:S(2)}) collective-permute-start(bf16[320,512]{1,0:T(8,128)(2,1)S(1)} %get-tuple-element.127.own_ref2.own_ref.o_ref), channel_id=1, source_target_pairs={{0,1},{1,0},{2,3},{3,2},{4,5},{5,4},{6,7},{7,6},{8,9},{9,8},{10,11... | collective-permute-start | bytes 983048 | tf_op jit(solution)/shard_map/ppermute | solution.py:514
  186.3 4.0 collective-permute-start.14
  203.7 48.2 %collective-permute-start.17 = (bf16[320,1024]{1,0:T(8,128)(2,1)}, bf16[320,1024]{1,0:T(8,128)(2,1)}, u32[]{:S(2)}, u32[]{:S(2)}) collective-permute-start(bf16[320,1024]{1,0:T(8,128)(2,1)} %get-tuple-element.139.dha_ref), channel_id=1, source_target_pairs={{0,1},{1,0},{2,3},{3,2},{4,5},{5,4},{6,7},{7,6},{8,9},{9,8},{10,11... | collective-permute-start | bytes 1966088 | tf_op jit(solution)/shard_map/ppermute | solution.py:514
  212.3 27.6 %collective-permute-start.15 = (bf16[320,1024]{1,0:T(8,128)(2,1)}, bf16[320,1024]{1,0:T(8,128)(2,1)}, u32[]{:S(2)}, u32[]{:S(2)}) collective-permute-start(bf16[320,1024]{1,0:T(8,128)(2,1)} %get-tuple-element.132.dha_ref), channel_id=1, source_target_pairs={{0,1},{1,0},{2,3},{3,2},{4,5},{5,4},{6,7},{7,6},{8,9},{9,8},{10,11... | collective-permute-start | bytes 1966088 | tf_op jit(solution)/shard_map/ppermute | solution.py:514
  221.9 30.0 %collective-permute-start.16 = (bf16[320,1024]{1,0:T(8,128)(2,1)}, bf16[320,1024]{1,0:T(8,128)(2,1)}, u32[]{:S(2)}, u32[]{:S(2)}) collective-permute-start(bf16[320,1024]{1,0:T(8,128)(2,1)} %get-tuple-element.138.dha_ref), channel_id=1, source_target_pairs={{0,1},{1,0},{2,3},{3,2},{4,5},{5,4},{6,7},{7,6},{8,9},{9,8},{10,11... | collective-permute-start | bytes 1966088 | tf_op jit(solution)/shard_map/ppermute | solution.py:514
  252.0 196.9 %reduce-scatter.5.cloned.1.call-start = ((), (), s32[]{:S(2)}) async-start(), calls=%async_computation.5 | async-start | bytes 4456448 | tf_op jit(solution)/shard_map/reduce_scatter | solution.py:840
  268.8 7.5 %collective-permute-start.18 = (bf16[2,320,1024]{2,1,0:T(8,128)(2,1)S(1)}, bf16[2,320,1024]{2,1,0:T(8,128)(2,1)S(1)}, u32[]{:S(2)}, u32[]{:S(2)}) collective-permute-start(bf16[2,320,1024]{2,1,0:T(8,128)(2,1)S(1)} %get-tuple-element.156), channel_id=1, source_target_pairs={{0,2},{2,0},{4,6},{6,4},{1,3},{3,1},{5,7},{7,5},{8,10},{10,8},{12,... | collective-permute-start | bytes 3932168 | tf_op jit(solution)/shard_map/ppermute | solution.py:517
  276.6 24.6 %collective-permute-start.19 = (bf16[320,1024]{1,0:T(8,128)(2,1)S(1)}, bf16[320,1024]{1,0:T(8,128)(2,1)S(1)}, u32[]{:S(2)}, u32[]{:S(2)}) collective-permute-start(bf16[320,1024]{1,0:T(8,128)(2,1)S(1)} %fusion), channel_id=1, source_target_pairs={{0,4},{2,6},{4,0},{6,2},{1,5},{3,7},{5,1},{7,3},{8,12},{10,14},{12... | collective-permute-start | bytes 1966088 | tf_op jit(solution)/shard_map/ppermute | solution.py:520
  288.9 26.2 %collective-permute-start.22 = (bf16[2,320,1024]{2,1,0:T(8,128)(2,1)S(1)}, bf16[2,320,1024]{2,1,0:T(8,128)(2,1)S(1)}, u32[]{:S(2)}, u32[]{:S(2)}) collective-permute-start(bf16[2,320,1024]{2,1,0:T(8,128)(2,1)S(1)} %get-tuple-element.171), channel_id=1, source_target_pairs={{0,2},{2,0},{4,6},{6,4},{1,3},{3,1},{5,7},{7,5},{8,10},{10,8},{12,... | collective-permute-start | bytes 3932168 | tf_op jit(solution)/shard_map/ppermute | solution.py:517
  311.4 4.9 %collective-permute-start.20 = (bf16[2,320,1024]{2,1,0:T(8,128)(2,1)S(1)}, bf16[2,320,1024]{2,1,0:T(8,128)(2,1)S(1)}, u32[]{:S(2)}, u32[]{:S(2)}) collective-permute-start(bf16[2,320,1024]{2,1,0:T(8,128)(2,1)S(1)} %get-tuple-element.169), channel_id=1, source_target_pairs={{0,2},{2,0},{4,6},{6,4},{1,3},{3,1},{5,7},{7,5},{8,10},{10,8},{12,... | collective-permute-start | bytes 3932168 | tf_op jit(solution)/shard_map/ppermute | solution.py:517
  311.4 33.8 %collective-permute-start.24 = (bf16[320,1024]{1,0:T(8,128)(2,1)S(1)}, bf16[320,1024]{1,0:T(8,128)(2,1)S(1)}, u32[]{:S(2)}, u32[]{:S(2)}) collective-permute-start(bf16[320,1024]{1,0:T(8,128)(2,1)S(1)} %copy-done.54), channel_id=1, source_target_pairs={{0,1},{1,0},{2,3},{3,2},{4,5},{5,4},{6,7},{7,6},{8,9},{9,8},{10,11... | collective-permute-start | bytes 1966088 | tf_op jit(solution)/shard_map/ppermute | solution.py:514
  313.0 33.0 %collective-permute-start.25 = (bf16[320,1024]{1,0:T(8,128)(2,1)S(1)}, bf16[320,1024]{1,0:T(8,128)(2,1)S(1)}, u32[]{:S(2)}, u32[]{:S(2)}) collective-permute-start(bf16[320,1024]{1,0:T(8,128)(2,1)S(1)} %get-tuple-element.174.da_ref), channel_id=1, source_target_pairs={{0,1},{1,0},{2,3},{3,2},{4,5},{5,4},{6,7},{7,6},{8,9},{9,8},{10,11... | collective-permute-start | bytes 1966088 | tf_op jit(solution)/shard_map/ppermute | solution.py:514
  315.3 27.5 %collective-permute-start.23 = (bf16[320,1024]{1,0:T(8,128)(2,1)S(1)}, bf16[320,1024]{1,0:T(8,128)(2,1)S(1)}, u32[]{:S(2)}, u32[]{:S(2)}) collective-permute-start(bf16[320,1024]{1,0:T(8,128)(2,1)S(1)} %fusion.2), channel_id=1, source_target_pairs={{0,4},{2,6},{4,0},{6,2},{1,5},{3,7},{5,1},{7,3},{8,12},{10,14},{12... | collective-permute-start | bytes 1966088 | tf_op jit(solution)/shard_map/ppermute | solution.py:520
  316.5 44.3 %collective-permute-start.21 = (bf16[320,1024]{1,0:T(8,128)(2,1)S(1)}, bf16[320,1024]{1,0:T(8,128)(2,1)S(1)}, u32[]{:S(2)}, u32[]{:S(2)}) collective-permute-start(bf16[320,1024]{1,0:T(8,128)(2,1)S(1)} %fusion.1), channel_id=1, source_target_pairs={{0,4},{2,6},{4,0},{6,2},{1,5},{3,7},{5,1},{7,3},{8,12},{10,14},{12... | collective-permute-start | bytes 1966088 | tf_op jit(solution)/shard_map/ppermute | solution.py:520
  373.3 17.9 %collective-permute-start.27 = (bf16[320,1024]{1,0:T(8,128)(2,1)}, bf16[320,1024]{1,0:T(8,128)(2,1)S(1)}, u32[]{:S(2)}, u32[]{:S(2)}) collective-permute-start(bf16[320,1024]{1,0:T(8,128)(2,1)} %copy-done.62), channel_id=1, source_target_pairs={{0,1},{1,0},{2,3},{3,2},{4,5},{5,4},{6,7},{7,6},{8,9},{9,8},{10,11... | collective-permute-start | bytes 1966088 | tf_op jit(solution)/shard_map/ppermute | solution.py:514
  374.9 30.3 %collective-permute-start.26 = (bf16[320,1024]{1,0:T(8,128)(2,1)}, bf16[320,1024]{1,0:T(8,128)(2,1)S(1)}, u32[]{:S(2)}, u32[]{:S(2)}) collective-permute-start(bf16[320,1024]{1,0:T(8,128)(2,1)} %copy-done.64), channel_id=1, source_target_pairs={{0,1},{1,0},{2,3},{3,2},{4,5},{5,4},{6,7},{7,6},{8,9},{9,8},{10,11... | collective-permute-start | bytes 1966088 | tf_op jit(solution)/shard_map/ppermute | solution.py:514
  375.4 15.8 %collective-permute-start.39 = (bf16[64,4224]{1,0:T(8,128)(2,1)}, bf16[64,4224]{1,0:T(8,128)(2,1)}, u32[]{:S(2)}, u32[]{:S(2)}) collective-permute-start(bf16[64,4224]{1,0:T(8,128)(2,1)} %reduce-scatter.3.cloned.1.call-done), channel_id=1, source_target_pairs={{0,4},{2,6},{4,0},{6,2},{1,5},{3,7},{5,1},{7,3},{8,12},{10,14},{12... | collective-permute-start | bytes 1622024 | tf_op jit(solution)/shard_map/ppermute | solution.py:520
  376.0 60.8 %collective-permute-start.29 = (bf16[320,1024]{1,0:T(8,128)(2,1)}, bf16[320,1024]{1,0:T(8,128)(2,1)}, u32[]{:S(2)}, u32[]{:S(2)}) collective-permute-start(bf16[320,1024]{1,0:T(8,128)(2,1)} %get-tuple-element.194.pa_ref), channel_id=1, source_target_pairs={{0,1},{1,0},{2,3},{3,2},{4,5},{5,4},{6,7},{7,6},{8,9},{9,8},{10,11... | collective-permute-start | bytes 1966088 | tf_op jit(solution)/shard_map/ppermute | solution.py:514
  377.5 61.6 %collective-permute-start.28 = (bf16[320,1024]{1,0:T(8,128)(2,1)S(1)}, bf16[320,1024]{1,0:T(8,128)(2,1)}, u32[]{:S(2)}, u32[]{:S(2)}) collective-permute-start(bf16[320,1024]{1,0:T(8,128)(2,1)S(1)} %copy-done.44), channel_id=1, source_target_pairs={{0,1},{1,0},{2,3},{3,2},{4,5},{5,4},{6,7},{7,6},{8,9},{9,8},{10,11... | collective-permute-start | bytes 1966088 | tf_op jit(solution)/shard_map/ppermute | solution.py:514
  391.2 50.7 %collective-permute-start.38 = (bf16[64,4224]{1,0:T(8,128)(2,1)}, bf16[64,4224]{1,0:T(8,128)(2,1)}, u32[]{:S(2)}, u32[]{:S(2)}) collective-permute-start(bf16[64,4224]{1,0:T(8,128)(2,1)} %reduce-scatter.3.cloned.1.call-done), channel_id=1, source_target_pairs={{0,2},{2,0},{4,6},{6,4},{1,3},{3,1},{5,7},{7,5},{8,10},{10,8},{12,... | collective-permute-start | bytes 1622024 | tf_op jit(solution)/shard_map/ppermute | solution.py:517
  391.2 50.7 %collective-permute-start.40 = (bf16[64,4224]{1,0:T(8,128)(2,1)}, bf16[64,4224]{1,0:T(8,128)(2,1)}, u32[]{:S(2)}, u32[]{:S(2)}) collective-permute-start(bf16[64,4224]{1,0:T(8,128)(2,1)} %collective-permute-done.39), channel_id=1, source_target_pairs={{0,2},{2,0},{4,6},{6,4},{1,3},{3,1},{5,7},{7,5},{8,10},{10,8},{12,... | collective-permute-start | bytes 1622024 | tf_op jit(solution)/shard_map/ppermute | solution.py:517
  405.2 1.9 collective-permute-start.34
  407.2 1.4 collective-permute-start.30
  408.6 3.9 collective-permute-start.35
  412.5 3.7 collective-permute-start.31
  416.1 3.9 collective-permute-start.36
  420.0 4.0 collective-permute-start.32
  424.1 5.5 %collective-permute-start.37 = (f32[2944]{0:T(1024)S(1)}, f32[2944]{0:T(1024)S(1)}, u32[]{:S(2)}, u32[]{:S(2)}) collective-permute-start(f32[2944]{0:T(1024)S(1)} %add.135), channel_id=1, source_target_pairs={{0,16},{8,24},{16,0},{24,8},{1,17},{9,25},{17,1},{25,9},{2,18},{10... | collective-permute-start | bytes 35336 | tf_op jit(solution)/shard_map/ppermute | solution.py:858
  429.6 11.7 %collective-permute-start.33 = (f32[1024]{0:T(1024)S(1)}, f32[1024]{0:T(1024)S(1)}, u32[]{:S(2)}, u32[]{:S(2)}) collective-permute-start(f32[1024]{0:T(1024)S(1)} %add.125), channel_id=1, source_target_pairs={{0,16},{8,24},{16,0},{24,8},{1,17},{9,25},{17,1},{25,9},{2,18},{10... | collective-permute-start | bytes 12296 | tf_op jit(solution)/shard_map/ppermute | solution.py:858
  449.7 10.8 %collective-permute-start.42 = (bf16[64,512]{1,0:T(8,128)(2,1)S(1)}, bf16[64,512]{1,0:T(8,128)(2,1)S(1)}, u32[]{:S(2)}, u32[]{:S(2)}) collective-permute-start(bf16[64,512]{1,0:T(8,128)(2,1)S(1)} %slice.92), channel_id=1, source_target_pairs={{0,4},{2,6},{4,0},{6,2},{1,5},{3,7},{5,1},{7,3},{8,12},{10,14},{12... | collective-permute-start | bytes 196616 | tf_op jit(solution)/shard_map/ppermute | solution.py:520
  450.4 11.8 %collective-permute-start.41 = (bf16[64,512]{1,0:T(8,128)(2,1)S(1)}, bf16[64,512]{1,0:T(8,128)(2,1)S(1)}, u32[]{:S(2)}, u32[]{:S(2)}) collective-permute-start(bf16[64,512]{1,0:T(8,128)(2,1)S(1)} %slice.92), channel_id=1, source_target_pairs={{0,2},{2,0},{4,6},{6,4},{1,3},{3,1},{5,7},{7,5},{8,10},{10,8},{12,... | collective-permute-start | bytes 196616 | tf_op jit(solution)/shard_map/ppermute | solution.py:517
  460.5 1.7 collective-permute-start.43
  (85 other events, 838.8 us)
Sparse Core Ops, SparseCore 0:
  10.8 47.9 all-gather.2
  61.6 103.3 all-gather.4
  252.1 121.1 reduce-scatter.2
  377.0 71.8 reduce-scatter.4

commit v4 on v3

--- a/solution.py
+++ b/solution.py
@@ -6,7 +6,7 @@
 from jax import lax
 from jax.experimental import pallas as pl
 from jax.experimental.pallas import tpu as pltpu
-from jax.sharding import PartitionSpec as P
+from jax.sharding import Mesh, PartitionSpec as P
 
 HEAD = 64
 GRID = 32
@@ -409,9 +409,11 @@
                 down_ref[at : at + size, :] = flipped
 
 
-def grads_kernel(n_ref, *refs, plan):
-    out_ref, flip_s, out_s, sem = refs[-4:]
-    refs = list(refs[:-4])
+def grads_kernel(n_ref, *refs, plan, split=None):
+    outs = 1 if split is None else 2
+    refs = list(refs)
+    *out_refs, flip_s, out_s, sem = refs[-outs - 3 :]
+    refs = refs[: -outs - 3]
 
     def take(count):
         mine = refs[:count]
@@ -443,14 +445,29 @@
                     flipped, joined(mine, slice(at, at + size))
                 ).astype(BF)
             column += span
-        copies.append(
-            pltpu.make_async_copy(
-                out_s.at[:, pl.ds(start, column - start)],
-                out_ref.at[:, pl.ds(start, column - start)],
-                sem.at[group],
+        if split is None:
+            copies.append(
+                pltpu.make_async_copy(
+                    out_s.at[:, pl.ds(start, column - start)],
+                    out_refs[0].at[:, pl.ds(start, column - start)],
+                    sem.at[group],
+                )
             )
-        )
-        copies[-1].start()
+            copies[-1].start()
+    if split is not None:
+        shards, part = split
+        low = n_ref[n_ref.shape[0] - 1]
+        for block in range(2 * shards):
+            for slot, parity in enumerate((1 - low, low)):
+                row = pl.multiple_of((2 * block + parity) * part, part)
+                copies.append(
+                    pltpu.make_async_copy(
+                        out_s.at[pl.ds(row, part), :],
+                        out_refs[slot].at[pl.ds(block * part, part), :],
+                        sem.at[2 * block + slot],
+                    )
+                )
+                copies[-1].start()
     for copy in copies:
         copy.wait()
 
@@ -500,24 +517,24 @@
     ff = ffn_gain.shape[0]
     ffp = -(-ff // LANES) * LANES
     pad = ffp - ff
-    ctx_size = lax.axis_size("ctx")
     tp_size = lax.axis_size("tp")
-    ctx = lax.axis_index("ctx")
+    pairs_of = ("far", "near")
+    ctx_size = lax.axis_size(pairs_of)
+    ctx = lax.axis_index(pairs_of)
     tp = lax.axis_index("tp")
     ff_total = ff * tp_size
-    both = ("shard", "ctx")
+    both = ("shard", *pairs_of)
     swap_tp = pair_perm(tp_size, 1)
-    swap_near = pair_perm(ctx_size, 1)
-    swap_far = pair_perm(ctx_size, 2)
+    swap_pair = pair_perm(2, 1)
 
     def swap(value):
         return lax.ppermute(value, "tp", swap_tp)
 
     def near(value):
-        return lax.ppermute(value, "ctx", swap_near)
+        return lax.ppermute(value, "near", swap_pair)
 
     def far(value):
-        return lax.ppermute(value, "ctx", swap_far)
+        return lax.ppermute(value, "far", swap_pair)
 
     def ordered(own, axis):
         other = swap(own)
@@ -578,7 +595,7 @@
             [image_of(i, rows, width), line, qkv_spec, rope_spec],
             [act, act_half, whole(rows, 2 * half)],
             name="qkv",
-            mib=24,
+            mib=14,
             flops=2 * rows * width * 3 * half,
             moved=6 * width * half + 8 * block_mb,
         )(tokens, ln1, full_qkv, tables)
@@ -602,7 +619,7 @@
                 pltpu.VMEM((LANES, 2 * rows), F32),
             ],
             name="attend",
-            mib=20,
+            mib=8,
             grid=half // LANES,
             flops=16 * rows * 4 * rows * half,
             moved=12 * block_mb,
@@ -640,7 +657,7 @@
             pltpu.SemaphoreType.DMA((4,)),
         ],
         name="middle",
-        mib=48,
+        mib=36,
         grid=images,
         flops=2 * images * rows * width * (width + 3 * ffp),
         moved=2 * width * (width + 3 * ffp) + images * (12 * block_mb + 6 * rows * ffp),
@@ -668,30 +685,30 @@
                 pltpu.SemaphoreType.DMA((3,)),
             ],
             name="ffn",
-            mib=36,
+            mib=26,
             flops=2 * rows * width * 3 * ffp,
             moved=6 * width * ffp + 12 * rows * ffp + 4 * block_mb,
         )(stats, stats_x, gate, up, dm, fgain, rest)
         s["dh2x"] = swap(s["dh2"])
-    def weight_grads(groups, tag):
+    def weight_grads(groups, tag, split=None):
         plan = [(masked, len(left), [len(right) for right in rights]) for masked, left, rights in groups]
         flat = [v for _, left, rights in groups for v in left + [w for right in rights for w in right]]
         columns = sum(right[0].shape[-1] for _, _, rights in groups for right in rights)
         return call(
-            functools.partial(grads_kernel, plan=plan),
-            shape(width, columns),
+            functools.partial(grads_kernel, plan=plan, split=split),
+            shape(width, columns) if split is None else (shape(width // 2, columns),) * 2,
             [SMEM] + [whole(*v.shape) for v in flat],
-            ANY,
+            ANY if split is None else (ANY, ANY),
             [
                 pltpu.VMEM((width, images * rows), BF),
                 pltpu.VMEM((width, columns), BF),
-                pltpu.SemaphoreType.DMA((len(groups),)),
+                pltpu.SemaphoreType.DMA((len(groups) if split is None else 4 * split[0],)),
             ],
             name=tag,
             flops=2 * images * rows * width * columns,
             moved=4 * width * columns,
-            mib=50 if columns > 2 * width else 36,
-        )(counts[:, 0], *flat)
+            mib=40 if columns > 2 * width else 26,
+        )(jnp.concatenate([counts[:, 0], (ctx % 2).astype(jnp.int32)[None]]), *flat)
 
     def of(key):
         return [s[key] for s in st]
@@ -720,7 +737,7 @@
                 pltpu.SemaphoreType.DMA((1,)),
             ],
             name="attn_norm_back",
-            mib=28,
+            mib=18,
             flops=2 * rows * width * width,
             moved=2 * width * width + 16 * block_mb,
         )(s["sc"], s["dh2"], s["dh2x"], x1, cotangent, ln2, s["o"], s["ox"], again, rest)
@@ -735,7 +752,7 @@
             [pltpu.VMEM((LANES, 2 * rows), F32)],
             grid=half // LANES,
             name="attend_back",
-            mib=20,
+            mib=12,
             flops=40 * rows * 4 * rows * half,
             moved=20 * block_mb,
         )(s["n"], s["q"], s["kv"], s["kvc"], s["kvf"], s["kvx"], s["o"], s["do"], s["lse"], tables)
@@ -757,7 +774,7 @@
             ],
             [whole(rows, 2 * half), act],
             name="qkv_back",
-            mib=24,
+            mib=14,
             flops=2 * rows * width * 3 * half,
             moved=6 * width * half + 10 * block_mb,
         )(s["keep"], s["recv"], s["far"], s["dq"], tables, full_qkv)
@@ -833,11 +850,12 @@
         held = [own, near(own), beyond, near(beyond)]
         return jnp.concatenate([lax.select_n(ctx ^ at, *held) for at in range(4)], axis=0)
 
-    grads_qkv = weight_grads(
-        [(False, of("h1"), [of("dq"), of("dkv")]), (False, of("dab"), [[attn_in]])], "grads_qkv"
-    )
-    grads_qkv, own_ffn = lax.optimization_barrier((grads_qkv, own_ffn))
-    own_qkv = lax.psum_scatter(grads_qkv, both, scatter_dimension=0, tiled=True)
+    send, keep = weight_grads(
+        [(False, of("h1"), [of("dq"), of("dkv")]), (False, of("dab"), [[attn_in]])], "grads_qkv", split=(shards, part)
+    )
+    grads_qkv = (keep.astype(F32) + near(send).astype(F32)).astype(BF)
+    grads_qkv, own_ffn = tie(grads_qkv, own_ffn)
+    own_qkv = lax.psum_scatter(grads_qkv, ("shard", "far"), scatter_dimension=0, tiled=True)
     grad_pairs, grad_down = call(
         finish_kernel,
         (shape(ff, 2, depth, dtype=F32), shape(ff, depth, dtype=F32)),
@@ -849,10 +867,8 @@
     )(around(own_ffn))
 
     def everywhere(value):
-        step = 1
-        while step < ctx_size:
-            value = value + lax.ppermute(value, "ctx", pair_perm(ctx_size, step))
-            step *= 2
+        value = value + near(value)
+        value = value + far(value)
         step = 1
         while step < shards:
             value = value + lax.ppermute(value, "shard", pair_perm(shards, step))
@@ -871,7 +887,7 @@
         own_qkv, grad_tokens, mixed, gain_ln1, gain_ffn, grad_pairs, grad_down
     )
     grad_pairs = jnp.transpose(grad_pairs, (1, 2, 0))
-    sum_qkv = lax.all_gather(own_qkv[:, : 3 * half], "ctx", axis=0, tiled=True).astype(F32)
+    sum_qkv = lax.all_gather(own_qkv[:, : 3 * half], pairs_of, axis=0, tiled=True).astype(F32)
     grad_proj = around(own_qkv[:, 3 * half :]).astype(F32).T
     grad_qkv = jnp.stack([sum_qkv[:, j * half : (j + 1) * half] for j in range(3)])
 
@@ -890,7 +906,11 @@
 
 
 def solution(mesh):
-    tokens = P("shard", "ctx", None)
+    size = dict(mesh.shape)
+    mesh = Mesh(
+        mesh.devices.reshape(size["shard"], size["ctx"] // 2, 2, size["tp"]), ("shard", "far", "near", "tp")
+    )
+    tokens = P("shard", ("far", "near"), None)
     matrix = P(None, "shard", "tp")
     flipped = P("tp", "shard")
     return jax.shard_map(

time: 480 us -> 470 us (0.979)
  waiting for transfers between devices: 181 us -> 165 us
  Pallas kernels: 169 us -> 176 us
  local copies, waits for them, and re-layouts: 56.1 us -> 50.4 us
    ppermute x25 -> x26, waiting for transfers between devices: 93.5 us -> 82.5 us  [the longest x10 77.5 us: far(): return lax.ppermute(value, 'far', swap_pair)]
    ppermute x25 -> x26, starting transfers between devices: 10.5 us -> 16.3 us  [the longest x10 14.1 us: far(): return lax.ppermute(value, 'far', swap_pair)]
    pallas_call x3, Pallas kernels: 36.6 us -> 42.3 us  [attention_back(): call(attend_back_kernel, (shape(rows, half), shape(2, rows, 2 * half), sh...]
    unnamed x177 -> x155, local copies, waits for them, and re-layouts: 45.8 us -> 40.1 us
    pallas_call x3, Pallas kernels: 29.8 us -> 35.3 us  [local(): call(attend_kernel, (shape(rows, half), shape(half // LANES, 1, 2 * rows,...]
  transfers between devices with their start and end apart: 48 -> 49, of which waited for: 20 -> 21; matrix products, arithmetic and copies ran while one was open for 4% -> 5% of each run, Pallas kernels for 30% -> 32%
where the time goes in v4:
time: 470 us; the launch traced here: 461 us
  Pallas kernels  176 us (37%)
  waiting for transfers between devices  165 us (35%)
  local copies, waits for them, and re-layouts  50.4 us (11%)
  starting transfers between devices  35.5 us (8%)
  between operations  14.9 us (3%)
  other arithmetic  11.4 us (2%)
  blocking collectives  8.88 us (2%)
    ppermute x10, waiting for transfers between devices, far(): return lax.ppermute(value, 'far', swap_pair)  77.5 us
    pallas_call x3, Pallas kernels, attention_back(): call(attend_back_kernel, (shape(rows, half), shape(2, rows, 2 * half), sh...  42.3 us
    unnamed x155, local copies, waits for them, and re-layouts  40.1 us
    all_gather x1, waiting for transfers between devices, local(): full_qkv = lax.all_gather(qkv_part, both, axis=1, tiled=True)  37 us
    pallas_call x3, Pallas kernels, local(): call(attend_kernel, (shape(rows, half), shape(half // LANES, 1, 2 * rows,...  35.3 us
    ppermute x15, waiting for transfers between devices, swap(): return lax.ppermute(value, 'tp', swap_tp)  32.6 us
    pallas_call x1, Pallas kernels, local(): call(middle_kernel, (shape(images, rows, width, dtype=F32), shape(images,...  20 us
    pallas_call x3, Pallas kernels, local(): call(functools.partial(ffn_kernel, total=ff_total), (shape(rows, ffp), sh...  18.7 us
  transfers between devices with their start and end apart: 49, of which 21 were waited for; matrix products, arithmetic and copies ran while one was open for 5% of the time, Pallas kernels for 32%

profile of v4, /device:TPU:0, one launch (start us, length us, event | category | flops | bytes accessed | tf_op | source)
XLA Modules:
  0.0 461.5 jit_solution(314567905390063851)
XLA Ops:
  10.2 3.0 collective-permute-start.13
  14.4 1.9 constant_dynamic-slice_fusion.1
  21.8 37.0 %all-gather.3.cloned.1.call-done.w_ref = bf16[3,1024,512]{2,1,0:T(8,128)(2,1)} async-done(((bf16[3,64,512]{2,1,0:T(8,128)(2,1)}), bf16[3,1024,512]{2,1,0:T(8,128)(2,1)}) %all-gather.3.cloned.1.call-update) | async-done | bytes 3145744 | tf_op jit(solution)/shard_map/all_gather | solution.py:549
  63.8 2.5 qkv.4
  69.3 18.6 %collective-permute-done.1.kv2 = bf16[320,1024]{1,0:T(8,128)(2,1)S(1)} collective-permute-done((bf16[320,1024]{1,0:T(8,128)(2,1)S(1)}, bf16[320,1024]{1,0:T(8,128)(2,1)S(1)}, u32[]{:S(2)}, u32[]{:S(2)}) %collective-permute-start.1) | collective-permute-done | bytes 655392 | tf_op jit(solution)/shard_map/ppermute | solution.py:537
  88.0 2.5 qkv.5
  93.2 8.8 %collective-permute-done.5.kv2 = bf16[320,1024]{1,0:T(8,128)(2,1)S(1)} collective-permute-done((bf16[320,1024]{1,0:T(8,128)(2,1)}, bf16[320,1024]{1,0:T(8,128)(2,1)S(1)}, u32[]{:S(2)}, u32[]{:S(2)}) %collective-permute-start.5) | collective-permute-done | bytes 655392 | tf_op jit(solution)/shard_map/ppermute | solution.py:537
  102.9 12.7 %attend.3 = (bf16[320,512]{1,0:T(8,128)(2,1)S(1)}, f32[4,1,640]{2,1,0:T(1,128)S(1)}) custom-call(s32[4]{0:T(128)S(1)} %get-tuple-element.268.n_ref, bf16[320,512]{1,0:T(8,128)(2,1)} %copy-done.21, bf16[320,1024]{1,0:T(8,128)(2,1)} %copy-done.12, bf16[320,1024]{1,0:T(8,128)(2,1)} %copy-done.66, bf16[320,1024]{1,0:T(8,128)(2,1)} %copy-done.65, ...), custom_call_target="tpu_custom_call" | custom-call | flops 209715200 | bytes 245760 | tf_op jit(solution)/shard_map/attend/pallas_call | solution.py:611
  115.6 11.3 %collective-permute-done.3.kv2 = bf16[320,1024]{1,0:T(8,128)(2,1)} collective-permute-done((bf16[320,1024]{1,0:T(8,128)(2,1)}, bf16[320,1024]{1,0:T(8,128)(2,1)}, u32[]{:S(2)}, u32[]{:S(2)}) %collective-permute-start.3) | collective-permute-done | bytes 655392 | tf_op jit(solution)/shard_map/ppermute | solution.py:537
  129.1 10.4 %attend.4 = (bf16[320,512]{1,0:T(8,128)(2,1)S(1)}, f32[4,1,640]{2,1,0:T(1,128)S(1)}) custom-call(s32[4]{0:T(128)S(1)} %get-tuple-element.267.n_ref, bf16[320,512]{1,0:T(8,128)(2,1)} %copy-done.20, bf16[320,1024]{1,0:T(8,128)(2,1)} %get-tuple-element.125.kv0, bf16[320,1024]{1,0:T(8,128)(2,1)} %collective-permute-done.4.kv1, bf16[320,1024]{1,0:T(8,128)(2,1)} %copy-done.64, ...), custom_call_target="tpu_custom_call" | custom-call | flops 209715200 | bytes 245760 | tf_op jit(solution)/shard_map/attend/pallas_call | solution.py:611
  141.1 12.2 %attend.5 = (bf16[320,512]{1,0:T(8,128)(2,1)S(1)}, f32[4,1,640]{2,1,0:T(1,128)S(1)}) custom-call(s32[4]{0:T(128)S(1)} %get-tuple-element.266.n_ref, bf16[320,512]{1,0:T(8,128)(2,1)} %copy-done.19, bf16[320,1024]{1,0:T(8,128)(2,1)} %get-tuple-element.121.kv0, bf16[320,1024]{1,0:T(8,128)(2,1)} %collective-permute-done.7.kv1, ...), custom_call_target="tpu_custom_call" | custom-call | flops 209715200 | bytes 245760 | tf_op jit(solution)/shard_map/attend/pallas_call | solution.py:611
  155.4 7.2 %collective-permute-done.11.other_ref2.other_ref = bf16[320,512]{1,0:T(8,128)(2,1)S(1)} collective-permute-done((bf16[320,512]{1,0:T(8,128)(2,1)S(1)}, bf16[320,512]{1,0:T(8,128)(2,1)S(1)}, u32[]{:S(2)}, u32[]{:S(2)}) %collective-permute-start.11) | collective-permute-done | bytes 327712 | tf_op jit(solution)/shard_map/ppermute | solution.py:531
  168.8 20.0 %middle.1 = (f32[3,320,1024]{2,1,0:T(8,128)}, bf16[3,320,1024]{2,1,0:T(8,128)(2,1)S(1)}, bf16[3,320,1408]{2,1,0:T(8,128)(2,1)S(1)}, bf16[3,320,1408]{2,1,0:T(8,1...) custom-call(s32[4]{0:T(128)S(1)} %get-tuple-element.269.sc_ref, ...), custom_call_target="tpu_custom_call" | custom-call | flops 644874240 | bytes 1915904 | tf_op jit(solution)/shard_map/middle/pallas_call | solution.py:633
  190.2 2.6 collective-permute-done.14.sb_ref
  192.8 6.2 %ffn.5 = (bf16[320,1408]{1,0:T(8,128)(2,1)S(1)}, bf16[320,1408]{1,0:T(8,128)(2,1)S(1)}, bf16[320,1408]{1,0:T(8,128)(2,1)S(1)}, bf16[320,1024]{1,0:T(8,128)(2,1)S...) custom-call(f32[3,8,384]{2,1,0:T(8,128)S(1)} %get-tuple-element.130.sa_ref, ...), custom_call_target="tpu_custom_call" | custom-call | flops 173015040 | bytes 960512 | tf_op jit(solution)/shard_map/ffn/pallas_call | solution.py:668
  200.4 6.2 %ffn.3 = (bf16[320,1408]{1,0:T(8,128)(2,1)S(1)}, bf16[320,1408]{1,0:T(8,128)(2,1)S(1)}, bf16[320,1408]{1,0:T(8,128)(2,1)S(1)}, bf16[320,1024]{1,0:T(8,128)(2,1)S...) custom-call(f32[3,8,384]{2,1,0:T(8,128)S(1)} %get-tuple-element.130.sa_ref, ...), custom_call_target="tpu_custom_call" | custom-call | flops 173015040 | bytes 960512 | tf_op jit(solution)/shard_map/ffn/pallas_call | solution.py:668
  208.1 6.4 %ffn.4 = (bf16[320,1408]{1,0:T(8,128)(2,1)S(1)}, bf16[320,1408]{1,0:T(8,128)(2,1)S(1)}, bf16[320,1408]{1,0:T(8,128)(2,1)S(1)}, bf16[320,1024]{1,0:T(8,128)(2,1)S...) custom-call(f32[3,8,384]{2,1,0:T(8,128)S(1)} %get-tuple-element.130.sa_ref, ...), custom_call_target="tpu_custom_call" | custom-call | flops 173015040 | bytes 960512 | tf_op jit(solution)/shard_map/ffn/pallas_call | solution.py:668
  220.0 12.1 %grads_ffn.1 = bf16[1024,4224]{1,0:T(8,128)(2,1)} custom-call(s32[4]{0:T(128)S(1)} %get-tuple-element.270.n_ref, bf16[3,320,1024]{2,1,0:T(8,128)(2,1)S(1)} %get-tuple-element.142.refs_0_, bf16[320,1408]{1,0:T(8,128)(2,1)S(1)} %get-tuple-element.143.refs_1_, bf16[320,1408]{1,0:T(8,128)(2,1)S(1)} %get-tuple-element.144.refs_2_, ...), custom_call_target="tpu_custom_call" | custom-call | flops 519045120 | bytes 1081344 | tf_op jit(solution)/shard_map/grads_ffn/pallas_call | solution.py:697
  232.2 2.1 copy-done.2
  236.8 5.4 %attn_norm_back.3 = (f32[320,1024]{1,0:T(8,128)S(1)}, bf16[320,1024]{1,0:T(8,128)(2,1)S(1)}, bf16[320,512]{1,0:T(8,128)(2,1)S(1)}, f32[1,1024]{1,0:T(1,128)S(1)}, f32[1,512]{1,0:T(1,128)S(1)}) custom-call(s32[2]{0:T(128)S(1)} %pad_add_fusion.1.sc_ref, bf16[320,1024]{1,0:T(8,128)(2,1)} %get-tuple-element.134.dha_ref, ...), custom_call_target="tpu_custom_call" | custom-call | flops 41943040 | bytes 458752 | tf_op jit(solution)/shard_map/attn_norm_back/pallas_call | solution.py:721
  245.9 14.8 %attend_back.3 = (bf16[320,512]{1,0:T(8,128)(2,1)S(1)}, bf16[2,320,1024]{2,1,0:T(8,128)(2,1)S(1)}, bf16[2,320,1024]{2,1,0:T(8,128)(2,1)S(1)}) custom-call(s32[4]{0:T(128)S(1)} %get-tuple-element.268.n_ref, bf16[320,512]{1,0:T(8,128)(2,1)} %copy-done.21, bf16[320,1024]{1,0:T(8,128)(2,1)} %copy-done.12, bf16[320,1024]{1,0:T(8,128)(2,1)} %copy-done.66, ...), custom_call_target="tpu_custom_call" | custom-call | flops 524288000 | bytes 409600 | tf_op jit(solution)/shard_map/attend_back/pallas_call | solution.py:747
  264.3 5.5 %attn_norm_back.4 = (f32[320,1024]{1,0:T(8,128)S(1)}, bf16[320,1024]{1,0:T(8,128)(2,1)S(1)}, bf16[320,512]{1,0:T(8,128)(2,1)S(1)}, f32[1,1024]{1,0:T(1,128)S(1)}, f32[1,512]{1,0:T(1,128)S(1)}) custom-call(s32[2]{0:T(128)S(1)} %pad_add_fusion.3.sc_ref, bf16[320,1024]{1,0:T(8,128)(2,1)} %get-tuple-element.140.dha_ref, ...), custom_call_target="tpu_custom_call" | custom-call | flops 41943040 | bytes 458752 | tf_op jit(solution)/shard_map/attn_norm_back/pallas_call | solution.py:721
  270.6 12.8 %attend_back.4 = (bf16[320,512]{1,0:T(8,128)(2,1)S(1)}, bf16[2,320,1024]{2,1,0:T(8,128)(2,1)S(1)}, bf16[2,320,1024]{2,1,0:T(8,128)(2,1)S(1)}) custom-call(s32[4]{0:T(128)S(1)} %get-tuple-element.267.n_ref, bf16[320,512]{1,0:T(8,128)(2,1)} %copy-done.20, bf16[320,1024]{1,0:T(8,128)(2,1)} %get-tuple-element.125.kv0, ...), custom_call_target="tpu_custom_call" | custom-call | flops 524288000 | bytes 409600 | tf_op jit(solution)/shard_map/attend_back/pallas_call | solution.py:747
  284.6 5.4 %attn_norm_back.5 = (f32[320,1024]{1,0:T(8,128)S(1)}, bf16[320,1024]{1,0:T(8,128)(2,1)S(1)}, bf16[320,512]{1,0:T(8,128)(2,1)S(1)}, f32[1,1024]{1,0:T(1,128)S(1)}, f32[1,512]{1,0:T(1,128)S(1)}) custom-call(s32[2]{0:T(128)S(1)} %pad_add_fusion.4.sc_ref, bf16[320,1024]{1,0:T(8,128)(2,1)} %get-tuple-element.141.dha_ref, ...), custom_call_target="tpu_custom_call" | custom-call | flops 41943040 | bytes 458752 | tf_op jit(solution)/shard_map/attn_norm_back/pallas_call | solution.py:721
  290.0 6.8 %collective-permute-done.19.far_ref = bf16[320,1024]{1,0:T(8,128)(2,1)S(1)} collective-permute-done((bf16[320,1024]{1,0:T(8,128)(2,1)S(1)}, bf16[320,1024]{1,0:T(8,128)(2,1)S(1)}, u32[]{:S(2)}, u32[]{:S(2)}) %collective-permute-start.19) | collective-permute-done | bytes 655392 | tf_op jit(solution)/shard_map/ppermute | solution.py:537
  296.8 14.6 %attend_back.5 = (bf16[320,512]{1,0:T(8,128)(2,1)S(1)}, bf16[2,320,1024]{2,1,0:T(8,128)(2,1)S(1)}, bf16[2,320,1024]{2,1,0:T(8,128)(2,1)S(1)}) custom-call(s32[4]{0:T(128)S(1)} %get-tuple-element.266.n_ref, bf16[320,512]{1,0:T(8,128)(2,1)} %copy-done.19, bf16[320,1024]{1,0:T(8,128)(2,1)} %get-tuple-element.121.kv0, ...), custom_call_target="tpu_custom_call" | custom-call | flops 524288000 | bytes 409600 | tf_op jit(solution)/shard_map/attend_back/pallas_call | solution.py:747
  313.1 2.1 collective-permute-start.25
  317.9 17.1 %collective-permute-done.23.far_ref = bf16[320,1024]{1,0:T(8,128)(2,1)S(1)} collective-permute-done((bf16[320,1024]{1,0:T(8,128)(2,1)S(1)}, bf16[320,1024]{1,0:T(8,128)(2,1)S(1)}, u32[]{:S(2)}, u32[]{:S(2)}) %collective-permute-start.23) | collective-permute-done | bytes 655392 | tf_op jit(solution)/shard_map/ppermute | solution.py:537
  337.3 5.5 %collective-permute-done.25.db_ref = bf16[320,1024]{1,0:T(8,128)(2,1)S(1)} collective-permute-done((bf16[320,1024]{1,0:T(8,128)(2,1)S(1)}, bf16[320,1024]{1,0:T(8,128)(2,1)S(1)}, u32[]{:S(2)}, u32[]{:S(2)}) %collective-permute-start.25) | collective-permute-done | bytes 655392 | tf_op jit(solution)/shard_map/ppermute | solution.py:531
  343.6 9.8 %collective-permute-done.21.far_ref = bf16[320,1024]{1,0:T(8,128)(2,1)S(1)} collective-permute-done((bf16[320,1024]{1,0:T(8,128)(2,1)S(1)}, bf16[320,1024]{1,0:T(8,128)(2,1)S(1)}, u32[]{:S(2)}, u32[]{:S(2)}) %collective-permute-start.21) | collective-permute-done | bytes 655392 | tf_op jit(solution)/shard_map/ppermute | solution.py:537
  355.7 5.8 %grads_qkv.1 = (bf16[512,2048]{1,0:T(8,128)(2,1)S(1)}, bf16[512,2048]{1,0:T(8,128)(2,1)S(1)}) custom-call(s32[4]{0:T(128)S(1)} %get-tuple-element.270.n_ref, bf16[320,1024]{1,0:T(8,128)(2,1)S(1)} %copy-done.45, bf16[320,1024]{1,0:T(8,128)(2,1)S(1)} %copy-done.47, bf16[320,1024]{1,0:T(8,128)(2,1)S(1)} %copy-done.49, ...), custom_call_target="tpu_custom_call" | custom-call | flops 251658240 | bytes 524288 | tf_op jit(solution)/shard_map/grads_qkv/pallas_call | solution.py:697
  361.6 4.1 collective-permute-done.26
  365.8 2.1 add_convert_fusion
  368.0 2.0 collective-permute-start.27
  370.0 2.5 collective-permute-start.40
  372.6 1.9 collective-permute-start.29
  374.6 11.2 %collective-permute-done.28.db_ref = bf16[320,1024]{1,0:T(8,128)(2,1)S(1)} collective-permute-done((bf16[320,1024]{1,0:T(8,128)(2,1)}, bf16[320,1024]{1,0:T(8,128)(2,1)S(1)}, u32[]{:S(2)}, u32[]{:S(2)}) %collective-permute-start.28) | collective-permute-done | bytes 655392 | tf_op jit(solution)/shard_map/ppermute | solution.py:531
  393.6 6.2 %collective-permute-done.27.db_ref = bf16[320,1024]{1,0:T(8,128)(2,1)S(1)} collective-permute-done((bf16[320,1024]{1,0:T(8,128)(2,1)}, bf16[320,1024]{1,0:T(8,128)(2,1)S(1)}, u32[]{:S(2)}, u32[]{:S(2)}) %collective-permute-start.27) | collective-permute-done | bytes 655392 | tf_op jit(solution)/shard_map/ppermute | solution.py:531
  403.1 2.5 collective-permute-start.36
  407.3 2.0 collective-permute-start.32
  410.9 3.7 collective-permute-done.37
  414.6 3.6 collective-permute-done.33
  418.6 4.3 collective-permute-done.38
  425.0 2.1 copy-done.4
  428.2 2.2 mixed.4.rest_0_
  430.4 2.2 mixed.5
  435.1 3.0 finish.1
  441.8 8.9 %all_gather.11 = bf16[256,1536]{1,0:T(8,128)(2,1)S(1)} all-gather(bf16[64,1536]{1,0:T(8,128)(2,1)S(1)} %slice.87), channel_id=1, replica_groups=mesh['shard'=4,'far'=2,'near'=2,'tp'=2] {'far','near'}, dimensions={0}, use_global_device_ids=true | all-gather | bytes 983040 | tf_op jit(solution)/shard_map/all_gather | solution.py:890
  (295 shorter events, 92.8 us)
Async XLA Ops:
  7.2 51.5 %all-gather.3.cloned.1.call-start = ((), (), s32[]{:S(2)}) async-start(), calls=%async_computation.2 | async-start | bytes 3342336 | tf_op jit(solution)/shard_map/all_gather | solution.py:549
  9.0 155.3 %all-gather.5.cloned.1.call-start = ((), (), s32[]{:S(2)}) async-start(), calls=%async_computation.3 | async-start | bytes 11419648 | tf_op jit(solution)/shard_map/all_gather | solution.py:563
  10.2 8.0 %collective-permute-start.13 = (bf16[64,512]{1,0:T(8,128)(2,1)S(1)}, bf16[64,512]{1,0:T(8,128)(2,1)S(1)}, u32[]{:S(2)}, u32[]{:S(2)}) collective-permute-start(bf16[64,512]{1,0:T(8,128)(2,1)S(1)} %bitcast.57), channel_id=1, source_target_pairs={{0,1},{1,0},{2,3},{3,2},{4,5},{5,4},{6,7},{7,6},{8,9},{9,8},{10,11... | collective-permute-start | bytes 196616 | tf_op jit(solution)/shard_map/ppermute | solution.py:531
  19.2 348.7 %reduce-scatter.3.cloned.1.call-start = ((), (), s32[]{:S(2)}) async-start(), calls=%async_computation.4 | async-start | bytes 9191424 | tf_op jit(solution)/shard_map/reduce_scatter | solution.py:846
  63.2 24.8 %collective-permute-start.1 = (bf16[320,1024]{1,0:T(8,128)(2,1)S(1)}, bf16[320,1024]{1,0:T(8,128)(2,1)S(1)}, u32[]{:S(2)}, u32[]{:S(2)}) collective-permute-start(bf16[320,1024]{1,0:T(8,128)(2,1)S(1)} %get-tuple-element.120.kv0), channel_id=1, source_target_pairs={{0,4},{4,0},{1,5},{5,1},{2,6},{6,2},{3,7},{7,3},{8,12},{12,8},{9,1... | collective-permute-start | bytes 1966088 | tf_op jit(solution)/shard_map/ppermute | solution.py:537
  63.8 29.2 %collective-permute-start = (bf16[320,1024]{1,0:T(8,128)(2,1)S(1)}, bf16[320,1024]{1,0:T(8,128)(2,1)S(1)}, u32[]{:S(2)}, u32[]{:S(2)}) collective-permute-start(bf16[320,1024]{1,0:T(8,128)(2,1)S(1)} %get-tuple-element.120.kv0), channel_id=1, source_target_pairs={{0,2},{2,0},{1,3},{3,1},{4,6},{6,4},{5,7},{7,5},{8,10},{10,8},{9,1... | collective-permute-start | bytes 1966088 | tf_op jit(solution)/shard_map/ppermute | solution.py:534
  67.9 34.2 %collective-permute-start.5 = (bf16[320,1024]{1,0:T(8,128)(2,1)}, bf16[320,1024]{1,0:T(8,128)(2,1)S(1)}, u32[]{:S(2)}, u32[]{:S(2)}) collective-permute-start(bf16[320,1024]{1,0:T(8,128)(2,1)} %get-tuple-element.125.kv0), channel_id=1, source_target_pairs={{0,4},{4,0},{1,5},{5,1},{2,6},{6,2},{3,7},{7,3},{8,12},{12,8},{9,1... | collective-permute-start | bytes 1966088 | tf_op jit(solution)/shard_map/ppermute | solution.py:537
  88.0 14.1 %collective-permute-start.2 = (bf16[320,1024]{1,0:T(8,128)(2,1)S(1)}, bf16[320,1024]{1,0:T(8,128)(2,1)S(1)}, u32[]{:S(2)}, u32[]{:S(2)}) collective-permute-start(bf16[320,1024]{1,0:T(8,128)(2,1)S(1)} %collective-permute-done.1.kv2), channel_id=1, source_target_pairs={{0,2},{2,0},{1,3},{3,1},{4,6},{6,4},{5,7},{7,5},{8,10},{10,8},{9,1... | collective-permute-start | bytes 1966088 | tf_op jit(solution)/shard_map/ppermute | solution.py:534
  92.1 34.8 %collective-permute-start.3 = (bf16[320,1024]{1,0:T(8,128)(2,1)}, bf16[320,1024]{1,0:T(8,128)(2,1)}, u32[]{:S(2)}, u32[]{:S(2)}) collective-permute-start(bf16[320,1024]{1,0:T(8,128)(2,1)} %get-tuple-element.121.kv0), channel_id=1, source_target_pairs={{0,4},{4,0},{1,5},{5,1},{2,6},{6,2},{3,7},{7,3},{8,12},{12,8},{9,1... | collective-permute-start | bytes 1966088 | tf_op jit(solution)/shard_map/ppermute | solution.py:537
  92.7 48.4 %collective-permute-start.7 = (bf16[320,1024]{1,0:T(8,128)(2,1)}, bf16[320,1024]{1,0:T(8,128)(2,1)}, u32[]{:S(2)}, u32[]{:S(2)}) collective-permute-start(bf16[320,1024]{1,0:T(8,128)(2,1)} %get-tuple-element.121.kv0), channel_id=1, source_target_pairs={{0,2},{2,0},{1,3},{3,1},{4,6},{6,4},{5,7},{7,5},{8,10},{10,8},{9,1... | collective-permute-start | bytes 1966088 | tf_op jit(solution)/shard_map/ppermute | solution.py:534
  92.9 35.6 %collective-permute-start.4 = (bf16[320,1024]{1,0:T(8,128)(2,1)}, bf16[320,1024]{1,0:T(8,128)(2,1)}, u32[]{:S(2)}, u32[]{:S(2)}) collective-permute-start(bf16[320,1024]{1,0:T(8,128)(2,1)} %get-tuple-element.125.kv0), channel_id=1, source_target_pairs={{0,2},{2,0},{1,3},{3,1},{4,6},{6,4},{5,7},{7,5},{8,10},{10,8},{9,1... | collective-permute-start | bytes 1966088 | tf_op jit(solution)/shard_map/ppermute | solution.py:534
  102.0 27.1 %collective-permute-start.6 = (bf16[320,1024]{1,0:T(8,128)(2,1)S(1)}, bf16[320,1024]{1,0:T(8,128)(2,1)}, u32[]{:S(2)}, u32[]{:S(2)}) collective-permute-start(bf16[320,1024]{1,0:T(8,128)(2,1)S(1)} %collective-permute-done.5.kv2), channel_id=1, source_target_pairs={{0,2},{2,0},{1,3},{3,1},{4,6},{6,4},{5,7},{7,5},{8,10},{10,8},{9,1... | collective-permute-start | bytes 1966088 | tf_op jit(solution)/shard_map/ppermute | solution.py:534
  126.9 14.3 %collective-permute-start.8 = (bf16[320,1024]{1,0:T(8,128)(2,1)}, bf16[320,1024]{1,0:T(8,128)(2,1)}, u32[]{:S(2)}, u32[]{:S(2)}) collective-permute-start(bf16[320,1024]{1,0:T(8,128)(2,1)} %collective-permute-done.3.kv2), channel_id=1, source_target_pairs={{0,2},{2,0},{1,3},{3,1},{4,6},{6,4},{5,7},{7,5},{8,10},{10,8},{9,1... | collective-permute-start | bytes 1966088 | tf_op jit(solution)/shard_map/ppermute | solution.py:534
  126.9 27.1 %collective-permute-start.12 = (f32[1,512]{1,0:T(1,128)S(1)}, f32[1,512]{1,0:T(1,128)S(1)}, u32[]{:S(2)}, u32[]{:S(2)}) collective-permute-start(f32[1,512]{1,0:T(1,128)S(1)} %bitcast.64), channel_id=1, source_target_pairs={{0,1},{1,0},{2,3},{3,2},{4,5},{5,4},{6,7},{7,6},{8,9},{9,8},{10,11... | collective-permute-start | bytes 6152 | tf_op jit(solution)/shard_map/ppermute | solution.py:531
  128.6 26.1 %collective-permute-start.9 = (bf16[320,512]{1,0:T(8,128)(2,1)S(1)}, bf16[320,512]{1,0:T(8,128)(2,1)S(1)}, u32[]{:S(2)}, u32[]{:S(2)}) collective-permute-start(bf16[320,512]{1,0:T(8,128)(2,1)S(1)} %get-tuple-element.123.own_ref0.own_ref.o_ref), channel_id=1, source_target_pairs={{0,1},{1,0},{2,3},{3,2},{4,5},{5,4},{6,7},{7,6},{8,9},{9,8},{10,11... | collective-permute-start | bytes 983048 | tf_op jit(solution)/shard_map/ppermute | solution.py:531
  139.6 14.4 %collective-permute-start.10 = (bf16[320,512]{1,0:T(8,128)(2,1)S(1)}, bf16[320,512]{1,0:T(8,128)(2,1)S(1)}, u32[]{:S(2)}, u32[]{:S(2)}) collective-permute-start(bf16[320,512]{1,0:T(8,128)(2,1)S(1)} %get-tuple-element.126.own_ref1.own_ref.o_ref), channel_id=1, source_target_pairs={{0,1},{1,0},{2,3},{3,2},{4,5},{5,4},{6,7},{7,6},{8,9},{9,8},{10,11... | collective-permute-start | bytes 983048 | tf_op jit(solution)/shard_map/ppermute | solution.py:531
  153.3 9.3 %collective-permute-start.11 = (bf16[320,512]{1,0:T(8,128)(2,1)S(1)}, bf16[320,512]{1,0:T(8,128)(2,1)S(1)}, u32[]{:S(2)}, u32[]{:S(2)}) collective-permute-start(bf16[320,512]{1,0:T(8,128)(2,1)S(1)} %get-tuple-element.129.own_ref2.own_ref.o_ref), channel_id=1, source_target_pairs={{0,1},{1,0},{2,3},{3,2},{4,5},{5,4},{6,7},{7,6},{8,9},{9,8},{10,11... | collective-permute-start | bytes 983048 | tf_op jit(solution)/shard_map/ppermute | solution.py:531
  188.8 4.0 collective-permute-start.14
  199.0 45.8 %collective-permute-start.17 = (bf16[320,1024]{1,0:T(8,128)(2,1)}, bf16[320,1024]{1,0:T(8,128)(2,1)}, u32[]{:S(2)}, u32[]{:S(2)}) collective-permute-start(bf16[320,1024]{1,0:T(8,128)(2,1)} %get-tuple-element.141.dha_ref), channel_id=1, source_target_pairs={{0,1},{1,0},{2,3},{3,2},{4,5},{5,4},{6,7},{7,6},{8,9},{9,8},{10,11... | collective-permute-start | bytes 1966088 | tf_op jit(solution)/shard_map/ppermute | solution.py:531
  207.4 24.7 %collective-permute-start.15 = (bf16[320,1024]{1,0:T(8,128)(2,1)}, bf16[320,1024]{1,0:T(8,128)(2,1)}, u32[]{:S(2)}, u32[]{:S(2)}) collective-permute-start(bf16[320,1024]{1,0:T(8,128)(2,1)} %get-tuple-element.134.dha_ref), channel_id=1, source_target_pairs={{0,1},{1,0},{2,3},{3,2},{4,5},{5,4},{6,7},{7,6},{8,9},{9,8},{10,11... | collective-permute-start | bytes 1966088 | tf_op jit(solution)/shard_map/ppermute | solution.py:531
  216.3 28.6 %collective-permute-start.16 = (bf16[320,1024]{1,0:T(8,128)(2,1)}, bf16[320,1024]{1,0:T(8,128)(2,1)}, u32[]{:S(2)}, u32[]{:S(2)}) collective-permute-start(bf16[320,1024]{1,0:T(8,128)(2,1)} %get-tuple-element.140.dha_ref), channel_id=1, source_target_pairs={{0,1},{1,0},{2,3},{3,2},{4,5},{5,4},{6,7},{7,6},{8,9},{9,8},{10,11... | collective-permute-start | bytes 1966088 | tf_op jit(solution)/shard_map/ppermute | solution.py:531
  244.8 193.3 %reduce-scatter.5.cloned.1.call-start = ((), (), s32[]{:S(2)}) async-start(), calls=%async_computation.5 | async-start | bytes 2359296 | tf_op jit(solution)/shard_map/reduce_scatter | solution.py:858
  260.7 9.1 %collective-permute-start.18 = (bf16[2,320,1024]{2,1,0:T(8,128)(2,1)S(1)}, bf16[2,320,1024]{2,1,0:T(8,128)(2,1)S(1)}, u32[]{:S(2)}, u32[]{:S(2)}) collective-permute-start(bf16[2,320,1024]{2,1,0:T(8,128)(2,1)S(1)} %get-tuple-element.158), channel_id=1, source_target_pairs={{0,2},{2,0},{1,3},{3,1},{4,6},{6,4},{5,7},{7,5},{8,10},{10,8},{9,1... | collective-permute-start | bytes 3932168 | tf_op jit(solution)/shard_map/ppermute | solution.py:534
  270.1 26.7 %collective-permute-start.19 = (bf16[320,1024]{1,0:T(8,128)(2,1)S(1)}, bf16[320,1024]{1,0:T(8,128)(2,1)S(1)}, u32[]{:S(2)}, u32[]{:S(2)}) collective-permute-start(bf16[320,1024]{1,0:T(8,128)(2,1)S(1)} %fusion), channel_id=1, source_target_pairs={{0,4},{4,0},{1,5},{5,1},{2,6},{6,2},{3,7},{7,3},{8,12},{12,8},{9,1... | collective-permute-start | bytes 1966088 | tf_op jit(solution)/shard_map/ppermute | solution.py:537
  283.4 31.8 %collective-permute-start.22 = (bf16[2,320,1024]{2,1,0:T(8,128)(2,1)S(1)}, bf16[2,320,1024]{2,1,0:T(8,128)(2,1)S(1)}, u32[]{:S(2)}, u32[]{:S(2)}) collective-permute-start(bf16[2,320,1024]{2,1,0:T(8,128)(2,1)S(1)} %get-tuple-element.173), channel_id=1, source_target_pairs={{0,2},{2,0},{1,3},{3,1},{4,6},{6,4},{5,7},{7,5},{8,10},{10,8},{9,1... | collective-permute-start | bytes 3932168 | tf_op jit(solution)/shard_map/ppermute | solution.py:534
  311.5 4.9 %collective-permute-start.20 = (bf16[2,320,1024]{2,1,0:T(8,128)(2,1)S(1)}, bf16[2,320,1024]{2,1,0:T(8,128)(2,1)S(1)}, u32[]{:S(2)}, u32[]{:S(2)}) collective-permute-start(bf16[2,320,1024]{2,1,0:T(8,128)(2,1)S(1)} %get-tuple-element.171), channel_id=1, source_target_pairs={{0,2},{2,0},{1,3},{3,1},{4,6},{6,4},{5,7},{7,5},{8,10},{10,8},{9,1... | collective-permute-start | bytes 3932168 | tf_op jit(solution)/shard_map/ppermute | solution.py:534
  311.6 25.7 %collective-permute-start.24 = (bf16[320,1024]{1,0:T(8,128)(2,1)S(1)}, bf16[320,1024]{1,0:T(8,128)(2,1)S(1)}, u32[]{:S(2)}, u32[]{:S(2)}) collective-permute-start(bf16[320,1024]{1,0:T(8,128)(2,1)S(1)} %copy-done.40), channel_id=1, source_target_pairs={{0,1},{1,0},{2,3},{3,2},{4,5},{5,4},{6,7},{7,6},{8,9},{9,8},{10,11... | collective-permute-start | bytes 1966088 | tf_op jit(solution)/shard_map/ppermute | solution.py:531
  313.1 29.6 %collective-permute-start.25 = (bf16[320,1024]{1,0:T(8,128)(2,1)S(1)}, bf16[320,1024]{1,0:T(8,128)(2,1)S(1)}, u32[]{:S(2)}, u32[]{:S(2)}) collective-permute-start(bf16[320,1024]{1,0:T(8,128)(2,1)S(1)} %get-tuple-element.176.da_ref), channel_id=1, source_target_pairs={{0,1},{1,0},{2,3},{3,2},{4,5},{5,4},{6,7},{7,6},{8,9},{9,8},{10,11... | collective-permute-start | bytes 1966088 | tf_op jit(solution)/shard_map/ppermute | solution.py:531
  315.5 19.5 %collective-permute-start.23 = (bf16[320,1024]{1,0:T(8,128)(2,1)S(1)}, bf16[320,1024]{1,0:T(8,128)(2,1)S(1)}, u32[]{:S(2)}, u32[]{:S(2)}) collective-permute-start(bf16[320,1024]{1,0:T(8,128)(2,1)S(1)} %fusion.2), channel_id=1, source_target_pairs={{0,4},{4,0},{1,5},{5,1},{2,6},{6,2},{3,7},{7,3},{8,12},{12,8},{9,1... | collective-permute-start | bytes 1966088 | tf_op jit(solution)/shard_map/ppermute | solution.py:537
  316.6 36.7 %collective-permute-start.21 = (bf16[320,1024]{1,0:T(8,128)(2,1)S(1)}, bf16[320,1024]{1,0:T(8,128)(2,1)S(1)}, u32[]{:S(2)}, u32[]{:S(2)}) collective-permute-start(bf16[320,1024]{1,0:T(8,128)(2,1)S(1)} %fusion.1), channel_id=1, source_target_pairs={{0,4},{4,0},{1,5},{5,1},{2,6},{6,2},{3,7},{7,3},{8,12},{12,8},{9,1... | collective-permute-start | bytes 1966088 | tf_op jit(solution)/shard_map/ppermute | solution.py:537
  361.6 4.2 collective-permute-start.26
  367.9 17.9 %collective-permute-start.28 = (bf16[320,1024]{1,0:T(8,128)(2,1)}, bf16[320,1024]{1,0:T(8,128)(2,1)S(1)}, u32[]{:S(2)}, u32[]{:S(2)}) collective-permute-start(bf16[320,1024]{1,0:T(8,128)(2,1)} %copy-done.56), channel_id=1, source_target_pairs={{0,1},{1,0},{2,3},{3,2},{4,5},{5,4},{6,7},{7,6},{8,9},{9,8},{10,11... | collective-permute-start | bytes 1966088 | tf_op jit(solution)/shard_map/ppermute | solution.py:531
  368.0 31.8 %collective-permute-start.27 = (bf16[320,1024]{1,0:T(8,128)(2,1)}, bf16[320,1024]{1,0:T(8,128)(2,1)S(1)}, u32[]{:S(2)}, u32[]{:S(2)}) collective-permute-start(bf16[320,1024]{1,0:T(8,128)(2,1)} %copy-done.58), channel_id=1, source_target_pairs={{0,1},{1,0},{2,3},{3,2},{4,5},{5,4},{6,7},{7,6},{8,9},{9,8},{10,11... | collective-permute-start | bytes 1966088 | tf_op jit(solution)/shard_map/ppermute | solution.py:531
  370.0 17.6 %collective-permute-start.40 = (bf16[64,4224]{1,0:T(8,128)(2,1)}, bf16[64,4224]{1,0:T(8,128)(2,1)}, u32[]{:S(2)}, u32[]{:S(2)}) collective-permute-start(bf16[64,4224]{1,0:T(8,128)(2,1)} %reduce-scatter.3.cloned.1.call-done), channel_id=1, source_target_pairs={{0,4},{4,0},{1,5},{5,1},{2,6},{6,2},{3,7},{7,3},{8,12},{12,8},{9,1... | collective-permute-start | bytes 1622024 | tf_op jit(solution)/shard_map/ppermute | solution.py:537
  372.5 55.7 %collective-permute-start.30 = (bf16[320,1024]{1,0:T(8,128)(2,1)}, bf16[320,1024]{1,0:T(8,128)(2,1)}, u32[]{:S(2)}, u32[]{:S(2)}) collective-permute-start(bf16[320,1024]{1,0:T(8,128)(2,1)} %copy-done.37), channel_id=1, source_target_pairs={{0,1},{1,0},{2,3},{3,2},{4,5},{5,4},{6,7},{7,6},{8,9},{9,8},{10,11... | collective-permute-start | bytes 1966088 | tf_op jit(solution)/shard_map/ppermute | solution.py:531
  372.6 57.7 %collective-permute-start.29 = (bf16[320,1024]{1,0:T(8,128)(2,1)}, bf16[320,1024]{1,0:T(8,128)(2,1)}, u32[]{:S(2)}, u32[]{:S(2)}) collective-permute-start(bf16[320,1024]{1,0:T(8,128)(2,1)} %copy-done.35), channel_id=1, source_target_pairs={{0,1},{1,0},{2,3},{3,2},{4,5},{5,4},{6,7},{7,6},{8,9},{9,8},{10,11... | collective-permute-start | bytes 1966088 | tf_op jit(solution)/shard_map/ppermute | solution.py:531
  385.8 47.4 %collective-permute-start.39 = (bf16[64,4224]{1,0:T(8,128)(2,1)}, bf16[64,4224]{1,0:T(8,128)(2,1)}, u32[]{:S(2)}, u32[]{:S(2)}) collective-permute-start(bf16[64,4224]{1,0:T(8,128)(2,1)} %reduce-scatter.3.cloned.1.call-done), channel_id=1, source_target_pairs={{0,2},{2,0},{1,3},{3,1},{4,6},{6,4},{5,7},{7,5},{8,10},{10,8},{9,1... | collective-permute-start | bytes 1622024 | tf_op jit(solution)/shard_map/ppermute | solution.py:534
  387.6 45.6 %collective-permute-start.41 = (bf16[64,4224]{1,0:T(8,128)(2,1)}, bf16[64,4224]{1,0:T(8,128)(2,1)}, u32[]{:S(2)}, u32[]{:S(2)}) collective-permute-start(bf16[64,4224]{1,0:T(8,128)(2,1)} %collective-permute-done.40), channel_id=1, source_target_pairs={{0,2},{2,0},{1,3},{3,1},{4,6},{6,4},{5,7},{7,5},{8,10},{10,8},{9,1... | collective-permute-start | bytes 1622024 | tf_op jit(solution)/shard_map/ppermute | solution.py:534
  399.8 1.9 collective-permute-start.35
  403.1 4.1 collective-permute-start.36
  407.3 3.6 collective-permute-start.32
  410.9 3.7 collective-permute-start.37
  414.6 3.6 collective-permute-start.33
  418.2 4.6 %collective-permute-start.38 = (f32[2944]{0:T(1024)S(1)}, f32[2944]{0:T(1024)S(1)}, u32[]{:S(2)}, u32[]{:S(2)}) collective-permute-start(f32[2944]{0:T(1024)S(1)} %add.149), channel_id=1, source_target_pairs={{0,16},{8,24},{16,0},{24,8},{1,17},{9,25},{17,1},{25,9},{2,18},{10... | collective-permute-start | bytes 35336 | tf_op jit(solution)/shard_map/ppermute | solution.py:874
  422.8 9.8 %collective-permute-start.34 = (f32[1024]{0:T(1024)S(1)}, f32[1024]{0:T(1024)S(1)}, u32[]{:S(2)}, u32[]{:S(2)}) collective-permute-start(f32[1024]{0:T(1024)S(1)} %add.139), channel_id=1, source_target_pairs={{0,16},{8,24},{16,0},{24,8},{1,17},{9,25},{17,1},{25,9},{2,18},{10... | collective-permute-start | bytes 12296 | tf_op jit(solution)/shard_map/ppermute | solution.py:874
  439.0 12.1 %collective-permute-start.43 = (bf16[64,512]{1,0:T(8,128)(2,1)S(1)}, bf16[64,512]{1,0:T(8,128)(2,1)S(1)}, u32[]{:S(2)}, u32[]{:S(2)}) collective-permute-start(bf16[64,512]{1,0:T(8,128)(2,1)S(1)} %slice.92), channel_id=1, source_target_pairs={{0,4},{4,0},{1,5},{5,1},{2,6},{6,2},{3,7},{7,3},{8,12},{12,8},{9,1... | collective-permute-start | bytes 196616 | tf_op jit(solution)/shard_map/ppermute | solution.py:537
  440.9 11.8 %collective-permute-start.42 = (bf16[64,512]{1,0:T(8,128)(2,1)S(1)}, bf16[64,512]{1,0:T(8,128)(2,1)S(1)}, u32[]{:S(2)}, u32[]{:S(2)}) collective-permute-start(bf16[64,512]{1,0:T(8,128)(2,1)S(1)} %slice.92), channel_id=1, source_target_pairs={{0,2},{2,0},{1,3},{3,1},{4,6},{6,4},{5,7},{7,5},{8,10},{10,8},{9,1... | collective-permute-start | bytes 196616 | tf_op jit(solution)/shard_map/ppermute | solution.py:534
  451.0 1.7 collective-permute-start.44
  (75 other events, 542.5 us)
Sparse Core Ops, SparseCore 0:
  10.8 47.8 all-gather.2
  61.6 102.6 all-gather.4
  245.0 120.7 reduce-scatter.2
  369.1 67.4 reduce-scatter.4

commit v5 on v4

--- a/solution.py
+++ b/solution.py
@@ -113,7 +113,7 @@
     return jnp.where(lane < HEAD, values[:rows], values[rows:])
 
 
-def attend_kernel(n_ref, q_ref, kv0, kv1, kv2, kv3, o_ref, lse_ref, m_s, l_s, acc_s):
+def attend_kernel(n_ref, q_ref, kv0, kv1, kv2, kv3, o_ref, lse_ref, m_s, l_s, acc_s, *, image):
     qb = split_pair(q_ref[...])
     m_s[...] = jnp.full(m_s.shape, -1e30, F32)
     l_s[...] = jnp.zeros(l_s.shape, F32)
@@ -132,7 +132,7 @@
         acc_s[...] = acc_s[...] * scale + dot_tn(kv_ref[:size, LANES:], e.astype(BF))
 
     for at, kv_ref in enumerate((kv0, kv1, kv2, kv3)):
-        count = n_ref[at]
+        count = n_ref[4 * image + at]
 
         @pl.when(count > TAIL)
         def _():
@@ -149,7 +149,7 @@
 
 
 def attend_back_kernel(
-    n_ref, q_ref, kv0, kv1, kv2, kv3, o_ref, do_ref, lse_ref, rope_ref, dq_ref, keep_ref, send_ref, dq_s
+    n_ref, q_ref, kv0, kv1, kv2, kv3, o_ref, do_ref, lse_ref, rope_ref, dq_ref, keep_ref, send_ref, dq_s, *, image
 ):
     rows = q_ref.shape[0]
     qb = split_pair(q_ref[...])
@@ -174,7 +174,7 @@
             out_ref[slot, size:, :] = jnp.zeros((rows - size, 2 * LANES), BF)
 
     for at, kv_ref in enumerate((kv0, kv1, kv2, kv3)):
-        count = n_ref[at]
+        count = n_ref[4 * image + at]
         out_ref = (keep_ref, send_ref)[at % 2]
         slot = at // 2
 
@@ -336,17 +336,17 @@
 def attn_norm_back_kernel(
     sc_ref, dha_ref, dhb_ref, x1_ref, cot_ref, ln2_ref, own_ref, other_ref, again_ref, w_ref,
     dx_ref, dab_ref, do_ref, dln2_ref, dgain_ref,
-    pj_s, o_s, e_s, f_s, sem,
+    pj_s, o_s, e_s, f_s, sem, *, image,
 ):
     width = x1_ref.shape[2]
     half = own_ref.shape[1]
     load = pltpu.make_async_copy(w_ref.at[:, pl.ds(0, width)], pj_s, sem.at[0])
     load.start()
-    tp = sc_ref[1]
+    tp = sc_ref[3]
     dh = dha_ref[...].astype(F32) + dhb_ref[...].astype(F32)
     normed, inv = row_norm(x1_ref[0], width)
     dln2_ref[...] = jnp.sum(dh * normed, axis=0, keepdims=True)
-    dy = valid_rows(cot_ref[0].astype(F32), sc_ref[0])
+    dy = valid_rows(cot_ref[0].astype(F32), sc_ref[image])
     dx = dy + row_norm_back(dh * ln2_ref[...], normed, inv, width)
     dx_ref[...] = dx
     dab_ref[...] = dx.astype(BF)
@@ -570,6 +570,8 @@
     tables = rope_tables(ctx * rows + jnp.arange(rows, dtype=jnp.int32))
     order = ctx ^ jnp.arange(4, dtype=jnp.int32)
     counts = jnp.clip(lengths[:, None] - rows * order[None, :], 0, rows)
+    valid = jnp.concatenate([counts[:, 0], tp.astype(jnp.int32)[None]])
+    all_counts = counts.reshape(images * 4)
 
     act = whole(rows, width)
     act_half = whole(rows, half)
@@ -587,8 +589,6 @@
     st = [dict() for _ in range(images)]
     for i in range(images):
         s = st[i]
-        s["n"] = counts[i]
-        s["sc"] = jnp.stack([counts[i, 0], tp.astype(jnp.int32)])
         s["h1"], s["q"], s["kv"] = call(
             qkv_kernel,
             (shape(rows, width), shape(rows, half), shape(rows, 2 * half)),
@@ -609,7 +609,7 @@
         s["kvx"] = in_hbm(near(s["kvf"]))
         s["kvf"], s["kv"] = in_hbm(s["kvf"]), in_hbm(s["kv"])
         s["o"], s["lse"] = call(
-            attend_kernel,
+            functools.partial(attend_kernel, image=i),
             (shape(rows, half), shape(half // LANES, 1, 2 * rows, dtype=F32)),
             [SMEM, pair_half] + [pair_kv] * 4,
             [pair_half, pair_line],
@@ -623,9 +623,9 @@
             grid=half // LANES,
             flops=16 * rows * 4 * rows * half,
             moved=12 * block_mb,
-        )(s["n"], s["q"], s["kv"], s["kvc"], s["kvf"], s["kvx"])
-        s["ox"] = swap(s["o"])
-    valid = jnp.concatenate([counts[:, 0], tp.astype(jnp.int32)[None]])
+        )(all_counts, s["q"], s["kv"], s["kvc"], s["kvf"], s["kvx"])
+        s["o"] = in_hbm(s["o"])
+        s["ox"] = in_hbm(swap(s["o"]))
 
     def each(*dims):
         return pl.BlockSpec((1,) + dims, lambda i: (i,) + (0,) * len(dims))
@@ -719,7 +719,7 @@
     def norm_back(i):
         s = st[i]
         s["dx"], s["dab"], s["do"], s["dln2"], s["dattn"] = call(
-            attn_norm_back_kernel,
+            functools.partial(attn_norm_back_kernel, image=i),
             (
                 shape(rows, width, dtype=F32),
                 shape(rows, width),
@@ -740,12 +740,12 @@
             mib=18,
             flops=2 * rows * width * width,
             moved=2 * width * width + 16 * block_mb,
-        )(s["sc"], s["dh2"], s["dh2x"], x1, cotangent, ln2, s["o"], s["ox"], again, rest)
+        )(valid, s["dh2"], s["dh2x"], x1, cotangent, ln2, s["o"], s["ox"], again, rest)
 
     def attention_back(i):
         s = st[i]
         s["dq"], s["keep"], s["send"] = call(
-            attend_back_kernel,
+            functools.partial(attend_back_kernel, image=i),
             (shape(rows, half), shape(2, rows, 2 * half), shape(2, rows, 2 * half)),
             [SMEM, pair_half] + [pair_kv] * 4 + [pair_half, pair_half, pair_line, rope_spec],
             [pair_half, pair_kv2, pair_kv2],
@@ -755,7 +755,7 @@
             mib=12,
             flops=40 * rows * 4 * rows * half,
             moved=20 * block_mb,
-        )(s["n"], s["q"], s["kv"], s["kvc"], s["kvf"], s["kvx"], s["o"], s["do"], s["lse"], tables)
+        )(all_counts, s["q"], s["kv"], s["kvc"], s["kvf"], s["kvx"], s["o"], s["do"], s["lse"], tables)
         s["recv"] = near(s["send"])
         s["mid"] = (s["keep"][1].astype(F32) + s["recv"][1].astype(F32)).astype(BF)
 

time: 470 us -> 464 us (0.987)
  waiting for transfers between devices: 165 us -> 177 us
  local copies, waits for them, and re-layouts: 50.4 us -> 40 us
  starting transfers between devices: 35.5 us -> 28.9 us
    ppermute x10, waiting for transfers between devices: 77.5 us -> 90.5 us  [far(): return lax.ppermute(value, 'far', swap_pair)]
    unnamed x155 -> x131, local copies, waits for them, and re-layouts: 40.1 us -> 30.2 us
    ppermute x10, starting transfers between devices: 14.1 us -> 8.23 us  [far(): return lax.ppermute(value, 'far', swap_pair)]
  transfers between devices with their start and end apart: 49 -> 49, of which waited for: 21 -> 22; matrix products, arithmetic and copies ran while one was open for 5% -> 4% of each run, Pallas kernels for 32% -> 33%
where the time goes in v5:
time: 464 us; the launch traced here: 456 us
  waiting for transfers between devices  177 us (38%)
  Pallas kernels  177 us (38%)
  local copies, waits for them, and re-layouts  40 us (9%)
  starting transfers between devices  28.9 us (6%)
  between operations  14.9 us (3%)
  other arithmetic  9.22 us (2%)
  blocking collectives  8.88 us (2%)
    ppermute x10, waiting for transfers between devices, far(): return lax.ppermute(value, 'far', swap_pair)  90.5 us
    pallas_call x3, Pallas kernels, attention_back(): call(functools.partial(attend_back_kernel, image=i), (shape(rows, half),...  42.4 us
    all_gather x1, waiting for transfers between devices, local(): full_qkv = lax.all_gather(qkv_part, both, axis=1, tiled=True)  37 us
    pallas_call x3, Pallas kernels, local(): call(functools.partial(attend_kernel, image=i), (shape(rows, half), shape...  35.3 us
    ppermute x15, waiting for transfers between devices, swap(): return lax.ppermute(value, 'tp', swap_tp)  32.4 us
    unnamed x131, local copies, waits for them, and re-layouts  30.2 us
    pallas_call x1, Pallas kernels, local(): call(middle_kernel, (shape(images, rows, width, dtype=F32), shape(images,...  20.9 us
    pallas_call x3, Pallas kernels, local(): call(functools.partial(ffn_kernel, total=ff_total), (shape(rows, ffp), sh...  18.7 us
  transfers between devices with their start and end apart: 49, of which 22 were waited for; matrix products, arithmetic and copies ran while one was open for 4% of the time, Pallas kernels for 33%

profile of v5, /device:TPU:0, one launch (start us, length us, event | category | flops | bytes accessed | tf_op | source)
XLA Modules:
  0.0 456.5 jit_solution(14647684398355718162)
XLA Ops:
  10.2 3.0 collective-permute-start.13
  14.4 1.9 constant_dynamic-slice_fusion.1
  21.8 37.0 %all-gather.3.cloned.1.call-done.w_ref = bf16[3,1024,512]{2,1,0:T(8,128)(2,1)} async-done(((bf16[3,64,512]{2,1,0:T(8,128)(2,1)}), bf16[3,1024,512]{2,1,0:T(8,128)(2,1)}) %all-gather.3.cloned.1.call-update) | async-done | bytes 3145744 | tf_op jit(solution)/shard_map/all_gather | solution.py:549
  58.8 1.9 copy-done.5
  60.7 2.5 qkv.3
  68.5 20.5 %collective-permute-done.1.kv2 = bf16[320,1024]{1,0:T(8,128)(2,1)} collective-permute-done((bf16[320,1024]{1,0:T(8,128)(2,1)}, bf16[320,1024]{1,0:T(8,128)(2,1)}, u32[]{:S(2)}, u32[]{:S(2)}) %collective-permute-start.1) | collective-permute-done | bytes 655392 | tf_op jit(solution)/shard_map/ppermute | solution.py:537
  89.1 2.5 qkv.5
  94.4 8.7 %collective-permute-done.5.kv2 = bf16[320,1024]{1,0:T(8,128)(2,1)} collective-permute-done((bf16[320,1024]{1,0:T(8,128)(2,1)S(1)}, bf16[320,1024]{1,0:T(8,128)(2,1)}, u32[]{:S(2)}, u32[]{:S(2)}) %collective-permute-start.5) | collective-permute-done | bytes 655392 | tf_op jit(solution)/shard_map/ppermute | solution.py:537
  103.1 12.6 %attend.3 = (bf16[320,512]{1,0:T(8,128)(2,1)S(1)}, f32[4,1,640]{2,1,0:T(1,128)S(1)}) custom-call(s32[12]{0:T(128)S(1)} %min.12.n_ref, bf16[320,512]{1,0:T(8,128)(2,1)} %copy-done.24, bf16[320,1024]{1,0:T(8,128)(2,1)} %get-tuple-element.120.kv0, bf16[320,1024]{1,0:T(8,128)(2,1)} %collective-permute-done.kv1, bf16[320,1024]{1,0:T(8,128)(2,1)} %collective-permute-done.1.kv2, ...), custom_call_target="tpu_custom_call" | custom-call | flops 209715200 | bytes 245760 | tf_op jit(solution)/shard_map/attend/pallas_call | solution.py:611
  115.8 13.1 %collective-permute-done.3.kv2 = bf16[320,1024]{1,0:T(8,128)(2,1)} collective-permute-done((bf16[320,1024]{1,0:T(8,128)(2,1)}, bf16[320,1024]{1,0:T(8,128)(2,1)}, u32[]{:S(2)}, u32[]{:S(2)}) %collective-permute-start.3) | collective-permute-done | bytes 655392 | tf_op jit(solution)/shard_map/ppermute | solution.py:537
  131.1 10.5 %attend.4 = (bf16[320,512]{1,0:T(8,128)(2,1)S(1)}, f32[4,1,640]{2,1,0:T(1,128)S(1)}) custom-call(s32[12]{0:T(128)S(1)} %min.12.n_ref, bf16[320,512]{1,0:T(8,128)(2,1)} %copy-done.23, bf16[320,1024]{1,0:T(8,128)(2,1)} %copy-done.15, bf16[320,1024]{1,0:T(8,128)(2,1)} %collective-permute-done.4.kv1, bf16[320,1024]{1,0:T(8,128)(2,1)} %collective-permute-done.5.kv2, ...), custom_call_target="tpu_custom_call" | custom-call | flops 209715200 | bytes 245760 | tf_op jit(solution)/shard_map/attend/pallas_call | solution.py:611
  143.2 12.2 %attend.5 = (bf16[320,512]{1,0:T(8,128)(2,1)S(1)}, f32[4,1,640]{2,1,0:T(1,128)S(1)}) custom-call(s32[12]{0:T(128)S(1)} %min.12.n_ref, bf16[320,512]{1,0:T(8,128)(2,1)} %copy-done.22, bf16[320,1024]{1,0:T(8,128)(2,1)} %get-tuple-element.121.kv0, bf16[320,1024]{1,0:T(8,128)(2,1)} %collective-permute-done.7.kv1, bf16[320,1024]{1,0:T(8,128)(2,1)} %collective-permute-done.3.kv2, ...), custom_call_target="tpu_custom_call" | custom-call | flops 209715200 | bytes 245760 | tf_op jit(solution)/shard_map/attend/pallas_call | solution.py:611
  157.5 7.2 %collective-permute-done.11.other_ref2.other_ref = bf16[320,512]{1,0:T(8,128)(2,1)} collective-permute-done((bf16[320,512]{1,0:T(8,128)(2,1)S(1)}, bf16[320,512]{1,0:T(8,128)(2,1)}, u32[]{:S(2)}, u32[]{:S(2)}) %collective-permute-start.11) | collective-permute-done | bytes 327712 | tf_op jit(solution)/shard_map/ppermute | solution.py:531
  166.9 20.9 %middle.1 = (f32[3,320,1024]{2,1,0:T(8,128)}, bf16[3,320,1024]{2,1,0:T(8,128)(2,1)S(1)}, bf16[3,320,1408]{2,1,0:T(8,128)(2,1)S(1)}, bf16[3,320,1408]{2,1,0:T(8,1...) custom-call(s32[4]{0:T(128)S(1)} %get-tuple-element.263.sc_ref, ...), custom_call_target="tpu_custom_call" | custom-call | flops 644874240 | bytes 1915904 | tf_op jit(solution)/shard_map/middle/pallas_call | solution.py:633
  189.3 2.5 collective-permute-done.14.sb_ref
  191.8 6.2 %ffn.5 = (bf16[320,1408]{1,0:T(8,128)(2,1)S(1)}, bf16[320,1408]{1,0:T(8,128)(2,1)S(1)}, bf16[320,1408]{1,0:T(8,128)(2,1)S(1)}, bf16[320,1024]{1,0:T(8,128)(2,1)S...) custom-call(f32[3,8,384]{2,1,0:T(8,128)S(1)} %get-tuple-element.130.sa_ref, ...), custom_call_target="tpu_custom_call" | custom-call | flops 173015040 | bytes 960512 | tf_op jit(solution)/shard_map/ffn/pallas_call | solution.py:668
  199.5 6.2 %ffn.3 = (bf16[320,1408]{1,0:T(8,128)(2,1)S(1)}, bf16[320,1408]{1,0:T(8,128)(2,1)S(1)}, bf16[320,1408]{1,0:T(8,128)(2,1)S(1)}, bf16[320,1024]{1,0:T(8,128)(2,1)S...) custom-call(f32[3,8,384]{2,1,0:T(8,128)S(1)} %get-tuple-element.130.sa_ref, ...), custom_call_target="tpu_custom_call" | custom-call | flops 173015040 | bytes 960512 | tf_op jit(solution)/shard_map/ffn/pallas_call | solution.py:668
  207.1 6.4 %ffn.4 = (bf16[320,1408]{1,0:T(8,128)(2,1)S(1)}, bf16[320,1408]{1,0:T(8,128)(2,1)S(1)}, bf16[320,1408]{1,0:T(8,128)(2,1)S(1)}, bf16[320,1024]{1,0:T(8,128)(2,1)S...) custom-call(f32[3,8,384]{2,1,0:T(8,128)S(1)} %get-tuple-element.130.sa_ref, ...), custom_call_target="tpu_custom_call" | custom-call | flops 173015040 | bytes 960512 | tf_op jit(solution)/shard_map/ffn/pallas_call | solution.py:668
  215.8 12.2 %grads_ffn.1 = bf16[1024,4224]{1,0:T(8,128)(2,1)} custom-call(s32[4]{0:T(128)S(1)} %get-tuple-element.264.n_ref, bf16[3,320,1024]{2,1,0:T(8,128)(2,1)S(1)} %get-tuple-element.142.refs_0_, bf16[320,1408]{1,0:T(8,128)(2,1)S(1)} %get-tuple-element.143.refs_1_, bf16[320,1408]{1,0:T(8,128)(2,1)S(1)} %get-tuple-element.144.refs_2_, ...), custom_call_target="tpu_custom_call" | custom-call | flops 519045120 | bytes 1081344 | tf_op jit(solution)/shard_map/grads_ffn/pallas_call | solution.py:697
  228.0 1.9 collective-permute-done.15.dhb_ref
  229.9 2.1 copy-done.2
  233.5 5.5 %attn_norm_back.3 = (f32[320,1024]{1,0:T(8,128)S(1)}, bf16[320,1024]{1,0:T(8,128)(2,1)S(1)}, bf16[320,512]{1,0:T(8,128)(2,1)S(1)}, f32[1,1024]{1,0:T(1,128)S(1)}, f32[1,512]{1,0:T(1,128)S(1)}) custom-call(s32[4]{0:T(128)S(1)} %get-tuple-element.263.sc_ref, bf16[320,1024]{1,0:T(8,128)(2,1)} %get-tuple-element.134.dha_ref, ...), custom_call_target="tpu_custom_call" | custom-call | flops 41943040 | bytes 458752 | tf_op jit(solution)/shard_map/attn_norm_back/pallas_call | solution.py:721
  242.1 14.9 %attend_back.3 = (bf16[320,512]{1,0:T(8,128)(2,1)S(1)}, bf16[2,320,1024]{2,1,0:T(8,128)(2,1)S(1)}, bf16[2,320,1024]{2,1,0:T(8,128)(2,1)S(1)}) custom-call(s32[12]{0:T(128)S(1)} %min.12.n_ref, bf16[320,512]{1,0:T(8,128)(2,1)} %copy-done.24, bf16[320,1024]{1,0:T(8,128)(2,1)} %get-tuple-element.120.kv0, bf16[320,1024]{1,0:T(8,128)(2,1)} %collective-permute-done.kv1, ...), custom_call_target="tpu_custom_call" | custom-call | flops 524288000 | bytes 409600 | tf_op jit(solution)/shard_map/attend_back/pallas_call | solution.py:747
  258.8 5.8 %attn_norm_back.4 = (f32[320,1024]{1,0:T(8,128)S(1)}, bf16[320,1024]{1,0:T(8,128)(2,1)S(1)}, bf16[320,512]{1,0:T(8,128)(2,1)S(1)}, f32[1,1024]{1,0:T(1,128)S(1)}, f32[1,512]{1,0:T(1,128)S(1)}) custom-call(s32[4]{0:T(128)S(1)} %get-tuple-element.263.sc_ref, bf16[320,1024]{1,0:T(8,128)(2,1)} %get-tuple-element.140.dha_ref, ...), custom_call_target="tpu_custom_call" | custom-call | flops 41943040 | bytes 458752 | tf_op jit(solution)/shard_map/attn_norm_back/pallas_call | solution.py:721
  265.6 12.8 %attend_back.4 = (bf16[320,512]{1,0:T(8,128)(2,1)S(1)}, bf16[2,320,1024]{2,1,0:T(8,128)(2,1)S(1)}, bf16[2,320,1024]{2,1,0:T(8,128)(2,1)S(1)}) custom-call(s32[12]{0:T(128)S(1)} %min.12.n_ref, bf16[320,512]{1,0:T(8,128)(2,1)} %copy-done.23, bf16[320,1024]{1,0:T(8,128)(2,1)} %copy-done.15, bf16[320,1024]{1,0:T(8,128)(2,1)} %collective-permute-done.4.kv1, ...), custom_call_target="tpu_custom_call" | custom-call | flops 524288000 | bytes 409600 | tf_op jit(solution)/shard_map/attend_back/pallas_call | solution.py:747
  278.6 5.4 %attn_norm_back.5 = (f32[320,1024]{1,0:T(8,128)S(1)}, bf16[320,1024]{1,0:T(8,128)(2,1)S(1)}, bf16[320,512]{1,0:T(8,128)(2,1)S(1)}, f32[1,1024]{1,0:T(1,128)S(1)}, f32[1,512]{1,0:T(1,128)S(1)}) custom-call(s32[4]{0:T(128)S(1)} %get-tuple-element.263.sc_ref, bf16[320,1024]{1,0:T(8,128)(2,1)S(1)} %get-tuple-element.141.dha_ref, ...), custom_call_target="tpu_custom_call" | custom-call | flops 41943040 | bytes 458752 | tf_op jit(solution)/shard_map/attn_norm_back/pallas_call | solution.py:721
  285.0 3.4 collective-permute-done.19.far_ref
  288.4 14.7 %attend_back.5 = (bf16[320,512]{1,0:T(8,128)(2,1)S(1)}, bf16[2,320,1024]{2,1,0:T(8,128)(2,1)S(1)}, bf16[2,320,1024]{2,1,0:T(8,128)(2,1)S(1)}) custom-call(s32[12]{0:T(128)S(1)} %min.12.n_ref, bf16[320,512]{1,0:T(8,128)(2,1)} %copy-done.22, bf16[320,1024]{1,0:T(8,128)(2,1)} %get-tuple-element.121.kv0, bf16[320,1024]{1,0:T(8,128)(2,1)} %collective-permute-done.7.kv1, ...), custom_call_target="tpu_custom_call" | custom-call | flops 524288000 | bytes 409600 | tf_op jit(solution)/shard_map/attend_back/pallas_call | solution.py:747
  309.5 23.1 %collective-permute-done.23.far_ref = bf16[320,1024]{1,0:T(8,128)(2,1)S(1)} collective-permute-done((bf16[320,1024]{1,0:T(8,128)(2,1)S(1)}, bf16[320,1024]{1,0:T(8,128)(2,1)S(1)}, u32[]{:S(2)}, u32[]{:S(2)}) %collective-permute-start.23) | collective-permute-done | bytes 655392 | tf_op jit(solution)/shard_map/ppermute | solution.py:537
  335.8 14.6 %collective-permute-done.21.far_ref = bf16[320,1024]{1,0:T(8,128)(2,1)S(1)} collective-permute-done((bf16[320,1024]{1,0:T(8,128)(2,1)S(1)}, bf16[320,1024]{1,0:T(8,128)(2,1)S(1)}, u32[]{:S(2)}, u32[]{:S(2)}) %collective-permute-start.21) | collective-permute-done | bytes 655392 | tf_op jit(solution)/shard_map/ppermute | solution.py:537
  352.8 5.8 %grads_qkv.1 = (bf16[512,2048]{1,0:T(8,128)(2,1)S(1)}, bf16[512,2048]{1,0:T(8,128)(2,1)S(1)}) custom-call(s32[4]{0:T(128)S(1)} %get-tuple-element.264.n_ref, bf16[320,1024]{1,0:T(8,128)(2,1)S(1)} %copy-done.37, bf16[320,1024]{1,0:T(8,128)(2,1)S(1)} %copy-done.39, bf16[320,1024]{1,0:T(8,128)(2,1)S(1)} %copy-done.41, ...), custom_call_target="tpu_custom_call" | custom-call | flops 251658240 | bytes 524288 | tf_op jit(solution)/shard_map/grads_qkv/pallas_call | solution.py:697
  358.7 4.1 collective-permute-done.26
  362.8 2.1 add_convert_fusion
  369.9 12.9 %collective-permute-done.28.db_ref = bf16[320,1024]{1,0:T(8,128)(2,1)S(1)} collective-permute-done((bf16[320,1024]{1,0:T(8,128)(2,1)}, bf16[320,1024]{1,0:T(8,128)(2,1)S(1)}, u32[]{:S(2)}, u32[]{:S(2)}) %collective-permute-start.28) | collective-permute-done | bytes 655392 | tf_op jit(solution)/shard_map/ppermute | solution.py:531
  386.2 1.9 tokens_back.3
  388.0 1.9 tokens_back.4
  389.9 6.9 %collective-permute-done.27.db_ref = bf16[320,1024]{1,0:T(8,128)(2,1)S(1)} collective-permute-done((bf16[320,1024]{1,0:T(8,128)(2,1)}, bf16[320,1024]{1,0:T(8,128)(2,1)S(1)}, u32[]{:S(2)}, u32[]{:S(2)}) %collective-permute-start.27) | collective-permute-done | bytes 655392 | tf_op jit(solution)/shard_map/ppermute | solution.py:531
  396.9 1.9 tokens_back.5
  400.9 3.1 collective-permute-done.36
  404.6 3.0 collective-permute-done.32
  407.6 3.7 collective-permute-done.37
  411.3 3.6 collective-permute-done.33
  414.9 4.6 %collective-permute-done.38 = f32[2944]{0:T(1024)S(1)} collective-permute-done((f32[2944]{0:T(1024)S(1)}, f32[2944]{0:T(1024)S(1)}, u32[]{:S(2)}, u32[]{:S(2)}) %collective-permute-start.38) | collective-permute-done | bytes 11808 | tf_op jit(solution)/shard_map/ppermute | solution.py:874
  421.3 2.1 copy-done.4
  424.5 2.2 mixed.4.rest_0_
  426.7 2.2 mixed.5
  431.3 3.0 finish.1
  436.9 8.9 %all_gather.11 = bf16[256,1536]{1,0:T(8,128)(2,1)S(1)} all-gather(bf16[64,1536]{1,0:T(8,128)(2,1)S(1)} %slice.63), channel_id=1, replica_groups=mesh['shard'=4,'far'=2,'near'=2,'tp'=2] {'far','near'}, dimensions={0}, use_global_device_ids=true | all-gather | bytes 983040 | tf_op jit(solution)/shard_map/all_gather | solution.py:890
  (267 shorter events, 75.7 us)
Async XLA Ops:
  7.2 51.6 %all-gather.3.cloned.1.call-start = ((), (), s32[]{:S(2)}) async-start(), calls=%async_computation.2 | async-start | bytes 3342336 | tf_op jit(solution)/shard_map/all_gather | solution.py:549
  9.0 156.3 %all-gather.5.cloned.1.call-start = ((), (), s32[]{:S(2)}) async-start(), calls=%async_computation.3 | async-start | bytes 11419648 | tf_op jit(solution)/shard_map/all_gather | solution.py:563
  10.2 8.0 %collective-permute-start.13 = (bf16[64,512]{1,0:T(8,128)(2,1)S(1)}, bf16[64,512]{1,0:T(8,128)(2,1)S(1)}, u32[]{:S(2)}, u32[]{:S(2)}) collective-permute-start(bf16[64,512]{1,0:T(8,128)(2,1)S(1)} %bitcast.48), channel_id=1, source_target_pairs={{0,1},{1,0},{2,3},{3,2},{4,5},{5,4},{6,7},{7,6},{8,9},{9,8},{10,11... | collective-permute-start | bytes 196616 | tf_op jit(solution)/shard_map/ppermute | solution.py:531
  19.2 345.7 %reduce-scatter.3.cloned.1.call-start = ((), (), s32[]{:S(2)}) async-start(), calls=%async_computation.4 | async-start | bytes 9191424 | tf_op jit(solution)/shard_map/reduce_scatter | solution.py:846
  64.0 25.1 %collective-permute-start.1 = (bf16[320,1024]{1,0:T(8,128)(2,1)}, bf16[320,1024]{1,0:T(8,128)(2,1)}, u32[]{:S(2)}, u32[]{:S(2)}) collective-permute-start(bf16[320,1024]{1,0:T(8,128)(2,1)} %get-tuple-element.120.kv0), channel_id=1, source_target_pairs={{0,4},{4,0},{1,5},{5,1},{2,6},{6,2},{3,7},{7,3},{8,12},{12,8},{9,1... | collective-permute-start | bytes 1966088 | tf_op jit(solution)/shard_map/ppermute | solution.py:537
  64.5 29.6 %collective-permute-start = (bf16[320,1024]{1,0:T(8,128)(2,1)}, bf16[320,1024]{1,0:T(8,128)(2,1)}, u32[]{:S(2)}, u32[]{:S(2)}) collective-permute-start(bf16[320,1024]{1,0:T(8,128)(2,1)} %get-tuple-element.120.kv0), channel_id=1, source_target_pairs={{0,2},{2,0},{1,3},{3,1},{4,6},{6,4},{5,7},{7,5},{8,10},{10,8},{9,1... | collective-permute-start | bytes 1966088 | tf_op jit(solution)/shard_map/ppermute | solution.py:534
  67.1 36.1 %collective-permute-start.5 = (bf16[320,1024]{1,0:T(8,128)(2,1)S(1)}, bf16[320,1024]{1,0:T(8,128)(2,1)}, u32[]{:S(2)}, u32[]{:S(2)}) collective-permute-start(bf16[320,1024]{1,0:T(8,128)(2,1)S(1)} %get-tuple-element.125.kv0), channel_id=1, source_target_pairs={{0,4},{4,0},{1,5},{5,1},{2,6},{6,2},{3,7},{7,3},{8,12},{12,8},{9,1... | collective-permute-start | bytes 1966088 | tf_op jit(solution)/shard_map/ppermute | solution.py:537
  89.1 14.1 %collective-permute-start.2 = (bf16[320,1024]{1,0:T(8,128)(2,1)}, bf16[320,1024]{1,0:T(8,128)(2,1)}, u32[]{:S(2)}, u32[]{:S(2)}) collective-permute-start(bf16[320,1024]{1,0:T(8,128)(2,1)} %collective-permute-done.1.kv2), channel_id=1, source_target_pairs={{0,2},{2,0},{1,3},{3,1},{4,6},{6,4},{5,7},{7,5},{8,10},{10,8},{9,1... | collective-permute-start | bytes 1966088 | tf_op jit(solution)/shard_map/ppermute | solution.py:534
  93.2 35.6 %collective-permute-start.3 = (bf16[320,1024]{1,0:T(8,128)(2,1)}, bf16[320,1024]{1,0:T(8,128)(2,1)}, u32[]{:S(2)}, u32[]{:S(2)}) collective-permute-start(bf16[320,1024]{1,0:T(8,128)(2,1)} %get-tuple-element.121.kv0), channel_id=1, source_target_pairs={{0,4},{4,0},{1,5},{5,1},{2,6},{6,2},{3,7},{7,3},{8,12},{12,8},{9,1... | collective-permute-start | bytes 1966088 | tf_op jit(solution)/shard_map/ppermute | solution.py:537
  93.9 49.3 %collective-permute-start.7 = (bf16[320,1024]{1,0:T(8,128)(2,1)}, bf16[320,1024]{1,0:T(8,128)(2,1)}, u32[]{:S(2)}, u32[]{:S(2)}) collective-permute-start(bf16[320,1024]{1,0:T(8,128)(2,1)} %get-tuple-element.121.kv0), channel_id=1, source_target_pairs={{0,2},{2,0},{1,3},{3,1},{4,6},{6,4},{5,7},{7,5},{8,10},{10,8},{9,1... | collective-permute-start | bytes 1966088 | tf_op jit(solution)/shard_map/ppermute | solution.py:534
  94.1 36.4 %collective-permute-start.4 = (bf16[320,1024]{1,0:T(8,128)(2,1)S(1)}, bf16[320,1024]{1,0:T(8,128)(2,1)}, u32[]{:S(2)}, u32[]{:S(2)}) collective-permute-start(bf16[320,1024]{1,0:T(8,128)(2,1)S(1)} %get-tuple-element.125.kv0), channel_id=1, source_target_pairs={{0,2},{2,0},{1,3},{3,1},{4,6},{6,4},{5,7},{7,5},{8,10},{10,8},{9,1... | collective-permute-start | bytes 1966088 | tf_op jit(solution)/shard_map/ppermute | solution.py:534
  103.1 28.0 %collective-permute-start.6 = (bf16[320,1024]{1,0:T(8,128)(2,1)}, bf16[320,1024]{1,0:T(8,128)(2,1)}, u32[]{:S(2)}, u32[]{:S(2)}) collective-permute-start(bf16[320,1024]{1,0:T(8,128)(2,1)} %collective-permute-done.5.kv2), channel_id=1, source_target_pairs={{0,2},{2,0},{1,3},{3,1},{4,6},{6,4},{5,7},{7,5},{8,10},{10,8},{9,1... | collective-permute-start | bytes 1966088 | tf_op jit(solution)/shard_map/ppermute | solution.py:534
  128.8 14.4 %collective-permute-start.8 = (bf16[320,1024]{1,0:T(8,128)(2,1)}, bf16[320,1024]{1,0:T(8,128)(2,1)}, u32[]{:S(2)}, u32[]{:S(2)}) collective-permute-start(bf16[320,1024]{1,0:T(8,128)(2,1)} %collective-permute-done.3.kv2), channel_id=1, source_target_pairs={{0,2},{2,0},{1,3},{3,1},{4,6},{6,4},{5,7},{7,5},{8,10},{10,8},{9,1... | collective-permute-start | bytes 1966088 | tf_op jit(solution)/shard_map/ppermute | solution.py:534
  128.8 27.2 %collective-permute-start.12 = (f32[1,512]{1,0:T(1,128)S(1)}, f32[1,512]{1,0:T(1,128)S(1)}, u32[]{:S(2)}, u32[]{:S(2)}) collective-permute-start(f32[1,512]{1,0:T(1,128)S(1)} %bitcast.55), channel_id=1, source_target_pairs={{0,1},{1,0},{2,3},{3,2},{4,5},{5,4},{6,7},{7,6},{8,9},{9,8},{10,11... | collective-permute-start | bytes 6152 | tf_op jit(solution)/shard_map/ppermute | solution.py:531
  130.5 25.5 %collective-permute-start.9 = (bf16[320,512]{1,0:T(8,128)(2,1)S(1)}, bf16[320,512]{1,0:T(8,128)(2,1)S(1)}, u32[]{:S(2)}, u32[]{:S(2)}) collective-permute-start(bf16[320,512]{1,0:T(8,128)(2,1)S(1)} %get-tuple-element.123.own_ref0.own_ref.o_ref), channel_id=1, source_target_pairs={{0,1},{1,0},{2,3},{3,2},{4,5},{5,4},{6,7},{7,6},{8,9},{9,8},{10,11... | collective-permute-start | bytes 983048 | tf_op jit(solution)/shard_map/ppermute | solution.py:531
  141.6 14.4 %collective-permute-start.10 = (bf16[320,512]{1,0:T(8,128)(2,1)S(1)}, bf16[320,512]{1,0:T(8,128)(2,1)S(1)}, u32[]{:S(2)}, u32[]{:S(2)}) collective-permute-start(bf16[320,512]{1,0:T(8,128)(2,1)S(1)} %get-tuple-element.126.own_ref1.own_ref.o_ref), channel_id=1, source_target_pairs={{0,1},{1,0},{2,3},{3,2},{4,5},{5,4},{6,7},{7,6},{8,9},{9,8},{10,11... | collective-permute-start | bytes 983048 | tf_op jit(solution)/shard_map/ppermute | solution.py:531
  155.4 9.4 %collective-permute-start.11 = (bf16[320,512]{1,0:T(8,128)(2,1)S(1)}, bf16[320,512]{1,0:T(8,128)(2,1)}, u32[]{:S(2)}, u32[]{:S(2)}) collective-permute-start(bf16[320,512]{1,0:T(8,128)(2,1)S(1)} %get-tuple-element.129.own_ref2.own_ref.o_ref), channel_id=1, source_target_pairs={{0,1},{1,0},{2,3},{3,2},{4,5},{5,4},{6,7},{7,6},{8,9},{9,8},{10,11... | collective-permute-start | bytes 983048 | tf_op jit(solution)/shard_map/ppermute | solution.py:531
  187.8 4.0 collective-permute-start.14
  198.0 43.0 %collective-permute-start.17 = (bf16[320,1024]{1,0:T(8,128)(2,1)S(1)}, bf16[320,1024]{1,0:T(8,128)(2,1)}, u32[]{:S(2)}, u32[]{:S(2)}) collective-permute-start(bf16[320,1024]{1,0:T(8,128)(2,1)S(1)} %get-tuple-element.141.dha_ref), channel_id=1, source_target_pairs={{0,1},{1,0},{2,3},{3,2},{4,5},{5,4},{6,7},{7,6},{8,9},{9,8},{10,11... | collective-permute-start | bytes 1966088 | tf_op jit(solution)/shard_map/ppermute | solution.py:531
  206.5 23.3 %collective-permute-start.15 = (bf16[320,1024]{1,0:T(8,128)(2,1)}, bf16[320,1024]{1,0:T(8,128)(2,1)}, u32[]{:S(2)}, u32[]{:S(2)}) collective-permute-start(bf16[320,1024]{1,0:T(8,128)(2,1)} %get-tuple-element.134.dha_ref), channel_id=1, source_target_pairs={{0,1},{1,0},{2,3},{3,2},{4,5},{5,4},{6,7},{7,6},{8,9},{9,8},{10,11... | collective-permute-start | bytes 1966088 | tf_op jit(solution)/shard_map/ppermute | solution.py:531
  214.4 27.6 %collective-permute-start.16 = (bf16[320,1024]{1,0:T(8,128)(2,1)}, bf16[320,1024]{1,0:T(8,128)(2,1)}, u32[]{:S(2)}, u32[]{:S(2)}) collective-permute-start(bf16[320,1024]{1,0:T(8,128)(2,1)} %get-tuple-element.140.dha_ref), channel_id=1, source_target_pairs={{0,1},{1,0},{2,3},{3,2},{4,5},{5,4},{6,7},{7,6},{8,9},{9,8},{10,11... | collective-permute-start | bytes 1966088 | tf_op jit(solution)/shard_map/ppermute | solution.py:531
  242.0 192.4 %reduce-scatter.5.cloned.1.call-start = ((), (), s32[]{:S(2)}) async-start(), calls=%async_computation.5 | async-start | bytes 2359296 | tf_op jit(solution)/shard_map/reduce_scatter | solution.py:858
  257.0 7.6 %collective-permute-start.18 = (bf16[2,320,1024]{2,1,0:T(8,128)(2,1)S(1)}, bf16[2,320,1024]{2,1,0:T(8,128)(2,1)S(1)}, u32[]{:S(2)}, u32[]{:S(2)}) collective-permute-start(bf16[2,320,1024]{2,1,0:T(8,128)(2,1)S(1)} %get-tuple-element.158), channel_id=1, source_target_pairs={{0,2},{2,0},{1,3},{3,1},{4,6},{6,4},{5,7},{7,5},{8,10},{10,8},{9,1... | collective-permute-start | bytes 3932168 | tf_op jit(solution)/shard_map/ppermute | solution.py:534
  264.9 23.5 %collective-permute-start.19 = (bf16[320,1024]{1,0:T(8,128)(2,1)S(1)}, bf16[320,1024]{1,0:T(8,128)(2,1)S(1)}, u32[]{:S(2)}, u32[]{:S(2)}) collective-permute-start(bf16[320,1024]{1,0:T(8,128)(2,1)S(1)} %fusion), channel_id=1, source_target_pairs={{0,4},{4,0},{1,5},{5,1},{2,6},{6,2},{3,7},{7,3},{8,12},{12,8},{9,1... | collective-permute-start | bytes 1966088 | tf_op jit(solution)/shard_map/ppermute | solution.py:537
  278.5 28.4 %collective-permute-start.22 = (bf16[2,320,1024]{2,1,0:T(8,128)(2,1)S(1)}, bf16[2,320,1024]{2,1,0:T(8,128)(2,1)S(1)}, u32[]{:S(2)}, u32[]{:S(2)}) collective-permute-start(bf16[2,320,1024]{2,1,0:T(8,128)(2,1)S(1)} %get-tuple-element.173), channel_id=1, source_target_pairs={{0,2},{2,0},{1,3},{3,1},{4,6},{6,4},{5,7},{7,5},{8,10},{10,8},{9,1... | collective-permute-start | bytes 3932168 | tf_op jit(solution)/shard_map/ppermute | solution.py:534
  303.1 4.9 %collective-permute-start.20 = (bf16[2,320,1024]{2,1,0:T(8,128)(2,1)S(1)}, bf16[2,320,1024]{2,1,0:T(8,128)(2,1)S(1)}, u32[]{:S(2)}, u32[]{:S(2)}) collective-permute-start(bf16[2,320,1024]{2,1,0:T(8,128)(2,1)S(1)} %get-tuple-element.171), channel_id=1, source_target_pairs={{0,2},{2,0},{1,3},{3,1},{4,6},{6,4},{5,7},{7,5},{8,10},{10,8},{9,1... | collective-permute-start | bytes 3932168 | tf_op jit(solution)/shard_map/ppermute | solution.py:534
  303.2 31.8 %collective-permute-start.24 = (bf16[320,1024]{1,0:T(8,128)(2,1)S(1)}, bf16[320,1024]{1,0:T(8,128)(2,1)S(1)}, u32[]{:S(2)}, u32[]{:S(2)}) collective-permute-start(bf16[320,1024]{1,0:T(8,128)(2,1)S(1)} %copy-done.32), channel_id=1, source_target_pairs={{0,1},{1,0},{2,3},{3,2},{4,5},{5,4},{6,7},{7,6},{8,9},{9,8},{10,11... | collective-permute-start | bytes 1966088 | tf_op jit(solution)/shard_map/ppermute | solution.py:531
  306.4 28.6 %collective-permute-start.25 = (bf16[320,1024]{1,0:T(8,128)(2,1)S(1)}, bf16[320,1024]{1,0:T(8,128)(2,1)S(1)}, u32[]{:S(2)}, u32[]{:S(2)}) collective-permute-start(bf16[320,1024]{1,0:T(8,128)(2,1)S(1)} %get-tuple-element.176.da_ref), channel_id=1, source_target_pairs={{0,1},{1,0},{2,3},{3,2},{4,5},{5,4},{6,7},{7,6},{8,9},{9,8},{10,11... | collective-permute-start | bytes 1966088 | tf_op jit(solution)/shard_map/ppermute | solution.py:531
  307.1 25.5 %collective-permute-start.23 = (bf16[320,1024]{1,0:T(8,128)(2,1)S(1)}, bf16[320,1024]{1,0:T(8,128)(2,1)S(1)}, u32[]{:S(2)}, u32[]{:S(2)}) collective-permute-start(bf16[320,1024]{1,0:T(8,128)(2,1)S(1)} %fusion.2), channel_id=1, source_target_pairs={{0,4},{4,0},{1,5},{5,1},{2,6},{6,2},{3,7},{7,3},{8,12},{12,8},{9,1... | collective-permute-start | bytes 1966088 | tf_op jit(solution)/shard_map/ppermute | solution.py:537
  308.3 42.1 %collective-permute-start.21 = (bf16[320,1024]{1,0:T(8,128)(2,1)S(1)}, bf16[320,1024]{1,0:T(8,128)(2,1)S(1)}, u32[]{:S(2)}, u32[]{:S(2)}) collective-permute-start(bf16[320,1024]{1,0:T(8,128)(2,1)S(1)} %fusion.1), channel_id=1, source_target_pairs={{0,4},{4,0},{1,5},{5,1},{2,6},{6,2},{3,7},{7,3},{8,12},{12,8},{9,1... | collective-permute-start | bytes 1966088 | tf_op jit(solution)/shard_map/ppermute | solution.py:537
  358.6 4.2 collective-permute-start.26
  365.0 17.9 %collective-permute-start.28 = (bf16[320,1024]{1,0:T(8,128)(2,1)}, bf16[320,1024]{1,0:T(8,128)(2,1)S(1)}, u32[]{:S(2)}, u32[]{:S(2)}) collective-permute-start(bf16[320,1024]{1,0:T(8,128)(2,1)} %copy-done.48), channel_id=1, source_target_pairs={{0,1},{1,0},{2,3},{3,2},{4,5},{5,4},{6,7},{7,6},{8,9},{9,8},{10,11... | collective-permute-start | bytes 1966088 | tf_op jit(solution)/shard_map/ppermute | solution.py:531
  366.4 30.4 %collective-permute-start.27 = (bf16[320,1024]{1,0:T(8,128)(2,1)}, bf16[320,1024]{1,0:T(8,128)(2,1)S(1)}, u32[]{:S(2)}, u32[]{:S(2)}) collective-permute-start(bf16[320,1024]{1,0:T(8,128)(2,1)} %copy-done.50), channel_id=1, source_target_pairs={{0,1},{1,0},{2,3},{3,2},{4,5},{5,4},{6,7},{7,6},{8,9},{9,8},{10,11... | collective-permute-start | bytes 1966088 | tf_op jit(solution)/shard_map/ppermute | solution.py:531
  367.1 16.9 %collective-permute-start.40 = (bf16[64,4224]{1,0:T(8,128)(2,1)}, bf16[64,4224]{1,0:T(8,128)(2,1)}, u32[]{:S(2)}, u32[]{:S(2)}) collective-permute-start(bf16[64,4224]{1,0:T(8,128)(2,1)} %reduce-scatter.3.cloned.1.call-done), channel_id=1, source_target_pairs={{0,4},{4,0},{1,5},{5,1},{2,6},{6,2},{3,7},{7,3},{8,12},{12,8},{9,1... | collective-permute-start | bytes 1622024 | tf_op jit(solution)/shard_map/ppermute | solution.py:537
  367.8 56.6 %collective-permute-start.30 = (bf16[320,1024]{1,0:T(8,128)(2,1)}, bf16[320,1024]{1,0:T(8,128)(2,1)}, u32[]{:S(2)}, u32[]{:S(2)}) collective-permute-start(bf16[320,1024]{1,0:T(8,128)(2,1)} %copy-done.29), channel_id=1, source_target_pairs={{0,1},{1,0},{2,3},{3,2},{4,5},{5,4},{6,7},{7,6},{8,9},{9,8},{10,11... | collective-permute-start | bytes 1966088 | tf_op jit(solution)/shard_map/ppermute | solution.py:531
  369.1 57.5 %collective-permute-start.29 = (bf16[320,1024]{1,0:T(8,128)(2,1)}, bf16[320,1024]{1,0:T(8,128)(2,1)}, u32[]{:S(2)}, u32[]{:S(2)}) collective-permute-start(bf16[320,1024]{1,0:T(8,128)(2,1)} %copy-done.27), channel_id=1, source_target_pairs={{0,1},{1,0},{2,3},{3,2},{4,5},{5,4},{6,7},{7,6},{8,9},{9,8},{10,11... | collective-permute-start | bytes 1966088 | tf_op jit(solution)/shard_map/ppermute | solution.py:531
  382.8 46.6 %collective-permute-start.39 = (bf16[64,4224]{1,0:T(8,128)(2,1)}, bf16[64,4224]{1,0:T(8,128)(2,1)}, u32[]{:S(2)}, u32[]{:S(2)}) collective-permute-start(bf16[64,4224]{1,0:T(8,128)(2,1)} %reduce-scatter.3.cloned.1.call-done), channel_id=1, source_target_pairs={{0,2},{2,0},{1,3},{3,1},{4,6},{6,4},{5,7},{7,5},{8,10},{10,8},{9,1... | collective-permute-start | bytes 1622024 | tf_op jit(solution)/shard_map/ppermute | solution.py:534
  383.9 45.5 %collective-permute-start.41 = (bf16[64,4224]{1,0:T(8,128)(2,1)}, bf16[64,4224]{1,0:T(8,128)(2,1)}, u32[]{:S(2)}, u32[]{:S(2)}) collective-permute-start(bf16[64,4224]{1,0:T(8,128)(2,1)} %collective-permute-done.40), channel_id=1, source_target_pairs={{0,2},{2,0},{1,3},{3,1},{4,6},{6,4},{5,7},{7,5},{8,10},{10,8},{9,1... | collective-permute-start | bytes 1622024 | tf_op jit(solution)/shard_map/ppermute | solution.py:534
  396.9 1.9 collective-permute-start.35
  400.2 3.8 collective-permute-start.36
  404.0 3.6 collective-permute-start.32
  407.6 3.7 collective-permute-start.37
  411.3 3.6 collective-permute-start.33
  414.9 4.6 %collective-permute-start.38 = (f32[2944]{0:T(1024)S(1)}, f32[2944]{0:T(1024)S(1)}, u32[]{:S(2)}, u32[]{:S(2)}) collective-permute-start(f32[2944]{0:T(1024)S(1)} %add.149), channel_id=1, source_target_pairs={{0,16},{8,24},{16,0},{24,8},{1,17},{9,25},{17,1},{25,9},{2,18},{10... | collective-permute-start | bytes 35336 | tf_op jit(solution)/shard_map/ppermute | solution.py:874
  419.5 9.4 %collective-permute-start.34 = (f32[1024]{0:T(1024)S(1)}, f32[1024]{0:T(1024)S(1)}, u32[]{:S(2)}, u32[]{:S(2)}) collective-permute-start(f32[1024]{0:T(1024)S(1)} %add.139), channel_id=1, source_target_pairs={{0,16},{8,24},{16,0},{24,8},{1,17},{9,25},{17,1},{25,9},{2,18},{10... | collective-permute-start | bytes 12296 | tf_op jit(solution)/shard_map/ppermute | solution.py:874
  435.2 10.8 %collective-permute-start.43 = (bf16[64,512]{1,0:T(8,128)(2,1)S(1)}, bf16[64,512]{1,0:T(8,128)(2,1)S(1)}, u32[]{:S(2)}, u32[]{:S(2)}) collective-permute-start(bf16[64,512]{1,0:T(8,128)(2,1)S(1)} %slice.68), channel_id=1, source_target_pairs={{0,4},{4,0},{1,5},{5,1},{2,6},{6,2},{3,7},{7,3},{8,12},{12,8},{9,1... | collective-permute-start | bytes 196616 | tf_op jit(solution)/shard_map/ppermute | solution.py:537
  435.9 11.8 %collective-permute-start.42 = (bf16[64,512]{1,0:T(8,128)(2,1)S(1)}, bf16[64,512]{1,0:T(8,128)(2,1)S(1)}, u32[]{:S(2)}, u32[]{:S(2)}) collective-permute-start(bf16[64,512]{1,0:T(8,128)(2,1)S(1)} %slice.68), channel_id=1, source_target_pairs={{0,2},{2,0},{1,3},{3,1},{4,6},{6,4},{5,7},{7,5},{8,10},{10,8},{9,1... | collective-permute-start | bytes 196616 | tf_op jit(solution)/shard_map/ppermute | solution.py:534
  446.1 1.7 collective-permute-start.44
  (63 other events, 578.1 us)
Sparse Core Ops, SparseCore 0:
  10.8 47.9 all-gather.2
  61.6 103.6 all-gather.4
  242.1 119.1 reduce-scatter.2
  365.1 67.9 reduce-scatter.4

commit v6 on v5

--- a/solution.py
+++ b/solution.py
@@ -121,8 +121,9 @@
 
     def step(kv_ref, count, size):
         s = dot_nt(kv_ref[:size, :LANES], qb)
-        key = lax.broadcasted_iota(jnp.int32, s.shape, 0)
-        s = jnp.where(key < count, s, -1e30)
+        if count is not None:
+            key = lax.broadcasted_iota(jnp.int32, s.shape, 0)
+            s = jnp.where(key < count, s, -1e30)
         m_old = m_s[...]
         m_new = jnp.maximum(m_old, jnp.max(s, axis=0, keepdims=True))
         scale = jnp.exp(m_old - m_new)
@@ -134,7 +135,11 @@
     for at, kv_ref in enumerate((kv0, kv1, kv2, kv3)):
         count = n_ref[4 * image + at]
 
-        @pl.when(count > TAIL)
+        @pl.when(count >= kv_ref.shape[0])
+        def _():
+            step(kv_ref, None, kv_ref.shape[0])
+
+        @pl.when((count > TAIL) & (count < kv_ref.shape[0]))
         def _():
             step(kv_ref, count, kv_ref.shape[0])
 
@@ -163,8 +168,10 @@
     def step(kv_ref, out_ref, slot, count, size):
         k = kv_ref[:size, :LANES]
         s = dot_nt(k, qb)
-        key = lax.broadcasted_iota(jnp.int32, s.shape, 0)
-        p = jnp.where(key < count, jnp.exp(s - lse), 0.0)
+        p = jnp.exp(s - lse)
+        if count is not None:
+            key = lax.broadcasted_iota(jnp.int32, s.shape, 0)
+            p = jnp.where(key < count, p, 0.0)
         dp = dot_nt(kv_ref[:size, LANES:], dob)
         ds = (p * (dp - delta)).astype(BF)
         out_ref[slot, :size, LANES:] = dot_nn(p.astype(BF), dob).astype(BF)
@@ -178,7 +185,11 @@
         out_ref = (keep_ref, send_ref)[at % 2]
         slot = at // 2
 
-        @pl.when(count > TAIL)
+        @pl.when(count >= kv_ref.shape[0])
+        def _():
+            step(kv_ref, out_ref, slot, None, kv_ref.shape[0])
+
+        @pl.when((count > TAIL) & (count < kv_ref.shape[0]))
         def _():
             step(kv_ref, out_ref, slot, count, kv_ref.shape[0])
 
@@ -595,7 +606,7 @@
             [image_of(i, rows, width), line, qkv_spec, rope_spec],
             [act, act_half, whole(rows, 2 * half)],
             name="qkv",
-            mib=14,
+            mib=10,
             flops=2 * rows * width * 3 * half,
             moved=6 * width * half + 8 * block_mb,
         )(tokens, ln1, full_qkv, tables)
@@ -619,7 +630,7 @@
                 pltpu.VMEM((LANES, 2 * rows), F32),
             ],
             name="attend",
-            mib=8,
+            mib=6,
             grid=half // LANES,
             flops=16 * rows * 4 * rows * half,
             moved=12 * block_mb,
@@ -657,7 +668,7 @@
             pltpu.SemaphoreType.DMA((4,)),
         ],
         name="middle",
-        mib=36,
+        mib=30,
         grid=images,
         flops=2 * images * rows * width * (width + 3 * ffp),
         moved=2 * width * (width + 3 * ffp) + images * (12 * block_mb + 6 * rows * ffp),
@@ -685,7 +696,7 @@
                 pltpu.SemaphoreType.DMA((3,)),
             ],
             name="ffn",
-            mib=26,
+            mib=20,
             flops=2 * rows * width * 3 * ffp,
             moved=6 * width * ffp + 12 * rows * ffp + 4 * block_mb,
         )(stats, stats_x, gate, up, dm, fgain, rest)
@@ -737,7 +748,7 @@
                 pltpu.SemaphoreType.DMA((1,)),
             ],
             name="attn_norm_back",
-            mib=18,
+            mib=14,
             flops=2 * rows * width * width,
             moved=2 * width * width + 16 * block_mb,
         )(valid, s["dh2"], s["dh2x"], x1, cotangent, ln2, s["o"], s["ox"], again, rest)
@@ -752,7 +763,7 @@
             [pltpu.VMEM((LANES, 2 * rows), F32)],
             grid=half // LANES,
             name="attend_back",
-            mib=12,
+            mib=9,
             flops=40 * rows * 4 * rows * half,
             moved=20 * block_mb,
         )(all_counts, s["q"], s["kv"], s["kvc"], s["kvf"], s["kvx"], s["o"], s["do"], s["lse"], tables)
@@ -774,7 +785,7 @@
             ],
             [whole(rows, 2 * half), act],
             name="qkv_back",
-            mib=14,
+            mib=10,
             flops=2 * rows * width * 3 * half,
             moved=6 * width * half + 10 * block_mb,
         )(s["keep"], s["recv"], s["far"], s["dq"], tables, full_qkv)

time: 464 us -> 464 us (level)
  Pallas kernels: 177 us -> 161 us
  starting transfers between devices: 28.9 us -> 41.1 us
    ppermute x4, starting transfers between devices: 0.03 us -> 9.17 us  [everywhere(): value = value + lax.ppermute(value, 'shard', pair_perm(shards, step))]
    pallas_call x3, Pallas kernels: 42.4 us -> 34 us  [attention_back(): call(functools.partial(attend_back_kernel, image=i), (shape(rows, half),...]
    pallas_call x3, Pallas kernels: 35.3 us -> 27.5 us  [local(): call(functools.partial(attend_kernel, image=i), (shape(rows, half), shape...]
    ppermute x4, waiting for transfers between devices: 11.9 us -> 5.54 us  [everywhere(): value = value + lax.ppermute(value, 'shard', pair_perm(shards, step))]
    reduce_scatter x1, waiting for transfers between devices: 0.01 us -> 5.53 us  [local(): own_ffn = lax.psum_scatter(grads_ffn, both, scatter_dimension=0, tiled=True)]
    unnamed x131 -> x135, local copies, waits for them, and re-layouts: 30.2 us -> 30.1 us
  transfers between devices with their start and end apart: 49 -> 49, of which waited for: 22 -> 24; matrix products, arithmetic and copies ran while one was open for 4% -> 4% of each run, Pallas kernels for 33% -> 30%
where the time goes in v6:
time: 464 us; the launch traced here: 455 us
  waiting for transfers between devices  180 us (39%)
  Pallas kernels  161 us (35%)
  starting transfers between devices  41.1 us (9%)
  local copies, waits for them, and re-layouts  40 us (9%)
  between operations  15.2 us (3%)
  other arithmetic  9.23 us (2%)
  blocking collectives  8.88 us (2%)
    ppermute x10, waiting for transfers between devices, far(): return lax.ppermute(value, 'far', swap_pair)  90.6 us
    all_gather x1, waiting for transfers between devices, local(): full_qkv = lax.all_gather(qkv_part, both, axis=1, tiled=True)  37 us
    pallas_call x3, Pallas kernels, attention_back(): call(functools.partial(attend_back_kernel, image=i), (shape(rows, half),...  34 us
    ppermute x15, waiting for transfers between devices, swap(): return lax.ppermute(value, 'tp', swap_tp)  32 us
    unnamed x135, local copies, waits for them, and re-layouts  30.1 us
    pallas_call x3, Pallas kernels, local(): call(functools.partial(attend_kernel, image=i), (shape(rows, half), shape...  27.5 us
    pallas_call x1, Pallas kernels, local(): call(middle_kernel, (shape(images, rows, width, dtype=F32), shape(images,...  20 us
    pallas_call x3, Pallas kernels, local(): call(functools.partial(ffn_kernel, total=ff_total), (shape(rows, ffp), sh...  18.7 us
  transfers between devices with their start and end apart: 49, of which 24 were waited for; matrix products, arithmetic and copies ran while one was open for 4% of the time, Pallas kernels for 30%

profile of v6, /device:TPU:0, one launch (start us, length us, event | category | flops | bytes accessed | tf_op | source)
XLA Modules:
  0.0 454.6 jit_solution(9156649518146197224)
XLA Ops:
  10.2 3.0 collective-permute-start.13
  14.4 1.9 constant_dynamic-slice_fusion.1
  21.8 37.0 %all-gather.3.cloned.1.call-done.w_ref = bf16[3,1024,512]{2,1,0:T(8,128)(2,1)} async-done(((bf16[3,64,512]{2,1,0:T(8,128)(2,1)}), bf16[3,1024,512]{2,1,0:T(8,128)(2,1)}) %all-gather.3.cloned.1.call-update) | async-done | bytes 3145744 | tf_op jit(solution)/shard_map/all_gather | solution.py:560
  60.7 2.5 qkv.3
  68.5 20.5 %collective-permute-done.1.kv2 = bf16[320,1024]{1,0:T(8,128)(2,1)} collective-permute-done((bf16[320,1024]{1,0:T(8,128)(2,1)}, bf16[320,1024]{1,0:T(8,128)(2,1)}, u32[]{:S(2)}, u32[]{:S(2)}) %collective-permute-start.1) | collective-permute-done | bytes 655392 | tf_op jit(solution)/shard_map/ppermute | solution.py:548
  89.1 2.5 qkv.5
  94.4 8.7 %collective-permute-done.5.kv2 = bf16[320,1024]{1,0:T(8,128)(2,1)} collective-permute-done((bf16[320,1024]{1,0:T(8,128)(2,1)S(1)}, bf16[320,1024]{1,0:T(8,128)(2,1)}, u32[]{:S(2)}, u32[]{:S(2)}) %collective-permute-start.5) | collective-permute-done | bytes 655392 | tf_op jit(solution)/shard_map/ppermute | solution.py:548
  103.1 8.0 %attend.3 = (bf16[320,512]{1,0:T(8,128)(2,1)S(1)}, f32[4,1,640]{2,1,0:T(1,128)S(1)}) custom-call(s32[12]{0:T(128)S(1)} %min.12.n_ref, bf16[320,512]{1,0:T(8,128)(2,1)} %copy-done.26, bf16[320,1024]{1,0:T(8,128)(2,1)} %get-tuple-element.120.kv0, bf16[320,1024]{1,0:T(8,128)(2,1)} %collective-permute-done.kv1, bf16[320,1024]{1,0:T(8,128)(2,1)} %collective-permute-done.1.kv2, ...), custom_call_target="tpu_custom_call" | custom-call | flops 209715200 | bytes 245760 | tf_op jit(solution)/shard_map/attend/pallas_call | solution.py:622
  111.2 17.6 %collective-permute-done.3.kv2 = bf16[320,1024]{1,0:T(8,128)(2,1)} collective-permute-done((bf16[320,1024]{1,0:T(8,128)(2,1)}, bf16[320,1024]{1,0:T(8,128)(2,1)}, u32[]{:S(2)}, u32[]{:S(2)}) %collective-permute-start.3) | collective-permute-done | bytes 655392 | tf_op jit(solution)/shard_map/ppermute | solution.py:548
  131.1 6.9 %attend.4 = (bf16[320,512]{1,0:T(8,128)(2,1)S(1)}, f32[4,1,640]{2,1,0:T(1,128)S(1)}) custom-call(s32[12]{0:T(128)S(1)} %min.12.n_ref, bf16[320,512]{1,0:T(8,128)(2,1)} %copy-done.25, bf16[320,1024]{1,0:T(8,128)(2,1)} %copy-done.17, bf16[320,1024]{1,0:T(8,128)(2,1)} %collective-permute-done.4.kv1, bf16[320,1024]{1,0:T(8,128)(2,1)} %collective-permute-done.5.kv2, ...), custom_call_target="tpu_custom_call" | custom-call | flops 209715200 | bytes 245760 | tf_op jit(solution)/shard_map/attend/pallas_call | solution.py:622
  139.6 12.6 %attend.5 = (bf16[320,512]{1,0:T(8,128)(2,1)S(1)}, f32[4,1,640]{2,1,0:T(1,128)S(1)}) custom-call(s32[12]{0:T(128)S(1)} %min.12.n_ref, bf16[320,512]{1,0:T(8,128)(2,1)} %copy-done.24, bf16[320,1024]{1,0:T(8,128)(2,1)} %get-tuple-element.121.kv0, bf16[320,1024]{1,0:T(8,128)(2,1)} %collective-permute-done.7.kv1, bf16[320,1024]{1,0:T(8,128)(2,1)} %collective-permute-done.3.kv2, ...), custom_call_target="tpu_custom_call" | custom-call | flops 209715200 | bytes 245760 | tf_op jit(solution)/shard_map/attend/pallas_call | solution.py:622
  154.3 7.3 %collective-permute-done.11.other_ref2.other_ref = bf16[320,512]{1,0:T(8,128)(2,1)} collective-permute-done((bf16[320,512]{1,0:T(8,128)(2,1)S(1)}, bf16[320,512]{1,0:T(8,128)(2,1)}, u32[]{:S(2)}, u32[]{:S(2)}) %collective-permute-start.11) | collective-permute-done | bytes 327712 | tf_op jit(solution)/shard_map/ppermute | solution.py:542
  161.6 3.7 all-gather.5.cloned.1.call-done.w_ref
  166.9 20.0 %middle.1 = (f32[3,320,1024]{2,1,0:T(8,128)S(1)}, bf16[3,320,1024]{2,1,0:T(8,128)(2,1)S(1)}, bf16[3,320,1408]{2,1,0:T(8,128)(2,1)S(1)}, bf16[3,320,1408]{2,1,0:T...) custom-call(s32[4]{0:T(128)S(1)} %get-tuple-element.263.sc_ref, ...), custom_call_target="tpu_custom_call" | custom-call | flops 644874240 | bytes 1915904 | tf_op jit(solution)/shard_map/middle/pallas_call | solution.py:644
  188.4 2.5 collective-permute-done.14.sb_ref
  190.9 6.2 %ffn.5 = (bf16[320,1408]{1,0:T(8,128)(2,1)S(1)}, bf16[320,1408]{1,0:T(8,128)(2,1)S(1)}, bf16[320,1408]{1,0:T(8,128)(2,1)S(1)}, bf16[320,1024]{1,0:T(8,128)(2,1)S...) custom-call(f32[3,8,384]{2,1,0:T(8,128)S(1)} %get-tuple-element.130.sa_ref, ...), custom_call_target="tpu_custom_call" | custom-call | flops 173015040 | bytes 960512 | tf_op jit(solution)/shard_map/ffn/pallas_call | solution.py:679
  198.6 6.2 %ffn.3 = (bf16[320,1408]{1,0:T(8,128)(2,1)S(1)}, bf16[320,1408]{1,0:T(8,128)(2,1)S(1)}, bf16[320,1408]{1,0:T(8,128)(2,1)S(1)}, bf16[320,1024]{1,0:T(8,128)(2,1)S...) custom-call(f32[3,8,384]{2,1,0:T(8,128)S(1)} %get-tuple-element.130.sa_ref, ...), custom_call_target="tpu_custom_call" | custom-call | flops 173015040 | bytes 960512 | tf_op jit(solution)/shard_map/ffn/pallas_call | solution.py:679
  206.2 6.4 %ffn.4 = (bf16[320,1408]{1,0:T(8,128)(2,1)S(1)}, bf16[320,1408]{1,0:T(8,128)(2,1)S(1)}, bf16[320,1408]{1,0:T(8,128)(2,1)S(1)}, bf16[320,1024]{1,0:T(8,128)(2,1)S...) custom-call(f32[3,8,384]{2,1,0:T(8,128)S(1)} %get-tuple-element.130.sa_ref, ...), custom_call_target="tpu_custom_call" | custom-call | flops 173015040 | bytes 960512 | tf_op jit(solution)/shard_map/ffn/pallas_call | solution.py:679
  214.9 12.2 %grads_ffn.1 = bf16[1024,4224]{1,0:T(8,128)(2,1)} custom-call(s32[4]{0:T(128)S(1)} %get-tuple-element.264.n_ref, bf16[3,320,1024]{2,1,0:T(8,128)(2,1)S(1)} %get-tuple-element.142.refs_0_, bf16[320,1408]{1,0:T(8,128)(2,1)S(1)} %get-tuple-element.143.refs_1_, bf16[320,1408]{1,0:T(8,128)(2,1)S(1)} %get-tuple-element.144.refs_2_, ...), custom_call_target="tpu_custom_call" | custom-call | flops 519045120 | bytes 1081344 | tf_op jit(solution)/shard_map/grads_ffn/pallas_call | solution.py:708
  229.0 2.1 copy-done.3
  232.6 5.5 %attn_norm_back.3 = (f32[320,1024]{1,0:T(8,128)S(1)}, bf16[320,1024]{1,0:T(8,128)(2,1)S(1)}, bf16[320,512]{1,0:T(8,128)(2,1)S(1)}, f32[1,1024]{1,0:T(1,128)S(1)}, f32[1,512]{1,0:T(1,128)S(1)}) custom-call(s32[4]{0:T(128)S(1)} %get-tuple-element.263.sc_ref, bf16[320,1024]{1,0:T(8,128)(2,1)} %get-tuple-element.134.dha_ref, ...), custom_call_target="tpu_custom_call" | custom-call | flops 41943040 | bytes 458752 | tf_op jit(solution)/shard_map/attn_norm_back/pallas_call | solution.py:732
  241.2 10.4 %attend_back.3 = (bf16[320,512]{1,0:T(8,128)(2,1)S(1)}, bf16[2,320,1024]{2,1,0:T(8,128)(2,1)S(1)}, bf16[2,320,1024]{2,1,0:T(8,128)(2,1)S(1)}) custom-call(s32[12]{0:T(128)S(1)} %min.12.n_ref, bf16[320,512]{1,0:T(8,128)(2,1)} %copy-done.26, bf16[320,1024]{1,0:T(8,128)(2,1)} %get-tuple-element.120.kv0, bf16[320,1024]{1,0:T(8,128)(2,1)} %collective-permute-done.kv1, ...), custom_call_target="tpu_custom_call" | custom-call | flops 524288000 | bytes 409600 | tf_op jit(solution)/shard_map/attend_back/pallas_call | solution.py:758
  253.4 5.9 %attn_norm_back.4 = (f32[320,1024]{1,0:T(8,128)S(1)}, bf16[320,1024]{1,0:T(8,128)(2,1)S(1)}, bf16[320,512]{1,0:T(8,128)(2,1)S(1)}, f32[1,1024]{1,0:T(1,128)S(1)}, f32[1,512]{1,0:T(1,128)S(1)}) custom-call(s32[4]{0:T(128)S(1)} %get-tuple-element.263.sc_ref, bf16[320,1024]{1,0:T(8,128)(2,1)} %get-tuple-element.140.dha_ref, ...), custom_call_target="tpu_custom_call" | custom-call | flops 41943040 | bytes 458752 | tf_op jit(solution)/shard_map/attn_norm_back/pallas_call | solution.py:732
  260.2 9.0 %attend_back.4 = (bf16[320,512]{1,0:T(8,128)(2,1)S(1)}, bf16[2,320,1024]{2,1,0:T(8,128)(2,1)S(1)}, bf16[2,320,1024]{2,1,0:T(8,128)(2,1)S(1)}) custom-call(s32[12]{0:T(128)S(1)} %min.12.n_ref, bf16[320,512]{1,0:T(8,128)(2,1)} %copy-done.25, bf16[320,1024]{1,0:T(8,128)(2,1)} %copy-done.17, bf16[320,1024]{1,0:T(8,128)(2,1)} %collective-permute-done.4.kv1, ...), custom_call_target="tpu_custom_call" | custom-call | flops 524288000 | bytes 409600 | tf_op jit(solution)/shard_map/attend_back/pallas_call | solution.py:758
  269.4 5.9 %attn_norm_back.5 = (f32[320,1024]{1,0:T(8,128)S(1)}, bf16[320,1024]{1,0:T(8,128)(2,1)S(1)}, bf16[320,512]{1,0:T(8,128)(2,1)S(1)}, f32[1,1024]{1,0:T(1,128)S(1)}, f32[1,512]{1,0:T(1,128)S(1)}) custom-call(s32[4]{0:T(128)S(1)} %get-tuple-element.263.sc_ref, bf16[320,1024]{1,0:T(8,128)(2,1)S(1)} %get-tuple-element.141.dha_ref, ...), custom_call_target="tpu_custom_call" | custom-call | flops 41943040 | bytes 458752 | tf_op jit(solution)/shard_map/attn_norm_back/pallas_call | solution.py:732
  276.3 2.4 collective-permute-done.19.far_ref
  278.7 14.6 %attend_back.5 = (bf16[320,512]{1,0:T(8,128)(2,1)S(1)}, bf16[2,320,1024]{2,1,0:T(8,128)(2,1)S(1)}, bf16[2,320,1024]{2,1,0:T(8,128)(2,1)S(1)}) custom-call(s32[12]{0:T(128)S(1)} %min.12.n_ref, bf16[320,512]{1,0:T(8,128)(2,1)} %copy-done.24, bf16[320,1024]{1,0:T(8,128)(2,1)} %get-tuple-element.121.kv0, bf16[320,1024]{1,0:T(8,128)(2,1)} %collective-permute-done.7.kv1, ...), custom_call_target="tpu_custom_call" | custom-call | flops 524288000 | bytes 409600 | tf_op jit(solution)/shard_map/attend_back/pallas_call | solution.py:758
  299.7 24.5 %collective-permute-done.23.far_ref = bf16[320,1024]{1,0:T(8,128)(2,1)S(1)} collective-permute-done((bf16[320,1024]{1,0:T(8,128)(2,1)S(1)}, bf16[320,1024]{1,0:T(8,128)(2,1)S(1)}, u32[]{:S(2)}, u32[]{:S(2)}) %collective-permute-start.23) | collective-permute-done | bytes 655392 | tf_op jit(solution)/shard_map/ppermute | solution.py:548
  327.4 12.1 %collective-permute-done.21.far_ref = bf16[320,1024]{1,0:T(8,128)(2,1)S(1)} collective-permute-done((bf16[320,1024]{1,0:T(8,128)(2,1)S(1)}, bf16[320,1024]{1,0:T(8,128)(2,1)S(1)}, u32[]{:S(2)}, u32[]{:S(2)}) %collective-permute-start.21) | collective-permute-done | bytes 655392 | tf_op jit(solution)/shard_map/ppermute | solution.py:548
  341.9 5.9 %grads_qkv.1 = (bf16[512,2048]{1,0:T(8,128)(2,1)S(1)}, bf16[512,2048]{1,0:T(8,128)(2,1)S(1)}) custom-call(s32[4]{0:T(128)S(1)} %get-tuple-element.264.n_ref, bf16[320,1024]{1,0:T(8,128)(2,1)S(1)} %copy-done.39, bf16[320,1024]{1,0:T(8,128)(2,1)S(1)} %copy-done.41, bf16[320,1024]{1,0:T(8,128)(2,1)S(1)} %copy-done.43, ...), custom_call_target="tpu_custom_call" | custom-call | flops 251658240 | bytes 524288 | tf_op jit(solution)/shard_map/grads_qkv/pallas_call | solution.py:708
  347.8 4.1 collective-permute-done.26
  352.0 2.1 add_convert_fusion
  354.1 5.5 %reduce-scatter.3.cloned.1.call-done = bf16[64,4224]{1,0:T(8,128)(2,1)} async-done(((bf16[1024,4224]{1,0:T(8,128)(2,1)}), bf16[64,4224]{1,0:T(8,128)(2,1)}) %reduce-scatter.3.cloned.1.call-update) | async-done | bytes 540688 | tf_op jit(solution)/shard_map/reduce_scatter | solution.py:857
  365.6 12.0 %collective-permute-done.28.db_ref = bf16[320,1024]{1,0:T(8,128)(2,1)S(1)} collective-permute-done((bf16[320,1024]{1,0:T(8,128)(2,1)}, bf16[320,1024]{1,0:T(8,128)(2,1)S(1)}, u32[]{:S(2)}, u32[]{:S(2)}) %collective-permute-start.28) | collective-permute-done | bytes 655392 | tf_op jit(solution)/shard_map/ppermute | solution.py:542
  382.4 1.9 tokens_back.4
  384.3 7.3 %collective-permute-done.27.db_ref = bf16[320,1024]{1,0:T(8,128)(2,1)S(1)} collective-permute-done((bf16[320,1024]{1,0:T(8,128)(2,1)}, bf16[320,1024]{1,0:T(8,128)(2,1)S(1)}, u32[]{:S(2)}, u32[]{:S(2)}) %collective-permute-start.27) | collective-permute-done | bytes 655392 | tf_op jit(solution)/shard_map/ppermute | solution.py:542
  396.6 2.1 collective-permute-done.36
  400.3 2.0 collective-permute-done.32
  402.3 2.5 collective-permute-start.37
  406.4 2.0 collective-permute-start.33
  410.0 2.3 collective-permute-start.38
  412.4 2.3 collective-permute-done.38
  414.7 2.3 collective-permute-start.34
  418.8 2.1 copy-done.5
  422.0 2.2 mixed.4.rest_0_
  424.2 2.2 mixed.5
  428.9 3.0 finish.1
  434.7 8.9 %all_gather.11 = bf16[256,1536]{1,0:T(8,128)(2,1)S(1)} all-gather(bf16[64,1536]{1,0:T(8,128)(2,1)S(1)} %slice.63), channel_id=1, replica_groups=mesh['shard'=4,'far'=2,'near'=2,'tp'=2] {'far','near'}, dimensions={0}, use_global_device_ids=true | all-gather | bytes 983040 | tf_op jit(solution)/shard_map/all_gather | solution.py:901
  (271 shorter events, 88.5 us)
Async XLA Ops:
  7.2 51.6 %all-gather.3.cloned.1.call-start = ((), (), s32[]{:S(2)}) async-start(), calls=%async_computation.2 | async-start | bytes 3342336 | tf_op jit(solution)/shard_map/all_gather | solution.py:560
  9.0 156.3 %all-gather.5.cloned.1.call-start = ((), (), s32[]{:S(2)}) async-start(), calls=%async_computation.3 | async-start | bytes 11419648 | tf_op jit(solution)/shard_map/all_gather | solution.py:574
  10.2 8.0 %collective-permute-start.13 = (bf16[64,512]{1,0:T(8,128)(2,1)S(1)}, bf16[64,512]{1,0:T(8,128)(2,1)S(1)}, u32[]{:S(2)}, u32[]{:S(2)}) collective-permute-start(bf16[64,512]{1,0:T(8,128)(2,1)S(1)} %bitcast.48), channel_id=1, source_target_pairs={{0,1},{1,0},{2,3},{3,2},{4,5},{5,4},{6,7},{7,6},{8,9},{9,8},{10,11... | collective-permute-start | bytes 196616 | tf_op jit(solution)/shard_map/ppermute | solution.py:542
  19.2 340.4 %reduce-scatter.3.cloned.1.call-start = ((), (), s32[]{:S(2)}) async-start(), calls=%async_computation.4 | async-start | bytes 9191424 | tf_op jit(solution)/shard_map/reduce_scatter | solution.py:857
  64.0 25.1 %collective-permute-start.1 = (bf16[320,1024]{1,0:T(8,128)(2,1)}, bf16[320,1024]{1,0:T(8,128)(2,1)}, u32[]{:S(2)}, u32[]{:S(2)}) collective-permute-start(bf16[320,1024]{1,0:T(8,128)(2,1)} %get-tuple-element.120.kv0), channel_id=1, source_target_pairs={{0,4},{4,0},{1,5},{5,1},{2,6},{6,2},{3,7},{7,3},{8,12},{12,8},{9,1... | collective-permute-start | bytes 1966088 | tf_op jit(solution)/shard_map/ppermute | solution.py:548
  64.5 29.5 %collective-permute-start = (bf16[320,1024]{1,0:T(8,128)(2,1)}, bf16[320,1024]{1,0:T(8,128)(2,1)}, u32[]{:S(2)}, u32[]{:S(2)}) collective-permute-start(bf16[320,1024]{1,0:T(8,128)(2,1)} %get-tuple-element.120.kv0), channel_id=1, source_target_pairs={{0,2},{2,0},{1,3},{3,1},{4,6},{6,4},{5,7},{7,5},{8,10},{10,8},{9,1... | collective-permute-start | bytes 1966088 | tf_op jit(solution)/shard_map/ppermute | solution.py:545
  67.1 36.0 %collective-permute-start.5 = (bf16[320,1024]{1,0:T(8,128)(2,1)S(1)}, bf16[320,1024]{1,0:T(8,128)(2,1)}, u32[]{:S(2)}, u32[]{:S(2)}) collective-permute-start(bf16[320,1024]{1,0:T(8,128)(2,1)S(1)} %get-tuple-element.125.kv0), channel_id=1, source_target_pairs={{0,4},{4,0},{1,5},{5,1},{2,6},{6,2},{3,7},{7,3},{8,12},{12,8},{9,1... | collective-permute-start | bytes 1966088 | tf_op jit(solution)/shard_map/ppermute | solution.py:548
  89.1 14.1 %collective-permute-start.2 = (bf16[320,1024]{1,0:T(8,128)(2,1)}, bf16[320,1024]{1,0:T(8,128)(2,1)}, u32[]{:S(2)}, u32[]{:S(2)}) collective-permute-start(bf16[320,1024]{1,0:T(8,128)(2,1)} %collective-permute-done.1.kv2), channel_id=1, source_target_pairs={{0,2},{2,0},{1,3},{3,1},{4,6},{6,4},{5,7},{7,5},{8,10},{10,8},{9,1... | collective-permute-start | bytes 1966088 | tf_op jit(solution)/shard_map/ppermute | solution.py:545
  93.1 35.7 %collective-permute-start.3 = (bf16[320,1024]{1,0:T(8,128)(2,1)}, bf16[320,1024]{1,0:T(8,128)(2,1)}, u32[]{:S(2)}, u32[]{:S(2)}) collective-permute-start(bf16[320,1024]{1,0:T(8,128)(2,1)} %get-tuple-element.121.kv0), channel_id=1, source_target_pairs={{0,4},{4,0},{1,5},{5,1},{2,6},{6,2},{3,7},{7,3},{8,12},{12,8},{9,1... | collective-permute-start | bytes 1966088 | tf_op jit(solution)/shard_map/ppermute | solution.py:548
  93.9 45.7 %collective-permute-start.7 = (bf16[320,1024]{1,0:T(8,128)(2,1)}, bf16[320,1024]{1,0:T(8,128)(2,1)}, u32[]{:S(2)}, u32[]{:S(2)}) collective-permute-start(bf16[320,1024]{1,0:T(8,128)(2,1)} %get-tuple-element.121.kv0), channel_id=1, source_target_pairs={{0,2},{2,0},{1,3},{3,1},{4,6},{6,4},{5,7},{7,5},{8,10},{10,8},{9,1... | collective-permute-start | bytes 1966088 | tf_op jit(solution)/shard_map/ppermute | solution.py:545
  94.1 36.4 %collective-permute-start.4 = (bf16[320,1024]{1,0:T(8,128)(2,1)S(1)}, bf16[320,1024]{1,0:T(8,128)(2,1)}, u32[]{:S(2)}, u32[]{:S(2)}) collective-permute-start(bf16[320,1024]{1,0:T(8,128)(2,1)S(1)} %get-tuple-element.125.kv0), channel_id=1, source_target_pairs={{0,2},{2,0},{1,3},{3,1},{4,6},{6,4},{5,7},{7,5},{8,10},{10,8},{9,1... | collective-permute-start | bytes 1966088 | tf_op jit(solution)/shard_map/ppermute | solution.py:545
  103.1 28.0 %collective-permute-start.6 = (bf16[320,1024]{1,0:T(8,128)(2,1)}, bf16[320,1024]{1,0:T(8,128)(2,1)}, u32[]{:S(2)}, u32[]{:S(2)}) collective-permute-start(bf16[320,1024]{1,0:T(8,128)(2,1)} %collective-permute-done.5.kv2), channel_id=1, source_target_pairs={{0,2},{2,0},{1,3},{3,1},{4,6},{6,4},{5,7},{7,5},{8,10},{10,8},{9,1... | collective-permute-start | bytes 1966088 | tf_op jit(solution)/shard_map/ppermute | solution.py:545
  128.8 10.7 %collective-permute-start.8 = (bf16[320,1024]{1,0:T(8,128)(2,1)}, bf16[320,1024]{1,0:T(8,128)(2,1)}, u32[]{:S(2)}, u32[]{:S(2)}) collective-permute-start(bf16[320,1024]{1,0:T(8,128)(2,1)} %collective-permute-done.3.kv2), channel_id=1, source_target_pairs={{0,2},{2,0},{1,3},{3,1},{4,6},{6,4},{5,7},{7,5},{8,10},{10,8},{9,1... | collective-permute-start | bytes 1966088 | tf_op jit(solution)/shard_map/ppermute | solution.py:545
  128.8 24.0 %collective-permute-start.12 = (f32[1,512]{1,0:T(1,128)S(1)}, f32[1,512]{1,0:T(1,128)S(1)}, u32[]{:S(2)}, u32[]{:S(2)}) collective-permute-start(f32[1,512]{1,0:T(1,128)S(1)} %bitcast.55), channel_id=1, source_target_pairs={{0,1},{1,0},{2,3},{3,2},{4,5},{5,4},{6,7},{7,6},{8,9},{9,8},{10,11... | collective-permute-start | bytes 6152 | tf_op jit(solution)/shard_map/ppermute | solution.py:542
  130.5 22.3 %collective-permute-start.9 = (bf16[320,512]{1,0:T(8,128)(2,1)S(1)}, bf16[320,512]{1,0:T(8,128)(2,1)S(1)}, u32[]{:S(2)}, u32[]{:S(2)}) collective-permute-start(bf16[320,512]{1,0:T(8,128)(2,1)S(1)} %get-tuple-element.123.own_ref0.own_ref.o_ref), channel_id=1, source_target_pairs={{0,1},{1,0},{2,3},{3,2},{4,5},{5,4},{6,7},{7,6},{8,9},{9,8},{10,11... | collective-permute-start | bytes 983048 | tf_op jit(solution)/shard_map/ppermute | solution.py:542
  138.0 14.8 %collective-permute-start.10 = (bf16[320,512]{1,0:T(8,128)(2,1)S(1)}, bf16[320,512]{1,0:T(8,128)(2,1)S(1)}, u32[]{:S(2)}, u32[]{:S(2)}) collective-permute-start(bf16[320,512]{1,0:T(8,128)(2,1)S(1)} %get-tuple-element.126.own_ref1.own_ref.o_ref), channel_id=1, source_target_pairs={{0,1},{1,0},{2,3},{3,2},{4,5},{5,4},{6,7},{7,6},{8,9},{9,8},{10,11... | collective-permute-start | bytes 983048 | tf_op jit(solution)/shard_map/ppermute | solution.py:542
  152.2 9.4 %collective-permute-start.11 = (bf16[320,512]{1,0:T(8,128)(2,1)S(1)}, bf16[320,512]{1,0:T(8,128)(2,1)}, u32[]{:S(2)}, u32[]{:S(2)}) collective-permute-start(bf16[320,512]{1,0:T(8,128)(2,1)S(1)} %get-tuple-element.129.own_ref2.own_ref.o_ref), channel_id=1, source_target_pairs={{0,1},{1,0},{2,3},{3,2},{4,5},{5,4},{6,7},{7,6},{8,9},{9,8},{10,11... | collective-permute-start | bytes 983048 | tf_op jit(solution)/shard_map/ppermute | solution.py:542
  186.9 4.0 collective-permute-start.14
  197.1 43.0 %collective-permute-start.17 = (bf16[320,1024]{1,0:T(8,128)(2,1)S(1)}, bf16[320,1024]{1,0:T(8,128)(2,1)}, u32[]{:S(2)}, u32[]{:S(2)}) collective-permute-start(bf16[320,1024]{1,0:T(8,128)(2,1)S(1)} %get-tuple-element.141.dha_ref), channel_id=1, source_target_pairs={{0,1},{1,0},{2,3},{3,2},{4,5},{5,4},{6,7},{7,6},{8,9},{9,8},{10,11... | collective-permute-start | bytes 1966088 | tf_op jit(solution)/shard_map/ppermute | solution.py:542
  205.6 23.3 %collective-permute-start.15 = (bf16[320,1024]{1,0:T(8,128)(2,1)}, bf16[320,1024]{1,0:T(8,128)(2,1)}, u32[]{:S(2)}, u32[]{:S(2)}) collective-permute-start(bf16[320,1024]{1,0:T(8,128)(2,1)} %get-tuple-element.134.dha_ref), channel_id=1, source_target_pairs={{0,1},{1,0},{2,3},{3,2},{4,5},{5,4},{6,7},{7,6},{8,9},{9,8},{10,11... | collective-permute-start | bytes 1966088 | tf_op jit(solution)/shard_map/ppermute | solution.py:542
  213.5 27.6 %collective-permute-start.16 = (bf16[320,1024]{1,0:T(8,128)(2,1)}, bf16[320,1024]{1,0:T(8,128)(2,1)}, u32[]{:S(2)}, u32[]{:S(2)}) collective-permute-start(bf16[320,1024]{1,0:T(8,128)(2,1)} %get-tuple-element.140.dha_ref), channel_id=1, source_target_pairs={{0,1},{1,0},{2,3},{3,2},{4,5},{5,4},{6,7},{7,6},{8,9},{9,8},{10,11... | collective-permute-start | bytes 1966088 | tf_op jit(solution)/shard_map/ppermute | solution.py:542
  241.1 190.9 %reduce-scatter.5.cloned.1.call-start = ((), (), s32[]{:S(2)}) async-start(), calls=%async_computation.5 | async-start | bytes 2359296 | tf_op jit(solution)/shard_map/reduce_scatter | solution.py:869
  251.6 7.8 %collective-permute-start.18 = (bf16[2,320,1024]{2,1,0:T(8,128)(2,1)S(1)}, bf16[2,320,1024]{2,1,0:T(8,128)(2,1)S(1)}, u32[]{:S(2)}, u32[]{:S(2)}) collective-permute-start(bf16[2,320,1024]{2,1,0:T(8,128)(2,1)S(1)} %get-tuple-element.158), channel_id=1, source_target_pairs={{0,2},{2,0},{1,3},{3,1},{4,6},{6,4},{5,7},{7,5},{8,10},{10,8},{9,1... | collective-permute-start | bytes 3932168 | tf_op jit(solution)/shard_map/ppermute | solution.py:545
  259.6 19.1 %collective-permute-start.19 = (bf16[320,1024]{1,0:T(8,128)(2,1)S(1)}, bf16[320,1024]{1,0:T(8,128)(2,1)S(1)}, u32[]{:S(2)}, u32[]{:S(2)}) collective-permute-start(bf16[320,1024]{1,0:T(8,128)(2,1)S(1)} %fusion), channel_id=1, source_target_pairs={{0,4},{4,0},{1,5},{5,1},{2,6},{6,2},{3,7},{7,3},{8,12},{12,8},{9,1... | collective-permute-start | bytes 1966088 | tf_op jit(solution)/shard_map/ppermute | solution.py:548
  269.3 27.8 %collective-permute-start.22 = (bf16[2,320,1024]{2,1,0:T(8,128)(2,1)S(1)}, bf16[2,320,1024]{2,1,0:T(8,128)(2,1)S(1)}, u32[]{:S(2)}, u32[]{:S(2)}) collective-permute-start(bf16[2,320,1024]{2,1,0:T(8,128)(2,1)S(1)} %get-tuple-element.173), channel_id=1, source_target_pairs={{0,2},{2,0},{1,3},{3,1},{4,6},{6,4},{5,7},{7,5},{8,10},{10,8},{9,1... | collective-permute-start | bytes 3932168 | tf_op jit(solution)/shard_map/ppermute | solution.py:545
  293.3 4.8 %collective-permute-start.20 = (bf16[2,320,1024]{2,1,0:T(8,128)(2,1)S(1)}, bf16[2,320,1024]{2,1,0:T(8,128)(2,1)S(1)}, u32[]{:S(2)}, u32[]{:S(2)}) collective-permute-start(bf16[2,320,1024]{2,1,0:T(8,128)(2,1)S(1)} %get-tuple-element.171), channel_id=1, source_target_pairs={{0,2},{2,0},{1,3},{3,1},{4,6},{6,4},{5,7},{7,5},{8,10},{10,8},{9,1... | collective-permute-start | bytes 3932168 | tf_op jit(solution)/shard_map/ppermute | solution.py:545
  293.4 33.2 %collective-permute-start.24 = (bf16[320,1024]{1,0:T(8,128)(2,1)S(1)}, bf16[320,1024]{1,0:T(8,128)(2,1)S(1)}, u32[]{:S(2)}, u32[]{:S(2)}) collective-permute-start(bf16[320,1024]{1,0:T(8,128)(2,1)S(1)} %copy-done.34), channel_id=1, source_target_pairs={{0,1},{1,0},{2,3},{3,2},{4,5},{5,4},{6,7},{7,6},{8,9},{9,8},{10,11... | collective-permute-start | bytes 1966088 | tf_op jit(solution)/shard_map/ppermute | solution.py:542
  296.4 31.0 %collective-permute-start.25 = (bf16[320,1024]{1,0:T(8,128)(2,1)S(1)}, bf16[320,1024]{1,0:T(8,128)(2,1)S(1)}, u32[]{:S(2)}, u32[]{:S(2)}) collective-permute-start(bf16[320,1024]{1,0:T(8,128)(2,1)S(1)} %get-tuple-element.176.da_ref), channel_id=1, source_target_pairs={{0,1},{1,0},{2,3},{3,2},{4,5},{5,4},{6,7},{7,6},{8,9},{9,8},{10,11... | collective-permute-start | bytes 1966088 | tf_op jit(solution)/shard_map/ppermute | solution.py:542
  297.3 26.9 %collective-permute-start.23 = (bf16[320,1024]{1,0:T(8,128)(2,1)S(1)}, bf16[320,1024]{1,0:T(8,128)(2,1)S(1)}, u32[]{:S(2)}, u32[]{:S(2)}) collective-permute-start(bf16[320,1024]{1,0:T(8,128)(2,1)S(1)} %fusion.2), channel_id=1, source_target_pairs={{0,4},{4,0},{1,5},{5,1},{2,6},{6,2},{3,7},{7,3},{8,12},{12,8},{9,1... | collective-permute-start | bytes 1966088 | tf_op jit(solution)/shard_map/ppermute | solution.py:548
  298.3 41.2 %collective-permute-start.21 = (bf16[320,1024]{1,0:T(8,128)(2,1)S(1)}, bf16[320,1024]{1,0:T(8,128)(2,1)S(1)}, u32[]{:S(2)}, u32[]{:S(2)}) collective-permute-start(bf16[320,1024]{1,0:T(8,128)(2,1)S(1)} %fusion.1), channel_id=1, source_target_pairs={{0,4},{4,0},{1,5},{5,1},{2,6},{6,2},{3,7},{7,3},{8,12},{12,8},{9,1... | collective-permute-start | bytes 1966088 | tf_op jit(solution)/shard_map/ppermute | solution.py:548
  347.8 4.2 collective-permute-start.26
  359.6 17.9 %collective-permute-start.28 = (bf16[320,1024]{1,0:T(8,128)(2,1)}, bf16[320,1024]{1,0:T(8,128)(2,1)S(1)}, u32[]{:S(2)}, u32[]{:S(2)}) collective-permute-start(bf16[320,1024]{1,0:T(8,128)(2,1)} %copy-done.50), channel_id=1, source_target_pairs={{0,1},{1,0},{2,3},{3,2},{4,5},{5,4},{6,7},{7,6},{8,9},{9,8},{10,11... | collective-permute-start | bytes 1966088 | tf_op jit(solution)/shard_map/ppermute | solution.py:542
  361.2 30.4 %collective-permute-start.27 = (bf16[320,1024]{1,0:T(8,128)(2,1)}, bf16[320,1024]{1,0:T(8,128)(2,1)S(1)}, u32[]{:S(2)}, u32[]{:S(2)}) collective-permute-start(bf16[320,1024]{1,0:T(8,128)(2,1)} %copy-done.52), channel_id=1, source_target_pairs={{0,1},{1,0},{2,3},{3,2},{4,5},{5,4},{6,7},{7,6},{8,9},{9,8},{10,11... | collective-permute-start | bytes 1966088 | tf_op jit(solution)/shard_map/ppermute | solution.py:542
  361.7 16.6 %collective-permute-start.40 = (bf16[64,4224]{1,0:T(8,128)(2,1)}, bf16[64,4224]{1,0:T(8,128)(2,1)}, u32[]{:S(2)}, u32[]{:S(2)}) collective-permute-start(bf16[64,4224]{1,0:T(8,128)(2,1)} %reduce-scatter.3.cloned.1.call-done), channel_id=1, source_target_pairs={{0,4},{4,0},{1,5},{5,1},{2,6},{6,2},{3,7},{7,3},{8,12},{12,8},{9,1... | collective-permute-start | bytes 1622024 | tf_op jit(solution)/shard_map/ppermute | solution.py:548
  363.4 58.5 %collective-permute-start.30 = (bf16[320,1024]{1,0:T(8,128)(2,1)}, bf16[320,1024]{1,0:T(8,128)(2,1)}, u32[]{:S(2)}, u32[]{:S(2)}) collective-permute-start(bf16[320,1024]{1,0:T(8,128)(2,1)} %copy-done.31), channel_id=1, source_target_pairs={{0,1},{1,0},{2,3},{3,2},{4,5},{5,4},{6,7},{7,6},{8,9},{9,8},{10,11... | collective-permute-start | bytes 1966088 | tf_op jit(solution)/shard_map/ppermute | solution.py:542
  365.0 59.2 %collective-permute-start.29 = (bf16[320,1024]{1,0:T(8,128)(2,1)}, bf16[320,1024]{1,0:T(8,128)(2,1)}, u32[]{:S(2)}, u32[]{:S(2)}) collective-permute-start(bf16[320,1024]{1,0:T(8,128)(2,1)} %copy-done.29), channel_id=1, source_target_pairs={{0,1},{1,0},{2,3},{3,2},{4,5},{5,4},{6,7},{7,6},{8,9},{9,8},{10,11... | collective-permute-start | bytes 1966088 | tf_op jit(solution)/shard_map/ppermute | solution.py:542
  377.6 49.4 %collective-permute-start.39 = (bf16[64,4224]{1,0:T(8,128)(2,1)}, bf16[64,4224]{1,0:T(8,128)(2,1)}, u32[]{:S(2)}, u32[]{:S(2)}) collective-permute-start(bf16[64,4224]{1,0:T(8,128)(2,1)} %reduce-scatter.3.cloned.1.call-done), channel_id=1, source_target_pairs={{0,2},{2,0},{1,3},{3,1},{4,6},{6,4},{5,7},{7,5},{8,10},{10,8},{9,1... | collective-permute-start | bytes 1622024 | tf_op jit(solution)/shard_map/ppermute | solution.py:545
  378.3 48.7 %collective-permute-start.41 = (bf16[64,4224]{1,0:T(8,128)(2,1)}, bf16[64,4224]{1,0:T(8,128)(2,1)}, u32[]{:S(2)}, u32[]{:S(2)}) collective-permute-start(bf16[64,4224]{1,0:T(8,128)(2,1)} %collective-permute-done.40), channel_id=1, source_target_pairs={{0,2},{2,0},{1,3},{3,1},{4,6},{6,4},{5,7},{7,5},{8,10},{10,8},{9,1... | collective-permute-start | bytes 1622024 | tf_op jit(solution)/shard_map/ppermute | solution.py:545
  391.6 1.9 collective-permute-start.35
  394.9 3.7 collective-permute-start.36
  398.7 3.6 collective-permute-start.32
  402.3 4.1 collective-permute-start.37
  406.4 3.6 collective-permute-start.33
  410.0 4.6 %collective-permute-start.38 = (f32[2944]{0:T(1024)S(1)}, f32[2944]{0:T(1024)S(1)}, u32[]{:S(2)}, u32[]{:S(2)}) collective-permute-start(f32[2944]{0:T(1024)S(1)} %add.149), channel_id=1, source_target_pairs={{0,16},{8,24},{16,0},{24,8},{1,17},{9,25},{17,1},{25,9},{2,18},{10... | collective-permute-start | bytes 35336 | tf_op jit(solution)/shard_map/ppermute | solution.py:885
  414.7 11.7 %collective-permute-start.34 = (f32[1024]{0:T(1024)S(1)}, f32[1024]{0:T(1024)S(1)}, u32[]{:S(2)}, u32[]{:S(2)}) collective-permute-start(f32[1024]{0:T(1024)S(1)} %add.139), channel_id=1, source_target_pairs={{0,16},{8,24},{16,0},{24,8},{1,17},{9,25},{17,1},{25,9},{2,18},{10... | collective-permute-start | bytes 12296 | tf_op jit(solution)/shard_map/ppermute | solution.py:885
  432.8 11.1 %collective-permute-start.43 = (bf16[64,512]{1,0:T(8,128)(2,1)S(1)}, bf16[64,512]{1,0:T(8,128)(2,1)S(1)}, u32[]{:S(2)}, u32[]{:S(2)}) collective-permute-start(bf16[64,512]{1,0:T(8,128)(2,1)S(1)} %slice.68), channel_id=1, source_target_pairs={{0,4},{4,0},{1,5},{5,1},{2,6},{6,2},{3,7},{7,3},{8,12},{12,8},{9,1... | collective-permute-start | bytes 196616 | tf_op jit(solution)/shard_map/ppermute | solution.py:548
  433.7 11.8 %collective-permute-start.42 = (bf16[64,512]{1,0:T(8,128)(2,1)S(1)}, bf16[64,512]{1,0:T(8,128)(2,1)S(1)}, u32[]{:S(2)}, u32[]{:S(2)}) collective-permute-start(bf16[64,512]{1,0:T(8,128)(2,1)S(1)} %slice.68), channel_id=1, source_target_pairs={{0,2},{2,0},{1,3},{3,1},{4,6},{6,4},{5,7},{7,5},{8,10},{10,8},{9,1... | collective-permute-start | bytes 196616 | tf_op jit(solution)/shard_map/ppermute | solution.py:545
  443.9 1.7 collective-permute-start.44
  (65 other events, 608.6 us)
Sparse Core Ops, SparseCore 0:
  10.8 47.9 all-gather.2
  61.6 103.6 all-gather.4
  241.2 118.3 reduce-scatter.2
  363.0 68.9 reduce-scatter.4
